TPU v7x, 128 devices: a whole 4x4x4 slice. The times are simulated.
128 devices in a mesh: tm: 32 (over x, y, core), head: 4 (over z).
Axes of the slice: x: 4, y: 4, z: 4, core: 2. Of those that a mesh axis runs over, the one named last changes fastest.
Arguments:
- activations: bfloat16 [8192, 5120], P('tm'), may hold values from -24 to 24
- frozen_query_weight: bfloat16 [5120, 1024], P(None, 'head'), may hold values from -0.078125 to 0.078125
- frozen_key_weight: bfloat16 [5120, 1024], P(None, 'head'), may hold values from -0.078125 to 0.078125
- frozen_value_weight: bfloat16 [5120, 1024], P(None, 'head'), may hold values from -0.078125 to 0.078125
- query_down_adapter: bfloat16 [5120, 128], replicated, may hold values from -0.078125 to 0.078125
- query_up_adapter: bfloat16 [128, 1024], P(None, 'head'), may hold values from -0.5 to 0.5
- value_down_adapter: bfloat16 [5120, 128], replicated, may hold values from -0.078125 to 0.078125
- value_up_adapter: bfloat16 [128, 1024], P(None, 'head'), may hold values from -0.5 to 0.5
- output_gradient: bfloat16 [8192, 1024], P('tm', 'head'), may hold values from -6 to 6
- levels: int32 [64, 64], replicated, may hold values from 1 to 4, as said below
- key_block_order: int32 [64, 64, 4], replicated, may hold values from 0 to 3, as said below
- slot_true_frame: int32 [64], replicated, may hold values from 0 to 63, each once
Outputs:
- attention_out: bfloat16 [8192, 1024], P('tm', 'head')
- grad_down_q: float32 [5120, 128], replicated
- grad_up_q: float32 [128, 1024], P(None, 'head')
- grad_down_v: float32 [5120, 128], replicated
- grad_up_v: float32 [128, 1024], P(None, 'head')
Inputs may be any that keep to these rules, and one draw needn't show every extreme that they name: levels[f, g] is 4 wherever |f - g| <= 1. Each key_block_order[f, g] is a permutation of the key blocks of one frame.
All inputs are finite; a program needn't handle non-finite values.
Results may differ from a plain program's by a relative error of at most 0.0303.
The roundings to bfloat16 on the way count: a program that leaves them out, or rounds other values in their place, can miss the bound.
Values may be sent and summed in bfloat16 or wider, within the bound.
No kernel may reach another device: no remote copies, remote signals or barrier semaphores. Data moves between devices by JAX's collectives and lax.ppermute only.
A program may use at most 192 MiB of HBM per device.

v0:
```python
import math

import jax
import jax.numpy as jnp
from jax import lax
from jax.sharding import PartitionSpec as P

HEAD_SIZE = 128
FT = 128
BLK = 32


NEGATIVE = -1e30


def slot_table(levels, key_block_order, slot_true_frame):
    frame_count = levels.shape[0]
    block_count = key_block_order.shape[2]
    ranks = jnp.arange(block_count, dtype=jnp.int32)
    hits = (key_block_order[:, :, :, None] == ranks[None, None, None, :]) & (
        ranks[None, None, :, None] < levels[:, :, None, None]
    )
    visible = jnp.sum(hits.astype(jnp.float32), axis=2)
    select = (slot_true_frame[:, None] == jnp.arange(frame_count, dtype=jnp.int32)[None, :]).astype(
        jnp.float32
    )
    slots = jnp.einsum("sf,fgb,tg->stb", select, visible, select)
    return slots.reshape(frame_count, frame_count * block_count)


def block_mask(table, q_start, q_count, k_start, k_count):
    query_slot = (q_start + jnp.arange(q_count, dtype=jnp.int32)) // FT
    key_index = (k_start + jnp.arange(k_count, dtype=jnp.int32)) // BLK
    rows = jnp.take(table, query_slot, axis=0)
    return jnp.take(rows, key_index, axis=1) > 0.5


def masked_scores(query_part, q_start, key_part, k_start, table, score_scale):
    visible = block_mask(table, q_start, query_part.shape[0], k_start, key_part.shape[0])
    scores = (
        jnp.einsum("qhd,khd->hqk", query_part, key_part, preferred_element_type=jnp.float32)
        * score_scale
    )
    return (visible, jnp.where(visible[None], scores, NEGATIVE))


def probabilities(visible, scores, row_peak, row_total):
    return (
        jnp.where(visible[None], jnp.exp(scores - row_peak[:, :, None]), 0.0)
        / row_total[:, :, None]
    )


def local(
    activations,
    frozen_query_weight,
    frozen_key_weight,
    frozen_value_weight,
    query_down_adapter,
    query_up_adapter,
    value_down_adapter,
    value_up_adapter,
    output_gradient,
    levels,
    key_block_order,
    slot_true_frame,
):
    single_float = jnp.float32
    brain_half_float = jnp.bfloat16
    tok_rows = activations.shape[0]
    width = frozen_query_weight.shape[1]
    head_count = width // HEAD_SIZE
    score_scale = HEAD_SIZE ** (-0.5)
    q_start = lax.axis_index("tm") * tok_rows
    query_rank_state = jnp.dot(
        activations, query_down_adapter, preferred_element_type=single_float
    ).astype(brain_half_float)
    value_rank_state = jnp.dot(
        activations, value_down_adapter, preferred_element_type=single_float
    ).astype(brain_half_float)
    query_matrix = (
        jnp.dot(activations, frozen_query_weight, preferred_element_type=single_float)
        + jnp.dot(query_rank_state, query_up_adapter, preferred_element_type=single_float)
    ).astype(brain_half_float)
    keys_local = jnp.dot(
        activations, frozen_key_weight, preferred_element_type=single_float
    ).astype(brain_half_float)
    values_local = (
        jnp.dot(activations, frozen_value_weight, preferred_element_type=single_float)
        + jnp.dot(value_rank_state, value_up_adapter, preferred_element_type=single_float)
    ).astype(brain_half_float)
    table = slot_table(levels, key_block_order, slot_true_frame)
    keys_all, values_all = (
        lax.all_gather(keys_local, "tm", axis=0, tiled=True),
        lax.all_gather(values_local, "tm", axis=0, tiled=True),
    )
    total_rows = keys_all.shape[0]
    key_block = math.gcd(total_rows, 1024)
    block_count = total_rows // key_block
    query_heads = query_matrix.reshape(tok_rows, head_count, HEAD_SIZE)
    grad_heads = output_gradient.reshape(tok_rows, head_count, HEAD_SIZE)
    key_blocks = keys_all.reshape(block_count, key_block, head_count, HEAD_SIZE)
    value_blocks = values_all.reshape(block_count, key_block, head_count, HEAD_SIZE)
    block_starts = jnp.arange(block_count, dtype=jnp.int32) * key_block

    def stat_step(carry, block_item):
        row_peak, row_total = carry
        key_part, start = block_item
        visible, scores = masked_scores(query_heads, q_start, key_part, start, table, score_scale)
        new_peak = jnp.maximum(row_peak, jnp.max(scores, axis=2))
        weights_raw = jnp.where(visible[None], jnp.exp(scores - new_peak[:, :, None]), 0.0)
        row_total = row_total * jnp.exp(row_peak - new_peak) + jnp.sum(weights_raw, axis=2)
        return ((new_peak, row_total), scores)

    start_stats = (
        jnp.full((head_count, tok_rows), NEGATIVE, single_float),
        jnp.zeros((head_count, tok_rows), single_float),
    )
    (row_peak, row_total), score_blocks = lax.scan(
        stat_step, start_stats, (key_blocks, block_starts)
    )

    def stored_probs(scores, start):
        visible = block_mask(table, q_start, tok_rows, start, key_block)
        return probabilities(visible, scores, row_peak, row_total)

    empty_out = jnp.zeros((tok_rows, head_count, HEAD_SIZE), single_float)

    def out_step(accum, block_item):
        scores, value_part, start = block_item
        probs_low = stored_probs(scores, start).astype(brain_half_float)
        term = jnp.einsum(
            "hqk,qhd->khd", probs_low, grad_heads, preferred_element_type=single_float
        ).reshape(key_block, width)
        return (
            accum
            + jnp.einsum(
                "hqk,khd->qhd", probs_low, value_part, preferred_element_type=single_float
            ),
            term,
        )

    accum, value_terms = lax.scan(out_step, empty_out, (score_blocks, value_blocks, block_starts))
    value_terms = value_terms.reshape(total_rows, width)
    attended = accum.astype(brain_half_float)
    row_delta = jnp.sum(grad_heads.astype(single_float) * attended.astype(single_float), axis=2).T

    def grad_step(accum, block_item):
        scores, key_part, value_part, start = block_item
        probs = stored_probs(scores, start)
        prob_grad = jnp.einsum(
            "qhd,khd->hqk", grad_heads, value_part, preferred_element_type=single_float
        )
        score_grad = (probs * (prob_grad - row_delta[:, :, None]) * score_scale).astype(
            brain_half_float
        )
        return (
            accum
            + jnp.einsum("hqk,khd->qhd", score_grad, key_part, preferred_element_type=single_float),
            None,
        )

    accum, unused = lax.scan(
        grad_step, empty_out, (score_blocks, key_blocks, value_blocks, block_starts)
    )
    query_gradient = accum.astype(brain_half_float).reshape(tok_rows, width)
    value_gradient = lax.psum_scatter(value_terms, "tm", scatter_dimension=0, tiled=True)
    value_gradient = value_gradient.astype(brain_half_float)
    up_grad_q = jnp.einsum(
        "tr,tw->rw", query_rank_state, query_gradient, preferred_element_type=single_float
    )
    up_grad_v = jnp.einsum(
        "tr,tw->rw", value_rank_state, value_gradient, preferred_element_type=single_float
    )
    query_rank_gradient = jnp.einsum(
        "ug,pg->up", query_gradient, query_up_adapter, preferred_element_type=single_float
    )
    value_rank_gradient = jnp.einsum(
        "ug,pg->up", value_gradient, value_up_adapter, preferred_element_type=single_float
    )
    query_rank_gradient, value_rank_gradient = lax.psum(
        (query_rank_gradient, value_rank_gradient), "head"
    )
    down_grad_q = jnp.einsum(
        "td,tr->dr",
        activations,
        query_rank_gradient.astype(brain_half_float),
        preferred_element_type=single_float,
    )
    down_grad_v = jnp.einsum(
        "td,tr->dr",
        activations,
        value_rank_gradient.astype(brain_half_float),
        preferred_element_type=single_float,
    )
    down_grad_q, up_grad_q, down_grad_v, up_grad_v = lax.psum(
        (down_grad_q, up_grad_q, down_grad_v, up_grad_v), "tm"
    )
    return (attended.reshape(tok_rows, width), down_grad_q, up_grad_q, down_grad_v, up_grad_v)


def solution(mesh):
    return jax.shard_map(
        local,
        mesh=mesh,
        in_specs=(
            P("tm", None),
            P(None, "head"),
            P(None, "head"),
            P(None, "head"),
            P(),
            P(None, "head"),
            P(),
            P(None, "head"),
            P("tm", "head"),
            P(),
            P(),
            P(),
        ),
        out_specs=(P("tm", "head"), P(), P(None, "head"), P(), P(None, "head")),
        check_vma=False,
    )
```

profile of v0, /device:TPU:1, one launch (start us, length us, event | category | flops | bytes accessed | tf_op | source)
XLA Modules:
  0.0 749.9 jit_solution(13342292469825118955)
XLA Ops:
  22.7 39.2 %all-gather.5.cloned.1.call-done = bf16[8192,256]{1,0:T(8,128)(2,1)} async-done(((bf16[256,256]{1,0:T(8,128)(2,1)}), bf16[8192,256]{1,0:T(8,128)(2,1)}) %all-gather.5.cloned.1.call-update) | async-done | bytes 4194320 | tf_op jit(solution)/shard_map/all_gather | solution.py:94
  61.9 6.9 reshape.67
  68.8 130.5 %while.48 = (s32[]{:T(128)}, f32[2,256]{1,0:T(2,128)S(1)}, f32[2,256]{1,0:T(2,128)S(1)}, f32[8,2,256,1024]{2,3,1,0:T(8,128)}, s32[]{:T(128)}, /*index=5*/f32[64,...) while((s32[]{:T(128)}, f32[2,256]{1,0:T(2,128)S(1)}, ...), condition=%wide.region_4.7_spmd.clone, body=%wide.region_1.6_spmd.clone.sunk | while | flops 138010368 | bytes 24555728 | solution.py:119
  71.4 4.7 gather_fusion.1
  87.7 4.7 gather_fusion.1
  104.1 4.7 gather_fusion.1
  120.4 4.7 gather_fusion.1
  136.7 4.7 gather_fusion.1
  153.0 4.7 gather_fusion.1
  169.3 4.7 gather_fusion.1
  185.6 4.7 gather_fusion.1
  199.3 6.9 reshape.65
  206.2 249.6 %while.49 = (s32[]{:T(128)}, f32[256,2,128]{0,2,1:T(8,128)S(1)}, f32[8,1024,256]{2,1,0:T(8,128)}, bf16[8,1024,2,128]{3,2,1,0:T(2,128)(2,1)}, s32[]{:T(128)}, /*i...) while((s32[]{:T(128)}, f32[256,2,128]{0,2,1:T(8,128)S(1)}, ...), condition=%wide.region_6.9_spmd.clone, body=%wide.region_5.8_spmd.clone.sunk | while | flops 271308032 | bytes 32135364 | solution.py:143
  208.7 4.7 gather_fusion.3
  239.9 4.7 gather_fusion.3
  271.1 4.7 gather_fusion.3
  302.3 4.7 gather_fusion.3
  333.5 4.7 gather_fusion.3
  364.7 4.7 gather_fusion.3
  395.9 4.7 gather_fusion.3
  427.0 4.7 gather_fusion.3
  458.3 135.9 %while.50 = (s32[]{:T(128)}, f32[256,2,128]{0,2,1:T(8,128)}, bf16[8,1024,2,128]{3,2,1,0:T(2,128)(2,1)}, s32[]{:T(128)}, f32[64,256]{1,0:T(8,128)S(1)}, /*index=5...) while((s32[]{:T(128)}, f32[256,2,128]{0,2,1:T(8,128)}, ...), condition=%wide.region_9.12_spmd.clone, body=%wide.region_8.11_spmd.clone.sunk | while | flops 272880896 | bytes 12214611 | solution.py:163
  460.8 4.7 gather_fusion.5
  477.9 4.7 gather_fusion.5
  495.0 4.7 gather_fusion.5
  512.5 4.7 gather_fusion.5
  529.4 4.7 gather_fusion.5
  546.3 4.7 gather_fusion.5
  563.1 4.7 gather_fusion.5
  579.9 4.7 gather_fusion.5
  599.1 16.9 %all-reduce.6 = (bf16[256,128]{1,0:T(8,128)(2,1)S(1)}, bf16[256,128]{1,0:T(8,128)(2,1)S(1)}) all-reduce(f32[256,128]{1,0:T(8,128)S(1)} %fusion.55, f32[256,128]{1,0:T(8,128)S(1)} %fusion.43), channel_id=1, replica_groups=mesh['tm'=32,'head'=4] {'head'}, use_global_device_ids=true, to_apply=%region_10.13 | all-reduce | flops 65536 | bytes 393216 | tf_op jit(solution)/shard_map/psum | solution.py:181
  622.6 113.0 %all-reduce.5.cloned.1.call-done = (f32[5120,128]{0,1:T(8,128)}, f32[128,256]{1,0:T(8,128)}, f32[5120,128]{0,1:T(8,128)}, f32[128,256]{1,0:T(8,128)}) async-done(((f32[5120,128]{0,1:T(8,128)}, f32[128,256]{1,0:T(8,128)}, f32[5120,128]{0,1:T(8,128)}, f32[128,256]{1,0:T(8,128)}), (f32[5120,128]{0,1:T(8,128)}, f32[128,256]{1,0:T(8,128)}, f32[5120,128]{0,1:T(8,128)}, ...) | async-done | bytes 5505040 | tf_op jit(solution)/shard_map/psum | solution.py:196
  (546 shorter events, 438.5 us)
Async XLA Ops:
  7.2 54.7 %all-gather.5.cloned.1.call-start = ((), (), s32[]{:S(2)}) async-start(), calls=%async_computation.2 | async-start | bytes 4325376 | tf_op jit(solution)/shard_map/all_gather | solution.py:94
  12.2 187.1 %all-gather.3.cloned.1.call-start = ((), (), s32[]{:S(2)}) async-start(), calls=%async_computation.1 | async-start | bytes 4325376 | tf_op jit(solution)/shard_map/all_gather | solution.py:95
  12.2 2.3 copy-start.17
  14.6 2.2 copy-start.16
  16.3 581.6 %reduce-scatter.2.cloned.1.call-start = ((), (), s32[]{:S(2)}) async-start(), calls=%async_computation.3 | async-start | bytes 8650752 | tf_op jit(solution)/shard_map/reduce_scatter | solution.py:167
  17.4 2.3 copy-start.4
  22.0 46.8 %copy-start.3 = (bf16[256,256]{0,1:T(8,128)(2,1)}, bf16[256,256]{0,1:T(8,128)(2,1)S(1)}, u32[]{:S(2)}) copy-start(bf16[256,256]{0,1:T(8,128)(2,1)S(1)} %copy.116) | copy-start | bytes 393220
  71.3 8.3 %copy-start.12 = (bf16[256,2,128]{2,0,1:T(8,128)(2,1)S(1)}, bf16[256,2,128]{2,0,1:T(8,128)(2,1)}, u32[]{:S(2)}) copy-start(bf16[256,2,128]{2,0,1:T(8,128)(2,1)} %get-tuple-element.1114) | copy-start | bytes 393220 | tf_op jit(solution)/shard_map/while
  81.4 2.3 copy-start.2
  87.7 8.3 %copy-start.12 = (bf16[256,2,128]{2,0,1:T(8,128)(2,1)S(1)}, bf16[256,2,128]{2,0,1:T(8,128)(2,1)}, u32[]{:S(2)}) copy-start(bf16[256,2,128]{2,0,1:T(8,128)(2,1)} %get-tuple-element.1114) | copy-start | bytes 393220 | tf_op jit(solution)/shard_map/while
  97.8 2.3 copy-start.2
  104.1 8.3 %copy-start.12 = (bf16[256,2,128]{2,0,1:T(8,128)(2,1)S(1)}, bf16[256,2,128]{2,0,1:T(8,128)(2,1)}, u32[]{:S(2)}) copy-start(bf16[256,2,128]{2,0,1:T(8,128)(2,1)} %get-tuple-element.1114) | copy-start | bytes 393220 | tf_op jit(solution)/shard_map/while
  114.1 2.2 copy-start.2
  120.4 8.3 %copy-start.12 = (bf16[256,2,128]{2,0,1:T(8,128)(2,1)S(1)}, bf16[256,2,128]{2,0,1:T(8,128)(2,1)}, u32[]{:S(2)}) copy-start(bf16[256,2,128]{2,0,1:T(8,128)(2,1)} %get-tuple-element.1114) | copy-start | bytes 393220 | tf_op jit(solution)/shard_map/while
  130.4 2.2 copy-start.2
  136.7 8.3 %copy-start.12 = (bf16[256,2,128]{2,0,1:T(8,128)(2,1)S(1)}, bf16[256,2,128]{2,0,1:T(8,128)(2,1)}, u32[]{:S(2)}) copy-start(bf16[256,2,128]{2,0,1:T(8,128)(2,1)} %get-tuple-element.1114) | copy-start | bytes 393220 | tf_op jit(solution)/shard_map/while
  146.7 2.2 copy-start.2
  153.0 8.3 %copy-start.12 = (bf16[256,2,128]{2,0,1:T(8,128)(2,1)S(1)}, bf16[256,2,128]{2,0,1:T(8,128)(2,1)}, u32[]{:S(2)}) copy-start(bf16[256,2,128]{2,0,1:T(8,128)(2,1)} %get-tuple-element.1114) | copy-start | bytes 393220 | tf_op jit(solution)/shard_map/while
  163.1 2.2 copy-start.2
  169.3 8.3 %copy-start.12 = (bf16[256,2,128]{2,0,1:T(8,128)(2,1)S(1)}, bf16[256,2,128]{2,0,1:T(8,128)(2,1)}, u32[]{:S(2)}) copy-start(bf16[256,2,128]{2,0,1:T(8,128)(2,1)} %get-tuple-element.1114) | copy-start | bytes 393220 | tf_op jit(solution)/shard_map/while
  185.6 8.3 %copy-start.12 = (bf16[256,2,128]{2,0,1:T(8,128)(2,1)S(1)}, bf16[256,2,128]{2,0,1:T(8,128)(2,1)}, u32[]{:S(2)}) copy-start(bf16[256,2,128]{2,0,1:T(8,128)(2,1)} %get-tuple-element.1114) | copy-start | bytes 393220 | tf_op jit(solution)/shard_map/while
  457.6 277.9 %all-reduce.5.cloned.1.call-start = ((), (), s32[]{:S(2)}) async-start(), calls=%async_computation.4 | async-start | bytes 11010048 | tf_op jit(solution)/shard_map/psum | solution.py:196
  471.6 3.8 copy-start.20
  488.7 3.8 copy-start.20
  505.6 4.3 copy-start.20
  523.2 3.7 copy-start.20
  540.1 3.7 copy-start.20
  556.9 3.6 copy-start.20
  573.8 3.6 copy-start.20
  590.6 3.6 copy-start.20
  738.8 3.3 copy-start.14
  738.8 3.9 copy-start.13
  (21 other events, 35.9 us)
Sparse Core Ops, SparseCore 0:
  12.3 49.5 all-gather.4
  64.8 45.3 all-gather.2
  457.8 89.7 reduce-scatter.1
  621.0 114.4 all-reduce.4
where the time goes:
time: 755 us; the launch traced here: 750 us
  local copies, waits for them, and re-layouts  351 us (46%)
  waiting for transfers between devices  152 us (20%)
  other arithmetic  116 us (15%)
  matrix products  96.5 us (13%)
  blocking collectives  16.9 us (2%)
  between operations  14.1 us (2%)
    psum x1, waiting for transfers between devices, local(): lax.psum((down_grad_q, up_grad_q, down_grad_v, up_grad_v), 'tm')  113 us
    gather x24, local copies, waits for them, and re-layouts, block_mask(): return jnp.take(rows, key_index, axis=1) > 0.5  112 us
    dynamic_slice x64, local copies, waits for them, and re-layouts, local(): lax.scan(stat_step, start_stats, (key_blocks, block_starts))  83.9 us
    dynamic_slice x16, local copies, waits for them, and re-layouts, local(): lax.scan(out_step, empty_out, (score_blocks, value_blocks, block_starts))  47.4 us
    all_gather x1, waiting for transfers between devices, local(): lax.all_gather(keys_local, 'tm', axis=0, tiled=True)  39.2 us
    dynamic_update_slice x16, local copies, waits for them, and re-layouts, local(): lax.scan(out_step, empty_out, (score_blocks, value_blocks, block_starts))  38.5 us
    gt x24, other arithmetic, block_mask(): return jnp.take(rows, key_index, axis=1) > 0.5  36.2 us
    dot_general x8, matrix products, grad_step(): jnp.einsum('hqk,khd->qhd', score_grad, key_part, preferred_element_type=s...  30.1 us
  transfers between devices with their start and end apart: 4, of which 2 were waited for; matrix products, arithmetic and copies ran while one was open for 38% of the time, Pallas kernels for 0%

commit v1 on v0

v1 whole, which is shorter than its diff:
```python
import math

import jax
import jax.numpy as jnp
from jax import lax
from jax.experimental import pallas as pl
from jax.experimental.pallas import tpu as pltpu
from jax.sharding import Mesh
from jax.sharding import PartitionSpec as P

HEAD = 128
FT = 128
BLK = 32
RANK = 128
CHUNK = 256
CB = CHUNK // BLK
SCALE = HEAD ** -0.5
SCALE2 = SCALE * math.log2(math.e)
NEG = -1e30
f32 = jnp.float32
bf16 = jnp.bfloat16
WIRE = bf16
VMEM = pl.BlockSpec(memory_space=pltpu.VMEM)
SMEM = pl.BlockSpec(memory_space=pltpu.SMEM)
PARAMS = pltpu.CompilerParams(vmem_limit_bytes=48 * 1024 * 1024)


def dot(a, b, ca=1, cb=0):
    return lax.dot_general(a, b, (((ca,), (cb,)), ((), ())), preferred_element_type=f32)


def proj_kernel(pos, act, wq, wk, wv, dq, dv, uq, uv, kv_keep, kv_send, q_keep, q_send, rank, aq, ak, av, ar):
    step = pl.program_id(0)

    @pl.when(step == 0)
    def _():
        aq[...] = jnp.zeros_like(aq)
        ak[...] = jnp.zeros_like(ak)
        av[...] = jnp.zeros_like(av)
        ar[...] = jnp.zeros_like(ar)

    a = act[...]
    ak[...] += dot(a, wk[...])
    av[...] += dot(a, wv[...])
    aq[...] += dot(a, wq[...])
    ar[:, :RANK] += dot(a, dq[...])
    ar[:, RANK:] += dot(a, dv[...])

    @pl.when(step == pl.num_programs(0) - 1)
    def _():
        low = ar[...].astype(bf16)
        rank[...] = low
        query = (aq[...] + dot(low[:, :RANK], uq[...])).astype(bf16)
        keys = ak[...].astype(bf16)
        values = (av[...] + dot(low[:, RANK:], uv[...])).astype(bf16)

        def put(kv, q, at):
            kv[:, :HEAD] = keys[:, at:at + HEAD]
            kv[:, HEAD:] = values[:, at:at + HEAD]
            q[...] = query[:, at:at + HEAD]

        @pl.when(pos[2] == 0)
        def _():
            put(kv_keep, q_keep, 0)
            put(kv_send, q_send, HEAD)

        @pl.when(pos[2] == 1)
        def _():
            put(kv_keep, q_keep, HEAD)
            put(kv_send, q_send, 0)


def project(pos, act, wq, wk, wv, dq, dv, uq, uv):
    rows, width = act.shape
    kt = 512
    cols = wq.shape[1]
    weight = pl.BlockSpec((kt, cols), lambda k: (k, 0))
    down = pl.BlockSpec((kt, RANK), lambda k: (k, 0))
    whole = lambda shape: pl.BlockSpec(shape, lambda k: (0, 0))
    shapes = [(rows, 2 * HEAD), (rows, 2 * HEAD), (rows, HEAD), (rows, HEAD), (rows, 2 * RANK)]
    return pl.pallas_call(
        proj_kernel,
        grid=(width // kt,),
        in_specs=[SMEM, pl.BlockSpec((rows, kt), lambda k: (0, k)), weight, weight, weight, down, down,
                  whole(uq.shape), whole(uv.shape)],
        out_specs=[whole(s) for s in shapes],
        out_shape=[jax.ShapeDtypeStruct(s, bf16) for s in shapes],
        scratch_shapes=[pltpu.VMEM((rows, cols), f32)] * 3 + [pltpu.VMEM((rows, 2 * RANK), f32)],
        compiler_params=PARAMS,
        cost_estimate=pl.CostEstimate(flops=2 * rows * width * 1024, bytes_accessed=13 << 20, transcendentals=0),
        name="project",
    )(pos, act, wq, wk, wv, dq, dv, uq, uv)


def lists_kernel(pos, slot, levels, order, out):
    x, y, c = pos[0], pos[1], pos[2]

    def frame(xx, yy, local):
        core = c if local < 2 else 1 - c
        return slot[((xx * 4 + yy) * 2 + core) * 2 + local % 2]

    for k in range(16):
        out[17, k] = frame(lax.rem(x + 4 - k // 4, 4), y, k % 4)
        out[18, k] = frame(x, lax.rem(y + 4 - k // 4, 4), k % 4)

    def one(q, _):
        f = out[18, q]

        def pair(k, n):
            g = out[17, k]
            for r in range(4):
                out[q, n + r] = k * 4 + order[f, g * 4 + r]
            return n + levels[f, g]

        n = lax.fori_loop(0, 16, pair, 0)
        for r in range(CB):
            out[q, n + r] = 0
        out[16, q] = n
        return 0

    lax.fori_loop(0, 16, one, 0)


def visible_lists(pos, slot, levels, order):
    return pl.pallas_call(
        lists_kernel,
        in_specs=[SMEM] * 4,
        out_specs=SMEM,
        out_shape=jax.ShapeDtypeStruct((24, 128), jnp.int32),
        name="lists",
    )(pos, slot, levels, order.reshape(64, 256))


def load_chunk(lists, f, ch, kvall, kvc):
    for i in range(CB):
        at = pl.multiple_of(lists[f, ch * CB + i] * BLK, BLK)
        kvc[i * BLK:(i + 1) * BLK, :] = kvall[pl.ds(at, BLK), :]


def fill_all(parts, whole):
    rows = parts[0].shape[0]
    for d, part in enumerate(parts):
        whole[d * rows:(d + 1) * rows, :] = part[...]


def stats_kernel(lists, q0, q1, q2, q3, g0, g1, g2, g3, k0, k1, k2, k3, out, qall, gall, kvall, kvc, both):
    fill_all((q0, q1, q2, q3), qall)
    fill_all((g0, g1, g2, g3), gall)
    fill_all((k0, k1, k2, k3), kvall)
    both[...] = jnp.zeros_like(both)
    row = lax.broadcasted_iota(jnp.int32, (CHUNK, HEAD), 0)

    def frame(f, _):
        at = pl.multiple_of(f * FT, FT)
        both[:FT, :HEAD] = qall[pl.ds(at, FT), :]
        both[FT:, HEAD:] = gall[pl.ds(at, FT), :]
        n = lists[16, f]

        def chunk(ch, carry):
            peak, total, delta = carry
            load_chunk(lists, f, ch, kvall, kvc)
            r = dot(kvc[...], both[...], 1, 1)
            s = jnp.where(row < (n - ch * CB) * BLK, r[:, :FT] * SCALE2, NEG)
            new = jnp.maximum(peak, jnp.max(s, axis=0, keepdims=True))
            p = jnp.exp2(s - new)
            fix = jnp.exp2(peak - new)
            total = total * fix + jnp.sum(p, axis=0, keepdims=True)
            delta = delta * fix + jnp.sum(p * r[:, FT:], axis=0, keepdims=True)
            return new, total, delta

        zero = jnp.zeros((1, FT), f32)
        peak, total, delta = lax.fori_loop(0, (n + CB - 1) // CB, chunk, (zero + NEG, zero, zero))
        out[pl.ds(f, 1), :] = peak
        out[pl.ds(16 + f, 1), :] = total
        out[pl.ds(32 + f, 1), :] = delta
        return 0

    lax.fori_loop(0, 16, frame, 0)


def row_stats(lists, qs, gs, kvs):
    return pl.pallas_call(
        stats_kernel,
        in_specs=[SMEM] + [VMEM] * 12,
        out_specs=VMEM,
        out_shape=jax.ShapeDtypeStruct((48, 128), f32),
        scratch_shapes=[pltpu.VMEM((2048, HEAD), bf16), pltpu.VMEM((2048, HEAD), bf16),
                        pltpu.VMEM((2048, 2 * HEAD), bf16), pltpu.VMEM((CHUNK, 2 * HEAD), bf16),
                        pltpu.VMEM((2 * FT, 2 * HEAD), bf16)],
        compiler_params=PARAMS,
        name="row_stats",
    )(lists, *qs, *gs, *kvs)


def grads_kernel(lists, s0, s1, s2, s3, q0, q1, q2, q3, g0, g1, g2, g3, k0, k1, k2, k3,
                 a0, a1, a2, a3, b0, b1, b2, b3, qall, gall, kvall, kvc, both, pair, acc, dva, norm):
    fill_all((q0, q1, q2, q3), qall)
    fill_all((g0, g1, g2, g3), gall)
    fill_all((k0, k1, k2, k3), kvall)
    both[...] = jnp.zeros_like(both)
    dva[...] = jnp.zeros_like(dva)
    for t in range(4):
        rows = [slice(4 * ((t - d) % 4), 4 * ((t - d) % 4) + 4) for d in range(4)]
        stats = [ref[...] for ref in (s0, s1, s2, s3)]
        peaks = [stats[d][0:16][rows[d]] for d in range(4)]
        peak = jnp.maximum(jnp.maximum(peaks[0], peaks[1]), jnp.maximum(peaks[2], peaks[3]))
        total = jnp.zeros_like(peak)
        delta = jnp.zeros_like(peak)
        for d in range(4):
            fix = jnp.exp2(peaks[d] - peak)
            total += fix * stats[d][16:32][rows[d]]
            delta += fix * stats[d][32:48][rows[d]]
        norm[4 * t:4 * t + 4, :] = peak + jnp.log2(total)
        norm[16 + 4 * t:20 + 4 * t, :] = delta / total
    row = lax.broadcasted_iota(jnp.int32, (CHUNK, HEAD), 0)

    def frame(f, _):
        at = pl.multiple_of(f * FT, FT)
        both[:FT, :HEAD] = qall[pl.ds(at, FT), :]
        both[FT:, HEAD:] = gall[pl.ds(at, FT), :]
        n = lists[16, f]
        lse = norm[pl.ds(f, 1), :]
        delta = norm[pl.ds(16 + f, 1), :]
        acc[pl.ds(at, FT), :] = jnp.zeros((FT, 2 * HEAD), f32)

        def chunk(ch, _):
            load_chunk(lists, f, ch, kvall, kvc)
            kv = kvc[...]
            r = dot(kv, both[...], 1, 1)
            s = jnp.where(row < (n - ch * CB) * BLK, r[:, :FT] * SCALE2, NEG)
            p = jnp.exp2(s - lse)
            low = p.astype(bf16)
            pair[:, :FT] = low
            pair[:, FT:] = (p * (r[:, FT:] - delta) * SCALE).astype(bf16)
            product = dot(pair[...], kv, 0, 0)
            acc[pl.ds(at, FT), :HEAD] += product[:FT, HEAD:]
            acc[pl.ds(at, FT), HEAD:] += product[FT:, :HEAD]
            dv = dot(low, gall[pl.ds(at, FT), :])
            for i in range(CB):
                to = pl.multiple_of(lists[f, ch * CB + i] * BLK, BLK)
                dva[pl.ds(to, BLK), :] += dv[i * BLK:(i + 1) * BLK, :]
            return 0

        lax.fori_loop(0, (n + CB - 1) // CB, chunk, 0)
        return 0

    lax.fori_loop(0, 16, frame, 0)
    for d, (a, b) in enumerate(zip((a0, a1, a2, a3), (b0, b1, b2, b3))):
        a[...] = acc[d * 512:(d + 1) * 512, :].astype(a.dtype)
        b[...] = dva[d * 512:(d + 1) * 512, :].astype(b.dtype)


def attention_grads(lists, stats, qs, gs, kvs):
    wire = [f32, WIRE, WIRE, WIRE]
    return pl.pallas_call(
        grads_kernel,
        in_specs=[SMEM] + [VMEM] * 16,
        out_specs=[VMEM] * 8,
        out_shape=[jax.ShapeDtypeStruct((512, 2 * HEAD), t) for t in wire]
        + [jax.ShapeDtypeStruct((512, HEAD), t) for t in wire],
        scratch_shapes=[pltpu.VMEM((2048, HEAD), bf16), pltpu.VMEM((2048, HEAD), bf16),
                        pltpu.VMEM((2048, 2 * HEAD), bf16), pltpu.VMEM((CHUNK, 2 * HEAD), bf16),
                        pltpu.VMEM((2 * FT, 2 * HEAD), bf16), pltpu.VMEM((CHUNK, 2 * FT), bf16),
                        pltpu.VMEM((2048, 2 * HEAD), f32), pltpu.VMEM((2048, HEAD), f32),
                        pltpu.VMEM((32, 128), f32)],
        compiler_params=PARAMS,
        name="attention_grads",
    )(lists, *stats, *qs, *gs, *kvs)


def finish_kernel(pos, a0, a1, a2, a3, b0, b1, b2, b3, rank_own, rank_other, uq, uv,
                  o_keep, o_send, rg_keep, rg_send, up):
    total = a0[...] + a1[...].astype(f32) + a2[...].astype(f32) + a3[...].astype(f32)
    out = total[:, :HEAD].astype(bf16)
    dq = total[:, HEAD:].astype(bf16)
    dv = (b0[...] + b1[...].astype(f32) + b2[...].astype(f32) + b3[...].astype(f32)).astype(bf16)
    o_keep[...] = out[:256]
    o_send[...] = out[256:]

    def rest(c):
        at = c * HEAD
        upq = uq[:, at:at + HEAD]
        upv = uv[:, at:at + HEAD]
        gq = dot(dq, upq, 1, 1)
        gv = dot(dv, upv, 1, 1)
        rg_keep[:, :RANK] = gq[:256]
        rg_keep[:, RANK:] = gv[:256]
        rg_send[:, :RANK] = gq[256:]
        rg_send[:, RANK:] = gv[256:]
        up[...] = jnp.zeros_like(up)
        up[:RANK, at:at + HEAD] = (dot(rank_own[:, :RANK], dq[:256], 0, 0)
                                   + dot(rank_other[:, :RANK], dq[256:], 0, 0))
        up[RANK:, at:at + HEAD] = (dot(rank_own[:, RANK:], dv[:256], 0, 0)
                                   + dot(rank_other[:, RANK:], dv[256:], 0, 0))

    for c in range(2):
        pl.when(pos[2] == c)(lambda c=c: rest(c))


def finish(pos, a, b, rank_own, rank_other, uq, uv):
    shapes = [((256, HEAD), bf16), ((256, HEAD), bf16), ((256, 256), f32), ((256, 256), f32), ((256, 256), f32)]
    return pl.pallas_call(
        finish_kernel,
        in_specs=[SMEM] + [VMEM] * 12,
        out_specs=[VMEM] * 5,
        out_shape=[jax.ShapeDtypeStruct(s, t) for s, t in shapes],
        compiler_params=PARAMS,
        name="finish",
    )(pos, *a, *b, rank_own, rank_other, uq, uv)


def ring(n, d):
    return [(i, (i + d) % n) for i in range(n)]


def swap(a):
    return lax.ppermute(a, "c", ring(2, 1))


def spread(a, axis):
    return [a] + [lax.ppermute(a, axis, ring(4, d)) for d in (1, 3, 2)]


def reorder(parts):
    return [parts[0], parts[1], parts[3], parts[2]]


def collect(parts, axis):
    return [parts[0]] + [lax.ppermute(parts[d], axis, ring(4, -d)) for d in (1, 2, 3)]


def half(a, index, size):
    return lax.dynamic_slice_in_dim(a, index * size, size, axis=1)


def local(act, wq, wk, wv, dq, uq, dv, uv, grad_out, levels, order, slot):
    x, y, c, z = (lax.axis_index(n).astype(jnp.int32) for n in ("x", "y", "c", "z"))
    pos = jnp.stack([x, y, c, z])
    g_other = swap(half(grad_out, 1 - c, HEAD))
    g = jnp.concatenate([half(grad_out, c, HEAD), g_other], axis=0)
    gs = reorder(spread(g, "y"))
    kv_keep, kv_send, q_keep, q_send, rank = project(pos, act, wq, wk, wv, dq, dv, uq, uv)
    kv = jnp.concatenate([kv_keep, swap(kv_send)], axis=0)
    kvs = reorder(spread(kv, "x"))
    q = jnp.concatenate([q_keep, swap(q_send)], axis=0)
    qs = reorder(spread(q, "y"))
    rank_other = swap(rank)
    lists = visible_lists(pos, slot, levels, order)
    stats = reorder(spread(row_stats(lists, qs, gs, kvs), "y"))
    parts = attention_grads(lists, stats, qs, gs, kvs)
    a = collect(parts[:4], "y")
    b = collect(parts[4:], "x")
    o_keep, o_send, rg_keep, rg_send, up = finish(pos, a, b, rank, rank_other, uq, uv)
    rg = rg_keep + swap(rg_send)
    rgs = spread(rg, "z")
    rank_grad = (rgs[0] + rgs[1] + rgs[2] + rgs[3]).astype(bf16)
    up = lax.psum(up, ("x", "y", "c"))
    o_other = swap(o_send)
    attended = jnp.where(c == 0, jnp.concatenate([o_keep, o_other], axis=1),
                         jnp.concatenate([o_other, o_keep], axis=1))
    cols = act.shape[1] // 4
    down = dot(half(act, z, cols), rank_grad, 0, 0)
    mine = lax.dynamic_slice_in_dim(down, c * (cols // 2), cols // 2, axis=0)
    theirs = swap(lax.dynamic_slice_in_dim(down, (1 - c) * (cols // 2), cols // 2, axis=0))
    down = lax.all_to_all(mine + theirs, ("x", "y"), 0, 0, tiled=True)
    down = jnp.sum(down.reshape(16, cols // 32, 256), axis=0).astype(bf16)
    wide = jnp.broadcast_to(down[None], (64, cols // 32, 256)).reshape(2 * cols, 256)
    wide = lax.all_to_all(wide, ("z", "x", "y"), 0, 0, tiled=True)
    other = swap(wide)
    first = jnp.where(c == 0, wide, other).reshape(4, 1, cols // 2, 256)
    second = jnp.where(c == 0, other, wide).reshape(4, 1, cols // 2, 256)
    full = jnp.concatenate([first, second], axis=1).reshape(4 * cols, 256).astype(f32)
    return attended, full[:, :RANK], up[:RANK], full[:, RANK:], up[RANK:]


def solution(mesh):
    torus = Mesh(mesh.devices.reshape(4, 4, 2, 4), ("x", "y", "c", "z"))
    tm = ("x", "y", "c")
    return jax.shard_map(
        local,
        mesh=torus,
        in_specs=(
            P(tm, None),
            P(None, "z"),
            P(None, "z"),
            P(None, "z"),
            P(),
            P(None, "z"),
            P(),
            P(None, "z"),
            P(tm, "z"),
            P(),
            P(),
            P(),
        ),
        out_specs=(P(tm, "z"), P(), P(None, "z"), P(), P(None, "z")),
        check_vma=False,
    )
```

time: 755 us -> 305 us (0.40)
  local copies, waits for them, and re-layouts: 351 us -> 13 us
  other arithmetic: 116 us -> 2.02 us
  matrix products: 96.5 us -> 1.49 us
  Pallas kernels: 0 us -> 68.2 us
  starting transfers between devices: 0.56 us -> 42.8 us
  waiting for transfers between devices: 152 us -> 121 us
  blocking collectives: 16.9 us -> 42.3 us
    gather x48 -> x0, local copies, waits for them, and re-layouts: 136 us -> none  [the longest x24 112 us: block_mask(): return jnp.take(rows, key_index, axis=1) > 0.5]
    dynamic_slice x80 -> x2, local copies, waits for them, and re-layouts: 131 us -> 0.94 us  [the longest x1 0.89 us: half(): return lax.dynamic_slice_in_dim(a, index * size, size, axis=1)]
    dot_general x46 -> x1, matrix products: 96.5 us -> 1.49 us  [dot(): lax.dot_general(a, b, (((ca,), (cb,)), ((), ())), preferred_element_type=...]
    pallas_call x0 -> x5, Pallas kernels: none -> 68.2 us  [the longest x1 30.1 us: attention_grads(): pl.pallas_call(grads_kernel, in_specs=[SMEM] + [VMEM] * 16, out_specs=[VM...]
    dynamic_update_slice x24 -> x0, local copies, waits for them, and re-layouts: 50.3 us -> none  [the longest x16 38.5 us: local(): lax.scan(out_step, empty_out, (score_blocks, value_blocks, block_starts))]
    ppermute x0 -> x29, starting transfers between devices: none -> 42.8 us  [the longest x15 22.8 us: spread(): return [a] + [lax.ppermute(a, axis, ring(4, d)) for d in (1, 3, 2)]]
    all_to_all x0 -> x2, blocking collectives: none -> 42.3 us  [the longest x1 25.3 us: local(): wide = lax.all_to_all(wide, ('z', 'x', 'y'), 0, 0, tiled=True)]
    all_gather x2 -> x0, waiting for transfers between devices: 39.2 us -> none  [the longest x1 39.2 us: local(): lax.all_gather(keys_local, 'tm', axis=0, tiled=True)]
  transfers between devices with their start and end apart: 4 -> 30, of which waited for: 2 -> 11; matrix products, arithmetic and copies ran while one was open for 38% -> 1% of each run, Pallas kernels for 0% -> 16%
where the time goes in v1:
time: 305 us
  waiting for transfers between devices  121 us (40%)
  Pallas kernels  68.2 us (22%)
  starting transfers between devices  42.8 us (14%)
  blocking collectives  42.3 us (14%)
  between operations  14.3 us (5%)
  local copies, waits for them, and re-layouts  13 us (4%)
    psum x1, waiting for transfers between devices, local(): up = lax.psum(up, ('x', 'y', 'c'))  93.7 us
    pallas_call x1, Pallas kernels, attention_grads(): pl.pallas_call(grads_kernel, in_specs=[SMEM] + [VMEM] * 16, out_specs=[VM...  30.1 us
    all_to_all x1, blocking collectives, local(): wide = lax.all_to_all(wide, ('z', 'x', 'y'), 0, 0, tiled=True)  25.3 us
    ppermute x15, starting transfers between devices, spread(): return [a] + [lax.ppermute(a, axis, ring(4, d)) for d in (1, 3, 2)]  22.8 us
    all_to_all x1, blocking collectives, local(): down = lax.all_to_all(mine + theirs, ('x', 'y'), 0, 0, tiled=True)  17 us
    pallas_call x1, Pallas kernels, row_stats(): pl.pallas_call(stats_kernel, in_specs=[SMEM] + [VMEM] * 12, out_specs=VME...  16.3 us
    ppermute x15, waiting for transfers between devices, spread(): return [a] + [lax.ppermute(a, axis, ring(4, d)) for d in (1, 3, 2)]  13.4 us
    ppermute x8, starting transfers between devices, swap(): return lax.ppermute(a, 'c', ring(2, 1))  12.3 us
  transfers between devices with their start and end apart: 30, of which 11 were waited for; matrix products, arithmetic and copies ran while one was open for 1% of the time, Pallas kernels for 16%

profile of v1, /device:TPU:1, one launch (start us, length us, event | category | flops | bytes accessed | tf_op | source)
XLA Modules:
  0.0 305.2 jit_solution(924505018621339688)
XLA Ops:
  8.1 1.5 collective-permute-start.4
  9.7 1.7 copy-done
  15.7 9.5 %project.1 = (bf16[256,256]{1,0:T(8,128)(2,1)S(1)}, bf16[256,256]{1,0:T(8,128)(2,1)S(1)}, bf16[256,128]{1,0:T(8,128)(2,1)S(1)}, bf16[256,128]{1,0:T(8,128)(2,1)S(1)}, bf16[256,256]{1,0:T(8,128)(2,1)S(1)}) custom-call(s32[4]{0:T(128)S(1)} %pad_add_fusion.pos, bf16[256,5120]{1,0:T(8,128)(2,1)S(1)} %copy-done, bf16[5120,256]{1,0:T(8,128)(2,1)} %wq.1, ...), custom_call_target="tpu_custom_call" | custom-call | flops 2684354560 | bytes 13631488 | tf_op jit(solution)/shard_map/project/pallas_call | solution.py:81
  25.9 2.9 collective-permute-start.7
  30.0 2.1 collective-permute-start.3
  32.0 2.5 collective-permute-start.11
  34.6 2.5 collective-permute-start.10
  39.0 2.6 collective-permute-start.1
  42.4 10.5 %lists.1 = s32[24,128]{1,0:T(8,128)} custom-call(s32[4]{0:T(128)} %copy-done.8, s32[64]{0:T(128)} %slot.1, s32[64,64]{1,0:T(8,128)} %levels.1, s32[64,256]{1,0:T(8,128)} %copy.19.order), custom_call_target="tpu_custom_call" | custom-call | tf_op jit(solution)/shard_map/lists/pallas_call | solution.py:125
  53.7 16.3 %row_stats.1.s0 = f32[48,128]{1,0:T(8,128)S(1)} custom-call(s32[24,128]{1,0:T(8,128)S(1)} %copy-done.7, bf16[512,128]{1,0:T(8,128)(2,1)S(1)} %constant_dynamic-update-slice_fusion.q0, bf16[512,128]{1,0:T(8,128)(2,1)S(1)} %collective-permute-done.1.q1, bf16[512,128]{1,0:T(8,128)(2,1)S(1)} %collective-permute-done.2.q2, ...), custom_call_target="tpu_custom_call" | custom-call | tf_op jit(solution)/shard_map/row_stats/pallas_call | solution.py:182
  70.1 3.2 %collective-permute-start.13 = (f32[48,128]{1,0:T(8,128)S(1)}, f32[48,128]{1,0:T(8,128)S(1)}, u32[]{:S(2)}, u32[]{:S(2)}) collective-permute-start(f32[48,128]{1,0:T(8,128)S(1)} %row_stats.1.s0), channel_id=1, source_target_pairs={{0,16},{8,24},{16,0},{24,8},{1,17},{9,25},{17,1},{25,9},{2,18},{10... | collective-permute-start | bytes 73736 | tf_op jit(solution)/shard_map/ppermute | solution.py:321
  73.3 3.0 collective-permute-start.21
  77.5 30.1 %attention_grads.1 = (f32[512,256]{1,0:T(8,128)S(1)}, bf16[512,256]{1,0:T(8,128)(2,1)S(1)}, bf16[512,256]{1,0:T(8,128)(2,1)S(1)}, bf16[512,256]{1,0:T(8,128)(2,1...) custom-call(s32[24,128]{1,0:T(8,128)S(1)} %copy-done.7, ...), custom_call_target="tpu_custom_call" | custom-call | tf_op jit(solution)/shard_map/attention_grads/pallas_call | solution.py:255
  108.0 2.4 collective-permute-start.15
  110.3 1.7 collective-permute-start.16
  112.9 1.7 collective-permute-start.19
  115.3 2.9 collective-permute-done.19.b2
  118.2 1.7 collective-permute-done.20.b3
  119.9 3.8 %collective-permute-done.17.a3 = bf16[512,256]{1,0:T(8,128)(2,1)S(1)} collective-permute-done((bf16[512,256]{1,0:T(8,128)(2,1)S(1)}, bf16[512,256]{1,0:T(8,128)(2,1)S(1)}, u32[]{:S(2)}, u32[]{:S(2)}) %collective-permute-start.17) | collective-permute-done | bytes 262176 | tf_op jit(solution)/shard_map/ppermute | solution.py:329
  123.7 1.7 finish.1
  125.4 2.5 collective-permute-start.23
  129.1 3.7 %collective-permute-start.26 = (f32[256,256]{1,0:T(8,128)S(1)}, f32[256,256]{1,0:T(8,128)S(1)}, u32[]{:S(2)}, u32[]{:S(2)}) collective-permute-start(f32[256,256]{1,0:T(8,128)S(1)} %add.35), channel_id=1, source_target_pairs={{0,2},{1,3},{2,0},{3,1},{4,6},{5,7},{6,4},{7,5},{8,10},{9,11},{10,... | collective-permute-start | bytes 786440 | tf_op jit(solution)/shard_map/ppermute | solution.py:321
  134.3 5.0 %collective-permute-done.26 = f32[256,256]{1,0:T(8,128)S(1)} collective-permute-done((f32[256,256]{1,0:T(8,128)S(1)}, f32[256,256]{1,0:T(8,128)S(1)}, u32[]{:S(2)}, u32[]{:S(2)}) %collective-permute-start.26) | collective-permute-done | bytes 262176 | tf_op jit(solution)/shard_map/ppermute | solution.py:321
  139.2 6.0 %collective-permute-done.25 = f32[256,256]{1,0:T(8,128)S(1)} collective-permute-done((f32[256,256]{1,0:T(8,128)S(1)}, f32[256,256]{1,0:T(8,128)S(1)}, u32[]{:S(2)}, u32[]{:S(2)}) %collective-permute-start.25) | collective-permute-done | bytes 262176 | tf_op jit(solution)/shard_map/ppermute | solution.py:321
  148.1 1.7 collective-permute-done.27
  149.9 17.0 %all_to_all.18 = f32[16,40,256]{2,1,0:T(8,128)S(1)} all-to-all(f32[16,40,256]{2,1,0:T(8,128)S(1)} %bitcast.17), channel_id=1, replica_groups=mesh['x'=4,'y'=4,'c'=2,'z'=4] {'x','y'}, dimensions={0} | all-to-all | bytes 1310720 | tf_op jit(solution)/shard_map/all_to_all | solution.py:365
  167.0 25.3 %all_to_all.19 = bf16[64,40,256]{2,1,0:T(8,128)(2,1)S(1)} all-to-all(bf16[64,40,256]{2,1,0:T(8,128)(2,1)S(1)} %broadcast_in_dim.2), channel_id=1, replica_groups=mesh['x'=4,'y'=4,'c'=2,'z'=4] {'z','x','y'}, dimensions={0} | all-to-all | bytes 2621440 | tf_op jit(solution)/shard_map/all_to_all | solution.py:368
  192.3 3.4 %collective-permute-start.28 = (bf16[2560,256]{1,0:T(8,128)(2,1)S(1)}, bf16[2560,256]{1,0:T(8,128)(2,1)S(1)}, u32[]{:S(2)}, u32[]{:S(2)}) collective-permute-start(bf16[2560,256]{1,0:T(8,128)(2,1)S(1)} %bitcast.16), channel_id=1, source_target_pairs={{0,4},{4,0},{1,5},{5,1},{2,6},{6,2},{3,7},{7,3},{8,12},{12,8},{9,1... | collective-permute-start | bytes 3932168 | tf_op jit(solution)/shard_map/ppermute | solution.py:317
  195.7 2.7 collective-permute-done.22
  199.2 93.7 %all-reduce.2.cloned.1.call-done = f32[256,256]{1,0:T(8,128)} async-done(((f32[256,256]{1,0:T(8,128)}), f32[256,256]{1,0:T(8,128)}) %all-reduce.2.cloned.1.call-update) | async-done | bytes 262160 | tf_op jit(solution)/shard_map/psum | solution.py:357
  292.9 1.7 fusion.4
  295.7 2.7 fusion.3
  (79 shorter events, 21.1 us)
Async XLA Ops:
  7.2 285.7 %all-reduce.2.cloned.1.call-start = ((), (), s32[]{:S(2)}) async-start(), calls=%async_computation.2 | async-start | bytes 524288 | tf_op jit(solution)/shard_map/psum | solution.py:357
  8.1 17.8 %collective-permute-start.4 = (bf16[256,128]{1,0:T(8,128)(2,1)S(1)}, bf16[256,128]{1,0:T(8,128)(2,1)S(1)}, u32[]{:S(2)}, u32[]{:S(2)}) collective-permute-start(bf16[256,128]{1,0:T(8,128)(2,1)S(1)} %get-tuple-element.48), channel_id=1, source_target_pairs={{0,4},{4,0},{1,5},{5,1},{2,6},{6,2},{3,7},{7,3},{8,12},{12,8},{9,1... | collective-permute-start | bytes 196616 | tf_op jit(solution)/shard_map/ppermute | solution.py:317
  25.3 4.6 %collective-permute-start = (bf16[256,128]{1,0:T(8,128)(2,1)S(1)}, bf16[256,128]{1,0:T(8,128)(2,1)S(1)}, u32[]{:S(2)}, u32[]{:S(2)}) collective-permute-start(bf16[256,128]{1,0:T(8,128)(2,1)S(1)} %get-tuple-element.24), channel_id=1, source_target_pairs={{0,4},{4,0},{1,5},{5,1},{2,6},{6,2},{3,7},{7,3},{8,12},{12,8},{9,1... | collective-permute-start | bytes 196616 | tf_op jit(solution)/shard_map/ppermute | solution.py:317
  25.4 6.6 %collective-permute-start.8 = (bf16[256,256]{1,0:T(8,128)(2,1)S(1)}, bf16[256,256]{1,0:T(8,128)(2,1)S(1)}, u32[]{:S(2)}, u32[]{:S(2)}) collective-permute-start(bf16[256,256]{1,0:T(8,128)(2,1)S(1)} %get-tuple-element.26), channel_id=1, source_target_pairs={{0,4},{4,0},{1,5},{5,1},{2,6},{6,2},{3,7},{7,3},{8,12},{12,8},{9,1... | collective-permute-start | bytes 393224 | tf_op jit(solution)/shard_map/ppermute | solution.py:317
  25.9 8.6 %collective-permute-start.7 = (bf16[512,128]{1,0:T(8,128)(2,1)S(1)}, bf16[512,128]{1,0:T(8,128)(2,1)S(1)}, u32[]{:S(2)}, u32[]{:S(2)}) collective-permute-start(bf16[512,128]{1,0:T(8,128)(2,1)S(1)} %pad_maximum_fusion.1.g0), channel_id=1, source_target_pairs={{0,24},{8,0},{16,8},{24,16},{1,25},{9,1},{17,9},{25,17},{2,26},{10... | collective-permute-start | bytes 393224 | tf_op jit(solution)/shard_map/ppermute | solution.py:321
  28.9 8.2 %collective-permute-start.6 = (bf16[512,128]{1,0:T(8,128)(2,1)S(1)}, bf16[512,128]{1,0:T(8,128)(2,1)S(1)}, u32[]{:S(2)}, u32[]{:S(2)}) collective-permute-start(bf16[512,128]{1,0:T(8,128)(2,1)S(1)} %pad_maximum_fusion.1.g0), channel_id=1, source_target_pairs={{0,16},{8,24},{16,0},{24,8},{1,17},{9,25},{17,1},{25,9},{2,18},{10... | collective-permute-start | bytes 393224 | tf_op jit(solution)/shard_map/ppermute | solution.py:321
  29.2 9.4 %collective-permute-start.5 = (bf16[512,128]{1,0:T(8,128)(2,1)S(1)}, bf16[512,128]{1,0:T(8,128)(2,1)S(1)}, u32[]{:S(2)}, u32[]{:S(2)}) collective-permute-start(bf16[512,128]{1,0:T(8,128)(2,1)S(1)} %pad_maximum_fusion.1.g0), channel_id=1, source_target_pairs={{0,8},{8,16},{16,24},{24,0},{1,9},{9,17},{17,25},{25,1},{2,10},{10... | collective-permute-start | bytes 393224 | tf_op jit(solution)/shard_map/ppermute | solution.py:321
  29.9 93.8 %copy-start.4 = (bf16[128,256]{1,0:T(8,128)(2,1)S(1)}, bf16[128,256]{1,0:T(8,128)(2,1)}, u32[]{:S(2)}) copy-start(bf16[128,256]{1,0:T(8,128)(2,1)} %uq.3) | copy-start | bytes 196612
  29.9 93.8 %copy-start.6 = (bf16[128,256]{1,0:T(8,128)(2,1)S(1)}, bf16[128,256]{1,0:T(8,128)(2,1)}, u32[]{:S(2)}) copy-start(bf16[128,256]{1,0:T(8,128)(2,1)} %uv.3) | copy-start | bytes 196612
  30.0 9.0 %collective-permute-start.3 = (bf16[512,128]{1,0:T(8,128)(2,1)S(1)}, bf16[512,128]{1,0:T(8,128)(2,1)S(1)}, u32[]{:S(2)}, u32[]{:S(2)}) collective-permute-start(bf16[512,128]{1,0:T(8,128)(2,1)S(1)} %constant_dynamic-update-slice_fusion.q0), channel_id=1, source_target_pairs={{0,24},{8,0},{16,8},{24,16},{1,25},{9,1},{17,9},{25,17},{2,26},{10... | collective-permute-start | bytes 393224 | tf_op jit(solution)/shard_map/ppermute | solution.py:321
  32.0 20.9 %collective-permute-start.11 = (bf16[512,256]{1,0:T(8,128)(2,1)S(1)}, bf16[512,256]{1,0:T(8,128)(2,1)S(1)}, u32[]{:S(2)}, u32[]{:S(2)}) collective-permute-start(bf16[512,256]{1,0:T(8,128)(2,1)S(1)} %constant_dynamic-update-slice_fusion.2.k0), channel_id=1, source_target_pairs={{0,96},{32,0},{64,32},{96,64},{1,97},{33,1},{65,33},{97,65},{2,98}... | collective-permute-start | bytes 786440 | tf_op jit(solution)/shard_map/ppermute | solution.py:321
  34.6 18.3 %collective-permute-start.10 = (bf16[512,256]{1,0:T(8,128)(2,1)S(1)}, bf16[512,256]{1,0:T(8,128)(2,1)S(1)}, u32[]{:S(2)}, u32[]{:S(2)}) collective-permute-start(bf16[512,256]{1,0:T(8,128)(2,1)S(1)} %constant_dynamic-update-slice_fusion.2.k0), channel_id=1, source_target_pairs={{0,64},{32,96},{64,0},{96,32},{1,65},{33,97},{65,1},{97,33},{2,66}... | collective-permute-start | bytes 786440 | tf_op jit(solution)/shard_map/ppermute | solution.py:321
  37.1 15.8 %collective-permute-start.9 = (bf16[512,256]{1,0:T(8,128)(2,1)S(1)}, bf16[512,256]{1,0:T(8,128)(2,1)S(1)}, u32[]{:S(2)}, u32[]{:S(2)}) collective-permute-start(bf16[512,256]{1,0:T(8,128)(2,1)S(1)} %constant_dynamic-update-slice_fusion.2.k0), channel_id=1, source_target_pairs={{0,32},{32,64},{64,96},{96,0},{1,33},{33,65},{65,97},{97,1},{2,34}... | collective-permute-start | bytes 786440 | tf_op jit(solution)/shard_map/ppermute | solution.py:321
  38.6 14.3 %collective-permute-start.2 = (bf16[512,128]{1,0:T(8,128)(2,1)S(1)}, bf16[512,128]{1,0:T(8,128)(2,1)S(1)}, u32[]{:S(2)}, u32[]{:S(2)}) collective-permute-start(bf16[512,128]{1,0:T(8,128)(2,1)S(1)} %constant_dynamic-update-slice_fusion.q0), channel_id=1, source_target_pairs={{0,16},{8,24},{16,0},{24,8},{1,17},{9,25},{17,1},{25,9},{2,18},{10... | collective-permute-start | bytes 393224 | tf_op jit(solution)/shard_map/ppermute | solution.py:321
  39.0 13.9 %collective-permute-start.1 = (bf16[512,128]{1,0:T(8,128)(2,1)S(1)}, bf16[512,128]{1,0:T(8,128)(2,1)S(1)}, u32[]{:S(2)}, u32[]{:S(2)}) collective-permute-start(bf16[512,128]{1,0:T(8,128)(2,1)S(1)} %constant_dynamic-update-slice_fusion.q0), channel_id=1, source_target_pairs={{0,8},{8,16},{16,24},{24,0},{1,9},{9,17},{17,25},{25,1},{2,10},{10... | collective-permute-start | bytes 393224 | tf_op jit(solution)/shard_map/ppermute | solution.py:321
  70.0 6.4 %collective-permute-start.14 = (f32[48,128]{1,0:T(8,128)S(1)}, f32[48,128]{1,0:T(8,128)S(1)}, u32[]{:S(2)}, u32[]{:S(2)}) collective-permute-start(f32[48,128]{1,0:T(8,128)S(1)} %row_stats.1.s0), channel_id=1, source_target_pairs={{0,24},{8,0},{16,8},{24,16},{1,25},{9,1},{17,9},{25,17},{2,26},{10... | collective-permute-start | bytes 73736 | tf_op jit(solution)/shard_map/ppermute | solution.py:321
  70.1 6.2 %collective-permute-start.13 = (f32[48,128]{1,0:T(8,128)S(1)}, f32[48,128]{1,0:T(8,128)S(1)}, u32[]{:S(2)}, u32[]{:S(2)}) collective-permute-start(f32[48,128]{1,0:T(8,128)S(1)} %row_stats.1.s0), channel_id=1, source_target_pairs={{0,16},{8,24},{16,0},{24,8},{1,17},{9,25},{17,1},{25,9},{2,18},{10... | collective-permute-start | bytes 73736 | tf_op jit(solution)/shard_map/ppermute | solution.py:321
  73.3 4.3 %collective-permute-start.12 = (f32[48,128]{1,0:T(8,128)S(1)}, f32[48,128]{1,0:T(8,128)S(1)}, u32[]{:S(2)}, u32[]{:S(2)}) collective-permute-start(f32[48,128]{1,0:T(8,128)S(1)} %row_stats.1.s0), channel_id=1, source_target_pairs={{0,8},{8,16},{16,24},{24,0},{1,9},{9,17},{17,25},{25,1},{2,10},{10... | collective-permute-start | bytes 73736 | tf_op jit(solution)/shard_map/ppermute | solution.py:321
  73.3 39.6 %collective-permute-start.21 = (bf16[256,256]{1,0:T(8,128)(2,1)S(1)}, bf16[256,256]{1,0:T(8,128)(2,1)S(1)}, u32[]{:S(2)}, u32[]{:S(2)}) collective-permute-start(bf16[256,256]{1,0:T(8,128)(2,1)S(1)} %get-tuple-element.35.rank_own), channel_id=1, source_target_pairs={{0,4},{4,0},{1,5},{5,1},{2,6},{6,2},{3,7},{7,3},{8,12},{12,8},{9,1... | collective-permute-start | bytes 393224 | tf_op jit(solution)/shard_map/ppermute | solution.py:317
  107.7 6.9 %collective-permute-start.18 = (bf16[512,128]{1,0:T(8,128)(2,1)S(1)}, bf16[512,128]{1,0:T(8,128)(2,1)S(1)}, u32[]{:S(2)}, u32[]{:S(2)}) collective-permute-start(bf16[512,128]{1,0:T(8,128)(2,1)S(1)} %get-tuple-element.32), channel_id=1, source_target_pairs={{0,96},{32,0},{64,32},{96,64},{1,97},{33,1},{65,33},{97,65},{2,98}... | collective-permute-start | bytes 393224 | tf_op jit(solution)/shard_map/ppermute | solution.py:329
  108.0 12.0 %collective-permute-start.15 = (bf16[512,256]{1,0:T(8,128)(2,1)S(1)}, bf16[512,256]{1,0:T(8,128)(2,1)S(1)}, u32[]{:S(2)}, u32[]{:S(2)}) collective-permute-start(bf16[512,256]{1,0:T(8,128)(2,1)S(1)} %get-tuple-element.28), channel_id=1, source_target_pairs={{0,24},{8,0},{16,8},{24,16},{1,25},{9,1},{17,9},{25,17},{2,26},{10... | collective-permute-start | bytes 786440 | tf_op jit(solution)/shard_map/ppermute | solution.py:329
  110.3 9.6 %collective-permute-start.16 = (bf16[512,256]{1,0:T(8,128)(2,1)S(1)}, bf16[512,256]{1,0:T(8,128)(2,1)S(1)}, u32[]{:S(2)}, u32[]{:S(2)}) collective-permute-start(bf16[512,256]{1,0:T(8,128)(2,1)S(1)} %get-tuple-element.29), channel_id=1, source_target_pairs={{0,16},{8,24},{16,0},{24,8},{1,17},{9,25},{17,1},{25,9},{2,18},{10... | collective-permute-start | bytes 786440 | tf_op jit(solution)/shard_map/ppermute | solution.py:329
  112.1 11.6 %collective-permute-start.17 = (bf16[512,256]{1,0:T(8,128)(2,1)S(1)}, bf16[512,256]{1,0:T(8,128)(2,1)S(1)}, u32[]{:S(2)}, u32[]{:S(2)}) collective-permute-start(bf16[512,256]{1,0:T(8,128)(2,1)S(1)} %get-tuple-element.30), channel_id=1, source_target_pairs={{0,8},{8,16},{16,24},{24,0},{1,9},{9,17},{17,25},{25,1},{2,10},{10... | collective-permute-start | bytes 786440 | tf_op jit(solution)/shard_map/ppermute | solution.py:329
  112.9 5.3 %collective-permute-start.19 = (bf16[512,128]{1,0:T(8,128)(2,1)S(1)}, bf16[512,128]{1,0:T(8,128)(2,1)S(1)}, u32[]{:S(2)}, u32[]{:S(2)}) collective-permute-start(bf16[512,128]{1,0:T(8,128)(2,1)S(1)} %get-tuple-element.33), channel_id=1, source_target_pairs={{0,64},{32,96},{64,0},{96,32},{1,65},{33,97},{65,1},{97,33},{2,66}... | collective-permute-start | bytes 393224 | tf_op jit(solution)/shard_map/ppermute | solution.py:329
  114.6 5.3 %collective-permute-start.20 = (bf16[512,128]{1,0:T(8,128)(2,1)S(1)}, bf16[512,128]{1,0:T(8,128)(2,1)S(1)}, u32[]{:S(2)}, u32[]{:S(2)}) collective-permute-start(bf16[512,128]{1,0:T(8,128)(2,1)S(1)} %get-tuple-element.34), channel_id=1, source_target_pairs={{0,32},{32,64},{64,96},{96,0},{1,33},{33,65},{65,97},{97,1},{2,34}... | collective-permute-start | bytes 393224 | tf_op jit(solution)/shard_map/ppermute | solution.py:329
  125.4 3.6 %collective-permute-start.23 = (f32[256,256]{1,0:T(8,128)S(1)}, f32[256,256]{1,0:T(8,128)S(1)}, u32[]{:S(2)}, u32[]{:S(2)}) collective-permute-start(f32[256,256]{1,0:T(8,128)S(1)} %get-tuple-element.39), channel_id=1, source_target_pairs={{0,4},{4,0},{1,5},{5,1},{2,6},{6,2},{3,7},{7,3},{8,12},{12,8},{9,1... | collective-permute-start | bytes 786440 | tf_op jit(solution)/shard_map/ppermute | solution.py:317
  129.1 10.1 %collective-permute-start.26 = (f32[256,256]{1,0:T(8,128)S(1)}, f32[256,256]{1,0:T(8,128)S(1)}, u32[]{:S(2)}, u32[]{:S(2)}) collective-permute-start(f32[256,256]{1,0:T(8,128)S(1)} %add.35), channel_id=1, source_target_pairs={{0,2},{1,3},{2,0},{3,1},{4,6},{5,7},{6,4},{7,5},{8,10},{9,11},{10,... | collective-permute-start | bytes 786440 | tf_op jit(solution)/shard_map/ppermute | solution.py:321
  132.8 12.5 %collective-permute-start.25 = (f32[256,256]{1,0:T(8,128)S(1)}, f32[256,256]{1,0:T(8,128)S(1)}, u32[]{:S(2)}, u32[]{:S(2)}) collective-permute-start(f32[256,256]{1,0:T(8,128)S(1)} %add.35), channel_id=1, source_target_pairs={{0,3},{1,0},{2,1},{3,2},{4,7},{5,4},{6,5},{7,6},{8,11},{9,8},{10,9... | collective-permute-start | bytes 786440 | tf_op jit(solution)/shard_map/ppermute | solution.py:321
  133.2 12.0 %collective-permute-start.24 = (f32[256,256]{1,0:T(8,128)S(1)}, f32[256,256]{1,0:T(8,128)S(1)}, u32[]{:S(2)}, u32[]{:S(2)}) collective-permute-start(f32[256,256]{1,0:T(8,128)S(1)} %add.35), channel_id=1, source_target_pairs={{0,1},{1,2},{2,3},{3,0},{4,5},{5,6},{6,7},{7,4},{8,9},{9,10},{10,1... | collective-permute-start | bytes 786440 | tf_op jit(solution)/shard_map/ppermute | solution.py:321
  146.8 3.0 collective-permute-start.27
  192.3 102.3 %collective-permute-start.28 = (bf16[2560,256]{1,0:T(8,128)(2,1)S(1)}, bf16[2560,256]{1,0:T(8,128)(2,1)S(1)}, u32[]{:S(2)}, u32[]{:S(2)}) collective-permute-start(bf16[2560,256]{1,0:T(8,128)(2,1)S(1)} %bitcast.16), channel_id=1, source_target_pairs={{0,4},{4,0},{1,5},{5,1},{2,6},{6,2},{3,7},{7,3},{8,12},{12,8},{9,1... | collective-permute-start | bytes 3932168 | tf_op jit(solution)/shard_map/ppermute | solution.py:317
  195.7 2.8 collective-permute-start.22
  (9 other events, 135.9 us)
Sparse Core Ops, SparseCore 0:
  195.9 97.0 all-reduce.1

commit v2 on v1

v2 whole, which is shorter than its diff:
```python
import math

import jax
import jax.numpy as jnp
from jax import lax
from jax.experimental import pallas as pl
from jax.experimental.pallas import tpu as pltpu
from jax.sharding import Mesh
from jax.sharding import PartitionSpec as P

HEAD = 128
FT = 128
BLK = 32
RANK = 128
CHUNK = 512
CB = CHUNK // BLK
CHAINS = 4
SCALE = HEAD ** -0.5
SCALE2 = SCALE * math.log2(math.e)
NEG = -1e30
f32 = jnp.float32
bf16 = jnp.bfloat16
WIRE = bf16
KT = 1280
VMEM = pl.BlockSpec(memory_space=pltpu.VMEM)
SMEM = pl.BlockSpec(memory_space=pltpu.SMEM)
ANY = pl.BlockSpec(memory_space=pl.ANY)
WIDE = pltpu.CompilerParams(vmem_limit_bytes=60 * 1024 * 1024)
PARAMS = pltpu.CompilerParams(vmem_limit_bytes=48 * 1024 * 1024)


def dot(a, b, ca=1, cb=0):
    return lax.dot_general(a, b, (((ca,), (cb,)), ((), ())), preferred_element_type=f32)


def by_core(pos, put, keep, send):
    for c in range(2):
        @pl.when(pos[2] == c)
        def _():
            put(keep, c * HEAD)
            put(send, (1 - c) * HEAD)


def kv_kernel(pos, act, wk, wv, down, up, after0, after1, keep, send, rank, ak, av, ar):
    step = pl.program_id(0)
    last = pl.num_programs(0) - 1
    a = act[...]
    parts = [(ak, wk), (av, wv), (ar, down)]

    @pl.when(step == 0)
    def _():
        for total, w in parts:
            total[...] = dot(a, w[...])

    @pl.when(step > 0)
    def _():
        for total, w in parts:
            total[...] += dot(a, w[...])

    @pl.when(step == last)
    def _():
        low = ar[...].astype(bf16)
        rank[...] = low
        keys = ak[...].astype(bf16)
        values = (av[...] + dot(low, up[...])).astype(bf16)

        def put(ref, at):
            ref[:, :HEAD] = keys[:, at:at + HEAD]
            ref[:, HEAD:] = values[:, at:at + HEAD]

        by_core(pos, put, keep, send)


def q_kernel(pos, act, wq, down, up, after0, after1, after2, after3, keep, send, rank, aq, ar):
    step = pl.program_id(0)
    last = pl.num_programs(0) - 1
    a = act[...]
    parts = [(aq, wq), (ar, down)]

    @pl.when(step == 0)
    def _():
        for total, w in parts:
            total[...] = dot(a, w[...])

    @pl.when(step > 0)
    def _():
        for total, w in parts:
            total[...] += dot(a, w[...])

    @pl.when(step == last)
    def _():
        low = ar[...].astype(bf16)
        rank[...] = low
        query = (aq[...] + dot(low, up[...])).astype(bf16)

        def put(ref, at):
            ref[...] = query[:, at:at + HEAD]

        by_core(pos, put, keep, send)


def project(kernel, name, pos, act, weights, down, up, lanes, after):
    rows, width = act.shape
    cols = weights[0].shape[1]
    n = len(weights)
    whole = lambda shape: pl.BlockSpec(shape, lambda k: (0, 0))
    shapes = [(rows, lanes), (rows, lanes), (rows, RANK)]
    return pl.pallas_call(
        kernel,
        grid=(width // KT,),
        in_specs=[SMEM, pl.BlockSpec((rows, KT), lambda k: (0, k))]
        + [pl.BlockSpec((KT, cols), lambda k: (k, 0))] * n
        + [pl.BlockSpec((KT, RANK), lambda k: (k, 0)), whole(up.shape)] + [ANY] * len(after),
        out_specs=[whole(s) for s in shapes],
        out_shape=[jax.ShapeDtypeStruct(s, bf16) for s in shapes],
        scratch_shapes=[pltpu.VMEM((rows, cols), f32)] * n + [pltpu.VMEM((rows, RANK), f32)],
        compiler_params=WIDE,
        cost_estimate=pl.CostEstimate(flops=2 * rows * width * (n * cols + RANK),
                                      bytes_accessed=2 * width * (rows + n * cols + RANK), transcendentals=0),
        name=name,
    )(pos, act, *weights, down, up, *after)


def project_kv(pos, act, wk, wv, dv, uv, *after):
    return project(kv_kernel, "project_kv", pos, act, [wk, wv], dv, uv, 2 * HEAD, after)


def project_q(pos, act, wq, dq, uq, *after):
    return project(q_kernel, "project_q", pos, act, [wq], dq, uq, HEAD, after)


def lists_kernel(pos, slot, packed, out):
    x, y, c = pos[0], pos[1], pos[2]

    def frame(xx, yy, local):
        core = c if local < 2 else 1 - c
        return slot[((xx * 4 + yy) * 2 + core) * 2 + local % 2]

    keys = [frame(lax.rem(x + 4 - k // 4, 4), y, k % 4) for k in range(16)]
    for q in range(16):
        out[17, q] = frame(x, lax.rem(y + 4 - q // 4, 4), q % 4)

    def one(q, _):
        f = out[17, q]
        n = 0
        for k in range(16):
            word = packed[f, keys[k]]
            for r in range(4):
                out[q, n + r] = k * 4 + ((word >> (2 * r)) & 3)
            n = n + (word >> 8)
        for r in range(CB):
            out[q, n + r] = 0
        out[16, q] = n
        return 0

    lax.fori_loop(0, 16, one, 0)


def visible_lists(pos, slot, levels, order):
    packed = levels * 256 + jnp.sum(order * jnp.array([1, 4, 16, 64], jnp.int32), axis=-1)
    return pl.pallas_call(
        lists_kernel,
        in_specs=[SMEM] * 3,
        out_specs=SMEM,
        out_shape=jax.ShapeDtypeStruct((24, 128), jnp.int32),
        name="lists",
    )(pos, slot, packed)


def fill_all(parts, whole):
    rows = parts[0].shape[0]
    for d, part in enumerate(parts):
        whole[d * rows:(d + 1) * rows, :] = part[...]


def load_chunk(lists, f, at, kvall):
    blocks = [kvall[pl.ds(pl.multiple_of(lists[f, at + i] * BLK, BLK), BLK), :] for i in range(CB)]
    return jnp.concatenate(blocks, axis=0)


def start_frames(lists, t, qall, gall, both):
    counts = []
    for j in range(CHAINS):
        f = t * CHAINS + j
        at = pl.multiple_of(f * FT, FT)
        both[j, :FT, :HEAD] = qall[pl.ds(at, FT), :]
        both[j, FT:, HEAD:] = gall[pl.ds(at, FT), :]
        counts.append(lists[16, f])
    chunks = [(n + CB - 1) // CB for n in counts]
    most = chunks[0]
    for n in chunks[1:]:
        most = jnp.maximum(most, n)
    return counts, chunks, most


def stats_kernel(lists, q0, q1, q2, q3, g0, g1, g2, g3, k0, k1, k2, k3, out, qall, gall, kvall, both):
    fill_all((q0, q1, q2, q3), qall)
    fill_all((g0, g1, g2, g3), gall)
    fill_all((k0, k1, k2, k3), kvall)
    both[...] = jnp.zeros_like(both)
    row = lax.broadcasted_iota(jnp.int32, (CHUNK, HEAD), 0)

    def frames(t, _):
        counts, chunks, most = start_frames(lists, t, qall, gall, both)

        def chunk(ch, carry):
            kvs = [load_chunk(lists, t * CHAINS + j, jnp.minimum(ch, chunks[j] - 1) * CB, kvall)
                   for j in range(CHAINS)]
            rs = [dot(kvs[j], both[j], 1, 1) for j in range(CHAINS)]
            after = []
            for j in range(CHAINS):
                peak, total, delta = carry[j]
                s = jnp.where(row < (counts[j] - ch * CB) * BLK, rs[j][:, :FT] * SCALE2, NEG)
                new = jnp.maximum(peak, jnp.max(s, axis=0, keepdims=True))
                p = jnp.exp2(s - new)
                fix = jnp.exp2(peak - new)
                total = total * fix + jnp.sum(p, axis=0, keepdims=True)
                delta = delta * fix + jnp.sum(p * rs[j][:, FT:], axis=0, keepdims=True)
                after.append((new, total, delta))
            return tuple(after)

        zero = jnp.zeros((1, FT), f32)
        carry = lax.fori_loop(0, most, chunk, ((zero + NEG, zero, zero),) * CHAINS)
        for j in range(CHAINS):
            for i in range(3):
                out[pl.ds(16 * i + t * CHAINS + j, 1), :] = carry[j][i]
        return 0

    lax.fori_loop(0, 16 // CHAINS, frames, 0)


def row_stats(lists, qs, gs, kvs):
    return pl.pallas_call(
        stats_kernel,
        in_specs=[SMEM] + [VMEM] * 12,
        out_specs=VMEM,
        out_shape=jax.ShapeDtypeStruct((48, 128), f32),
        scratch_shapes=[pltpu.VMEM((2048, HEAD), bf16), pltpu.VMEM((2048, HEAD), bf16),
                        pltpu.VMEM((2048, 2 * HEAD), bf16), pltpu.VMEM((CHAINS, 2 * FT, 2 * HEAD), bf16)],
        compiler_params=PARAMS,
        name="row_stats",
    )(lists, *qs, *gs, *kvs)


def grads_kernel(lists, s0, s1, s2, s3, q0, q1, q2, q3, g0, g1, g2, g3, k0, k1, k2, k3,
                 a0, a1, a2, a3, b0, b1, b2, b3, qall, gall, kvall, both, acc, dva, norm):
    fill_all((q0, q1, q2, q3), qall)
    fill_all((g0, g1, g2, g3), gall)
    fill_all((k0, k1, k2, k3), kvall)
    both[...] = jnp.zeros_like(both)
    dva[...] = jnp.zeros_like(dva)
    for t in range(4):
        rows = [slice(4 * ((t - d) % 4), 4 * ((t - d) % 4) + 4) for d in range(4)]
        stats = [ref[...] for ref in (s0, s1, s2, s3)]
        peaks = [stats[d][0:16][rows[d]] for d in range(4)]
        peak = jnp.maximum(jnp.maximum(peaks[0], peaks[1]), jnp.maximum(peaks[2], peaks[3]))
        total = jnp.zeros_like(peak)
        delta = jnp.zeros_like(peak)
        for d in range(4):
            fix = jnp.exp2(peaks[d] - peak)
            total += fix * stats[d][16:32][rows[d]]
            delta += fix * stats[d][32:48][rows[d]]
        norm[4 * t:4 * t + 4, :] = peak + jnp.log2(total)
        norm[16 + 4 * t:20 + 4 * t, :] = delta / total
    row = lax.broadcasted_iota(jnp.int32, (CHUNK, HEAD), 0)

    def frames(t, _):
        counts, chunks, most = start_frames(lists, t, qall, gall, both)
        lse = [norm[pl.ds(t * CHAINS + j, 1), :] for j in range(CHAINS)]
        delta = [norm[pl.ds(16 + t * CHAINS + j, 1), :] for j in range(CHAINS)]
        acc[...] = jnp.zeros_like(acc)

        def chunk(ch, _):
            at = [jnp.minimum(ch, chunks[j] - 1) * CB for j in range(CHAINS)]
            kvs = [load_chunk(lists, t * CHAINS + j, at[j], kvall) for j in range(CHAINS)]
            rs = [dot(kvs[j], both[j], 1, 1) for j in range(CHAINS)]
            lows, pairs = [], []
            for j in range(CHAINS):
                s = jnp.where(row < (counts[j] - ch * CB) * BLK, rs[j][:, :FT] * SCALE2, NEG)
                p = jnp.exp2(s - lse[j])
                low = p.astype(bf16)
                ds = (p * (rs[j][:, FT:] - delta[j]) * SCALE).astype(bf16)
                lows.append(low)
                pairs.append(jnp.concatenate([low, ds], axis=1))
            for j in range(CHAINS):
                product = dot(kvs[j], pairs[j], 0, 0)
                acc[j, 0] += product[HEAD:, :FT]
                acc[j, 1] += product[:HEAD, FT:]
            dvs = [dot(lows[j], both[j, FT:, HEAD:]) for j in range(CHAINS)]
            for i in range(CB):
                for j in range(CHAINS):
                    to = pl.multiple_of(lists[t * CHAINS + j, at[j] + i] * BLK, BLK)
                    dva[j, pl.ds(to, BLK), :] += dvs[j][i * BLK:(i + 1) * BLK, :]
            return 0

        lax.fori_loop(0, most, chunk, 0)
        for j in range(CHAINS):
            f = t * CHAINS + j
            at = pl.multiple_of(lax.rem(f, 4) * FT, FT)
            for d, a in enumerate((a0, a1, a2, a3)):
                def put():
                    a[pl.ds(at, FT), :HEAD] = acc[j, 0].T.astype(a.dtype)
                    a[pl.ds(at, FT), HEAD:] = acc[j, 1].T.astype(a.dtype)

                pl.when(f // 4 == d)(put)
        return 0

    lax.fori_loop(0, 16 // CHAINS, frames, 0)
    for d, b in enumerate((b0, b1, b2, b3)):
        total = dva[0, d * 512:(d + 1) * 512, :]
        for j in range(1, CHAINS):
            total += dva[j, d * 512:(d + 1) * 512, :]
        b[...] = total.astype(b.dtype)


def attention_grads(lists, stats, qs, gs, kvs):
    wire = [f32, WIRE, WIRE, WIRE]
    return pl.pallas_call(
        grads_kernel,
        in_specs=[SMEM] + [VMEM] * 16,
        out_specs=[VMEM] * 8,
        out_shape=[jax.ShapeDtypeStruct((512, 2 * HEAD), t) for t in wire]
        + [jax.ShapeDtypeStruct((512, HEAD), t) for t in wire],
        scratch_shapes=[pltpu.VMEM((2048, HEAD), bf16), pltpu.VMEM((2048, HEAD), bf16),
                        pltpu.VMEM((2048, 2 * HEAD), bf16), pltpu.VMEM((CHAINS, 2 * FT, 2 * HEAD), bf16),
                        pltpu.VMEM((CHAINS, 2, HEAD, FT), f32), pltpu.VMEM((CHAINS, 2048, HEAD), f32),
                        pltpu.VMEM((32, 128), f32)],
        compiler_params=PARAMS,
        name="attention_grads",
    )(lists, *stats, *qs, *gs, *kvs)


def finish_kernel(pos, a0, a1, a2, a3, b0, b1, b2, b3, rq_own, rq_other, rv_own, rv_other, uq, uv,
                  o_keep, o_send, rg_keep, rg_send, up):
    total = a0[...] + a1[...].astype(f32) + a2[...].astype(f32) + a3[...].astype(f32)
    out = total[:, :HEAD].astype(bf16)
    dq = total[:, HEAD:].astype(bf16)
    dv = (b0[...] + b1[...].astype(f32) + b2[...].astype(f32) + b3[...].astype(f32)).astype(bf16)
    o_keep[...] = out[:256]
    o_send[...] = out[256:]
    up[:, :HEAD] = dot(rq_own[...], dq[:256], 0, 0) + dot(rq_other[...], dq[256:], 0, 0)
    up[:, HEAD:] = dot(rv_own[...], dv[:256], 0, 0) + dot(rv_other[...], dv[256:], 0, 0)
    for c in range(2):
        @pl.when(pos[2] == c)
        def _():
            gq = dot(dq, uq[:, c * HEAD:(c + 1) * HEAD], 1, 1)
            gv = dot(dv, uv[:, c * HEAD:(c + 1) * HEAD], 1, 1)
            rg_keep[:, :RANK] = gq[:256]
            rg_keep[:, RANK:] = gv[:256]
            rg_send[:, :RANK] = gq[256:]
            rg_send[:, RANK:] = gv[256:]


def finish(pos, a, b, ranks, uq, uv):
    shapes = [((256, HEAD), bf16), ((256, HEAD), bf16), ((256, 256), f32), ((256, 256), f32), ((128, 256), f32)]
    return pl.pallas_call(
        finish_kernel,
        in_specs=[SMEM] + [VMEM] * 14,
        out_specs=[VMEM] * 5,
        out_shape=[jax.ShapeDtypeStruct(s, t) for s, t in shapes],
        compiler_params=PARAMS,
        name="finish",
    )(pos, *a, *b, *ranks, uq, uv)


def quarter_kernel(pos, keep, other, r0, r1, r2, r3):
    for d, out in enumerate((r0, r1, r2, r3)):
        at = pl.multiple_of(lax.rem(pos[3] + d, 4) * 64, 64)
        out[...] = keep[pl.ds(at, 64), :] + other[pl.ds(at, 64), :]


def quarters(pos, keep, other):
    return pl.pallas_call(
        quarter_kernel,
        in_specs=[SMEM, VMEM, VMEM],
        out_specs=[VMEM] * 4,
        out_shape=[jax.ShapeDtypeStruct((64, 256), f32)] * 4,
        compiler_params=PARAMS,
        name="quarters",
    )(pos, keep, other)


def down_kernel(pos, act_t, r0, r1, r2, r3, mine, theirs, rg):
    for d, r in enumerate((r0, r1, r2, r3)):
        at = pl.multiple_of(lax.rem(pos[3] + 4 - d, 4) * 64, 64)
        rg[pl.ds(at, 64), :] = r[...]
    rows = mine.shape[0]
    for c in range(2):
        @pl.when(pos[2] == c)
        def _():
            mine[...] = dot(act_t[c * rows:(c + 1) * rows, :], rg[...])
            theirs[...] = dot(act_t[(1 - c) * rows:(2 - c) * rows, :], rg[...])


def down_terms(pos, act_t, rgs):
    rows = act_t.shape[0] // 2
    return pl.pallas_call(
        down_kernel,
        in_specs=[SMEM] + [VMEM] * 5,
        out_specs=[VMEM] * 2,
        out_shape=[jax.ShapeDtypeStruct((rows, 256), f32)] * 2,
        scratch_shapes=[pltpu.VMEM((256, 256), bf16)],
        compiler_params=PARAMS,
        name="down_terms",
    )(pos, act_t, *rgs)


def pack_kernel(mine, theirs, up, out):
    for i in range(16):
        out[i, :40, :] = mine[i * 40:(i + 1) * 40, :] + theirs[i * 40:(i + 1) * 40, :]
        out[i, 40:, :] = up[i * 8:(i + 1) * 8, :]


def pack(mine, theirs, up):
    return pl.pallas_call(
        pack_kernel,
        in_specs=[VMEM] * 3,
        out_specs=VMEM,
        out_shape=jax.ShapeDtypeStruct((16, 48, 256), f32),
        compiler_params=PARAMS,
        name="pack",
    )(mine, theirs, up)


def emit_kernel(pos, own, other, o_keep, o_other, att, down_q, up_q, down_v, up_v):
    zz = pl.program_id(0)
    halves = [own, other]
    for c in range(2):
        @pl.when(pos[2] == c)
        def _():
            for cc in range(2):
                src = halves[(c + cc) % 2]
                for i in range(16):
                    part = src[zz * 16 + i].astype(f32)
                    at = cc * 640 + i * 40
                    down_q[at:at + 40, :] = part[:40, :RANK]
                    down_v[at:at + 40, :] = part[:40, RANK:]

            @pl.when(zz == 0)
            def _():
                outs = [o_keep, o_other]
                for cc in range(2):
                    src = halves[(c + cc) % 2]
                    att[:, cc * HEAD:(cc + 1) * HEAD] = outs[(c + cc) % 2][...]
                    for i in range(16):
                        part = src[pos[3] * 16 + i].astype(f32)
                        up_q[i * 8:(i + 1) * 8, cc * HEAD:(cc + 1) * HEAD] = part[40:, :HEAD]
                        up_v[i * 8:(i + 1) * 8, cc * HEAD:(cc + 1) * HEAD] = part[40:, HEAD:]


def emit(pos, own, other, o_keep, o_other):
    whole = lambda a: pl.BlockSpec(a, lambda k: (0,) * len(a))
    return pl.pallas_call(
        emit_kernel,
        grid=(4,),
        in_specs=[SMEM] + [whole(a.shape) for a in (own, other, o_keep, o_other)],
        out_specs=[whole((256, 256)), pl.BlockSpec((1280, RANK), lambda k: (k, 0)), whole((RANK, 256)),
                   pl.BlockSpec((1280, RANK), lambda k: (k, 0)), whole((RANK, 256))],
        out_shape=[jax.ShapeDtypeStruct((256, 256), bf16), jax.ShapeDtypeStruct((5120, RANK), f32),
                   jax.ShapeDtypeStruct((RANK, 256), f32), jax.ShapeDtypeStruct((5120, RANK), f32),
                   jax.ShapeDtypeStruct((RANK, 256), f32)],
        compiler_params=PARAMS,
        name="emit",
    )(pos, own, other, o_keep, o_other)


def ring(n, d):
    return [(i, (i + d) % n) for i in range(n)]


def swap(a):
    return lax.ppermute(a, "c", ring(2, 1))


def spread(a, axis):
    one, three, two = [lax.ppermute(a, axis, ring(4, d)) for d in (1, 3, 2)]
    return [a, one, two, three]


def collect(parts, axis):
    return [parts[0]] + [lax.ppermute(parts[d], axis, ring(4, -d)) for d in (1, 2, 3)]


def half(a, index, size):
    return lax.dynamic_slice_in_dim(a, index * size, size, axis=1)


def local(act, wq, wk, wv, dq, uq, dv, uv, grad_out, levels, order, slot):
    x, y, c, z = (lax.axis_index(n).astype(jnp.int32) for n in ("x", "y", "c", "z"))
    pos = jnp.stack([x, y, c, z])
    g_other = swap(half(grad_out, 1 - c, HEAD))
    lists = visible_lists(pos, slot, levels, order)
    g = jnp.concatenate([half(grad_out, c, HEAD), g_other], axis=0)
    gs = spread(g, "y")
    kv_keep, kv_send, rv = project_kv(pos, act, wk, wv, dv, uv, g, lists)
    kv = jnp.concatenate([kv_keep, swap(kv_send)], axis=0)
    kvs = spread(kv, "x")
    q_keep, q_send, rq = project_q(pos, act, wq, dq, uq, kv, *gs[1:])
    q = jnp.concatenate([q_keep, swap(q_send)], axis=0)
    qs = spread(q, "y")
    act_t = half(act, z, act.shape[1] // 4).T
    stats = spread(row_stats(lists, qs, gs, kvs), "y")
    parts = attention_grads(lists, stats, qs, gs, kvs)
    ranks = (rq, swap(rq), rv, swap(rv))
    a = collect(parts[:4], "y")
    b = collect(parts[4:], "x")
    o_keep, o_send, rg_keep, rg_send, up = finish(pos, a, b, ranks, uq, uv)
    q0, q1, q2, q3 = quarters(pos, rg_keep, swap(rg_send))
    mine = q0 + lax.ppermute(q1, "z", ring(4, 1)) + lax.ppermute(q2, "z", ring(4, 2)) + lax.ppermute(q3, "z", ring(4, 3))
    mine, theirs = down_terms(pos, act_t, spread(mine.astype(bf16), "z"))
    o_other = swap(o_send)
    down = lax.all_to_all(pack(mine, swap(theirs), up), ("x", "y"), 0, 0, tiled=True)
    down = jnp.sum(down, axis=0).astype(bf16)
    wide = jnp.broadcast_to(down[None], (64,) + down.shape)
    wide = lax.all_to_all(wide, ("z", "x", "y"), 0, 0, tiled=True)
    att, down_q, up_q, down_v, up_v = emit(pos, wide, swap(wide), o_keep, o_other)
    return att, down_q, up_q, down_v, up_v


def solution(mesh):
    torus = Mesh(mesh.devices.reshape(4, 4, 2, 4), ("x", "y", "c", "z"))
    tm = ("x", "y", "c")
    return jax.shard_map(
        local,
        mesh=torus,
        in_specs=(
            P(tm, None),
            P(None, "z"),
            P(None, "z"),
            P(None, "z"),
            P(),
            P(None, "z"),
            P(),
            P(None, "z"),
            P(tm, "z"),
            P(),
            P(),
            P(),
        ),
        out_specs=(P(tm, "z"), P(), P(None, "z"), P(), P(None, "z")),
        check_vma=False,
    )
```

time: 305 us -> 186 us (0.61)
  waiting for transfers between devices: 121 us -> 45.4 us
  Pallas kernels: 68.2 us -> 44 us
  between operations: 14.3 us -> 0.87 us
  starting transfers between devices: 42.8 us -> 36.9 us
  local copies, waits for them, and re-layouts: 13 us -> 8.49 us
  blocking collectives: 42.3 us -> 45.4 us
    psum x1 -> x0, waiting for transfers between devices: 93.7 us -> none  [local(): up = lax.psum(up, ('x', 'y', 'c'))]
    pallas_call x1, Pallas kernels: 30.1 us -> 12.8 us  [attention_grads(): pl.pallas_call(grads_kernel, in_specs=[SMEM] + [VMEM] * 16, out_specs=[VM...]
    ppermute x15 -> x18, waiting for transfers between devices: 13.4 us -> 29.6 us  [the longest x15 27 us: spread(): one, three, two = [lax.ppermute(a, axis, ring(4, d)) for d in (1, 3, 2)]]
    pallas_call x1, Pallas kernels: 16.3 us -> 6.62 us  [row_stats(): pl.pallas_call(stats_kernel, in_specs=[SMEM] + [VMEM] * 12, out_specs=VME...]
    ppermute x6, starting transfers between devices: 7.62 us -> 2.95 us  [collect(): lax.ppermute(parts[d], axis, ring(4, -d))]
    slice x2 -> x0, local copies, waits for them, and re-layouts: 4.38 us -> none  [local(): return (attended, full[:, :RANK], up[:RANK], full[:, RANK:], up[RANK:])]
    ppermute x15 -> x18, starting transfers between devices: 22.8 us -> 19.6 us  [the longest x15 13.9 us: spread(): one, three, two = [lax.ppermute(a, axis, ring(4, d)) for d in (1, 3, 2)]]
    pallas_call x3 -> x8, Pallas kernels: 21.7 us -> 24.6 us  [the longest x2 12.5 us: project(): pl.pallas_call(kernel, grid=(width // KT,), in_specs=[SMEM, pl.BlockSpec(...]
  transfers between devices with their start and end apart: 30 -> 33, of which waited for: 11 -> 21; matrix products, arithmetic and copies ran while one was open for 1% -> 3% of each run, Pallas kernels for 16% -> 10%
where the time goes in v2:
time: 186 us; the launch traced here: 185 us
  waiting for transfers between devices  45.4 us (24%)
  blocking collectives  45.4 us (24%)
  Pallas kernels  44 us (24%)
  starting transfers between devices  36.9 us (20%)
  local copies, waits for them, and re-layouts  8.49 us (5%)
  other arithmetic  3.85 us (2%)
    all_to_all x1, blocking collectives, local(): wide = lax.all_to_all(wide, ('z', 'x', 'y'), 0, 0, tiled=True)  27.1 us
    ppermute x15, waiting for transfers between devices, spread(): one, three, two = [lax.ppermute(a, axis, ring(4, d)) for d in (1, 3, 2)]  27 us
    all_to_all x1, blocking collectives, local(): lax.all_to_all(pack(mine, swap(theirs), up), ('x', 'y'), 0, 0, tiled=True)  18.2 us
    ppermute x9, starting transfers between devices, swap(): return lax.ppermute(a, 'c', ring(2, 1))  14.3 us
    ppermute x15, starting transfers between devices, spread(): one, three, two = [lax.ppermute(a, axis, ring(4, d)) for d in (1, 3, 2)]  13.9 us
    pallas_call x1, Pallas kernels, attention_grads(): pl.pallas_call(grads_kernel, in_specs=[SMEM] + [VMEM] * 16, out_specs=[VM...  12.8 us
    pallas_call x2, Pallas kernels, project(): pl.pallas_call(kernel, grid=(width // KT,), in_specs=[SMEM, pl.BlockSpec(...  12.5 us
    ppermute x6, waiting for transfers between devices, collect(): lax.ppermute(parts[d], axis, ring(4, -d))  8.58 us
  transfers between devices with their start and end apart: 33, of which 21 were waited for; matrix products, arithmetic and copies ran while one was open for 3% of the time, Pallas kernels for 10%

profile of v2, /device:TPU:1, one launch (start us, length us, event | category | flops | bytes accessed | tf_op | source)
XLA Modules:
  0.0 184.9 jit_solution(3993314440568642576)
XLA Ops:
  1.5 1.5 collective-permute-start
  4.1 1.4 multiply_add_fusion.packed
  6.1 6.0 %lists.1.after1 = s32[24,128]{1,0:T(8,128)} custom-call(s32[4]{0:T(128)} %pad_add_fusion.pos, s32[64]{0:T(128)} %slot.1, s32[64,64]{1,0:T(8,128)} %multiply_add_fusion.packed), custom_call_target="tpu_custom_call" | custom-call | tf_op jit(solution)/shard_map/lists/pallas_call | solution.py:161
  12.8 6.9 %project_kv.1 = (bf16[256,256]{1,0:T(8,128)(2,1)}, bf16[256,256]{1,0:T(8,128)(2,1)}, bf16[256,128]{1,0:T(8,128)(2,1)}) custom-call(s32[4]{0:T(128)} %pad_add_fusion.pos, bf16[256,5120]{1,0:T(8,128)(2,1)} %act.3, bf16[5120,256]{1,0:T(8,128)(2,1)} %wk.1, bf16[5120,256]{1,0:T(8,128)(2,1)} %wv.1, bf16[5120,128]{1,0:T(8,128)(2,1)} %down.2, bf16[128,256]{1,0:T(8,128)(2,1)} %uv.1, ...), custom_call_target="tpu_custom_call" | custom-call | flops 1677721600 | bytes 9175040 | tf_op jit(solution)/shard_map/project_kv/pallas_call | solution.py:108
  19.7 2.9 %collective-permute-start.4 = (bf16[512,128]{1,0:T(8,128)(2,1)S(1)}, bf16[512,128]{1,0:T(8,128)(2,1)S(1)}, u32[]{:S(2)}, u32[]{:S(2)}) collective-permute-start(bf16[512,128]{1,0:T(8,128)(2,1)S(1)} %copy-done.2), channel_id=1, source_target_pairs={{0,24},{8,0},{16,8},{24,16},{1,25},{9,1},{17,9},{25,17},{2,26},{10... | collective-permute-start | bytes 393224 | tf_op jit(solution)/shard_map/ppermute | solution.py:476
  24.6 3.1 %collective-permute-done.4.after3.g3 = bf16[512,128]{1,0:T(8,128)(2,1)S(1)} collective-permute-done((bf16[512,128]{1,0:T(8,128)(2,1)S(1)}, bf16[512,128]{1,0:T(8,128)(2,1)S(1)}, u32[]{:S(2)}, u32[]{:S(2)}) %collective-permute-start.4) | collective-permute-done | bytes 131104 | tf_op jit(solution)/shard_map/ppermute | solution.py:476
  28.4 3.9 %collective-permute-done.2.after1.g1 = bf16[512,128]{1,0:T(8,128)(2,1)S(1)} collective-permute-done((bf16[512,128]{1,0:T(8,128)(2,1)S(1)}, bf16[512,128]{1,0:T(8,128)(2,1)S(1)}, u32[]{:S(2)}, u32[]{:S(2)}) %collective-permute-start.2) | collective-permute-done | bytes 131104 | tf_op jit(solution)/shard_map/ppermute | solution.py:476
  33.0 5.6 %project_q.1 = (bf16[256,128]{1,0:T(8,128)(2,1)}, bf16[256,128]{1,0:T(8,128)(2,1)}, bf16[256,128]{1,0:T(8,128)(2,1)}) custom-call(s32[4]{0:T(128)} %pad_add_fusion.pos, bf16[256,5120]{1,0:T(8,128)(2,1)} %act.3, bf16[5120,256]{1,0:T(8,128)(2,1)} %wq.1, bf16[5120,128]{1,0:T(8,128)(2,1)} %down.3, bf16[128,256]{1,0:T(8,128)(2,1)} %uq.1, ...), custom_call_target="tpu_custom_call" | custom-call | flops 1006632960 | bytes 6553600 | tf_op jit(solution)/shard_map/project_q/pallas_call | solution.py:108
  40.8 2.5 %collective-permute-start.11 = (bf16[512,256]{1,0:T(8,128)(2,1)}, bf16[512,256]{1,0:T(8,128)(2,1)S(1)}, u32[]{:S(2)}, u32[]{:S(2)}) collective-permute-start(bf16[512,256]{1,0:T(8,128)(2,1)} %copy-done), channel_id=1, source_target_pairs={{0,96},{32,0},{64,32},{96,64},{1,97},{33,1},{65,33},{97,65},{2,98}... | collective-permute-start | bytes 786440 | tf_op jit(solution)/shard_map/ppermute | solution.py:476
  45.5 4.5 %collective-permute-done.7.q2 = bf16[512,128]{1,0:T(8,128)(2,1)S(1)} collective-permute-done((bf16[512,128]{1,0:T(8,128)(2,1)S(1)}, bf16[512,128]{1,0:T(8,128)(2,1)S(1)}, u32[]{:S(2)}, u32[]{:S(2)}) %collective-permute-start.7) | collective-permute-done | bytes 131104 | tf_op jit(solution)/shard_map/ppermute | solution.py:476
  50.0 3.4 %collective-permute-done.6.q1 = bf16[512,128]{1,0:T(8,128)(2,1)S(1)} collective-permute-done((bf16[512,128]{1,0:T(8,128)(2,1)S(1)}, bf16[512,128]{1,0:T(8,128)(2,1)S(1)}, u32[]{:S(2)}, u32[]{:S(2)}) %collective-permute-start.6) | collective-permute-done | bytes 131104 | tf_op jit(solution)/shard_map/ppermute | solution.py:476
  53.4 5.5 %collective-permute-done.9.k1 = bf16[512,256]{1,0:T(8,128)(2,1)S(1)} collective-permute-done((bf16[512,256]{1,0:T(8,128)(2,1)}, bf16[512,256]{1,0:T(8,128)(2,1)S(1)}, u32[]{:S(2)}, u32[]{:S(2)}) %collective-permute-start.9) | collective-permute-done | bytes 262176 | tf_op jit(solution)/shard_map/ppermute | solution.py:476
  62.5 6.6 %row_stats.1.s0 = f32[48,128]{1,0:T(8,128)S(1)} custom-call(s32[24,128]{1,0:T(8,128)S(1)} %copy-done.11, bf16[512,128]{1,0:T(8,128)(2,1)S(1)} %constant_dynamic-update-slice_fusion.2.q0, bf16[512,128]{1,0:T(8,128)(2,1)S(1)} %collective-permute-done.6.q1, bf16[512,128]{1,0:T(8,128)(2,1)S(1)} %collective-permute-done.7.q2, ...), custom_call_target="tpu_custom_call" | custom-call | tf_op jit(solution)/shard_map/row_stats/pallas_call | solution.py:233
  69.4 2.6 %collective-permute-start.13 = (f32[48,128]{1,0:T(8,128)S(1)}, f32[48,128]{1,0:T(8,128)S(1)}, u32[]{:S(2)}, u32[]{:S(2)}) collective-permute-start(f32[48,128]{1,0:T(8,128)S(1)} %row_stats.1.s0), channel_id=1, source_target_pairs={{0,16},{8,24},{16,0},{24,8},{1,17},{9,25},{17,1},{25,9},{2,18},{10... | collective-permute-start | bytes 73736 | tf_op jit(solution)/shard_map/ppermute | solution.py:476
  73.6 2.3 %collective-permute-done.12.s1 = f32[48,128]{1,0:T(8,128)S(1)} collective-permute-done((f32[48,128]{1,0:T(8,128)S(1)}, f32[48,128]{1,0:T(8,128)S(1)}, u32[]{:S(2)}, u32[]{:S(2)}) %collective-permute-start.12) | collective-permute-done | bytes 24608 | tf_op jit(solution)/shard_map/ppermute | solution.py:476
  76.0 12.8 %attention_grads.1 = (f32[512,256]{1,0:T(8,128)S(1)}, bf16[512,256]{1,0:T(8,128)(2,1)S(1)}, bf16[512,256]{1,0:T(8,128)(2,1)S(1)}, bf16[512,256]{1,0:T(8,128)(2,1...) custom-call(s32[24,128]{1,0:T(8,128)S(1)} %copy-done.11, ...), custom_call_target="tpu_custom_call" | custom-call | tf_op jit(solution)/shard_map/attention_grads/pallas_call | solution.py:318
  90.6 3.3 %collective-permute-start.21 = (bf16[256,128]{1,0:T(8,128)(2,1)S(1)}, bf16[256,128]{1,0:T(8,128)(2,1)S(1)}, u32[]{:S(2)}, u32[]{:S(2)}) collective-permute-start(bf16[256,128]{1,0:T(8,128)(2,1)S(1)} %copy-done.13), channel_id=1, source_target_pairs={{0,4},{4,0},{1,5},{5,1},{2,6},{6,2},{3,7},{7,3},{8,12},{12,8},{9,1... | collective-permute-start | bytes 196616 | tf_op jit(solution)/shard_map/ppermute | solution.py:472
  95.9 5.1 %collective-permute-done.19.b2 = bf16[512,128]{1,0:T(8,128)(2,1)S(1)} collective-permute-done((bf16[512,128]{1,0:T(8,128)(2,1)S(1)}, bf16[512,128]{1,0:T(8,128)(2,1)S(1)}, u32[]{:S(2)}, u32[]{:S(2)}) %collective-permute-start.19) | collective-permute-done | bytes 131104 | tf_op jit(solution)/shard_map/ppermute | solution.py:481
  101.0 3.5 %collective-permute-done.20.b3 = bf16[512,128]{1,0:T(8,128)(2,1)S(1)} collective-permute-done((bf16[512,128]{1,0:T(8,128)(2,1)S(1)}, bf16[512,128]{1,0:T(8,128)(2,1)S(1)}, u32[]{:S(2)}, u32[]{:S(2)}) %collective-permute-start.20) | collective-permute-done | bytes 131104 | tf_op jit(solution)/shard_map/ppermute | solution.py:481
  106.6 1.2 collective-permute-done.23.other
  108.3 1.7 collective-permute-start.24
  110.0 3.3 %collective-permute-start.25 = (f32[64,256]{1,0:T(8,128)S(1)}, f32[64,256]{1,0:T(8,128)S(1)}, u32[]{:S(2)}, u32[]{:S(2)}) collective-permute-start(f32[64,256]{1,0:T(8,128)S(1)} %get-tuple-element.48), channel_id=1, source_target_pairs={{0,2},{1,3},{2,0},{3,1},{4,6},{5,7},{6,4},{7,5},{8,10},{9,11},{10,... | collective-permute-start | bytes 196616 | tf_op jit(solution)/shard_map/ppermute | solution.py:509
  114.3 2.0 %collective-permute-done.25 = f32[64,256]{1,0:T(8,128)S(1)} collective-permute-done((f32[64,256]{1,0:T(8,128)S(1)}, f32[64,256]{1,0:T(8,128)S(1)}, u32[]{:S(2)}, u32[]{:S(2)}) %collective-permute-start.25) | collective-permute-done | bytes 65568 | tf_op jit(solution)/shard_map/ppermute | solution.py:509
  116.8 1.7 collective-permute-start.29
  120.5 2.2 %collective-permute-done.28.r2 = bf16[64,256]{1,0:T(8,128)(2,1)S(1)} collective-permute-done((bf16[64,256]{1,0:T(8,128)(2,1)S(1)}, bf16[64,256]{1,0:T(8,128)(2,1)S(1)}, u32[]{:S(2)}, u32[]{:S(2)}) %collective-permute-start.28) | collective-permute-done | bytes 32800 | tf_op jit(solution)/shard_map/ppermute | solution.py:476
  124.0 3.6 %collective-permute-start.30 = (f32[640,256]{1,0:T(8,128)S(1)}, f32[640,256]{1,0:T(8,128)S(1)}, u32[]{:S(2)}, u32[]{:S(2)}) collective-permute-start(f32[640,256]{1,0:T(8,128)S(1)} %get-tuple-element.51), channel_id=1, source_target_pairs={{0,4},{4,0},{1,5},{5,1},{2,6},{6,2},{3,7},{7,3},{8,12},{12,8},{9,1... | collective-permute-start | bytes 1966088 | tf_op jit(solution)/shard_map/ppermute | solution.py:472
  127.6 1.7 collective-permute-done.30.theirs
  129.4 18.2 %all_to_all.10 = f32[16,48,256]{2,1,0:T(8,128)S(1)} all-to-all(f32[16,48,256]{2,1,0:T(8,128)S(1)} %pack.1), channel_id=1, replica_groups=mesh['x'=4,'y'=4,'c'=2,'z'=4] {'x','y'}, dimensions={0} | all-to-all | bytes 1572864 | tf_op jit(solution)/shard_map/all_to_all | solution.py:512
  147.8 27.1 %all_to_all.11.own = bf16[64,48,256]{2,1,0:T(8,128)(2,1)S(1)} all-to-all(bf16[64,48,256]{2,1,0:T(8,128)(2,1)S(1)} %broadcast_in_dim.2), channel_id=1, replica_groups=mesh['x'=4,'y'=4,'c'=2,'z'=4] {'z','x','y'}, dimensions={0} | all-to-all | bytes 3145728 | tf_op jit(solution)/shard_map/all_to_all | solution.py:515
  174.9 3.4 %collective-permute-start.31 = (bf16[64,48,256]{2,1,0:T(8,128)(2,1)S(1)}, bf16[64,48,256]{2,1,0:T(8,128)(2,1)S(1)}, u32[]{:S(2)}, u32[]{:S(2)}) collective-permute-start(bf16[64,48,256]{2,1,0:T(8,128)(2,1)S(1)} %all_to_all.11.own), channel_id=1, source_target_pairs={{0,4},{4,0},{1,5},{5,1},{2,6},{6,2},{3,7},{7,3},{8,12},{12,8},{9,1... | collective-permute-start | bytes 4718600 | tf_op jit(solution)/shard_map/ppermute | solution.py:472
  178.3 3.1 %collective-permute-done.32.o_other = bf16[256,128]{1,0:T(8,128)(2,1)S(1)} collective-permute-done((bf16[256,128]{1,0:T(8,128)(2,1)S(1)}, bf16[256,128]{1,0:T(8,128)(2,1)S(1)}, u32[]{:S(2)}, u32[]{:S(2)}) %collective-permute-start.32) | collective-permute-done | bytes 65568 | tf_op jit(solution)/shard_map/ppermute | solution.py:472
  181.5 3.4 %emit.1 = (bf16[256,256]{1,0:T(8,128)(2,1)}, f32[5120,128]{1,0:T(8,128)}, f32[128,256]{1,0:T(8,128)}, f32[5120,128]{1,0:T(8,128)}, f32[128,256]{1,0:T(8,128)}) custom-call(s32[4]{0:T(128)S(1)} %copy-done.14, bf16[64,48,256]{2,1,0:T(8,128)(2,1)S(1)} %all_to_all.11.own, bf16[64,48,256]{2,1,0:T(8,128)(2,1)S(1)} %collective-permute-done.31.other, ...), custom_call_target="tpu_custom_call" | custom-call | tf_op jit(solution)/shard_map/emit/pallas_call | solution.py:453
  (90 shorter events, 28.1 us)
Async XLA Ops:
  1.5 10.6 %collective-permute-start = (bf16[256,128]{1,0:T(8,128)(2,1)S(1)}, bf16[256,128]{1,0:T(8,128)(2,1)S(1)}, u32[]{:S(2)}, u32[]{:S(2)}) collective-permute-start(bf16[256,128]{1,0:T(8,128)(2,1)S(1)} %get-tuple-element.56), channel_id=1, source_target_pairs={{0,4},{4,0},{1,5},{5,1},{2,6},{6,2},{3,7},{7,3},{8,12},{12,8},{9,1... | collective-permute-start | bytes 196616 | tf_op jit(solution)/shard_map/ppermute | solution.py:472
  19.7 4.9 %collective-permute-start.1 = (bf16[256,256]{1,0:T(8,128)(2,1)}, bf16[256,256]{1,0:T(8,128)(2,1)S(1)}, u32[]{:S(2)}, u32[]{:S(2)}) collective-permute-start(bf16[256,256]{1,0:T(8,128)(2,1)} %get-tuple-element.31), channel_id=1, source_target_pairs={{0,4},{4,0},{1,5},{5,1},{2,6},{6,2},{3,7},{7,3},{8,12},{12,8},{9,1... | collective-permute-start | bytes 393224 | tf_op jit(solution)/shard_map/ppermute | solution.py:472
  19.7 8.0 %collective-permute-start.4 = (bf16[512,128]{1,0:T(8,128)(2,1)S(1)}, bf16[512,128]{1,0:T(8,128)(2,1)S(1)}, u32[]{:S(2)}, u32[]{:S(2)}) collective-permute-start(bf16[512,128]{1,0:T(8,128)(2,1)S(1)} %copy-done.2), channel_id=1, source_target_pairs={{0,24},{8,0},{16,8},{24,16},{1,25},{9,1},{17,9},{25,17},{2,26},{10... | collective-permute-start | bytes 393224 | tf_op jit(solution)/shard_map/ppermute | solution.py:476
  22.6 5.8 %collective-permute-start.3 = (bf16[512,128]{1,0:T(8,128)(2,1)S(1)}, bf16[512,128]{1,0:T(8,128)(2,1)S(1)}, u32[]{:S(2)}, u32[]{:S(2)}) collective-permute-start(bf16[512,128]{1,0:T(8,128)(2,1)S(1)} %copy-done.2), channel_id=1, source_target_pairs={{0,16},{8,24},{16,0},{24,8},{1,17},{9,25},{17,1},{25,9},{2,18},{10... | collective-permute-start | bytes 393224 | tf_op jit(solution)/shard_map/ppermute | solution.py:476
  23.0 9.4 %collective-permute-start.2 = (bf16[512,128]{1,0:T(8,128)(2,1)S(1)}, bf16[512,128]{1,0:T(8,128)(2,1)S(1)}, u32[]{:S(2)}, u32[]{:S(2)}) collective-permute-start(bf16[512,128]{1,0:T(8,128)(2,1)S(1)} %copy-done.2), channel_id=1, source_target_pairs={{0,8},{8,16},{16,24},{24,0},{1,9},{9,17},{17,25},{25,1},{2,10},{10... | collective-permute-start | bytes 393224 | tf_op jit(solution)/shard_map/ppermute | solution.py:476
  40.3 4.8 %collective-permute-start.8 = (bf16[512,128]{1,0:T(8,128)(2,1)S(1)}, bf16[512,128]{1,0:T(8,128)(2,1)S(1)}, u32[]{:S(2)}, u32[]{:S(2)}) collective-permute-start(bf16[512,128]{1,0:T(8,128)(2,1)S(1)} %constant_dynamic-update-slice_fusion.2.q0), channel_id=1, source_target_pairs={{0,24},{8,0},{16,8},{24,16},{1,25},{9,1},{17,9},{25,17},{2,26},{10... | collective-permute-start | bytes 393224 | tf_op jit(solution)/shard_map/ppermute | solution.py:476
  40.8 12.6 %collective-permute-start.11 = (bf16[512,256]{1,0:T(8,128)(2,1)}, bf16[512,256]{1,0:T(8,128)(2,1)S(1)}, u32[]{:S(2)}, u32[]{:S(2)}) collective-permute-start(bf16[512,256]{1,0:T(8,128)(2,1)} %copy-done), channel_id=1, source_target_pairs={{0,96},{32,0},{64,32},{96,64},{1,97},{33,1},{65,33},{97,65},{2,98}... | collective-permute-start | bytes 786440 | tf_op jit(solution)/shard_map/ppermute | solution.py:476
  43.3 10.1 %collective-permute-start.10 = (bf16[512,256]{1,0:T(8,128)(2,1)}, bf16[512,256]{1,0:T(8,128)(2,1)S(1)}, u32[]{:S(2)}, u32[]{:S(2)}) collective-permute-start(bf16[512,256]{1,0:T(8,128)(2,1)} %copy-done), channel_id=1, source_target_pairs={{0,64},{32,96},{64,0},{96,32},{1,65},{33,97},{65,1},{97,33},{2,66}... | collective-permute-start | bytes 786440 | tf_op jit(solution)/shard_map/ppermute | solution.py:476
  43.8 15.0 %collective-permute-start.9 = (bf16[512,256]{1,0:T(8,128)(2,1)}, bf16[512,256]{1,0:T(8,128)(2,1)S(1)}, u32[]{:S(2)}, u32[]{:S(2)}) collective-permute-start(bf16[512,256]{1,0:T(8,128)(2,1)} %copy-done), channel_id=1, source_target_pairs={{0,32},{32,64},{64,96},{96,0},{1,33},{33,65},{65,97},{97,1},{2,34}... | collective-permute-start | bytes 786440 | tf_op jit(solution)/shard_map/ppermute | solution.py:476
  44.4 5.6 %collective-permute-start.7 = (bf16[512,128]{1,0:T(8,128)(2,1)S(1)}, bf16[512,128]{1,0:T(8,128)(2,1)S(1)}, u32[]{:S(2)}, u32[]{:S(2)}) collective-permute-start(bf16[512,128]{1,0:T(8,128)(2,1)S(1)} %constant_dynamic-update-slice_fusion.2.q0), channel_id=1, source_target_pairs={{0,16},{8,24},{16,0},{24,8},{1,17},{9,25},{17,1},{25,9},{2,18},{10... | collective-permute-start | bytes 393224 | tf_op jit(solution)/shard_map/ppermute | solution.py:476
  45.1 8.2 %collective-permute-start.6 = (bf16[512,128]{1,0:T(8,128)(2,1)S(1)}, bf16[512,128]{1,0:T(8,128)(2,1)S(1)}, u32[]{:S(2)}, u32[]{:S(2)}) collective-permute-start(bf16[512,128]{1,0:T(8,128)(2,1)S(1)} %constant_dynamic-update-slice_fusion.2.q0), channel_id=1, source_target_pairs={{0,8},{8,16},{16,24},{24,0},{1,9},{9,17},{17,25},{25,1},{2,10},{10... | collective-permute-start | bytes 393224 | tf_op jit(solution)/shard_map/ppermute | solution.py:476
  69.1 4.0 %collective-permute-start.14 = (f32[48,128]{1,0:T(8,128)S(1)}, f32[48,128]{1,0:T(8,128)S(1)}, u32[]{:S(2)}, u32[]{:S(2)}) collective-permute-start(f32[48,128]{1,0:T(8,128)S(1)} %row_stats.1.s0), channel_id=1, source_target_pairs={{0,24},{8,0},{16,8},{24,16},{1,25},{9,1},{17,9},{25,17},{2,26},{10... | collective-permute-start | bytes 73736 | tf_op jit(solution)/shard_map/ppermute | solution.py:476
  69.4 4.2 %collective-permute-start.13 = (f32[48,128]{1,0:T(8,128)S(1)}, f32[48,128]{1,0:T(8,128)S(1)}, u32[]{:S(2)}, u32[]{:S(2)}) collective-permute-start(f32[48,128]{1,0:T(8,128)S(1)} %row_stats.1.s0), channel_id=1, source_target_pairs={{0,16},{8,24},{16,0},{24,8},{1,17},{9,25},{17,1},{25,9},{2,18},{10... | collective-permute-start | bytes 73736 | tf_op jit(solution)/shard_map/ppermute | solution.py:476
  72.1 3.9 %collective-permute-start.12 = (f32[48,128]{1,0:T(8,128)S(1)}, f32[48,128]{1,0:T(8,128)S(1)}, u32[]{:S(2)}, u32[]{:S(2)}) collective-permute-start(f32[48,128]{1,0:T(8,128)S(1)} %row_stats.1.s0), channel_id=1, source_target_pairs={{0,8},{8,16},{16,24},{24,0},{1,9},{9,17},{17,25},{25,1},{2,10},{10... | collective-permute-start | bytes 73736 | tf_op jit(solution)/shard_map/ppermute | solution.py:476
  72.1 18.5 %collective-permute-start.22 = (bf16[256,128]{1,0:T(8,128)(2,1)S(1)}, bf16[256,128]{1,0:T(8,128)(2,1)S(1)}, u32[]{:S(2)}, u32[]{:S(2)}) collective-permute-start(bf16[256,128]{1,0:T(8,128)(2,1)S(1)} %copy-done.12), channel_id=1, source_target_pairs={{0,4},{4,0},{1,5},{5,1},{2,6},{6,2},{3,7},{7,3},{8,12},{12,8},{9,1... | collective-permute-start | bytes 196616 | tf_op jit(solution)/shard_map/ppermute | solution.py:472
  88.8 6.5 %collective-permute-start.18 = (bf16[512,128]{1,0:T(8,128)(2,1)S(1)}, bf16[512,128]{1,0:T(8,128)(2,1)S(1)}, u32[]{:S(2)}, u32[]{:S(2)}) collective-permute-start(bf16[512,128]{1,0:T(8,128)(2,1)S(1)} %get-tuple-element.39), channel_id=1, source_target_pairs={{0,96},{32,0},{64,32},{96,64},{1,97},{33,1},{65,33},{97,65},{2,98}... | collective-permute-start | bytes 393224 | tf_op jit(solution)/shard_map/ppermute | solution.py:481
  89.0 15.4 %collective-permute-start.15 = (bf16[512,256]{1,0:T(8,128)(2,1)S(1)}, bf16[512,256]{1,0:T(8,128)(2,1)S(1)}, u32[]{:S(2)}, u32[]{:S(2)}) collective-permute-start(bf16[512,256]{1,0:T(8,128)(2,1)S(1)} %get-tuple-element.35), channel_id=1, source_target_pairs={{0,24},{8,0},{16,8},{24,16},{1,25},{9,1},{17,9},{25,17},{2,26},{10... | collective-permute-start | bytes 786440 | tf_op jit(solution)/shard_map/ppermute | solution.py:481
  89.5 15.0 %collective-permute-start.16 = (bf16[512,256]{1,0:T(8,128)(2,1)S(1)}, bf16[512,256]{1,0:T(8,128)(2,1)S(1)}, u32[]{:S(2)}, u32[]{:S(2)}) collective-permute-start(bf16[512,256]{1,0:T(8,128)(2,1)S(1)} %get-tuple-element.36), channel_id=1, source_target_pairs={{0,16},{8,24},{16,0},{24,8},{1,17},{9,25},{17,1},{25,9},{2,18},{10... | collective-permute-start | bytes 786440 | tf_op jit(solution)/shard_map/ppermute | solution.py:481
  89.9 14.6 %collective-permute-start.17 = (bf16[512,256]{1,0:T(8,128)(2,1)S(1)}, bf16[512,256]{1,0:T(8,128)(2,1)S(1)}, u32[]{:S(2)}, u32[]{:S(2)}) collective-permute-start(bf16[512,256]{1,0:T(8,128)(2,1)S(1)} %get-tuple-element.37), channel_id=1, source_target_pairs={{0,8},{8,16},{16,24},{24,0},{1,9},{9,17},{17,25},{25,1},{2,10},{10... | collective-permute-start | bytes 786440 | tf_op jit(solution)/shard_map/ppermute | solution.py:481
  90.6 4.2 %collective-permute-start.21 = (bf16[256,128]{1,0:T(8,128)(2,1)S(1)}, bf16[256,128]{1,0:T(8,128)(2,1)S(1)}, u32[]{:S(2)}, u32[]{:S(2)}) collective-permute-start(bf16[256,128]{1,0:T(8,128)(2,1)S(1)} %copy-done.13), channel_id=1, source_target_pairs={{0,4},{4,0},{1,5},{5,1},{2,6},{6,2},{3,7},{7,3},{8,12},{12,8},{9,1... | collective-permute-start | bytes 196616 | tf_op jit(solution)/shard_map/ppermute | solution.py:472
  94.7 6.2 %collective-permute-start.19 = (bf16[512,128]{1,0:T(8,128)(2,1)S(1)}, bf16[512,128]{1,0:T(8,128)(2,1)S(1)}, u32[]{:S(2)}, u32[]{:S(2)}) collective-permute-start(bf16[512,128]{1,0:T(8,128)(2,1)S(1)} %get-tuple-element.40), channel_id=1, source_target_pairs={{0,64},{32,96},{64,0},{96,32},{1,65},{33,97},{65,1},{97,33},{2,66}... | collective-permute-start | bytes 393224 | tf_op jit(solution)/shard_map/ppermute | solution.py:481
  95.3 9.2 %collective-permute-start.20 = (bf16[512,128]{1,0:T(8,128)(2,1)S(1)}, bf16[512,128]{1,0:T(8,128)(2,1)S(1)}, u32[]{:S(2)}, u32[]{:S(2)}) collective-permute-start(bf16[512,128]{1,0:T(8,128)(2,1)S(1)} %get-tuple-element.41), channel_id=1, source_target_pairs={{0,32},{32,64},{64,96},{96,0},{1,33},{33,65},{65,97},{97,1},{2,34}... | collective-permute-start | bytes 393224 | tf_op jit(solution)/shard_map/ppermute | solution.py:481
  105.7 2.1 %collective-permute-start.23 = (f32[256,256]{1,0:T(8,128)S(1)}, f32[256,256]{1,0:T(8,128)S(1)}, u32[]{:S(2)}, u32[]{:S(2)}) collective-permute-start(f32[256,256]{1,0:T(8,128)S(1)} %get-tuple-element.45), channel_id=1, source_target_pairs={{0,4},{4,0},{1,5},{5,1},{2,6},{6,2},{3,7},{7,3},{8,12},{12,8},{9,1... | collective-permute-start | bytes 786440 | tf_op jit(solution)/shard_map/ppermute | solution.py:472
  108.3 6.0 %collective-permute-start.24 = (f32[64,256]{1,0:T(8,128)S(1)}, f32[64,256]{1,0:T(8,128)S(1)}, u32[]{:S(2)}, u32[]{:S(2)}) collective-permute-start(f32[64,256]{1,0:T(8,128)S(1)} %get-tuple-element.47), channel_id=1, source_target_pairs={{0,1},{1,2},{2,3},{3,0},{4,5},{5,6},{6,7},{7,4},{8,9},{9,10},{10,1... | collective-permute-start | bytes 196616 | tf_op jit(solution)/shard_map/ppermute | solution.py:509
  110.0 6.3 %collective-permute-start.25 = (f32[64,256]{1,0:T(8,128)S(1)}, f32[64,256]{1,0:T(8,128)S(1)}, u32[]{:S(2)}, u32[]{:S(2)}) collective-permute-start(f32[64,256]{1,0:T(8,128)S(1)} %get-tuple-element.48), channel_id=1, source_target_pairs={{0,2},{1,3},{2,0},{3,1},{4,6},{5,7},{6,4},{7,5},{8,10},{9,11},{10,... | collective-permute-start | bytes 196616 | tf_op jit(solution)/shard_map/ppermute | solution.py:509
  113.3 3.4 %collective-permute-start.26 = (f32[64,256]{1,0:T(8,128)S(1)}, f32[64,256]{1,0:T(8,128)S(1)}, u32[]{:S(2)}, u32[]{:S(2)}) collective-permute-start(f32[64,256]{1,0:T(8,128)S(1)} %get-tuple-element.49), channel_id=1, source_target_pairs={{0,3},{1,0},{2,1},{3,2},{4,7},{5,4},{6,5},{7,6},{8,11},{9,8},{10,9... | collective-permute-start | bytes 196616 | tf_op jit(solution)/shard_map/ppermute | solution.py:509
  116.8 3.8 %collective-permute-start.29 = (bf16[64,256]{1,0:T(8,128)(2,1)S(1)}, bf16[64,256]{1,0:T(8,128)(2,1)S(1)}, u32[]{:S(2)}, u32[]{:S(2)}) collective-permute-start(bf16[64,256]{1,0:T(8,128)(2,1)S(1)} %add_convert_fusion.r0), channel_id=1, source_target_pairs={{0,3},{1,0},{2,1},{3,2},{4,7},{5,4},{6,5},{7,6},{8,11},{9,8},{10,9... | collective-permute-start | bytes 98312 | tf_op jit(solution)/shard_map/ppermute | solution.py:476
  118.5 4.3 %collective-permute-start.28 = (bf16[64,256]{1,0:T(8,128)(2,1)S(1)}, bf16[64,256]{1,0:T(8,128)(2,1)S(1)}, u32[]{:S(2)}, u32[]{:S(2)}) collective-permute-start(bf16[64,256]{1,0:T(8,128)(2,1)S(1)} %add_convert_fusion.r0), channel_id=1, source_target_pairs={{0,2},{1,3},{2,0},{3,1},{4,6},{5,7},{6,4},{7,5},{8,10},{9,11},{10,... | collective-permute-start | bytes 98312 | tf_op jit(solution)/shard_map/ppermute | solution.py:476
  119.1 4.0 %collective-permute-start.27 = (bf16[64,256]{1,0:T(8,128)(2,1)S(1)}, bf16[64,256]{1,0:T(8,128)(2,1)S(1)}, u32[]{:S(2)}, u32[]{:S(2)}) collective-permute-start(bf16[64,256]{1,0:T(8,128)(2,1)S(1)} %add_convert_fusion.r0), channel_id=1, source_target_pairs={{0,1},{1,2},{2,3},{3,0},{4,5},{5,6},{6,7},{7,4},{8,9},{9,10},{10,1... | collective-permute-start | bytes 98312 | tf_op jit(solution)/shard_map/ppermute | solution.py:476
  124.0 5.3 %collective-permute-start.30 = (f32[640,256]{1,0:T(8,128)S(1)}, f32[640,256]{1,0:T(8,128)S(1)}, u32[]{:S(2)}, u32[]{:S(2)}) collective-permute-start(f32[640,256]{1,0:T(8,128)S(1)} %get-tuple-element.51), channel_id=1, source_target_pairs={{0,4},{4,0},{1,5},{5,1},{2,6},{6,2},{3,7},{7,3},{8,12},{12,8},{9,1... | collective-permute-start | bytes 1966088 | tf_op jit(solution)/shard_map/ppermute | solution.py:472
  174.9 6.5 %collective-permute-start.31 = (bf16[64,48,256]{2,1,0:T(8,128)(2,1)S(1)}, bf16[64,48,256]{2,1,0:T(8,128)(2,1)S(1)}, u32[]{:S(2)}, u32[]{:S(2)}) collective-permute-start(bf16[64,48,256]{2,1,0:T(8,128)(2,1)S(1)} %all_to_all.11.own), channel_id=1, source_target_pairs={{0,4},{4,0},{1,5},{5,1},{2,6},{6,2},{3,7},{7,3},{8,12},{12,8},{9,1... | collective-permute-start | bytes 4718600 | tf_op jit(solution)/shard_map/ppermute | solution.py:472
  178.3 3.1 %collective-permute-start.32 = (bf16[256,128]{1,0:T(8,128)(2,1)S(1)}, bf16[256,128]{1,0:T(8,128)(2,1)S(1)}, u32[]{:S(2)}, u32[]{:S(2)}) collective-permute-start(bf16[256,128]{1,0:T(8,128)(2,1)S(1)} %get-tuple-element.54), channel_id=1, source_target_pairs={{0,4},{4,0},{1,5},{5,1},{2,6},{6,2},{3,7},{7,3},{8,12},{12,8},{9,1... | collective-permute-start | bytes 196616 | tf_op jit(solution)/shard_map/ppermute | solution.py:472
  (16 other events, 360.5 us)

commit v3 on v2

--- a/solution.py
+++ b/solution.py
@@ -20,7 +20,7 @@
 NEG = -1e30
 f32 = jnp.float32
 bf16 = jnp.bfloat16
-WIRE = bf16
+WIRE = f32
 KT = 1280
 VMEM = pl.BlockSpec(memory_space=pltpu.VMEM)
 SMEM = pl.BlockSpec(memory_space=pltpu.SMEM)
@@ -41,11 +41,11 @@
             put(send, (1 - c) * HEAD)
 
 
-def kv_kernel(pos, act, wk, wv, down, up, after0, after1, keep, send, rank, ak, av, ar):
+def proj_kernel(pos, act, wq, wk, wv, down_q, down_v, up_q, up_v, keep, send, rank_q, rank_v, aq, ak, av, rq, rv):
     step = pl.program_id(0)
     last = pl.num_programs(0) - 1
     a = act[...]
-    parts = [(ak, wk), (av, wv), (ar, down)]
+    parts = [(ak, wk), (av, wv), (rv, down_v), (aq, wq), (rq, down_q)]
 
     @pl.when(step == 0)
     def _():
@@ -59,74 +59,41 @@
 
     @pl.when(step == last)
     def _():
-        low = ar[...].astype(bf16)
-        rank[...] = low
+        low_q = rq[...].astype(bf16)
+        low_v = rv[...].astype(bf16)
+        rank_q[...] = low_q
+        rank_v[...] = low_v
         keys = ak[...].astype(bf16)
-        values = (av[...] + dot(low, up[...])).astype(bf16)
+        values = (av[...] + dot(low_v, up_v[...])).astype(bf16)
+        query = (aq[...] + dot(low_q, up_q[...])).astype(bf16)
 
         def put(ref, at):
             ref[:, :HEAD] = keys[:, at:at + HEAD]
-            ref[:, HEAD:] = values[:, at:at + HEAD]
+            ref[:, HEAD:2 * HEAD] = values[:, at:at + HEAD]
+            ref[:, 2 * HEAD:] = query[:, at:at + HEAD]
 
         by_core(pos, put, keep, send)
 
 
-def q_kernel(pos, act, wq, down, up, after0, after1, after2, after3, keep, send, rank, aq, ar):
-    step = pl.program_id(0)
-    last = pl.num_programs(0) - 1
-    a = act[...]
-    parts = [(aq, wq), (ar, down)]
-
-    @pl.when(step == 0)
-    def _():
-        for total, w in parts:
-            total[...] = dot(a, w[...])
-
-    @pl.when(step > 0)
-    def _():
-        for total, w in parts:
-            total[...] += dot(a, w[...])
-
-    @pl.when(step == last)
-    def _():
-        low = ar[...].astype(bf16)
-        rank[...] = low
-        query = (aq[...] + dot(low, up[...])).astype(bf16)
-
-        def put(ref, at):
-            ref[...] = query[:, at:at + HEAD]
-
-        by_core(pos, put, keep, send)
-
-
-def project(kernel, name, pos, act, weights, down, up, lanes, after):
+def project(pos, act, wq, wk, wv, down_q, down_v, up_q, up_v):
     rows, width = act.shape
-    cols = weights[0].shape[1]
-    n = len(weights)
+    cols = wq.shape[1]
     whole = lambda shape: pl.BlockSpec(shape, lambda k: (0, 0))
-    shapes = [(rows, lanes), (rows, lanes), (rows, RANK)]
-    return pl.pallas_call(
-        kernel,
+    shapes = [(rows, 3 * HEAD), (rows, 3 * HEAD), (rows, RANK), (rows, RANK)]
+    return pl.pallas_call(
+        proj_kernel,
         grid=(width // KT,),
         in_specs=[SMEM, pl.BlockSpec((rows, KT), lambda k: (0, k))]
-        + [pl.BlockSpec((KT, cols), lambda k: (k, 0))] * n
-        + [pl.BlockSpec((KT, RANK), lambda k: (k, 0)), whole(up.shape)] + [ANY] * len(after),
+        + [pl.BlockSpec((KT, cols), lambda k: (k, 0))] * 3
+        + [pl.BlockSpec((KT, RANK), lambda k: (k, 0))] * 2 + [whole(up_q.shape), whole(up_v.shape)],
         out_specs=[whole(s) for s in shapes],
         out_shape=[jax.ShapeDtypeStruct(s, bf16) for s in shapes],
-        scratch_shapes=[pltpu.VMEM((rows, cols), f32)] * n + [pltpu.VMEM((rows, RANK), f32)],
+        scratch_shapes=[pltpu.VMEM((rows, cols), f32)] * 3 + [pltpu.VMEM((rows, RANK), f32)] * 2,
         compiler_params=WIDE,
-        cost_estimate=pl.CostEstimate(flops=2 * rows * width * (n * cols + RANK),
-                                      bytes_accessed=2 * width * (rows + n * cols + RANK), transcendentals=0),
-        name=name,
-    )(pos, act, *weights, down, up, *after)
-
-
-def project_kv(pos, act, wk, wv, dv, uv, *after):
-    return project(kv_kernel, "project_kv", pos, act, [wk, wv], dv, uv, 2 * HEAD, after)
-
-
-def project_q(pos, act, wq, dq, uq, *after):
-    return project(q_kernel, "project_q", pos, act, [wq], dq, uq, HEAD, after)
+        cost_estimate=pl.CostEstimate(flops=2 * rows * width * (3 * cols + 2 * RANK),
+                                      bytes_accessed=2 * width * (rows + 3 * cols + 2 * RANK), transcendentals=0),
+        name="project",
+    )(pos, act, wq, wk, wv, down_q, down_v, up_q, up_v)
 
 
 def lists_kernel(pos, slot, packed, out):
@@ -171,6 +138,18 @@
     rows = parts[0].shape[0]
     for d, part in enumerate(parts):
         whole[d * rows:(d + 1) * rows, :] = part[...]
+
+
+def fill_grads(pos, gathered, whole):
+    for c in range(2):
+        @pl.when(pos[2] == c)
+        def _():
+            for d in range(4):
+                chip = lax.rem(pos[1] + 4 - d, 4)
+                for i, core in enumerate((c, 1 - c)):
+                    at = pl.multiple_of((chip * 2 + core) * 256, 256)
+                    to = d * 512 + i * 256
+                    whole[to:to + 256, :] = gathered[pl.ds(at, 256), c * HEAD:(c + 1) * HEAD]
 
 
 def load_chunk(lists, f, at, kvall):
@@ -193,9 +172,9 @@
     return counts, chunks, most
 
 
-def stats_kernel(lists, q0, q1, q2, q3, g0, g1, g2, g3, k0, k1, k2, k3, out, qall, gall, kvall, both):
+def stats_kernel(pos, lists, q0, q1, q2, q3, g, k0, k1, k2, k3, out, qall, gall, kvall, both):
     fill_all((q0, q1, q2, q3), qall)
-    fill_all((g0, g1, g2, g3), gall)
+    fill_grads(pos, g, gall)
     fill_all((k0, k1, k2, k3), kvall)
     both[...] = jnp.zeros_like(both)
     row = lax.broadcasted_iota(jnp.int32, (CHUNK, HEAD), 0)
@@ -229,23 +208,23 @@
     lax.fori_loop(0, 16 // CHAINS, frames, 0)
 
 
-def row_stats(lists, qs, gs, kvs):
+def row_stats(pos, lists, qs, g, kvs):
     return pl.pallas_call(
         stats_kernel,
-        in_specs=[SMEM] + [VMEM] * 12,
+        in_specs=[SMEM, SMEM] + [VMEM] * 9,
         out_specs=VMEM,
         out_shape=jax.ShapeDtypeStruct((48, 128), f32),
         scratch_shapes=[pltpu.VMEM((2048, HEAD), bf16), pltpu.VMEM((2048, HEAD), bf16),
                         pltpu.VMEM((2048, 2 * HEAD), bf16), pltpu.VMEM((CHAINS, 2 * FT, 2 * HEAD), bf16)],
         compiler_params=PARAMS,
         name="row_stats",
-    )(lists, *qs, *gs, *kvs)
-
-
-def grads_kernel(lists, s0, s1, s2, s3, q0, q1, q2, q3, g0, g1, g2, g3, k0, k1, k2, k3,
-                 a0, a1, a2, a3, b0, b1, b2, b3, qall, gall, kvall, both, acc, dva, norm):
+    )(pos, lists, *qs, g, *kvs)
+
+
+def grads_kernel(pos, lists, s0, s1, s2, s3, q0, q1, q2, q3, g, k0, k1, k2, k3,
+                 o, a0, a1, a2, a3, b0, b1, b2, b3, qall, gall, kvall, both, acc, dva, norm):
     fill_all((q0, q1, q2, q3), qall)
-    fill_all((g0, g1, g2, g3), gall)
+    fill_grads(pos, g, gall)
     fill_all((k0, k1, k2, k3), kvall)
     both[...] = jnp.zeros_like(both)
     dva[...] = jnp.zeros_like(dva)
@@ -297,12 +276,13 @@
         for j in range(CHAINS):
             f = t * CHAINS + j
             at = pl.multiple_of(lax.rem(f, 4) * FT, FT)
+            chip = lax.rem(pos[1] + 4 - f // 4, 4)
+            o[pl.ds(pl.multiple_of(chip * 512 + at, FT), FT), :] = acc[j, 0].T
             for d, a in enumerate((a0, a1, a2, a3)):
-                def put():
-                    a[pl.ds(at, FT), :HEAD] = acc[j, 0].T.astype(a.dtype)
-                    a[pl.ds(at, FT), HEAD:] = acc[j, 1].T.astype(a.dtype)
-
-                pl.when(f // 4 == d)(put)
+                @pl.when(f // 4 == d)
+                def _():
+                    a[pl.ds(at, FT), :] = acc[j, 1].T.astype(a.dtype)
+
         return 0
 
     lax.fori_loop(0, 16 // CHAINS, frames, 0)
@@ -313,33 +293,27 @@
         b[...] = total.astype(b.dtype)
 
 
-def attention_grads(lists, stats, qs, gs, kvs):
+def attention_grads(pos, lists, stats, qs, g, kvs):
     wire = [f32, WIRE, WIRE, WIRE]
     return pl.pallas_call(
         grads_kernel,
-        in_specs=[SMEM] + [VMEM] * 16,
-        out_specs=[VMEM] * 8,
-        out_shape=[jax.ShapeDtypeStruct((512, 2 * HEAD), t) for t in wire]
-        + [jax.ShapeDtypeStruct((512, HEAD), t) for t in wire],
+        in_specs=[SMEM, SMEM] + [VMEM] * 13,
+        out_specs=[VMEM] * 9,
+        out_shape=[jax.ShapeDtypeStruct((2048, HEAD), f32)]
+        + [jax.ShapeDtypeStruct((512, HEAD), t) for t in wire + wire],
         scratch_shapes=[pltpu.VMEM((2048, HEAD), bf16), pltpu.VMEM((2048, HEAD), bf16),
                         pltpu.VMEM((2048, 2 * HEAD), bf16), pltpu.VMEM((CHAINS, 2 * FT, 2 * HEAD), bf16),
                         pltpu.VMEM((CHAINS, 2, HEAD, FT), f32), pltpu.VMEM((CHAINS, 2048, HEAD), f32),
                         pltpu.VMEM((32, 128), f32)],
         compiler_params=PARAMS,
         name="attention_grads",
-    )(lists, *stats, *qs, *gs, *kvs)
+    )(pos, lists, *stats, *qs, g, *kvs)
 
 
 def finish_kernel(pos, a0, a1, a2, a3, b0, b1, b2, b3, rq_own, rq_other, rv_own, rv_other, uq, uv,
-                  o_keep, o_send, rg_keep, rg_send, up):
-    total = a0[...] + a1[...].astype(f32) + a2[...].astype(f32) + a3[...].astype(f32)
-    out = total[:, :HEAD].astype(bf16)
-    dq = total[:, HEAD:].astype(bf16)
+                  rg_keep, rg_send, up):
+    dq = (a0[...] + a1[...].astype(f32) + a2[...].astype(f32) + a3[...].astype(f32)).astype(bf16)
     dv = (b0[...] + b1[...].astype(f32) + b2[...].astype(f32) + b3[...].astype(f32)).astype(bf16)
-    o_keep[...] = out[:256]
-    o_send[...] = out[256:]
-    up[:, :HEAD] = dot(rq_own[...], dq[:256], 0, 0) + dot(rq_other[...], dq[256:], 0, 0)
-    up[:, HEAD:] = dot(rv_own[...], dv[:256], 0, 0) + dot(rv_other[...], dv[256:], 0, 0)
     for c in range(2):
         @pl.when(pos[2] == c)
         def _():
@@ -349,66 +323,47 @@
             rg_keep[:, RANK:] = gv[:256]
             rg_send[:, :RANK] = gq[256:]
             rg_send[:, RANK:] = gv[256:]
+    up[:, :HEAD] = dot(rq_own[...], dq[:256], 0, 0) + dot(rq_other[...], dq[256:], 0, 0)
+    up[:, HEAD:] = dot(rv_own[...], dv[:256], 0, 0) + dot(rv_other[...], dv[256:], 0, 0)
 
 
 def finish(pos, a, b, ranks, uq, uv):
-    shapes = [((256, HEAD), bf16), ((256, HEAD), bf16), ((256, 256), f32), ((256, 256), f32), ((128, 256), f32)]
     return pl.pallas_call(
         finish_kernel,
         in_specs=[SMEM] + [VMEM] * 14,
-        out_specs=[VMEM] * 5,
-        out_shape=[jax.ShapeDtypeStruct(s, t) for s, t in shapes],
+        out_specs=[VMEM] * 3,
+        out_shape=[jax.ShapeDtypeStruct((r, 256), f32) for r in (256, 256, 128)],
         compiler_params=PARAMS,
         name="finish",
     )(pos, *a, *b, *ranks, uq, uv)
 
 
-def quarter_kernel(pos, keep, other, r0, r1, r2, r3):
-    for d, out in enumerate((r0, r1, r2, r3)):
-        at = pl.multiple_of(lax.rem(pos[3] + d, 4) * 64, 64)
-        out[...] = keep[pl.ds(at, 64), :] + other[pl.ds(at, 64), :]
-
-
-def quarters(pos, keep, other):
-    return pl.pallas_call(
-        quarter_kernel,
-        in_specs=[SMEM, VMEM, VMEM],
-        out_specs=[VMEM] * 4,
-        out_shape=[jax.ShapeDtypeStruct((64, 256), f32)] * 4,
-        compiler_params=PARAMS,
-        name="quarters",
-    )(pos, keep, other)
-
-
-def down_kernel(pos, act_t, r0, r1, r2, r3, mine, theirs, rg):
-    for d, r in enumerate((r0, r1, r2, r3)):
-        at = pl.multiple_of(lax.rem(pos[3] + 4 - d, 4) * 64, 64)
-        rg[pl.ds(at, 64), :] = r[...]
+def down_kernel(pos, act_t, own, r1, r2, r3, after, mine, theirs):
+    rg = (own[...] + r1[...].astype(f32) + r2[...].astype(f32) + r3[...].astype(f32)).astype(bf16)
     rows = mine.shape[0]
     for c in range(2):
         @pl.when(pos[2] == c)
         def _():
-            mine[...] = dot(act_t[c * rows:(c + 1) * rows, :], rg[...])
-            theirs[...] = dot(act_t[(1 - c) * rows:(2 - c) * rows, :], rg[...])
-
-
-def down_terms(pos, act_t, rgs):
+            mine[...] = dot(act_t[c * rows:(c + 1) * rows, :], rg)
+            theirs[...] = dot(act_t[(1 - c) * rows:(2 - c) * rows, :], rg)
+
+
+def down_terms(pos, act_t, own, others, after):
     rows = act_t.shape[0] // 2
     return pl.pallas_call(
         down_kernel,
-        in_specs=[SMEM] + [VMEM] * 5,
+        in_specs=[SMEM] + [VMEM] * 5 + [ANY],
         out_specs=[VMEM] * 2,
         out_shape=[jax.ShapeDtypeStruct((rows, 256), f32)] * 2,
-        scratch_shapes=[pltpu.VMEM((256, 256), bf16)],
         compiler_params=PARAMS,
         name="down_terms",
-    )(pos, act_t, *rgs)
+    )(pos, act_t, own, *others, after)
 
 
 def pack_kernel(mine, theirs, up, out):
     for i in range(16):
-        out[i, :40, :] = mine[i * 40:(i + 1) * 40, :] + theirs[i * 40:(i + 1) * 40, :]
-        out[i, 40:, :] = up[i * 8:(i + 1) * 8, :]
+        part = mine[i * 40:(i + 1) * 40, :] + theirs[i * 40:(i + 1) * 40, :]
+        out[i, :, :] = jnp.concatenate([part, up[i * 8:(i + 1) * 8, :]], axis=0).astype(out.dtype)
 
 
 def pack(mine, theirs, up):
@@ -416,7 +371,7 @@
         pack_kernel,
         in_specs=[VMEM] * 3,
         out_specs=VMEM,
-        out_shape=jax.ShapeDtypeStruct((16, 48, 256), f32),
+        out_shape=jax.ShapeDtypeStruct((16, 48, 256), bf16),
         compiler_params=PARAMS,
         name="pack",
     )(mine, theirs, up)
@@ -464,6 +419,26 @@
     )(pos, own, other, o_keep, o_other)
 
 
+def total_kernel(parts, after, out):
+    total = parts[0].astype(f32)
+    for i in range(1, 16):
+        total += parts[i].astype(f32)
+    low = total.astype(bf16)
+    for i in range(64):
+        out[i, :, :] = low
+
+
+def total_for_all(parts, after):
+    return pl.pallas_call(
+        total_kernel,
+        in_specs=[VMEM, ANY],
+        out_specs=VMEM,
+        out_shape=jax.ShapeDtypeStruct((64, 48, 256), bf16),
+        compiler_params=PARAMS,
+        name="total_for_all",
+    )(parts, after)
+
+
 def ring(n, d):
     return [(i, (i + d) % n) for i in range(n)]
 
@@ -488,31 +463,24 @@
 def local(act, wq, wk, wv, dq, uq, dv, uv, grad_out, levels, order, slot):
     x, y, c, z = (lax.axis_index(n).astype(jnp.int32) for n in ("x", "y", "c", "z"))
     pos = jnp.stack([x, y, c, z])
-    g_other = swap(half(grad_out, 1 - c, HEAD))
+    g = lax.all_gather(grad_out, ("y", "c"), axis=0, tiled=True)
+    keep, send, rq, rv = project(pos, act, wq, wk, wv, dq, dv, uq, uv)
     lists = visible_lists(pos, slot, levels, order)
-    g = jnp.concatenate([half(grad_out, c, HEAD), g_other], axis=0)
-    gs = spread(g, "y")
-    kv_keep, kv_send, rv = project_kv(pos, act, wk, wv, dv, uv, g, lists)
-    kv = jnp.concatenate([kv_keep, swap(kv_send)], axis=0)
-    kvs = spread(kv, "x")
-    q_keep, q_send, rq = project_q(pos, act, wq, dq, uq, kv, *gs[1:])
-    q = jnp.concatenate([q_keep, swap(q_send)], axis=0)
-    qs = spread(q, "y")
+    whole = jnp.concatenate([keep, swap(send)], axis=0)
+    kvs = spread(whole[:, :2 * HEAD], "x")
+    qs = spread(whole[:, 2 * HEAD:], "y")
     act_t = half(act, z, act.shape[1] // 4).T
-    stats = spread(row_stats(lists, qs, gs, kvs), "y")
-    parts = attention_grads(lists, stats, qs, gs, kvs)
-    ranks = (rq, swap(rq), rv, swap(rv))
+    stats = spread(row_stats(pos, lists, qs, g, kvs), "y")
+    o, *parts = attention_grads(pos, lists, stats, qs, g, kvs)
     a = collect(parts[:4], "y")
     b = collect(parts[4:], "x")
-    o_keep, o_send, rg_keep, rg_send, up = finish(pos, a, b, ranks, uq, uv)
-    q0, q1, q2, q3 = quarters(pos, rg_keep, swap(rg_send))
-    mine = q0 + lax.ppermute(q1, "z", ring(4, 1)) + lax.ppermute(q2, "z", ring(4, 2)) + lax.ppermute(q3, "z", ring(4, 3))
-    mine, theirs = down_terms(pos, act_t, spread(mine.astype(bf16), "z"))
-    o_other = swap(o_send)
-    down = lax.all_to_all(pack(mine, swap(theirs), up), ("x", "y"), 0, 0, tiled=True)
-    down = jnp.sum(down, axis=0).astype(bf16)
-    wide = jnp.broadcast_to(down[None], (64,) + down.shape)
-    wide = lax.all_to_all(wide, ("z", "x", "y"), 0, 0, tiled=True)
+    o = lax.psum_scatter(o, "y", scatter_dimension=0, tiled=True).astype(bf16)
+    o_keep, o_other = o[:256], swap(o[256:])
+    rg_keep, rg_send, up = finish(pos, a, b, (rq, swap(rq), rv, swap(rv)), uq, uv)
+    rg = rg_keep + swap(rg_send)
+    mine, theirs = down_terms(pos, act_t, rg, spread(rg.astype(bf16), "z")[1:], o)
+    terms = lax.all_to_all(pack(mine, swap(theirs), up), ("x", "y"), 0, 0, tiled=True)
+    wide = lax.all_to_all(total_for_all(terms, o_other), ("z", "x", "y"), 0, 0, tiled=True)
     att, down_q, up_q, down_v, up_v = emit(pos, wide, swap(wide), o_keep, o_other)
     return att, down_q, up_q, down_v, up_v
 

time: 186 us -> 173 us (0.930)
  blocking collectives: 45.4 us -> 26.2 us
  between operations: 0.87 us -> 14.2 us
  starting transfers between devices: 36.9 us -> 30.8 us
  waiting for transfers between devices: 45.4 us -> 50.7 us
  local copies, waits for them, and re-layouts: 8.49 us -> 5.76 us
    all_to_all x2 -> x1, blocking collectives: 45.4 us -> 26.2 us  [local(): lax.all_to_all(total_for_all(terms, o_other), ('z', 'x', 'y'), 0, 0, tile...]
    ppermute x15 -> x12, waiting for transfers between devices: 27 us -> 16 us  [spread(): one, three, two = [lax.ppermute(a, axis, ring(4, d)) for d in (1, 3, 2)]]
    ppermute x6, waiting for transfers between devices: 8.58 us -> 19 us  [collect(): lax.ppermute(parts[d], axis, ring(4, -d))]
    all_to_all x0 -> x1, waiting for transfers between devices: none -> 7.59 us  [local(): lax.all_to_all(pack(mine, swap(theirs), up), ('x', 'y'), 0, 0, tiled=True)]
    ppermute x3 -> x0, starting transfers between devices: 5.73 us -> none  [the longest x1 3.3 us: local(): lax.ppermute(q2, 'z', ring(4, 2))]
    ppermute x9 -> x7, starting transfers between devices: 14.3 us -> 9.66 us  [swap(): return lax.ppermute(a, 'c', ring(2, 1))]
    all_to_all x0 -> x1, starting transfers between devices: none -> 3.9 us  [local(): lax.all_to_all(pack(mine, swap(theirs), up), ('x', 'y'), 0, 0, tiled=True)]
    ppermute x3 -> x0, waiting for transfers between devices: 2.66 us -> none  [the longest x1 1.97 us: local(): lax.ppermute(q2, 'z', ring(4, 2))]
  transfers between devices with their start and end apart: 33 -> 28, of which waited for: 21 -> 18; matrix products, arithmetic and copies ran while one was open for 3% -> 3% of each run, Pallas kernels for 10% -> 9%
where the time goes in v3:
time: 173 us
  waiting for transfers between devices  50.7 us (29%)
  Pallas kernels  42.5 us (25%)
  starting transfers between devices  30.8 us (18%)
  blocking collectives  26.2 us (15%)
  between operations  14.2 us (8%)
  local copies, waits for them, and re-layouts  5.76 us (3%)
  other arithmetic  2.37 us (1%)
    all_to_all x1, blocking collectives, local(): lax.all_to_all(total_for_all(terms, o_other), ('z', 'x', 'y'), 0, 0, tile...  26.2 us
    ppermute x6, waiting for transfers between devices, collect(): lax.ppermute(parts[d], axis, ring(4, -d))  19 us
    ppermute x12, waiting for transfers between devices, spread(): one, three, two = [lax.ppermute(a, axis, ring(4, d)) for d in (1, 3, 2)]  16 us
    pallas_call x1, Pallas kernels, attention_grads(): pl.pallas_call(grads_kernel, in_specs=[SMEM, SMEM] + [VMEM] * 13, out_spe...  14.7 us
    ppermute x12, starting transfers between devices, spread(): one, three, two = [lax.ppermute(a, axis, ring(4, d)) for d in (1, 3, 2)]  13.7 us
    ppermute x7, starting transfers between devices, swap(): return lax.ppermute(a, 'c', ring(2, 1))  9.66 us
    pallas_call x1, Pallas kernels, project(): pl.pallas_call(proj_kernel, grid=(width // KT,), in_specs=[SMEM, pl.Block...  8.73 us
    all_to_all x1, waiting for transfers between devices, local(): lax.all_to_all(pack(mine, swap(theirs), up), ('x', 'y'), 0, 0, tiled=True)  7.59 us
  transfers between devices with their start and end apart: 28, of which 18 were waited for; matrix products, arithmetic and copies ran while one was open for 3% of the time, Pallas kernels for 9%

profile of v3, /device:TPU:1, one launch (start us, length us, event | category | flops | bytes accessed | tf_op | source)
XLA Modules:
  0.0 172.5 jit_solution(16680403917378432297)
XLA Ops:
  8.6 8.7 %project.1 = (bf16[256,384]{1,0:T(8,128)(2,1)}, bf16[256,384]{1,0:T(8,128)(2,1)}, bf16[256,128]{1,0:T(8,128)(2,1)}, bf16[256,128]{1,0:T(8,128)(2,1)}) custom-call(s32[4]{0:T(128)} %pad_add_fusion.pos, bf16[256,5120]{1,0:T(8,128)(2,1)} %act.1, bf16[5120,256]{1,0:T(8,128)(2,1)} %wq.1, bf16[5120,256]{1,0:T(8,128)(2,1)} %wk.1, bf16[5120,256]{1,0:T(8,128)(2,1)} %wv.1, ...), custom_call_target="tpu_custom_call" | custom-call | flops 2684354560 | bytes 13107200 | tf_op jit(solution)/shard_map/project/pallas_call | solution.py:83
  17.3 1.5 collective-permute-start
  20.1 2.9 %collective-permute-start.3 = (bf16[512,128]{1,0:T(8,128)(2,1)S(1)}, bf16[512,128]{1,0:T(8,128)(2,1)S(1)}, u32[]{:S(2)}, u32[]{:S(2)}) collective-permute-start(bf16[512,128]{1,0:T(8,128)(2,1)S(1)} %slice.16.q0), channel_id=1, source_target_pairs={{0,24},{8,0},{16,8},{24,16},{1,25},{9,1},{17,9},{25,17},{2,26},{10... | collective-permute-start | bytes 393224 | tf_op jit(solution)/shard_map/ppermute | solution.py:451
  23.0 2.6 %collective-permute-start.6 = (bf16[512,256]{1,0:T(8,128)(2,1)S(1)}, bf16[512,256]{1,0:T(8,128)(2,1)S(1)}, u32[]{:S(2)}, u32[]{:S(2)}) collective-permute-start(bf16[512,256]{1,0:T(8,128)(2,1)S(1)} %slice.17.k0), channel_id=1, source_target_pairs={{0,96},{32,0},{64,32},{96,64},{1,97},{33,1},{65,33},{97,65},{2,98}... | collective-permute-start | bytes 786440 | tf_op jit(solution)/shard_map/ppermute | solution.py:451
  28.6 6.0 %lists.1 = s32[24,128]{1,0:T(8,128)} custom-call(s32[4]{0:T(128)} %pad_add_fusion.pos, s32[64]{0:T(128)} %slot.1, s32[64,64]{1,0:T(8,128)} %multiply_add_fusion.packed), custom_call_target="tpu_custom_call" | custom-call | tf_op jit(solution)/shard_map/lists/pallas_call | solution.py:128
  34.6 3.4 %collective-permute-done.1.q1 = bf16[512,128]{1,0:T(8,128)(2,1)S(1)} collective-permute-done((bf16[512,128]{1,0:T(8,128)(2,1)S(1)}, bf16[512,128]{1,0:T(8,128)(2,1)S(1)}, u32[]{:S(2)}, u32[]{:S(2)}) %collective-permute-start.1) | collective-permute-done | bytes 131104 | tf_op jit(solution)/shard_map/ppermute | solution.py:451
  38.1 2.9 %collective-permute-done.4.k1 = bf16[512,256]{1,0:T(8,128)(2,1)S(1)} collective-permute-done((bf16[512,256]{1,0:T(8,128)(2,1)S(1)}, bf16[512,256]{1,0:T(8,128)(2,1)S(1)}, u32[]{:S(2)}, u32[]{:S(2)}) %collective-permute-start.4) | collective-permute-done | bytes 262176 | tf_op jit(solution)/shard_map/ppermute | solution.py:451
  40.9 1.2 copy-done
  42.9 6.7 %row_stats.1.s0 = f32[48,128]{1,0:T(8,128)S(1)} custom-call(s32[4]{0:T(128)S(1)} %copy-done.6, s32[24,128]{1,0:T(8,128)S(1)} %copy-done.3, bf16[512,128]{1,0:T(8,128)(2,1)S(1)} %slice.16.q0, bf16[512,128]{1,0:T(8,128)(2,1)S(1)} %collective-permute-done.1.q1, bf16[512,128]{1,0:T(8,128)(2,1)S(1)} %collective-permute-done.2.q2, ...), custom_call_target="tpu_custom_call" | custom-call | tf_op jit(solution)/shard_map/row_stats/pallas_call | solution.py:212
  50.2 1.0 collective-permute-start.7
  51.1 1.2 collective-permute-done.9.s3
  52.3 2.0 %collective-permute-done.8.s2 = f32[48,128]{1,0:T(8,128)S(1)} collective-permute-done((f32[48,128]{1,0:T(8,128)S(1)}, f32[48,128]{1,0:T(8,128)S(1)}, u32[]{:S(2)}, u32[]{:S(2)}) %collective-permute-start.8) | collective-permute-done | bytes 24608 | tf_op jit(solution)/shard_map/ppermute | solution.py:451
  54.7 14.7 %attention_grads.1 = (f32[2048,128]{1,0:T(8,128)}, f32[512,128]{1,0:T(8,128)S(1)}, f32[512,128]{1,0:T(8,128)S(1)}, f32[512,128]{1,0:T(8,128)S(1)}, f32[512,128]{...) custom-call(s32[4]{0:T(128)S(1)} %copy-done.6, ...), custom_call_target="tpu_custom_call" | custom-call | tf_op jit(solution)/shard_map/attention_grads/pallas_call | solution.py:298
  70.8 1.6 collective-permute-start.10
  72.4 2.4 %collective-permute-start.16 = (bf16[256,128]{1,0:T(8,128)(2,1)S(1)}, bf16[256,128]{1,0:T(8,128)(2,1)S(1)}, u32[]{:S(2)}, u32[]{:S(2)}) collective-permute-start(bf16[256,128]{1,0:T(8,128)(2,1)S(1)} %copy-done.4), channel_id=1, source_target_pairs={{0,4},{4,0},{1,5},{5,1},{2,6},{6,2},{3,7},{7,3},{8,12},{12,8},{9,1... | collective-permute-start | bytes 196616 | tf_op jit(solution)/shard_map/ppermute | solution.py:447
  77.3 7.4 %collective-permute-done.11.a2 = f32[512,128]{1,0:T(8,128)S(1)} collective-permute-done((f32[512,128]{1,0:T(8,128)}, f32[512,128]{1,0:T(8,128)S(1)}, u32[]{:S(2)}, u32[]{:S(2)}) %collective-permute-start.11) | collective-permute-done | bytes 262176 | tf_op jit(solution)/shard_map/ppermute | solution.py:456
  84.6 11.4 %collective-permute-done.12.a3 = f32[512,128]{1,0:T(8,128)S(1)} collective-permute-done((f32[512,128]{1,0:T(8,128)S(1)}, f32[512,128]{1,0:T(8,128)S(1)}, u32[]{:S(2)}, u32[]{:S(2)}) %collective-permute-start.12) | collective-permute-done | bytes 262176 | tf_op jit(solution)/shard_map/ppermute | solution.py:456
  96.0 1.2 finish.1
  97.9 1.2 collective-permute-done.18
  99.1 3.8 %collective-permute-start.21 = (bf16[256,256]{1,0:T(8,128)(2,1)S(1)}, bf16[256,256]{1,0:T(8,128)(2,1)S(1)}, u32[]{:S(2)}, u32[]{:S(2)}) collective-permute-start(bf16[256,256]{1,0:T(8,128)(2,1)S(1)} %get-tuple-element.41), channel_id=1, source_target_pairs={{0,3},{1,0},{2,1},{3,2},{4,7},{5,4},{6,5},{7,6},{8,11},{9,8},{10,9... | collective-permute-start | bytes 393224 | tf_op jit(solution)/shard_map/ppermute | solution.py:451
  103.6 1.1 constant_dynamic-slice_fusion
  105.0 1.0 convert_element_type.7.after
  106.0 2.6 %collective-permute-done.21.r3 = bf16[256,256]{1,0:T(8,128)(2,1)S(1)} collective-permute-done((bf16[256,256]{1,0:T(8,128)(2,1)S(1)}, bf16[256,256]{1,0:T(8,128)(2,1)S(1)}, u32[]{:S(2)}, u32[]{:S(2)}) %collective-permute-start.21) | collective-permute-done | bytes 131104 | tf_op jit(solution)/shard_map/ppermute | solution.py:451
  108.9 3.2 %collective-permute-done.19.r1 = bf16[256,256]{1,0:T(8,128)(2,1)S(1)} collective-permute-done((bf16[256,256]{1,0:T(8,128)(2,1)S(1)}, bf16[256,256]{1,0:T(8,128)(2,1)S(1)}, u32[]{:S(2)}, u32[]{:S(2)}) %collective-permute-start.19) | collective-permute-done | bytes 131104 | tf_op jit(solution)/shard_map/ppermute | solution.py:451
  112.0 0.9 down_terms.1
  113.8 1.7 collective-permute-done.22.theirs
  116.4 3.9 %all-to-all-start = ((bf16[16,48,256]{2,1,0:T(8,128)(2,1)}), bf16[16,48,256]{2,1,0:T(8,128)(2,1)S(1)}, u32[]{:S(2)}, u32[]{:S(2)}) async-start(bf16[16,48,256]{2,1,0:T(8,128)(2,1)} %pack.1), calls=%async_computation.1 | async-start | bytes 786432 | tf_op jit(solution)/shard_map/all_to_all | solution.py:482
  121.9 7.6 %all-to-all-done.parts = bf16[16,48,256]{2,1,0:T(8,128)(2,1)S(1)} async-done(((bf16[16,48,256]{2,1,0:T(8,128)(2,1)}), bf16[16,48,256]{2,1,0:T(8,128)(2,1)S(1)}, u32[]{:S(2)}, u32[]{:S(2)}) %all-to-all-start) | async-done | bytes 393248 | tf_op jit(solution)/shard_map/all_to_all | solution.py:482
  129.7 26.2 %all_to_all.10.own = bf16[64,48,256]{2,1,0:T(8,128)(2,1)S(1)} all-to-all(bf16[64,48,256]{2,1,0:T(8,128)(2,1)S(1)} %total_for_all.1), channel_id=1, replica_groups=mesh['x'=4,'y'=4,'c'=2,'z'=4] {'z','x','y'}, dimensions={0} | all-to-all | bytes 3145728 | tf_op jit(solution)/shard_map/all_to_all | solution.py:483
  155.8 3.4 %collective-permute-start.24 = (bf16[64,48,256]{2,1,0:T(8,128)(2,1)S(1)}, bf16[64,48,256]{2,1,0:T(8,128)(2,1)S(1)}, u32[]{:S(2)}, u32[]{:S(2)}) collective-permute-start(bf16[64,48,256]{2,1,0:T(8,128)(2,1)S(1)} %all_to_all.10.own), channel_id=1, source_target_pairs={{0,4},{4,0},{1,5},{5,1},{2,6},{6,2},{3,7},{7,3},{8,12},{12,8},{9,1... | collective-permute-start | bytes 4718600 | tf_op jit(solution)/shard_map/ppermute | solution.py:447
  159.2 3.0 %collective-permute-done.24.other = bf16[64,48,256]{2,1,0:T(8,128)(2,1)S(1)} collective-permute-done((bf16[64,48,256]{2,1,0:T(8,128)(2,1)S(1)}, bf16[64,48,256]{2,1,0:T(8,128)(2,1)S(1)}, u32[]{:S(2)}, u32[]{:S(2)}) %collective-permute-start.24) | collective-permute-done | bytes 1572896 | tf_op jit(solution)/shard_map/ppermute | solution.py:447
  162.3 3.4 %emit.1 = (bf16[256,256]{1,0:T(8,128)(2,1)}, f32[5120,128]{1,0:T(8,128)}, f32[128,256]{1,0:T(8,128)}, f32[5120,128]{1,0:T(8,128)}, f32[128,256]{1,0:T(8,128)}) custom-call(s32[4]{0:T(128)S(1)} %copy-done.6, bf16[64,48,256]{2,1,0:T(8,128)(2,1)S(1)} %all_to_all.10.own, bf16[64,48,256]{2,1,0:T(8,128)(2,1)S(1)} %collective-permute-done.24.other, ...), custom_call_target="tpu_custom_call" | custom-call | tf_op jit(solution)/shard_map/emit/pallas_call | solution.py:408
  (72 shorter events, 16.8 us)
Async XLA Ops:
  7.2 33.8 %all-gather.2.cloned.1.call-start = ((), (), s32[]{:S(2)}) async-start(), calls=%async_computation.3 | async-start | bytes 1179648 | tf_op jit(solution)/shard_map/all_gather | solution.py:466
  7.9 97.1 %reduce-scatter.2.cloned.1.call-start = ((), (), s32[]{:S(2)}) async-start(), calls=%async_computation.4 | async-start | bytes 1310720 | tf_op jit(solution)/shard_map/reduce_scatter | solution.py:477
  8.6 32.4 %copy-start.6 = (s32[4]{0:T(128)S(1)}, s32[4]{0:T(128)}, u32[]{:S(2)}) copy-start(s32[4]{0:T(128)} %pad_add_fusion.pos) | copy-start | bytes 52
  17.3 2.8 %collective-permute-start = (bf16[256,384]{1,0:T(8,128)(2,1)}, bf16[256,384]{1,0:T(8,128)(2,1)S(1)}, u32[]{:S(2)}, u32[]{:S(2)}) collective-permute-start(bf16[256,384]{1,0:T(8,128)(2,1)} %get-tuple-element.24), channel_id=1, source_target_pairs={{0,4},{4,0},{1,5},{5,1},{2,6},{6,2},{3,7},{7,3},{8,12},{12,8},{9,1... | collective-permute-start | bytes 589832 | tf_op jit(solution)/shard_map/ppermute | solution.py:447
  20.1 7.2 %collective-permute-start.3 = (bf16[512,128]{1,0:T(8,128)(2,1)S(1)}, bf16[512,128]{1,0:T(8,128)(2,1)S(1)}, u32[]{:S(2)}, u32[]{:S(2)}) collective-permute-start(bf16[512,128]{1,0:T(8,128)(2,1)S(1)} %slice.16.q0), channel_id=1, source_target_pairs={{0,24},{8,0},{16,8},{24,16},{1,25},{9,1},{17,9},{25,17},{2,26},{10... | collective-permute-start | bytes 393224 | tf_op jit(solution)/shard_map/ppermute | solution.py:451
  23.0 15.0 %collective-permute-start.6 = (bf16[512,256]{1,0:T(8,128)(2,1)S(1)}, bf16[512,256]{1,0:T(8,128)(2,1)S(1)}, u32[]{:S(2)}, u32[]{:S(2)}) collective-permute-start(bf16[512,256]{1,0:T(8,128)(2,1)S(1)} %slice.17.k0), channel_id=1, source_target_pairs={{0,96},{32,0},{64,32},{96,64},{1,97},{33,1},{65,33},{97,65},{2,98}... | collective-permute-start | bytes 786440 | tf_op jit(solution)/shard_map/ppermute | solution.py:451
  25.6 12.5 %collective-permute-start.5 = (bf16[512,256]{1,0:T(8,128)(2,1)S(1)}, bf16[512,256]{1,0:T(8,128)(2,1)S(1)}, u32[]{:S(2)}, u32[]{:S(2)}) collective-permute-start(bf16[512,256]{1,0:T(8,128)(2,1)S(1)} %slice.17.k0), channel_id=1, source_target_pairs={{0,64},{32,96},{64,0},{96,32},{1,65},{33,97},{65,1},{97,33},{2,66}... | collective-permute-start | bytes 786440 | tf_op jit(solution)/shard_map/ppermute | solution.py:451
  26.1 14.8 %collective-permute-start.4 = (bf16[512,256]{1,0:T(8,128)(2,1)S(1)}, bf16[512,256]{1,0:T(8,128)(2,1)S(1)}, u32[]{:S(2)}, u32[]{:S(2)}) collective-permute-start(bf16[512,256]{1,0:T(8,128)(2,1)S(1)} %slice.17.k0), channel_id=1, source_target_pairs={{0,32},{32,64},{64,96},{96,0},{1,33},{33,65},{65,97},{97,1},{2,34}... | collective-permute-start | bytes 786440 | tf_op jit(solution)/shard_map/ppermute | solution.py:451
  26.9 7.7 %collective-permute-start.2 = (bf16[512,128]{1,0:T(8,128)(2,1)S(1)}, bf16[512,128]{1,0:T(8,128)(2,1)S(1)}, u32[]{:S(2)}, u32[]{:S(2)}) collective-permute-start(bf16[512,128]{1,0:T(8,128)(2,1)S(1)} %slice.16.q0), channel_id=1, source_target_pairs={{0,16},{8,24},{16,0},{24,8},{1,17},{9,25},{17,1},{25,9},{2,18},{10... | collective-permute-start | bytes 393224 | tf_op jit(solution)/shard_map/ppermute | solution.py:451
  27.3 10.7 %collective-permute-start.1 = (bf16[512,128]{1,0:T(8,128)(2,1)S(1)}, bf16[512,128]{1,0:T(8,128)(2,1)S(1)}, u32[]{:S(2)}, u32[]{:S(2)}) collective-permute-start(bf16[512,128]{1,0:T(8,128)(2,1)S(1)} %slice.16.q0), channel_id=1, source_target_pairs={{0,8},{8,16},{16,24},{24,0},{1,9},{9,17},{17,25},{25,1},{2,10},{10... | collective-permute-start | bytes 393224 | tf_op jit(solution)/shard_map/ppermute | solution.py:451
  28.0 68.0 %copy-start.1 = (bf16[128,256]{1,0:T(8,128)(2,1)S(1)}, bf16[128,256]{1,0:T(8,128)(2,1)}, u32[]{:S(2)}) copy-start(bf16[128,256]{1,0:T(8,128)(2,1)} %uq.1) | copy-start | bytes 196612
  28.0 68.0 %copy-start.2 = (bf16[128,256]{1,0:T(8,128)(2,1)S(1)}, bf16[128,256]{1,0:T(8,128)(2,1)}, u32[]{:S(2)}) copy-start(bf16[128,256]{1,0:T(8,128)(2,1)} %uv.1) | copy-start | bytes 196612
  42.9 32.0 %copy-start.5 = (bf16[256,128]{1,0:T(8,128)(2,1)S(1)}, bf16[256,128]{1,0:T(8,128)(2,1)}, u32[]{:S(2)}) copy-start(bf16[256,128]{1,0:T(8,128)(2,1)} %get-tuple-element.34.rv_own) | copy-start | bytes 196612
  49.6 2.7 %collective-permute-start.9 = (f32[48,128]{1,0:T(8,128)S(1)}, f32[48,128]{1,0:T(8,128)S(1)}, u32[]{:S(2)}, u32[]{:S(2)}) collective-permute-start(f32[48,128]{1,0:T(8,128)S(1)} %row_stats.1.s0), channel_id=1, source_target_pairs={{0,24},{8,0},{16,8},{24,16},{1,25},{9,1},{17,9},{25,17},{2,26},{10... | collective-permute-start | bytes 73736 | tf_op jit(solution)/shard_map/ppermute | solution.py:451
  50.1 4.2 %collective-permute-start.8 = (f32[48,128]{1,0:T(8,128)S(1)}, f32[48,128]{1,0:T(8,128)S(1)}, u32[]{:S(2)}, u32[]{:S(2)}) collective-permute-start(f32[48,128]{1,0:T(8,128)S(1)} %row_stats.1.s0), channel_id=1, source_target_pairs={{0,16},{8,24},{16,0},{24,8},{1,17},{9,25},{17,1},{25,9},{2,18},{10... | collective-permute-start | bytes 73736 | tf_op jit(solution)/shard_map/ppermute | solution.py:451
  50.2 4.6 %collective-permute-start.7 = (f32[48,128]{1,0:T(8,128)S(1)}, f32[48,128]{1,0:T(8,128)S(1)}, u32[]{:S(2)}, u32[]{:S(2)}) collective-permute-start(f32[48,128]{1,0:T(8,128)S(1)} %row_stats.1.s0), channel_id=1, source_target_pairs={{0,8},{8,16},{16,24},{24,0},{1,9},{9,17},{17,25},{25,1},{2,10},{10... | collective-permute-start | bytes 73736 | tf_op jit(solution)/shard_map/ppermute | solution.py:451
  70.8 6.2 %collective-permute-start.10 = (f32[512,128]{1,0:T(8,128)}, f32[512,128]{1,0:T(8,128)S(1)}, u32[]{:S(2)}, u32[]{:S(2)}) collective-permute-start(f32[512,128]{1,0:T(8,128)} %copy-done.8), channel_id=1, source_target_pairs={{0,24},{8,0},{16,8},{24,16},{1,25},{9,1},{17,9},{25,17},{2,26},{10... | collective-permute-start | bytes 786440 | tf_op jit(solution)/shard_map/ppermute | solution.py:456
  72.4 3.3 %collective-permute-start.16 = (bf16[256,128]{1,0:T(8,128)(2,1)S(1)}, bf16[256,128]{1,0:T(8,128)(2,1)S(1)}, u32[]{:S(2)}, u32[]{:S(2)}) collective-permute-start(bf16[256,128]{1,0:T(8,128)(2,1)S(1)} %copy-done.4), channel_id=1, source_target_pairs={{0,4},{4,0},{1,5},{5,1},{2,6},{6,2},{3,7},{7,3},{8,12},{12,8},{9,1... | collective-permute-start | bytes 196616 | tf_op jit(solution)/shard_map/ppermute | solution.py:447
  74.8 1.3 collective-permute-start.17
  74.9 9.7 %collective-permute-start.11 = (f32[512,128]{1,0:T(8,128)}, f32[512,128]{1,0:T(8,128)S(1)}, u32[]{:S(2)}, u32[]{:S(2)}) collective-permute-start(f32[512,128]{1,0:T(8,128)} %copy-done.7), channel_id=1, source_target_pairs={{0,16},{8,24},{16,0},{24,8},{1,17},{9,25},{17,1},{25,9},{2,18},{10... | collective-permute-start | bytes 786440 | tf_op jit(solution)/shard_map/ppermute | solution.py:456
  75.5 20.5 %collective-permute-start.12 = (f32[512,128]{1,0:T(8,128)S(1)}, f32[512,128]{1,0:T(8,128)S(1)}, u32[]{:S(2)}, u32[]{:S(2)}) collective-permute-start(f32[512,128]{1,0:T(8,128)S(1)} %get-tuple-element.28), channel_id=1, source_target_pairs={{0,8},{8,16},{16,24},{24,0},{1,9},{9,17},{17,25},{25,1},{2,10},{10... | collective-permute-start | bytes 786440 | tf_op jit(solution)/shard_map/ppermute | solution.py:456
  75.7 20.3 %collective-permute-start.13 = (f32[512,128]{1,0:T(8,128)S(1)}, f32[512,128]{1,0:T(8,128)S(1)}, u32[]{:S(2)}, u32[]{:S(2)}) collective-permute-start(f32[512,128]{1,0:T(8,128)S(1)} %get-tuple-element.30), channel_id=1, source_target_pairs={{0,96},{32,0},{64,32},{96,64},{1,97},{33,1},{65,33},{97,65},{2,98}... | collective-permute-start | bytes 786440 | tf_op jit(solution)/shard_map/ppermute | solution.py:456
  76.1 19.9 %collective-permute-start.14 = (f32[512,128]{1,0:T(8,128)S(1)}, f32[512,128]{1,0:T(8,128)S(1)}, u32[]{:S(2)}, u32[]{:S(2)}) collective-permute-start(f32[512,128]{1,0:T(8,128)S(1)} %get-tuple-element.31), channel_id=1, source_target_pairs={{0,64},{32,96},{64,0},{96,32},{1,65},{33,97},{65,1},{97,33},{2,66}... | collective-permute-start | bytes 786440 | tf_op jit(solution)/shard_map/ppermute | solution.py:456
  77.0 19.0 %collective-permute-start.15 = (f32[512,128]{1,0:T(8,128)S(1)}, f32[512,128]{1,0:T(8,128)S(1)}, u32[]{:S(2)}, u32[]{:S(2)}) collective-permute-start(f32[512,128]{1,0:T(8,128)S(1)} %get-tuple-element.32), channel_id=1, source_target_pairs={{0,32},{32,64},{64,96},{96,0},{1,33},{33,65},{65,97},{97,1},{2,34}... | collective-permute-start | bytes 786440 | tf_op jit(solution)/shard_map/ppermute | solution.py:456
  97.2 1.8 %collective-permute-start.18 = (f32[256,256]{1,0:T(8,128)S(1)}, f32[256,256]{1,0:T(8,128)S(1)}, u32[]{:S(2)}, u32[]{:S(2)}) collective-permute-start(f32[256,256]{1,0:T(8,128)S(1)} %get-tuple-element.36), channel_id=1, source_target_pairs={{0,4},{4,0},{1,5},{5,1},{2,6},{6,2},{3,7},{7,3},{8,12},{12,8},{9,1... | collective-permute-start | bytes 786440 | tf_op jit(solution)/shard_map/ppermute | solution.py:447
  99.1 9.4 %collective-permute-start.21 = (bf16[256,256]{1,0:T(8,128)(2,1)S(1)}, bf16[256,256]{1,0:T(8,128)(2,1)S(1)}, u32[]{:S(2)}, u32[]{:S(2)}) collective-permute-start(bf16[256,256]{1,0:T(8,128)(2,1)S(1)} %get-tuple-element.41), channel_id=1, source_target_pairs={{0,3},{1,0},{2,1},{3,2},{4,7},{5,4},{6,5},{7,6},{8,11},{9,8},{10,9... | collective-permute-start | bytes 393224 | tf_op jit(solution)/shard_map/ppermute | solution.py:451
  102.9 6.0 %collective-permute-start.20 = (bf16[256,256]{1,0:T(8,128)(2,1)S(1)}, bf16[256,256]{1,0:T(8,128)(2,1)S(1)}, u32[]{:S(2)}, u32[]{:S(2)}) collective-permute-start(bf16[256,256]{1,0:T(8,128)(2,1)S(1)} %get-tuple-element.41), channel_id=1, source_target_pairs={{0,2},{1,3},{2,0},{3,1},{4,6},{5,7},{6,4},{7,5},{8,10},{9,11},{10,... | collective-permute-start | bytes 393224 | tf_op jit(solution)/shard_map/ppermute | solution.py:451
  102.9 9.1 %collective-permute-start.19 = (bf16[256,256]{1,0:T(8,128)(2,1)S(1)}, bf16[256,256]{1,0:T(8,128)(2,1)S(1)}, u32[]{:S(2)}, u32[]{:S(2)}) collective-permute-start(bf16[256,256]{1,0:T(8,128)(2,1)S(1)} %get-tuple-element.41), channel_id=1, source_target_pairs={{0,1},{1,2},{2,3},{3,0},{4,5},{5,6},{6,7},{7,4},{8,9},{9,10},{10,1... | collective-permute-start | bytes 393224 | tf_op jit(solution)/shard_map/ppermute | solution.py:451
  113.0 2.6 %collective-permute-start.22 = (f32[640,256]{1,0:T(8,128)S(1)}, f32[640,256]{1,0:T(8,128)S(1)}, u32[]{:S(2)}, u32[]{:S(2)}) collective-permute-start(f32[640,256]{1,0:T(8,128)S(1)} %get-tuple-element.39), channel_id=1, source_target_pairs={{0,4},{4,0},{1,5},{5,1},{2,6},{6,2},{3,7},{7,3},{8,12},{12,8},{9,1... | collective-permute-start | bytes 1966088 | tf_op jit(solution)/shard_map/ppermute | solution.py:447
  116.4 13.1 %all-to-all-start = ((bf16[16,48,256]{2,1,0:T(8,128)(2,1)}), bf16[16,48,256]{2,1,0:T(8,128)(2,1)S(1)}, u32[]{:S(2)}, u32[]{:S(2)}) async-start(bf16[16,48,256]{2,1,0:T(8,128)(2,1)} %pack.1), calls=%async_computation.1 | async-start | bytes 786432 | tf_op jit(solution)/shard_map/all_to_all | solution.py:482
  120.3 1.6 collective-permute-start.23
  155.8 6.4 %collective-permute-start.24 = (bf16[64,48,256]{2,1,0:T(8,128)(2,1)S(1)}, bf16[64,48,256]{2,1,0:T(8,128)(2,1)S(1)}, u32[]{:S(2)}, u32[]{:S(2)}) collective-permute-start(bf16[64,48,256]{2,1,0:T(8,128)(2,1)S(1)} %all_to_all.10.own), channel_id=1, source_target_pairs={{0,4},{4,0},{1,5},{5,1},{2,6},{6,2},{3,7},{7,3},{8,12},{12,8},{9,1... | collective-permute-start | bytes 4718600 | tf_op jit(solution)/shard_map/ppermute | solution.py:447
  (8 other events, 88.6 us)
Sparse Core Ops, SparseCore 0:
  9.7 29.1 all-gather.1
  70.9 28.9 reduce-scatter.1

commit v4 on v3

--- a/solution.py
+++ b/solution.py
@@ -33,15 +33,15 @@
     return lax.dot_general(a, b, (((ca,), (cb,)), ((), ())), preferred_element_type=f32)
 
 
-def by_core(pos, put, keep, send):
+def by_core(put, keep, send):
     for c in range(2):
-        @pl.when(pos[2] == c)
+        @pl.when(lax.axis_index("c") == c)
         def _():
             put(keep, c * HEAD)
             put(send, (1 - c) * HEAD)
 
 
-def proj_kernel(pos, act, wq, wk, wv, down_q, down_v, up_q, up_v, keep, send, rank_q, rank_v, aq, ak, av, rq, rv):
+def proj_kernel(act, wq, wk, wv, down_q, down_v, up_q, up_v, grad, keep, send, rank, aq, ak, av, rq, rv):
     step = pl.program_id(0)
     last = pl.num_programs(0) - 1
     a = act[...]
@@ -61,8 +61,8 @@
     def _():
         low_q = rq[...].astype(bf16)
         low_v = rv[...].astype(bf16)
-        rank_q[...] = low_q
-        rank_v[...] = low_v
+        rank[:, :RANK] = low_q
+        rank[:, RANK:] = low_v
         keys = ak[...].astype(bf16)
         values = (av[...] + dot(low_v, up_v[...])).astype(bf16)
         query = (aq[...] + dot(low_q, up_q[...])).astype(bf16)
@@ -70,22 +70,23 @@
         def put(ref, at):
             ref[:, :HEAD] = keys[:, at:at + HEAD]
             ref[:, HEAD:2 * HEAD] = values[:, at:at + HEAD]
-            ref[:, 2 * HEAD:] = query[:, at:at + HEAD]
-
-        by_core(pos, put, keep, send)
-
-
-def project(pos, act, wq, wk, wv, down_q, down_v, up_q, up_v):
+            ref[:, 2 * HEAD:3 * HEAD] = query[:, at:at + HEAD]
+            ref[:, 3 * HEAD:] = grad[:, at:at + HEAD]
+
+        by_core(put, keep, send)
+
+
+def project(act, wq, wk, wv, down_q, down_v, up_q, up_v, grad):
     rows, width = act.shape
     cols = wq.shape[1]
     whole = lambda shape: pl.BlockSpec(shape, lambda k: (0, 0))
-    shapes = [(rows, 3 * HEAD), (rows, 3 * HEAD), (rows, RANK), (rows, RANK)]
+    shapes = [(rows, 4 * HEAD), (rows, 4 * HEAD), (rows, 2 * RANK)]
     return pl.pallas_call(
         proj_kernel,
         grid=(width // KT,),
-        in_specs=[SMEM, pl.BlockSpec((rows, KT), lambda k: (0, k))]
+        in_specs=[pl.BlockSpec((rows, KT), lambda k: (0, k))]
         + [pl.BlockSpec((KT, cols), lambda k: (k, 0))] * 3
-        + [pl.BlockSpec((KT, RANK), lambda k: (k, 0))] * 2 + [whole(up_q.shape), whole(up_v.shape)],
+        + [pl.BlockSpec((KT, RANK), lambda k: (k, 0))] * 2 + [whole(up_q.shape), whole(up_v.shape), whole(grad.shape)],
         out_specs=[whole(s) for s in shapes],
         out_shape=[jax.ShapeDtypeStruct(s, bf16) for s in shapes],
         scratch_shapes=[pltpu.VMEM((rows, cols), f32)] * 3 + [pltpu.VMEM((rows, RANK), f32)] * 2,
@@ -93,11 +94,28 @@
         cost_estimate=pl.CostEstimate(flops=2 * rows * width * (3 * cols + 2 * RANK),
                                       bytes_accessed=2 * width * (rows + 3 * cols + 2 * RANK), transcendentals=0),
         name="project",
-    )(pos, act, wq, wk, wv, down_q, down_v, up_q, up_v)
-
-
-def lists_kernel(pos, slot, packed, out):
-    x, y, c = pos[0], pos[1], pos[2]
+    )(act, wq, wk, wv, down_q, down_v, up_q, up_v, grad)
+
+
+def assemble_kernel(keep, other, kv, qg):
+    kv[:256, :] = keep[:, :256]
+    kv[256:, :] = other[:, :256]
+    qg[:256, :] = keep[:, 256:]
+    qg[256:, :] = other[:, 256:]
+
+
+def assemble(keep, other):
+    return pl.pallas_call(
+        assemble_kernel,
+        in_specs=[VMEM] * 2,
+        out_specs=[VMEM] * 2,
+        out_shape=[jax.ShapeDtypeStruct((512, 256), bf16)] * 2,
+        name="assemble",
+    )(keep, other)
+
+
+def lists_kernel(slot, packed, out):
+    x, y, c = (lax.axis_index(n) for n in ("x", "y", "c"))
 
     def frame(xx, yy, local):
         core = c if local < 2 else 1 - c
@@ -123,15 +141,15 @@
     lax.fori_loop(0, 16, one, 0)
 
 
-def visible_lists(pos, slot, levels, order):
+def visible_lists(slot, levels, order):
     packed = levels * 256 + jnp.sum(order * jnp.array([1, 4, 16, 64], jnp.int32), axis=-1)
     return pl.pallas_call(
         lists_kernel,
-        in_specs=[SMEM] * 3,
+        in_specs=[SMEM] * 2,
         out_specs=SMEM,
         out_shape=jax.ShapeDtypeStruct((24, 128), jnp.int32),
         name="lists",
-    )(pos, slot, packed)
+    )(slot, packed)
 
 
 def fill_all(parts, whole):
@@ -140,30 +158,18 @@
         whole[d * rows:(d + 1) * rows, :] = part[...]
 
 
-def fill_grads(pos, gathered, whole):
-    for c in range(2):
-        @pl.when(pos[2] == c)
-        def _():
-            for d in range(4):
-                chip = lax.rem(pos[1] + 4 - d, 4)
-                for i, core in enumerate((c, 1 - c)):
-                    at = pl.multiple_of((chip * 2 + core) * 256, 256)
-                    to = d * 512 + i * 256
-                    whole[to:to + 256, :] = gathered[pl.ds(at, 256), c * HEAD:(c + 1) * HEAD]
-
-
 def load_chunk(lists, f, at, kvall):
     blocks = [kvall[pl.ds(pl.multiple_of(lists[f, at + i] * BLK, BLK), BLK), :] for i in range(CB)]
     return jnp.concatenate(blocks, axis=0)
 
 
-def start_frames(lists, t, qall, gall, both):
+def start_frames(lists, t, qgall, both):
     counts = []
     for j in range(CHAINS):
         f = t * CHAINS + j
         at = pl.multiple_of(f * FT, FT)
-        both[j, :FT, :HEAD] = qall[pl.ds(at, FT), :]
-        both[j, FT:, HEAD:] = gall[pl.ds(at, FT), :]
+        both[j, :FT, :HEAD] = qgall[pl.ds(at, FT), :HEAD]
+        both[j, FT:, HEAD:] = qgall[pl.ds(at, FT), HEAD:]
         counts.append(lists[16, f])
     chunks = [(n + CB - 1) // CB for n in counts]
     most = chunks[0]
@@ -172,15 +178,14 @@
     return counts, chunks, most
 
 
-def stats_kernel(pos, lists, q0, q1, q2, q3, g, k0, k1, k2, k3, out, qall, gall, kvall, both):
-    fill_all((q0, q1, q2, q3), qall)
-    fill_grads(pos, g, gall)
+def stats_kernel(lists, q0, q1, q2, q3, k0, k1, k2, k3, out, qgall, kvall, both):
+    fill_all((q0, q1, q2, q3), qgall)
     fill_all((k0, k1, k2, k3), kvall)
     both[...] = jnp.zeros_like(both)
     row = lax.broadcasted_iota(jnp.int32, (CHUNK, HEAD), 0)
 
     def frames(t, _):
-        counts, chunks, most = start_frames(lists, t, qall, gall, both)
+        counts, chunks, most = start_frames(lists, t, qgall, both)
 
         def chunk(ch, carry):
             kvs = [load_chunk(lists, t * CHAINS + j, jnp.minimum(ch, chunks[j] - 1) * CB, kvall)
@@ -208,23 +213,22 @@
     lax.fori_loop(0, 16 // CHAINS, frames, 0)
 
 
-def row_stats(pos, lists, qs, g, kvs):
+def row_stats(lists, qgs, kvs):
     return pl.pallas_call(
         stats_kernel,
-        in_specs=[SMEM, SMEM] + [VMEM] * 9,
+        in_specs=[SMEM] + [VMEM] * 8,
         out_specs=VMEM,
         out_shape=jax.ShapeDtypeStruct((48, 128), f32),
-        scratch_shapes=[pltpu.VMEM((2048, HEAD), bf16), pltpu.VMEM((2048, HEAD), bf16),
-                        pltpu.VMEM((2048, 2 * HEAD), bf16), pltpu.VMEM((CHAINS, 2 * FT, 2 * HEAD), bf16)],
+        scratch_shapes=[pltpu.VMEM((2048, 2 * HEAD), bf16), pltpu.VMEM((2048, 2 * HEAD), bf16),
+                        pltpu.VMEM((CHAINS, 2 * FT, 2 * HEAD), bf16)],
         compiler_params=PARAMS,
         name="row_stats",
-    )(pos, lists, *qs, g, *kvs)
-
-
-def grads_kernel(pos, lists, s0, s1, s2, s3, q0, q1, q2, q3, g, k0, k1, k2, k3,
-                 o, a0, a1, a2, a3, b0, b1, b2, b3, qall, gall, kvall, both, acc, dva, norm):
-    fill_all((q0, q1, q2, q3), qall)
-    fill_grads(pos, g, gall)
+    )(lists, *qgs, *kvs)
+
+
+def grads_kernel(lists, s0, s1, s2, s3, q0, q1, q2, q3, k0, k1, k2, k3,
+                 o0, o1, o2, o3, a0, a1, a2, a3, b0, b1, b2, b3, qgall, kvall, both, acc, dva, norm):
+    fill_all((q0, q1, q2, q3), qgall)
     fill_all((k0, k1, k2, k3), kvall)
     both[...] = jnp.zeros_like(both)
     dva[...] = jnp.zeros_like(dva)
@@ -244,7 +248,7 @@
     row = lax.broadcasted_iota(jnp.int32, (CHUNK, HEAD), 0)
 
     def frames(t, _):
-        counts, chunks, most = start_frames(lists, t, qall, gall, both)
+        counts, chunks, most = start_frames(lists, t, qgall, both)
         lse = [norm[pl.ds(t * CHAINS + j, 1), :] for j in range(CHAINS)]
         delta = [norm[pl.ds(16 + t * CHAINS + j, 1), :] for j in range(CHAINS)]
         acc[...] = jnp.zeros_like(acc)
@@ -276,11 +280,10 @@
         for j in range(CHAINS):
             f = t * CHAINS + j
             at = pl.multiple_of(lax.rem(f, 4) * FT, FT)
-            chip = lax.rem(pos[1] + 4 - f // 4, 4)
-            o[pl.ds(pl.multiple_of(chip * 512 + at, FT), FT), :] = acc[j, 0].T
-            for d, a in enumerate((a0, a1, a2, a3)):
+            for d, (o, a) in enumerate(zip((o0, o1, o2, o3), (a0, a1, a2, a3))):
                 @pl.when(f // 4 == d)
                 def _():
+                    o[pl.ds(at, FT), :] = acc[j, 0].T.astype(o.dtype)
                     a[pl.ds(at, FT), :] = acc[j, 1].T.astype(a.dtype)
 
         return 0
@@ -293,29 +296,28 @@
         b[...] = total.astype(b.dtype)
 
 
-def attention_grads(pos, lists, stats, qs, g, kvs):
-    wire = [f32, WIRE, WIRE, WIRE]
+def attention_grads(lists, stats, qgs, kvs):
+    wire = [f32, bf16, bf16, bf16] + [WIRE] * 8
     return pl.pallas_call(
         grads_kernel,
-        in_specs=[SMEM, SMEM] + [VMEM] * 13,
-        out_specs=[VMEM] * 9,
-        out_shape=[jax.ShapeDtypeStruct((2048, HEAD), f32)]
-        + [jax.ShapeDtypeStruct((512, HEAD), t) for t in wire + wire],
-        scratch_shapes=[pltpu.VMEM((2048, HEAD), bf16), pltpu.VMEM((2048, HEAD), bf16),
-                        pltpu.VMEM((2048, 2 * HEAD), bf16), pltpu.VMEM((CHAINS, 2 * FT, 2 * HEAD), bf16),
+        in_specs=[SMEM] + [VMEM] * 12,
+        out_specs=[VMEM] * 12,
+        out_shape=[jax.ShapeDtypeStruct((512, HEAD), t) for t in wire],
+        scratch_shapes=[pltpu.VMEM((2048, 2 * HEAD), bf16), pltpu.VMEM((2048, 2 * HEAD), bf16),
+                        pltpu.VMEM((CHAINS, 2 * FT, 2 * HEAD), bf16),
                         pltpu.VMEM((CHAINS, 2, HEAD, FT), f32), pltpu.VMEM((CHAINS, 2048, HEAD), f32),
                         pltpu.VMEM((32, 128), f32)],
         compiler_params=PARAMS,
         name="attention_grads",
-    )(pos, lists, *stats, *qs, g, *kvs)
-
-
-def finish_kernel(pos, a0, a1, a2, a3, b0, b1, b2, b3, rq_own, rq_other, rv_own, rv_other, uq, uv,
+    )(lists, *stats, *qgs, *kvs)
+
+
+def finish_kernel(a0, a1, a2, a3, b0, b1, b2, b3, own, other, uq, uv, after,
                   rg_keep, rg_send, up):
     dq = (a0[...] + a1[...].astype(f32) + a2[...].astype(f32) + a3[...].astype(f32)).astype(bf16)
     dv = (b0[...] + b1[...].astype(f32) + b2[...].astype(f32) + b3[...].astype(f32)).astype(bf16)
     for c in range(2):
-        @pl.when(pos[2] == c)
+        @pl.when(lax.axis_index("c") == c)
         def _():
             gq = dot(dq, uq[:, c * HEAD:(c + 1) * HEAD], 1, 1)
             gv = dot(dv, uv[:, c * HEAD:(c + 1) * HEAD], 1, 1)
@@ -323,41 +325,41 @@
             rg_keep[:, RANK:] = gv[:256]
             rg_send[:, :RANK] = gq[256:]
             rg_send[:, RANK:] = gv[256:]
-    up[:, :HEAD] = dot(rq_own[...], dq[:256], 0, 0) + dot(rq_other[...], dq[256:], 0, 0)
-    up[:, HEAD:] = dot(rv_own[...], dv[:256], 0, 0) + dot(rv_other[...], dv[256:], 0, 0)
-
-
-def finish(pos, a, b, ranks, uq, uv):
+    up[:, :HEAD] = dot(own[:, :RANK], dq[:256], 0, 0) + dot(other[:, :RANK], dq[256:], 0, 0)
+    up[:, HEAD:] = dot(own[:, RANK:], dv[:256], 0, 0) + dot(other[:, RANK:], dv[256:], 0, 0)
+
+
+def finish(a, b, own, other, uq, uv, after):
     return pl.pallas_call(
         finish_kernel,
-        in_specs=[SMEM] + [VMEM] * 14,
+        in_specs=[VMEM] * 12 + [ANY],
         out_specs=[VMEM] * 3,
         out_shape=[jax.ShapeDtypeStruct((r, 256), f32) for r in (256, 256, 128)],
         compiler_params=PARAMS,
         name="finish",
-    )(pos, *a, *b, *ranks, uq, uv)
-
-
-def down_kernel(pos, act_t, own, r1, r2, r3, after, mine, theirs):
+    )(*a, *b, own, other, uq, uv, after)
+
+
+def down_kernel(act_t, own, r1, r2, r3, after, mine, theirs):
     rg = (own[...] + r1[...].astype(f32) + r2[...].astype(f32) + r3[...].astype(f32)).astype(bf16)
     rows = mine.shape[0]
     for c in range(2):
-        @pl.when(pos[2] == c)
+        @pl.when(lax.axis_index("c") == c)
         def _():
             mine[...] = dot(act_t[c * rows:(c + 1) * rows, :], rg)
             theirs[...] = dot(act_t[(1 - c) * rows:(2 - c) * rows, :], rg)
 
 
-def down_terms(pos, act_t, own, others, after):
+def down_terms(act_t, own, others, after):
     rows = act_t.shape[0] // 2
     return pl.pallas_call(
         down_kernel,
-        in_specs=[SMEM] + [VMEM] * 5 + [ANY],
+        in_specs=[VMEM] * 5 + [ANY],
         out_specs=[VMEM] * 2,
         out_shape=[jax.ShapeDtypeStruct((rows, 256), f32)] * 2,
         compiler_params=PARAMS,
         name="down_terms",
-    )(pos, act_t, own, *others, after)
+    )(act_t, own, *others, after)
 
 
 def pack_kernel(mine, theirs, up, out):
@@ -377,11 +379,11 @@
     )(mine, theirs, up)
 
 
-def emit_kernel(pos, own, other, o_keep, o_other, att, down_q, up_q, down_v, up_v):
+def emit_kernel(own, other, o_keep, o_other, att, down_q, up_q, down_v, up_v):
     zz = pl.program_id(0)
     halves = [own, other]
     for c in range(2):
-        @pl.when(pos[2] == c)
+        @pl.when(lax.axis_index("c") == c)
         def _():
             for cc in range(2):
                 src = halves[(c + cc) % 2]
@@ -398,17 +400,17 @@
                     src = halves[(c + cc) % 2]
                     att[:, cc * HEAD:(cc + 1) * HEAD] = outs[(c + cc) % 2][...]
                     for i in range(16):
-                        part = src[pos[3] * 16 + i].astype(f32)
+                        part = src[lax.axis_index("z") * 16 + i].astype(f32)
                         up_q[i * 8:(i + 1) * 8, cc * HEAD:(cc + 1) * HEAD] = part[40:, :HEAD]
                         up_v[i * 8:(i + 1) * 8, cc * HEAD:(cc + 1) * HEAD] = part[40:, HEAD:]
 
 
-def emit(pos, own, other, o_keep, o_other):
+def emit(own, other, o_keep, o_other):
     whole = lambda a: pl.BlockSpec(a, lambda k: (0,) * len(a))
     return pl.pallas_call(
         emit_kernel,
         grid=(4,),
-        in_specs=[SMEM] + [whole(a.shape) for a in (own, other, o_keep, o_other)],
+        in_specs=[whole(a.shape) for a in (own, other, o_keep, o_other)],
         out_specs=[whole((256, 256)), pl.BlockSpec((1280, RANK), lambda k: (k, 0)), whole((RANK, 256)),
                    pl.BlockSpec((1280, RANK), lambda k: (k, 0)), whole((RANK, 256))],
         out_shape=[jax.ShapeDtypeStruct((256, 256), bf16), jax.ShapeDtypeStruct((5120, RANK), f32),
@@ -416,7 +418,7 @@
                    jax.ShapeDtypeStruct((RANK, 256), f32)],
         compiler_params=PARAMS,
         name="emit",
-    )(pos, own, other, o_keep, o_other)
+    )(own, other, o_keep, o_other)
 
 
 def total_kernel(parts, after, out):
@@ -461,27 +463,26 @@
 
 
 def local(act, wq, wk, wv, dq, uq, dv, uv, grad_out, levels, order, slot):
-    x, y, c, z = (lax.axis_index(n).astype(jnp.int32) for n in ("x", "y", "c", "z"))
-    pos = jnp.stack([x, y, c, z])
-    g = lax.all_gather(grad_out, ("y", "c"), axis=0, tiled=True)
-    keep, send, rq, rv = project(pos, act, wq, wk, wv, dq, dv, uq, uv)
-    lists = visible_lists(pos, slot, levels, order)
-    whole = jnp.concatenate([keep, swap(send)], axis=0)
-    kvs = spread(whole[:, :2 * HEAD], "x")
-    qs = spread(whole[:, 2 * HEAD:], "y")
+    z = lax.axis_index("z")
+    keep, send, rank = project(act, wq, wk, wv, dq, dv, uq, uv, grad_out)
+    kv, qg = assemble(keep, swap(send))
+    kvs = spread(kv, "x")
+    qgs = spread(qg, "y")
+    lists = visible_lists(slot, levels, order)
     act_t = half(act, z, act.shape[1] // 4).T
-    stats = spread(row_stats(pos, lists, qs, g, kvs), "y")
-    o, *parts = attention_grads(pos, lists, stats, qs, g, kvs)
-    a = collect(parts[:4], "y")
-    b = collect(parts[4:], "x")
-    o = lax.psum_scatter(o, "y", scatter_dimension=0, tiled=True).astype(bf16)
+    stats = spread(row_stats(lists, qgs, kvs), "y")
+    parts = attention_grads(lists, stats, qgs, kvs)
+    a = collect(parts[4:8], "y")
+    b = collect(parts[8:], "x")
+    o0, o1, o2, o3 = collect(parts[:4], "y")
+    o = (o0 + o1.astype(f32) + o2.astype(f32) + o3.astype(f32)).astype(bf16)
     o_keep, o_other = o[:256], swap(o[256:])
-    rg_keep, rg_send, up = finish(pos, a, b, (rq, swap(rq), rv, swap(rv)), uq, uv)
+    rg_keep, rg_send, up = finish(a, b, rank, swap(rank), uq, uv, act_t)
     rg = rg_keep + swap(rg_send)
-    mine, theirs = down_terms(pos, act_t, rg, spread(rg.astype(bf16), "z")[1:], o)
+    mine, theirs = down_terms(act_t, rg, spread(rg.astype(bf16), "z")[1:], o)
     terms = lax.all_to_all(pack(mine, swap(theirs), up), ("x", "y"), 0, 0, tiled=True)
     wide = lax.all_to_all(total_for_all(terms, o_other), ("z", "x", "y"), 0, 0, tiled=True)
-    att, down_q, up_q, down_v, up_v = emit(pos, wide, swap(wide), o_keep, o_other)
+    att, down_q, up_q, down_v, up_v = emit(wide, swap(wide), o_keep, o_other)
     return att, down_q, up_q, down_v, up_v
 
 

time: 173 us -> 163 us (0.942)
  between operations: 14.2 us -> 0.85 us
  starting transfers between devices: 30.8 us -> 41 us
  waiting for transfers between devices: 50.7 us -> 44 us
  local copies, waits for them, and re-layouts: 5.76 us -> 7.95 us
    ppermute x6 -> x9, waiting for transfers between devices: 19 us -> 13.8 us  [collect(): lax.ppermute(parts[d], axis, ring(4, -d))]
    ppermute x6 -> x9, starting transfers between devices: 3.44 us -> 8.63 us  [collect(): lax.ppermute(parts[d], axis, ring(4, -d))]
    ppermute x12, starting transfers between devices: 13.7 us -> 17.7 us  [spread(): one, three, two = [lax.ppermute(a, axis, ring(4, d)) for d in (1, 3, 2)]]
    unnamed x26 -> x29, local copies, waits for them, and re-layouts: 4.56 us -> 5.98 us
    ppermute x7 -> x6, starting transfers between devices: 9.66 us -> 10.7 us  [swap(): return lax.ppermute(a, 'c', ring(2, 1))]
    pallas_call x7 -> x8, Pallas kernels: 41.6 us -> 40.6 us  [the longest x1 13.5 us: attention_grads(): pl.pallas_call(grads_kernel, in_specs=[SMEM] + [VMEM] * 12, out_specs=[VM...]
    ppermute x7 -> x6, waiting for transfers between devices: 7.36 us -> 7.04 us  [swap(): return lax.ppermute(a, 'c', ring(2, 1))]
  transfers between devices with their start and end apart: 28 -> 28, of which waited for: 18 -> 15; matrix products, arithmetic and copies ran while one was open for 3% -> 3% of each run, Pallas kernels for 9% -> 4%
where the time goes in v4:
time: 163 us
  waiting for transfers between devices  44 us (27%)
  Pallas kernels  41.5 us (25%)
  starting transfers between devices  41 us (25%)
  blocking collectives  26.7 us (16%)
  local copies, waits for them, and re-layouts  7.95 us (5%)
    all_to_all x1, blocking collectives, local(): lax.all_to_all(total_for_all(terms, o_other), ('z', 'x', 'y'), 0, 0, tile...  26.7 us
    ppermute x12, starting transfers between devices, spread(): one, three, two = [lax.ppermute(a, axis, ring(4, d)) for d in (1, 3, 2)]  17.7 us
    ppermute x12, waiting for transfers between devices, spread(): one, three, two = [lax.ppermute(a, axis, ring(4, d)) for d in (1, 3, 2)]  15.6 us
    ppermute x9, waiting for transfers between devices, collect(): lax.ppermute(parts[d], axis, ring(4, -d))  13.8 us
    pallas_call x1, Pallas kernels, attention_grads(): pl.pallas_call(grads_kernel, in_specs=[SMEM] + [VMEM] * 12, out_specs=[VM...  13.5 us
    ppermute x6, starting transfers between devices, swap(): return lax.ppermute(a, 'c', ring(2, 1))  10.7 us
    pallas_call x1, Pallas kernels, project(): pl.pallas_call(proj_kernel, grid=(width // KT,), in_specs=[pl.BlockSpec((...  8.86 us
    ppermute x9, starting transfers between devices, collect(): lax.ppermute(parts[d], axis, ring(4, -d))  8.63 us
  transfers between devices with their start and end apart: 28, of which 15 were waited for; matrix products, arithmetic and copies ran while one was open for 3% of the time, Pallas kernels for 4%

profile of v4, /device:TPU:1, one launch (start us, length us, event | category | flops | bytes accessed | tf_op | source)
XLA Modules:
  0.0 162.9 jit_solution(4397524719765848381)
XLA Ops:
  0.7 8.9 %project.1 = (bf16[256,512]{1,0:T(8,128)(2,1)}, bf16[256,512]{1,0:T(8,128)(2,1)}, bf16[256,256]{1,0:T(8,128)(2,1)}) custom-call(bf16[256,5120]{1,0:T(8,128)(2,1)} %act.1, bf16[5120,256]{1,0:T(8,128)(2,1)} %wq.1, bf16[5120,256]{1,0:T(8,128)(2,1)} %wk.1, bf16[5120,256]{1,0:T(8,128)(2,1)} %wv.1, bf16[5120,128]{1,0:T(8,128)(2,1)} %down_q.1, ...), custom_call_target="tpu_custom_call" | custom-call | flops 2684354560 | bytes 13107200 | tf_op jit(solution)/shard_map/project/pallas_call | solution.py:84
  9.5 1.5 collective-permute-start
  11.0 1.4 collective-permute-done.other
  13.1 1.8 %assemble.1 = (bf16[512,256]{1,0:T(8,128)(2,1)}, bf16[512,256]{1,0:T(8,128)(2,1)}) custom-call(bf16[256,512]{1,0:T(8,128)(2,1)} %get-tuple-element.27.keep, bf16[256,512]{1,0:T(8,128)(2,1)} %copy-done.10), custom_call_target="tpu_custom_call" | custom-call | tf_op jit(solution)/shard_map/assemble/pallas_call | solution.py:108
  14.9 2.8 %collective-permute-start.3 = (bf16[512,256]{1,0:T(8,128)(2,1)}, bf16[512,256]{1,0:T(8,128)(2,1)S(1)}, u32[]{:S(2)}, u32[]{:S(2)}) collective-permute-start(bf16[512,256]{1,0:T(8,128)(2,1)} %get-tuple-element.29.q0), channel_id=1, source_target_pairs={{0,24},{8,0},{16,8},{24,16},{1,25},{9,1},{17,9},{25,17},{2,26},{10... | collective-permute-start | bytes 786440 | tf_op jit(solution)/shard_map/ppermute | solution.py:453
  18.8 2.5 %collective-permute-start.6 = (bf16[512,256]{1,0:T(8,128)(2,1)}, bf16[512,256]{1,0:T(8,128)(2,1)S(1)}, u32[]{:S(2)}, u32[]{:S(2)}) collective-permute-start(bf16[512,256]{1,0:T(8,128)(2,1)} %get-tuple-element.30.k0), channel_id=1, source_target_pairs={{0,96},{32,0},{64,32},{96,64},{1,97},{33,1},{65,33},{97,65},{2,98}... | collective-permute-start | bytes 786440 | tf_op jit(solution)/shard_map/ppermute | solution.py:453
  21.8 7.1 %collective-permute-done.3.q3 = bf16[512,256]{1,0:T(8,128)(2,1)S(1)} collective-permute-done((bf16[512,256]{1,0:T(8,128)(2,1)}, bf16[512,256]{1,0:T(8,128)(2,1)S(1)}, u32[]{:S(2)}, u32[]{:S(2)}) %collective-permute-start.3) | collective-permute-done | bytes 262176 | tf_op jit(solution)/shard_map/ppermute | solution.py:453
  28.9 1.2 collective-permute-start.4
  30.9 6.0 %lists.1 = s32[24,128]{1,0:T(8,128)} custom-call(s32[64]{0:T(128)} %slot.1, s32[64,64]{1,0:T(8,128)} %multiply_add_fusion.packed), custom_call_target="tpu_custom_call" | custom-call | tf_op jit(solution)/shard_map/lists/pallas_call | solution.py:146
  39.5 6.6 %row_stats.1.s0 = f32[48,128]{1,0:T(8,128)S(1)} custom-call(s32[24,128]{1,0:T(8,128)S(1)} %copy-done.5, bf16[512,256]{1,0:T(8,128)(2,1)S(1)} %copy-done.1, bf16[512,256]{1,0:T(8,128)(2,1)S(1)} %collective-permute-done.1.q1, bf16[512,256]{1,0:T(8,128)(2,1)S(1)} %collective-permute-done.2.q2, bf16[512,256]{1,0:T(8,128)(2,1)S(1)} %collective-permute-done.3.q3, ...), custom_call_target="tpu_custom_call" | custom-call | tf_op jit(solution)/shard_map/row_stats/pallas_call | solution.py:217
  46.2 3.5 %collective-permute-start.9 = (f32[48,128]{1,0:T(8,128)S(1)}, f32[48,128]{1,0:T(8,128)S(1)}, u32[]{:S(2)}, u32[]{:S(2)}) collective-permute-start(f32[48,128]{1,0:T(8,128)S(1)} %row_stats.1.s0), channel_id=1, source_target_pairs={{0,24},{8,0},{16,8},{24,16},{1,25},{9,1},{17,9},{25,17},{2,26},{10... | collective-permute-start | bytes 73736 | tf_op jit(solution)/shard_map/ppermute | solution.py:453
  50.6 3.2 %collective-permute-done.8.s2 = f32[48,128]{1,0:T(8,128)S(1)} collective-permute-done((f32[48,128]{1,0:T(8,128)S(1)}, f32[48,128]{1,0:T(8,128)S(1)}, u32[]{:S(2)}, u32[]{:S(2)}) %collective-permute-start.8) | collective-permute-done | bytes 24608 | tf_op jit(solution)/shard_map/ppermute | solution.py:453
  53.9 13.5 %attention_grads.1 = (f32[512,128]{1,0:T(8,128)S(1)}, bf16[512,128]{1,0:T(8,128)(2,1)S(1)}, bf16[512,128]{1,0:T(8,128)(2,1)S(1)}, bf16[512,128]{1,0:T(8,128)(2,1...) custom-call(s32[24,128]{1,0:T(8,128)S(1)} %copy-done.5, ...), custom_call_target="tpu_custom_call" | custom-call | tf_op jit(solution)/shard_map/attention_grads/pallas_call | solution.py:301
  69.2 3.8 %collective-permute-start.16 = (bf16[256,256]{1,0:T(8,128)(2,1)S(1)}, bf16[256,256]{1,0:T(8,128)(2,1)S(1)}, u32[]{:S(2)}, u32[]{:S(2)}) collective-permute-start(bf16[256,256]{1,0:T(8,128)(2,1)S(1)} %copy-done.4), channel_id=1, source_target_pairs={{0,4},{4,0},{1,5},{5,1},{2,6},{6,2},{3,7},{7,3},{8,12},{12,8},{9,1... | collective-permute-start | bytes 393224 | tf_op jit(solution)/shard_map/ppermute | solution.py:449
  75.1 1.3 collective-permute-start.13
  77.8 2.0 %constant_dynamic-slice_fusion = bf16[256,1280]{1,0:T(8,128)(2,1)} fusion(bf16[256,5120]{1,0:T(8,128)(2,1)} %act.1, s32[]{:T(128)S(6)} %select_n.3), kind=kLoop, calls=%fused_computation.3 | loop fusion | bytes 1310724 | tf_op jit(solution)/shard_map/dynamic_slice | solution.py:462
  79.8 1.3 copy.19
  81.1 1.6 collective-permute-done.11.a2
  82.7 5.9 %collective-permute-done.12.a3 = f32[512,128]{1,0:T(8,128)S(1)} collective-permute-done((f32[512,128]{1,0:T(8,128)}, f32[512,128]{1,0:T(8,128)S(1)}, u32[]{:S(2)}, u32[]{:S(2)}) %collective-permute-start.12) | collective-permute-done | bytes 262176 | tf_op jit(solution)/shard_map/ppermute | solution.py:458
  88.6 3.3 %collective-permute-done.15.b3 = f32[512,128]{1,0:T(8,128)S(1)} collective-permute-done((f32[512,128]{1,0:T(8,128)}, f32[512,128]{1,0:T(8,128)S(1)}, u32[]{:S(2)}, u32[]{:S(2)}) %collective-permute-start.15) | collective-permute-done | bytes 262176 | tf_op jit(solution)/shard_map/ppermute | solution.py:458
  93.1 2.4 %collective-permute-start.21 = (bf16[512,128]{1,0:T(8,128)(2,1)S(1)}, bf16[512,128]{1,0:T(8,128)(2,1)S(1)}, u32[]{:S(2)}, u32[]{:S(2)}) collective-permute-start(bf16[512,128]{1,0:T(8,128)(2,1)S(1)} %copy-done.9), channel_id=1, source_target_pairs={{0,24},{8,0},{16,8},{24,16},{1,25},{9,1},{17,9},{25,17},{2,26},{10... | collective-permute-start | bytes 393224 | tf_op jit(solution)/shard_map/ppermute | solution.py:458
  96.5 3.8 %collective-permute-start.20 = (bf16[256,256]{1,0:T(8,128)(2,1)S(1)}, bf16[256,256]{1,0:T(8,128)(2,1)S(1)}, u32[]{:S(2)}, u32[]{:S(2)}) collective-permute-start(bf16[256,256]{1,0:T(8,128)(2,1)S(1)} %get-tuple-element.49), channel_id=1, source_target_pairs={{0,3},{1,0},{2,1},{3,2},{4,7},{5,4},{6,5},{7,6},{8,11},{9,8},{10,9... | collective-permute-start | bytes 393224 | tf_op jit(solution)/shard_map/ppermute | solution.py:453
  101.0 1.6 collective-permute-start.18
  102.6 2.3 %collective-permute-done.23 = bf16[512,128]{1,0:T(8,128)(2,1)S(1)} collective-permute-done((bf16[512,128]{1,0:T(8,128)(2,1)S(1)}, bf16[512,128]{1,0:T(8,128)(2,1)S(1)}, u32[]{:S(2)}, u32[]{:S(2)}) %collective-permute-start.23) | collective-permute-done | bytes 131104 | tf_op jit(solution)/shard_map/ppermute | solution.py:458
  105.8 4.1 %collective-permute-done.18.r1 = bf16[256,256]{1,0:T(8,128)(2,1)S(1)} collective-permute-done((bf16[256,256]{1,0:T(8,128)(2,1)S(1)}, bf16[256,256]{1,0:T(8,128)(2,1)S(1)}, u32[]{:S(2)}, u32[]{:S(2)}) %collective-permute-start.18) | collective-permute-done | bytes 131104 | tf_op jit(solution)/shard_map/ppermute | solution.py:453
  111.1 1.7 %collective-permute-done.24.theirs = f32[640,256]{1,0:T(8,128)S(1)} collective-permute-done((f32[640,256]{1,0:T(8,128)S(1)}, f32[640,256]{1,0:T(8,128)S(1)}, u32[]{:S(2)}, u32[]{:S(2)}) %collective-permute-start.24) | collective-permute-done | bytes 655392 | tf_op jit(solution)/shard_map/ppermute | solution.py:449
  113.6 3.9 %all-to-all-start = ((bf16[16,48,256]{2,1,0:T(8,128)(2,1)}), bf16[16,48,256]{2,1,0:T(8,128)(2,1)S(1)}, u32[]{:S(2)}, u32[]{:S(2)}) async-start(bf16[16,48,256]{2,1,0:T(8,128)(2,1)} %pack.1), calls=%async_computation | async-start | bytes 786432 | tf_op jit(solution)/shard_map/all_to_all | solution.py:483
  119.2 7.6 %all-to-all-done.parts = bf16[16,48,256]{2,1,0:T(8,128)(2,1)S(1)} async-done(((bf16[16,48,256]{2,1,0:T(8,128)(2,1)}), bf16[16,48,256]{2,1,0:T(8,128)(2,1)S(1)}, u32[]{:S(2)}, u32[]{:S(2)}) %all-to-all-start) | async-done | bytes 393248 | tf_op jit(solution)/shard_map/all_to_all | solution.py:483
  126.9 26.7 %all_to_all.10.own = bf16[64,48,256]{2,1,0:T(8,128)(2,1)S(1)} all-to-all(bf16[64,48,256]{2,1,0:T(8,128)(2,1)S(1)} %total_for_all.1), channel_id=1, replica_groups=mesh['x'=4,'y'=4,'c'=2,'z'=4] {'z','x','y'}, dimensions={0} | all-to-all | bytes 3145728 | tf_op jit(solution)/shard_map/all_to_all | solution.py:484
  153.6 3.4 %collective-permute-start.26 = (bf16[64,48,256]{2,1,0:T(8,128)(2,1)S(1)}, bf16[64,48,256]{2,1,0:T(8,128)(2,1)S(1)}, u32[]{:S(2)}, u32[]{:S(2)}) collective-permute-start(bf16[64,48,256]{2,1,0:T(8,128)(2,1)S(1)} %all_to_all.10.own), channel_id=1, source_target_pairs={{0,4},{4,0},{1,5},{5,1},{2,6},{6,2},{3,7},{7,3},{8,12},{12,8},{9,1... | collective-permute-start | bytes 4718600 | tf_op jit(solution)/shard_map/ppermute | solution.py:449
  157.0 3.0 %collective-permute-done.26.other = bf16[64,48,256]{2,1,0:T(8,128)(2,1)S(1)} collective-permute-done((bf16[64,48,256]{2,1,0:T(8,128)(2,1)S(1)}, bf16[64,48,256]{2,1,0:T(8,128)(2,1)S(1)}, u32[]{:S(2)}, u32[]{:S(2)}) %collective-permute-start.26) | collective-permute-done | bytes 1572896 | tf_op jit(solution)/shard_map/ppermute | solution.py:449
  160.1 2.8 %emit.1 = (bf16[256,256]{1,0:T(8,128)(2,1)}, f32[5120,128]{1,0:T(8,128)}, f32[128,256]{1,0:T(8,128)}, f32[5120,128]{1,0:T(8,128)}, f32[128,256]{1,0:T(8,128)}) custom-call(bf16[64,48,256]{2,1,0:T(8,128)(2,1)S(1)} %all_to_all.10.own, bf16[64,48,256]{2,1,0:T(8,128)(2,1)S(1)} %collective-permute-done.26.other, bf16[256,128]{1,0:T(8,128)(2,1)S(1)} %get-tuple-element.51.o_keep, ...), custom_call_target="tpu_custom_call" | custom-call | tf_op jit(solution)/shard_map/emit/pallas_call | solution.py:410
  (70 shorter events, 19.5 us)
Async XLA Ops:
  0.7 29.6 %copy-start.12 = (s32[64,64]{1,0:T(8,128)S(1)}, s32[64,64]{1,0:T(8,128)}, u32[]{:S(2)}) copy-start(s32[64,64]{1,0:T(8,128)} %param.22) | copy-start | bytes 49156
  9.5 59.7 %copy-start.4 = (bf16[256,256]{1,0:T(8,128)(2,1)S(1)}, bf16[256,256]{1,0:T(8,128)(2,1)}, u32[]{:S(2)}) copy-start(bf16[256,256]{1,0:T(8,128)(2,1)} %get-tuple-element.39.own) | copy-start | bytes 393220
  9.5 2.9 %collective-permute-start = (bf16[256,512]{1,0:T(8,128)(2,1)}, bf16[256,512]{1,0:T(8,128)(2,1)S(1)}, u32[]{:S(2)}, u32[]{:S(2)}) collective-permute-start(bf16[256,512]{1,0:T(8,128)(2,1)} %get-tuple-element.28), channel_id=1, source_target_pairs={{0,4},{4,0},{1,5},{5,1},{2,6},{6,2},{3,7},{7,3},{8,12},{12,8},{9,1... | collective-permute-start | bytes 786440 | tf_op jit(solution)/shard_map/ppermute | solution.py:449
  14.9 13.9 %collective-permute-start.3 = (bf16[512,256]{1,0:T(8,128)(2,1)}, bf16[512,256]{1,0:T(8,128)(2,1)S(1)}, u32[]{:S(2)}, u32[]{:S(2)}) collective-permute-start(bf16[512,256]{1,0:T(8,128)(2,1)} %get-tuple-element.29.q0), channel_id=1, source_target_pairs={{0,24},{8,0},{16,8},{24,16},{1,25},{9,1},{17,9},{25,17},{2,26},{10... | collective-permute-start | bytes 786440 | tf_op jit(solution)/shard_map/ppermute | solution.py:453
  17.8 19.1 %collective-permute-start.2 = (bf16[512,256]{1,0:T(8,128)(2,1)}, bf16[512,256]{1,0:T(8,128)(2,1)S(1)}, u32[]{:S(2)}, u32[]{:S(2)}) collective-permute-start(bf16[512,256]{1,0:T(8,128)(2,1)} %get-tuple-element.29.q0), channel_id=1, source_target_pairs={{0,16},{8,24},{16,0},{24,8},{1,17},{9,25},{17,1},{25,9},{2,18},{10... | collective-permute-start | bytes 786440 | tf_op jit(solution)/shard_map/ppermute | solution.py:453
  18.1 18.8 %collective-permute-start.1 = (bf16[512,256]{1,0:T(8,128)(2,1)}, bf16[512,256]{1,0:T(8,128)(2,1)S(1)}, u32[]{:S(2)}, u32[]{:S(2)}) collective-permute-start(bf16[512,256]{1,0:T(8,128)(2,1)} %get-tuple-element.29.q0), channel_id=1, source_target_pairs={{0,8},{8,16},{16,24},{24,0},{1,9},{9,17},{17,25},{25,1},{2,10},{10... | collective-permute-start | bytes 786440 | tf_op jit(solution)/shard_map/ppermute | solution.py:453
  18.8 18.1 %collective-permute-start.6 = (bf16[512,256]{1,0:T(8,128)(2,1)}, bf16[512,256]{1,0:T(8,128)(2,1)S(1)}, u32[]{:S(2)}, u32[]{:S(2)}) collective-permute-start(bf16[512,256]{1,0:T(8,128)(2,1)} %get-tuple-element.30.k0), channel_id=1, source_target_pairs={{0,96},{32,0},{64,32},{96,64},{1,97},{33,1},{65,33},{97,65},{2,98}... | collective-permute-start | bytes 786440 | tf_op jit(solution)/shard_map/ppermute | solution.py:453
  21.3 15.6 %collective-permute-start.5 = (bf16[512,256]{1,0:T(8,128)(2,1)}, bf16[512,256]{1,0:T(8,128)(2,1)S(1)}, u32[]{:S(2)}, u32[]{:S(2)}) collective-permute-start(bf16[512,256]{1,0:T(8,128)(2,1)} %get-tuple-element.30.k0), channel_id=1, source_target_pairs={{0,64},{32,96},{64,0},{96,32},{1,65},{33,97},{65,1},{97,33},{2,66}... | collective-permute-start | bytes 786440 | tf_op jit(solution)/shard_map/ppermute | solution.py:453
  28.9 8.0 %collective-permute-start.4 = (bf16[512,256]{1,0:T(8,128)(2,1)}, bf16[512,256]{1,0:T(8,128)(2,1)S(1)}, u32[]{:S(2)}, u32[]{:S(2)}) collective-permute-start(bf16[512,256]{1,0:T(8,128)(2,1)} %get-tuple-element.30.k0), channel_id=1, source_target_pairs={{0,32},{32,64},{64,96},{96,0},{1,33},{33,65},{65,97},{97,1},{2,34}... | collective-permute-start | bytes 786440 | tf_op jit(solution)/shard_map/ppermute | solution.py:453
  46.1 45.8 %copy-start.2 = (bf16[128,256]{1,0:T(8,128)(2,1)S(1)}, bf16[128,256]{1,0:T(8,128)(2,1)}, u32[]{:S(2)}) copy-start(bf16[128,256]{1,0:T(8,128)(2,1)} %uq.1) | copy-start | bytes 196612
  46.1 45.8 %copy-start.3 = (bf16[128,256]{1,0:T(8,128)(2,1)S(1)}, bf16[128,256]{1,0:T(8,128)(2,1)}, u32[]{:S(2)}) copy-start(bf16[128,256]{1,0:T(8,128)(2,1)} %uv.1) | copy-start | bytes 196612
  46.2 4.5 %collective-permute-start.9 = (f32[48,128]{1,0:T(8,128)S(1)}, f32[48,128]{1,0:T(8,128)S(1)}, u32[]{:S(2)}, u32[]{:S(2)}) collective-permute-start(f32[48,128]{1,0:T(8,128)S(1)} %row_stats.1.s0), channel_id=1, source_target_pairs={{0,24},{8,0},{16,8},{24,16},{1,25},{9,1},{17,9},{25,17},{2,26},{10... | collective-permute-start | bytes 73736 | tf_op jit(solution)/shard_map/ppermute | solution.py:453
  49.7 4.2 %collective-permute-start.8 = (f32[48,128]{1,0:T(8,128)S(1)}, f32[48,128]{1,0:T(8,128)S(1)}, u32[]{:S(2)}, u32[]{:S(2)}) collective-permute-start(f32[48,128]{1,0:T(8,128)S(1)} %row_stats.1.s0), channel_id=1, source_target_pairs={{0,16},{8,24},{16,0},{24,8},{1,17},{9,25},{17,1},{25,9},{2,18},{10... | collective-permute-start | bytes 73736 | tf_op jit(solution)/shard_map/ppermute | solution.py:453
  49.7 4.2 %collective-permute-start.7 = (f32[48,128]{1,0:T(8,128)S(1)}, f32[48,128]{1,0:T(8,128)S(1)}, u32[]{:S(2)}, u32[]{:S(2)}) collective-permute-start(f32[48,128]{1,0:T(8,128)S(1)} %row_stats.1.s0), channel_id=1, source_target_pairs={{0,8},{8,16},{16,24},{24,0},{1,9},{9,17},{17,25},{25,1},{2,10},{10... | collective-permute-start | bytes 73736 | tf_op jit(solution)/shard_map/ppermute | solution.py:453
  68.7 8.8 %collective-permute-start.10 = (f32[512,128]{1,0:T(8,128)S(1)}, f32[512,128]{1,0:T(8,128)S(1)}, u32[]{:S(2)}, u32[]{:S(2)}) collective-permute-start(f32[512,128]{1,0:T(8,128)S(1)} %get-tuple-element.32), channel_id=1, source_target_pairs={{0,24},{8,0},{16,8},{24,16},{1,25},{9,1},{17,9},{25,17},{2,26},{10... | collective-permute-start | bytes 786440 | tf_op jit(solution)/shard_map/ppermute | solution.py:458
  69.2 7.1 %collective-permute-start.16 = (bf16[256,256]{1,0:T(8,128)(2,1)S(1)}, bf16[256,256]{1,0:T(8,128)(2,1)S(1)}, u32[]{:S(2)}, u32[]{:S(2)}) collective-permute-start(bf16[256,256]{1,0:T(8,128)(2,1)S(1)} %copy-done.4), channel_id=1, source_target_pairs={{0,4},{4,0},{1,5},{5,1},{2,6},{6,2},{3,7},{7,3},{8,12},{12,8},{9,1... | collective-permute-start | bytes 393224 | tf_op jit(solution)/shard_map/ppermute | solution.py:449
  73.0 9.7 %collective-permute-start.11 = (f32[512,128]{1,0:T(8,128)}, f32[512,128]{1,0:T(8,128)S(1)}, u32[]{:S(2)}, u32[]{:S(2)}) collective-permute-start(f32[512,128]{1,0:T(8,128)} %get-tuple-element.33), channel_id=1, source_target_pairs={{0,16},{8,24},{16,0},{24,8},{1,17},{9,25},{17,1},{25,9},{2,18},{10... | collective-permute-start | bytes 786440 | tf_op jit(solution)/shard_map/ppermute | solution.py:458
  74.0 14.6 %collective-permute-start.12 = (f32[512,128]{1,0:T(8,128)}, f32[512,128]{1,0:T(8,128)S(1)}, u32[]{:S(2)}, u32[]{:S(2)}) collective-permute-start(f32[512,128]{1,0:T(8,128)} %get-tuple-element.34), channel_id=1, source_target_pairs={{0,8},{8,16},{16,24},{24,0},{1,9},{9,17},{17,25},{25,1},{2,10},{10... | collective-permute-start | bytes 786440 | tf_op jit(solution)/shard_map/ppermute | solution.py:458
  75.1 13.5 %collective-permute-start.13 = (f32[512,128]{1,0:T(8,128)}, f32[512,128]{1,0:T(8,128)S(1)}, u32[]{:S(2)}, u32[]{:S(2)}) collective-permute-start(f32[512,128]{1,0:T(8,128)} %get-tuple-element.36), channel_id=1, source_target_pairs={{0,96},{32,0},{64,32},{96,64},{1,97},{33,1},{65,33},{97,65},{2,98}... | collective-permute-start | bytes 786440 | tf_op jit(solution)/shard_map/ppermute | solution.py:458
  76.3 12.2 %collective-permute-start.14 = (f32[512,128]{1,0:T(8,128)}, f32[512,128]{1,0:T(8,128)S(1)}, u32[]{:S(2)}, u32[]{:S(2)}) collective-permute-start(f32[512,128]{1,0:T(8,128)} %get-tuple-element.37), channel_id=1, source_target_pairs={{0,64},{32,96},{64,0},{96,32},{1,65},{33,97},{65,1},{97,33},{2,66}... | collective-permute-start | bytes 786440 | tf_op jit(solution)/shard_map/ppermute | solution.py:458
  77.5 14.4 %collective-permute-start.15 = (f32[512,128]{1,0:T(8,128)}, f32[512,128]{1,0:T(8,128)S(1)}, u32[]{:S(2)}, u32[]{:S(2)}) collective-permute-start(f32[512,128]{1,0:T(8,128)} %get-tuple-element.38), channel_id=1, source_target_pairs={{0,32},{32,64},{64,96},{96,0},{1,33},{33,65},{65,97},{97,1},{2,34}... | collective-permute-start | bytes 786440 | tf_op jit(solution)/shard_map/ppermute | solution.py:458
  92.5 3.9 %collective-permute-start.17 = (f32[256,256]{1,0:T(8,128)S(1)}, f32[256,256]{1,0:T(8,128)S(1)}, u32[]{:S(2)}, u32[]{:S(2)}) collective-permute-start(f32[256,256]{1,0:T(8,128)S(1)} %get-tuple-element.41), channel_id=1, source_target_pairs={{0,4},{4,0},{1,5},{5,1},{2,6},{6,2},{3,7},{7,3},{8,12},{12,8},{9,1... | collective-permute-start | bytes 786440 | tf_op jit(solution)/shard_map/ppermute | solution.py:449
  93.1 7.9 %collective-permute-start.21 = (bf16[512,128]{1,0:T(8,128)(2,1)S(1)}, bf16[512,128]{1,0:T(8,128)(2,1)S(1)}, u32[]{:S(2)}, u32[]{:S(2)}) collective-permute-start(bf16[512,128]{1,0:T(8,128)(2,1)S(1)} %copy-done.9), channel_id=1, source_target_pairs={{0,24},{8,0},{16,8},{24,16},{1,25},{9,1},{17,9},{25,17},{2,26},{10... | collective-permute-start | bytes 393224 | tf_op jit(solution)/shard_map/ppermute | solution.py:458
  95.5 7.1 %collective-permute-start.22 = (bf16[512,128]{1,0:T(8,128)(2,1)S(1)}, bf16[512,128]{1,0:T(8,128)(2,1)S(1)}, u32[]{:S(2)}, u32[]{:S(2)}) collective-permute-start(bf16[512,128]{1,0:T(8,128)(2,1)S(1)} %copy-done.7), channel_id=1, source_target_pairs={{0,16},{8,24},{16,0},{24,8},{1,17},{9,25},{17,1},{25,9},{2,18},{10... | collective-permute-start | bytes 393224 | tf_op jit(solution)/shard_map/ppermute | solution.py:458
  95.6 9.3 %collective-permute-start.23 = (bf16[512,128]{1,0:T(8,128)(2,1)S(1)}, bf16[512,128]{1,0:T(8,128)(2,1)S(1)}, u32[]{:S(2)}, u32[]{:S(2)}) collective-permute-start(bf16[512,128]{1,0:T(8,128)(2,1)S(1)} %get-tuple-element.45), channel_id=1, source_target_pairs={{0,8},{8,16},{16,24},{24,0},{1,9},{9,17},{17,25},{25,1},{2,10},{10... | collective-permute-start | bytes 393224 | tf_op jit(solution)/shard_map/ppermute | solution.py:458
  96.5 9.4 %collective-permute-start.20 = (bf16[256,256]{1,0:T(8,128)(2,1)S(1)}, bf16[256,256]{1,0:T(8,128)(2,1)S(1)}, u32[]{:S(2)}, u32[]{:S(2)}) collective-permute-start(bf16[256,256]{1,0:T(8,128)(2,1)S(1)} %get-tuple-element.49), channel_id=1, source_target_pairs={{0,3},{1,0},{2,1},{3,2},{4,7},{5,4},{6,5},{7,6},{8,11},{9,8},{10,9... | collective-permute-start | bytes 393224 | tf_op jit(solution)/shard_map/ppermute | solution.py:453
  100.3 5.6 %collective-permute-start.19 = (bf16[256,256]{1,0:T(8,128)(2,1)S(1)}, bf16[256,256]{1,0:T(8,128)(2,1)S(1)}, u32[]{:S(2)}, u32[]{:S(2)}) collective-permute-start(bf16[256,256]{1,0:T(8,128)(2,1)S(1)} %get-tuple-element.49), channel_id=1, source_target_pairs={{0,2},{1,3},{2,0},{3,1},{4,6},{5,7},{6,4},{7,5},{8,10},{9,11},{10,... | collective-permute-start | bytes 393224 | tf_op jit(solution)/shard_map/ppermute | solution.py:453
  101.0 9.0 %collective-permute-start.18 = (bf16[256,256]{1,0:T(8,128)(2,1)S(1)}, bf16[256,256]{1,0:T(8,128)(2,1)S(1)}, u32[]{:S(2)}, u32[]{:S(2)}) collective-permute-start(bf16[256,256]{1,0:T(8,128)(2,1)S(1)} %get-tuple-element.49), channel_id=1, source_target_pairs={{0,1},{1,2},{2,3},{3,0},{4,5},{5,6},{6,7},{7,4},{8,9},{9,10},{10,1... | collective-permute-start | bytes 393224 | tf_op jit(solution)/shard_map/ppermute | solution.py:453
  110.4 2.4 %collective-permute-start.24 = (f32[640,256]{1,0:T(8,128)S(1)}, f32[640,256]{1,0:T(8,128)S(1)}, u32[]{:S(2)}, u32[]{:S(2)}) collective-permute-start(f32[640,256]{1,0:T(8,128)S(1)} %get-tuple-element.47), channel_id=1, source_target_pairs={{0,4},{4,0},{1,5},{5,1},{2,6},{6,2},{3,7},{7,3},{8,12},{12,8},{9,1... | collective-permute-start | bytes 1966088 | tf_op jit(solution)/shard_map/ppermute | solution.py:449
  113.6 13.2 %all-to-all-start = ((bf16[16,48,256]{2,1,0:T(8,128)(2,1)}), bf16[16,48,256]{2,1,0:T(8,128)(2,1)S(1)}, u32[]{:S(2)}, u32[]{:S(2)}) async-start(bf16[16,48,256]{2,1,0:T(8,128)(2,1)} %pack.1), calls=%async_computation | async-start | bytes 786432 | tf_op jit(solution)/shard_map/all_to_all | solution.py:483
  117.6 1.6 %collective-permute-start.25 = (bf16[256,128]{1,0:T(8,128)(2,1)S(1)}, bf16[256,128]{1,0:T(8,128)(2,1)S(1)}, u32[]{:S(2)}, u32[]{:S(2)}) collective-permute-start(bf16[256,128]{1,0:T(8,128)(2,1)S(1)} %get-tuple-element.52), channel_id=1, source_target_pairs={{0,4},{4,0},{1,5},{5,1},{2,6},{6,2},{3,7},{7,3},{8,12},{12,8},{9,1... | collective-permute-start | bytes 196616 | tf_op jit(solution)/shard_map/ppermute | solution.py:449
  153.6 6.4 %collective-permute-start.26 = (bf16[64,48,256]{2,1,0:T(8,128)(2,1)S(1)}, bf16[64,48,256]{2,1,0:T(8,128)(2,1)S(1)}, u32[]{:S(2)}, u32[]{:S(2)}) collective-permute-start(bf16[64,48,256]{2,1,0:T(8,128)(2,1)S(1)} %all_to_all.10.own), channel_id=1, source_target_pairs={{0,4},{4,0},{1,5},{5,1},{2,6},{6,2},{3,7},{7,3},{8,12},{12,8},{9,1... | collective-permute-start | bytes 4718600 | tf_op jit(solution)/shard_map/ppermute | solution.py:449
  (10 other events, 89.9 us)

commit v5 on v4

--- a/solution.py
+++ b/solution.py
@@ -26,7 +26,7 @@
 SMEM = pl.BlockSpec(memory_space=pltpu.SMEM)
 ANY = pl.BlockSpec(memory_space=pl.ANY)
 WIDE = pltpu.CompilerParams(vmem_limit_bytes=60 * 1024 * 1024)
-PARAMS = pltpu.CompilerParams(vmem_limit_bytes=48 * 1024 * 1024)
+PARAMS = pltpu.CompilerParams(vmem_limit_bytes=20 * 1024 * 1024)
 
 
 def dot(a, b, ca=1, cb=0):
@@ -110,6 +110,7 @@
         in_specs=[VMEM] * 2,
         out_specs=[VMEM] * 2,
         out_shape=[jax.ShapeDtypeStruct((512, 256), bf16)] * 2,
+        compiler_params=PARAMS,
         name="assemble",
     )(keep, other)
 
@@ -127,9 +128,9 @@
 
     def one(q, _):
         f = out[17, q]
+        words = [packed[f, keys[k]] for k in range(16)]
         n = 0
-        for k in range(16):
-            word = packed[f, keys[k]]
+        for k, word in enumerate(words):
             for r in range(4):
                 out[q, n + r] = k * 4 + ((word >> (2 * r)) & 3)
             n = n + (word >> 8)
@@ -148,6 +149,7 @@
         in_specs=[SMEM] * 2,
         out_specs=SMEM,
         out_shape=jax.ShapeDtypeStruct((24, 128), jnp.int32),
+        compiler_params=PARAMS,
         name="lists",
     )(slot, packed)
 
@@ -388,7 +390,7 @@
             for cc in range(2):
                 src = halves[(c + cc) % 2]
                 for i in range(16):
-                    part = src[zz * 16 + i].astype(f32)
+                    part = src[i, pl.ds(pl.multiple_of(zz * 48, 16), 48), :].astype(f32)
                     at = cc * 640 + i * 40
                     down_q[at:at + 40, :] = part[:40, :RANK]
                     down_v[at:at + 40, :] = part[:40, RANK:]
@@ -400,7 +402,7 @@
                     src = halves[(c + cc) % 2]
                     att[:, cc * HEAD:(cc + 1) * HEAD] = outs[(c + cc) % 2][...]
                     for i in range(16):
-                        part = src[lax.axis_index("z") * 16 + i].astype(f32)
+                        part = src[i, pl.ds(pl.multiple_of(lax.axis_index("z") * 48, 16), 48), :].astype(f32)
                         up_q[i * 8:(i + 1) * 8, cc * HEAD:(cc + 1) * HEAD] = part[40:, :HEAD]
                         up_v[i * 8:(i + 1) * 8, cc * HEAD:(cc + 1) * HEAD] = part[40:, HEAD:]
 
@@ -425,20 +427,36 @@
     total = parts[0].astype(f32)
     for i in range(1, 16):
         total += parts[i].astype(f32)
-    low = total.astype(bf16)
-    for i in range(64):
-        out[i, :, :] = low
-
-
-def total_for_all(parts, after):
+    out[...] = total.astype(bf16)
+
+
+def add_up(parts, after):
     return pl.pallas_call(
         total_kernel,
         in_specs=[VMEM, ANY],
         out_specs=VMEM,
-        out_shape=jax.ShapeDtypeStruct((64, 48, 256), bf16),
-        compiler_params=PARAMS,
-        name="total_for_all",
+        out_shape=jax.ShapeDtypeStruct((48, 256), bf16),
+        compiler_params=PARAMS,
+        name="add_up",
     )(parts, after)
+
+
+def copies_kernel(p0, p1, p2, p3, out):
+    for d, part in enumerate((p0, p1, p2, p3)):
+        at = pl.multiple_of(lax.rem(lax.axis_index("z") + 4 - d, 4) * 48, 16)
+        for i in range(16):
+            out[i, pl.ds(at, 48), :] = part[...]
+
+
+def copies(parts):
+    return pl.pallas_call(
+        copies_kernel,
+        in_specs=[VMEM] * 4,
+        out_specs=VMEM,
+        out_shape=jax.ShapeDtypeStruct((16, 192, 256), bf16),
+        compiler_params=PARAMS,
+        name="copies",
+    )(*parts)
 
 
 def ring(n, d):
@@ -481,7 +499,8 @@
     rg = rg_keep + swap(rg_send)
     mine, theirs = down_terms(act_t, rg, spread(rg.astype(bf16), "z")[1:], o)
     terms = lax.all_to_all(pack(mine, swap(theirs), up), ("x", "y"), 0, 0, tiled=True)
-    wide = lax.all_to_all(total_for_all(terms, o_other), ("z", "x", "y"), 0, 0, tiled=True)
+    wide = copies(spread(add_up(terms, o_other), "z"))
+    wide = lax.all_to_all(wide, ("x", "y"), 0, 0, tiled=True)
     att, down_q, up_q, down_v, up_v = emit(wide, swap(wide), o_keep, o_other)
     return att, down_q, up_q, down_v, up_v
 

time: 163 us -> 161 us (0.988)
  blocking collectives: 26.7 us -> 22 us
  waiting for transfers between devices: 44 us -> 48 us
  starting transfers between devices: 41 us -> 43.8 us
  local copies, waits for them, and re-layouts: 7.95 us -> 5.6 us
  Pallas kernels: 41.5 us -> 39.8 us
    all_to_all x1, blocking collectives: 26.7 us -> 22 us  [local(): wide = lax.all_to_all(wide, ('x', 'y'), 0, 0, tiled=True)]
    ppermute x12 -> x15, waiting for transfers between devices: 15.6 us -> 18.8 us  [spread(): one, three, two = [lax.ppermute(a, axis, ring(4, d)) for d in (1, 3, 2)]]
    unnamed x29 -> x25, local copies, waits for them, and re-layouts: 5.98 us -> 3.63 us
    ppermute x6, starting transfers between devices: 10.7 us -> 12.7 us  [swap(): return lax.ppermute(a, 'c', ring(2, 1))]
    pallas_call x1, Pallas kernels: 1.84 us -> 0.03 us  [assemble(): pl.pallas_call(assemble_kernel, in_specs=[VMEM] * 2, out_specs=[VMEM] * 2...]
    ppermute x12 -> x15, starting transfers between devices: 17.7 us -> 18.9 us  [spread(): one, three, two = [lax.ppermute(a, axis, ring(4, d)) for d in (1, 3, 2)]]
  transfers between devices with their start and end apart: 28 -> 31, of which waited for: 15 -> 17; matrix products, arithmetic and copies ran while one was open for 3% -> 2% of each run, Pallas kernels for 4% -> 4%
where the time goes in v5:
time: 161 us; the launch traced here: 160 us
  waiting for transfers between devices  48 us (30%)
  starting transfers between devices  43.8 us (27%)
  Pallas kernels  39.8 us (25%)
  blocking collectives  22 us (14%)
  local copies, waits for them, and re-layouts  5.6 us (3%)
    all_to_all x1, blocking collectives, local(): wide = lax.all_to_all(wide, ('x', 'y'), 0, 0, tiled=True)  22 us
    ppermute x15, starting transfers between devices, spread(): one, three, two = [lax.ppermute(a, axis, ring(4, d)) for d in (1, 3, 2)]  18.9 us
    ppermute x15, waiting for transfers between devices, spread(): one, three, two = [lax.ppermute(a, axis, ring(4, d)) for d in (1, 3, 2)]  18.8 us
    ppermute x9, waiting for transfers between devices, collect(): lax.ppermute(parts[d], axis, ring(4, -d))  14.6 us
    pallas_call x1, Pallas kernels, attention_grads(): pl.pallas_call(grads_kernel, in_specs=[SMEM] + [VMEM] * 12, out_specs=[VM...  13.5 us
    ppermute x6, starting transfers between devices, swap(): return lax.ppermute(a, 'c', ring(2, 1))  12.7 us
    pallas_call x1, Pallas kernels, project(): pl.pallas_call(proj_kernel, grid=(width // KT,), in_specs=[pl.BlockSpec((...  8.86 us
    ppermute x9, starting transfers between devices, collect(): lax.ppermute(parts[d], axis, ring(4, -d))  8.22 us
  transfers between devices with their start and end apart: 31, of which 17 were waited for; matrix products, arithmetic and copies ran while one was open for 2% of the time, Pallas kernels for 4%

profile of v5, /device:TPU:1, one launch (start us, length us, event | category | flops | bytes accessed | tf_op | source)
XLA Modules:
  0.0 160.3 jit_solution(13845837161706884053)
XLA Ops:
  0.7 8.9 %project.1 = (bf16[256,512]{1,0:T(8,128)(2,1)}, bf16[256,512]{1,0:T(8,128)(2,1)}, bf16[256,256]{1,0:T(8,128)(2,1)}) custom-call(bf16[256,5120]{1,0:T(8,128)(2,1)} %act.1, bf16[5120,256]{1,0:T(8,128)(2,1)} %wq.1, bf16[5120,256]{1,0:T(8,128)(2,1)} %wk.1, bf16[5120,256]{1,0:T(8,128)(2,1)} %wv.1, bf16[5120,128]{1,0:T(8,128)(2,1)} %down_q.1, ...), custom_call_target="tpu_custom_call" | custom-call | flops 2684354560 | bytes 13107200 | tf_op jit(solution)/shard_map/project/pallas_call | solution.py:84
  9.5 1.5 collective-permute-start
  11.0 1.4 collective-permute-done.other
  13.4 2.9 %collective-permute-start.3 = (bf16[512,256]{1,0:T(8,128)(2,1)S(1)}, bf16[512,256]{1,0:T(8,128)(2,1)S(1)}, u32[]{:S(2)}, u32[]{:S(2)}) collective-permute-start(bf16[512,256]{1,0:T(8,128)(2,1)S(1)} %get-tuple-element.29.q0), channel_id=1, source_target_pairs={{0,24},{8,0},{16,8},{24,16},{1,25},{9,1},{17,9},{25,17},{2,26},{10... | collective-permute-start | bytes 786440 | tf_op jit(solution)/shard_map/ppermute | solution.py:471
  17.3 2.5 %collective-permute-start.6 = (bf16[512,256]{1,0:T(8,128)(2,1)S(1)}, bf16[512,256]{1,0:T(8,128)(2,1)S(1)}, u32[]{:S(2)}, u32[]{:S(2)}) collective-permute-start(bf16[512,256]{1,0:T(8,128)(2,1)S(1)} %get-tuple-element.30.k0), channel_id=1, source_target_pairs={{0,96},{32,0},{64,32},{96,64},{1,97},{33,1},{65,33},{97,65},{2,98}... | collective-permute-start | bytes 786440 | tf_op jit(solution)/shard_map/ppermute | solution.py:471
  20.3 6.8 %collective-permute-done.3.q3 = bf16[512,256]{1,0:T(8,128)(2,1)S(1)} collective-permute-done((bf16[512,256]{1,0:T(8,128)(2,1)S(1)}, bf16[512,256]{1,0:T(8,128)(2,1)S(1)}, u32[]{:S(2)}, u32[]{:S(2)}) %collective-permute-start.3) | collective-permute-done | bytes 262176 | tf_op jit(solution)/shard_map/ppermute | solution.py:471
  28.5 6.0 %lists.1 = s32[24,128]{1,0:T(8,128)S(1)} custom-call(s32[64]{0:T(128)S(1)} %copy-done.4, s32[64,64]{1,0:T(8,128)S(1)} %multiply_add_fusion.packed), custom_call_target="tpu_custom_call" | custom-call | tf_op jit(solution)/shard_map/lists/pallas_call | solution.py:147
  34.7 6.6 %row_stats.1.s0 = f32[48,128]{1,0:T(8,128)S(1)} custom-call(s32[24,128]{1,0:T(8,128)S(1)} %lists.1, bf16[512,256]{1,0:T(8,128)(2,1)S(1)} %get-tuple-element.29.q0, bf16[512,256]{1,0:T(8,128)(2,1)S(1)} %collective-permute-done.1.q1, bf16[512,256]{1,0:T(8,128)(2,1)S(1)} %collective-permute-done.2.q2, bf16[512,256]{1,0:T(8,128)(2,1)S(1)} %collective-permute-done.3.q3, ...), custom_call_target="tpu_custom_call" | custom-call | tf_op jit(solution)/shard_map/row_stats/pallas_call | solution.py:219
  41.3 3.8 %collective-permute-start.9 = (f32[48,128]{1,0:T(8,128)S(1)}, f32[48,128]{1,0:T(8,128)S(1)}, u32[]{:S(2)}, u32[]{:S(2)}) collective-permute-start(f32[48,128]{1,0:T(8,128)S(1)} %row_stats.1.s0), channel_id=1, source_target_pairs={{0,24},{8,0},{16,8},{24,16},{1,25},{9,1},{17,9},{25,17},{2,26},{10... | collective-permute-start | bytes 73736 | tf_op jit(solution)/shard_map/ppermute | solution.py:471
  46.1 3.3 %collective-permute-done.8.s2 = f32[48,128]{1,0:T(8,128)S(1)} collective-permute-done((f32[48,128]{1,0:T(8,128)S(1)}, f32[48,128]{1,0:T(8,128)S(1)}, u32[]{:S(2)}, u32[]{:S(2)}) %collective-permute-start.8) | collective-permute-done | bytes 24608 | tf_op jit(solution)/shard_map/ppermute | solution.py:471
  49.4 13.5 %attention_grads.1 = (f32[512,128]{1,0:T(8,128)S(1)}, bf16[512,128]{1,0:T(8,128)(2,1)S(1)}, bf16[512,128]{1,0:T(8,128)(2,1)S(1)}, bf16[512,128]{1,0:T(8,128)(2,1...) custom-call(s32[24,128]{1,0:T(8,128)S(1)} %lists.1, ...), custom_call_target="tpu_custom_call" | custom-call | tf_op jit(solution)/shard_map/attention_grads/pallas_call | solution.py:303
  64.6 3.8 %collective-permute-start.16 = (bf16[256,256]{1,0:T(8,128)(2,1)S(1)}, bf16[256,256]{1,0:T(8,128)(2,1)S(1)}, u32[]{:S(2)}, u32[]{:S(2)}) collective-permute-start(bf16[256,256]{1,0:T(8,128)(2,1)S(1)} %copy-done.3), channel_id=1, source_target_pairs={{0,4},{4,0},{1,5},{5,1},{2,6},{6,2},{3,7},{7,3},{8,12},{12,8},{9,1... | collective-permute-start | bytes 393224 | tf_op jit(solution)/shard_map/ppermute | solution.py:467
  70.5 1.3 collective-permute-start.13
  72.9 2.0 %constant_dynamic-slice_fusion = bf16[256,1280]{1,0:T(8,128)(2,1)} fusion(bf16[256,5120]{1,0:T(8,128)(2,1)} %act.1, s32[]{:T(128)S(6)} %select_n.3), kind=kLoop, calls=%fused_computation.3 | loop fusion | bytes 1310724 | tf_op jit(solution)/shard_map/dynamic_slice | solution.py:480
  74.9 1.3 copy.19
  76.3 1.9 %collective-permute-done.11.a2 = f32[512,128]{1,0:T(8,128)S(1)} collective-permute-done((f32[512,128]{1,0:T(8,128)}, f32[512,128]{1,0:T(8,128)S(1)}, u32[]{:S(2)}, u32[]{:S(2)}) %collective-permute-start.11) | collective-permute-done | bytes 262176 | tf_op jit(solution)/shard_map/ppermute | solution.py:476
  78.2 5.9 %collective-permute-done.12.a3 = f32[512,128]{1,0:T(8,128)S(1)} collective-permute-done((f32[512,128]{1,0:T(8,128)}, f32[512,128]{1,0:T(8,128)S(1)}, u32[]{:S(2)}, u32[]{:S(2)}) %collective-permute-start.12) | collective-permute-done | bytes 262176 | tf_op jit(solution)/shard_map/ppermute | solution.py:476
  84.1 3.3 %collective-permute-done.15.b3 = f32[512,128]{1,0:T(8,128)S(1)} collective-permute-done((f32[512,128]{1,0:T(8,128)}, f32[512,128]{1,0:T(8,128)S(1)}, u32[]{:S(2)}, u32[]{:S(2)}) %collective-permute-start.15) | collective-permute-done | bytes 262176 | tf_op jit(solution)/shard_map/ppermute | solution.py:476
  88.6 1.6 collective-permute-start.21
  91.9 3.8 %collective-permute-start.20 = (bf16[256,256]{1,0:T(8,128)(2,1)S(1)}, bf16[256,256]{1,0:T(8,128)(2,1)S(1)}, u32[]{:S(2)}, u32[]{:S(2)}) collective-permute-start(bf16[256,256]{1,0:T(8,128)(2,1)S(1)} %get-tuple-element.49), channel_id=1, source_target_pairs={{0,3},{1,0},{2,1},{3,2},{4,7},{5,4},{6,5},{7,6},{8,11},{9,8},{10,9... | collective-permute-start | bytes 393224 | tf_op jit(solution)/shard_map/ppermute | solution.py:471
  96.5 3.4 %collective-permute-done.23 = bf16[512,128]{1,0:T(8,128)(2,1)S(1)} collective-permute-done((bf16[512,128]{1,0:T(8,128)(2,1)S(1)}, bf16[512,128]{1,0:T(8,128)(2,1)S(1)}, u32[]{:S(2)}, u32[]{:S(2)}) %collective-permute-start.23) | collective-permute-done | bytes 131104 | tf_op jit(solution)/shard_map/ppermute | solution.py:476
  100.0 1.3 collective-permute-done.20.r3
  101.3 3.2 %collective-permute-done.18.r1 = bf16[256,256]{1,0:T(8,128)(2,1)S(1)} collective-permute-done((bf16[256,256]{1,0:T(8,128)(2,1)S(1)}, bf16[256,256]{1,0:T(8,128)(2,1)S(1)}, u32[]{:S(2)}, u32[]{:S(2)}) %collective-permute-start.18) | collective-permute-done | bytes 131104 | tf_op jit(solution)/shard_map/ppermute | solution.py:471
  104.9 1.2 collective-permute-start.24
  106.2 1.7 %collective-permute-done.24.theirs = f32[640,256]{1,0:T(8,128)S(1)} collective-permute-done((f32[640,256]{1,0:T(8,128)S(1)}, f32[640,256]{1,0:T(8,128)S(1)}, u32[]{:S(2)}, u32[]{:S(2)}) %collective-permute-start.24) | collective-permute-done | bytes 655392 | tf_op jit(solution)/shard_map/ppermute | solution.py:467
  108.7 3.9 %all-to-all-start = ((bf16[16,48,256]{2,1,0:T(8,128)(2,1)}), bf16[16,48,256]{2,1,0:T(8,128)(2,1)S(1)}, u32[]{:S(2)}, u32[]{:S(2)}) async-start(bf16[16,48,256]{2,1,0:T(8,128)(2,1)} %pack.1), calls=%async_computation | async-start | bytes 786432 | tf_op jit(solution)/shard_map/all_to_all | solution.py:501
  114.3 7.6 %all-to-all-done.parts = bf16[16,48,256]{2,1,0:T(8,128)(2,1)S(1)} async-done(((bf16[16,48,256]{2,1,0:T(8,128)(2,1)}), bf16[16,48,256]{2,1,0:T(8,128)(2,1)S(1)}, u32[]{:S(2)}, u32[]{:S(2)}) %all-to-all-start) | async-done | bytes 393248 | tf_op jit(solution)/shard_map/all_to_all | solution.py:501
  124.7 2.6 %collective-permute-done.27.p2 = bf16[48,256]{1,0:T(8,128)(2,1)S(1)} collective-permute-done((bf16[48,256]{1,0:T(8,128)(2,1)S(1)}, bf16[48,256]{1,0:T(8,128)(2,1)S(1)}, u32[]{:S(2)}, u32[]{:S(2)}) %collective-permute-start.27) | collective-permute-done | bytes 24608 | tf_op jit(solution)/shard_map/ppermute | solution.py:471
  127.5 22.0 %all_to_all.10.own = bf16[16,192,256]{2,1,0:T(8,128)(2,1)S(1)} all-to-all(bf16[16,192,256]{2,1,0:T(8,128)(2,1)S(1)} %copies.1), channel_id=1, replica_groups=mesh['x'=4,'y'=4,'c'=2,'z'=4] {'x','y'}, dimensions={0} | all-to-all | bytes 3145728 | tf_op jit(solution)/shard_map/all_to_all | solution.py:503
  149.5 4.9 %collective-permute-start.29 = (bf16[16,192,256]{2,1,0:T(8,128)(2,1)S(1)}, bf16[16,192,256]{2,1,0:T(8,128)(2,1)S(1)}, u32[]{:S(2)}, u32[]{:S(2)}) collective-permute-start(bf16[16,192,256]{2,1,0:T(8,128)(2,1)S(1)} %all_to_all.10.own), channel_id=1, source_target_pairs={{0,4},{4,0},{1,5},{5,1},{2,6},{6,2},{3,7},{7,3},{8,12},{12,8},{9,1... | collective-permute-start | bytes 4718600 | tf_op jit(solution)/shard_map/ppermute | solution.py:467
  154.4 3.0 %collective-permute-done.29.other = bf16[16,192,256]{2,1,0:T(8,128)(2,1)S(1)} collective-permute-done((bf16[16,192,256]{2,1,0:T(8,128)(2,1)S(1)}, bf16[16,192,256]{2,1,0:T(8,128)(2,1)S(1)}, u32[]{:S(2)}, u32[]{:S(2)}) %collective-permute-start.29) | collective-permute-done | bytes 1572896 | tf_op jit(solution)/shard_map/ppermute | solution.py:467
  157.4 2.8 %emit.1 = (bf16[256,256]{1,0:T(8,128)(2,1)}, f32[5120,128]{1,0:T(8,128)}, f32[128,256]{1,0:T(8,128)}, f32[5120,128]{1,0:T(8,128)}, f32[128,256]{1,0:T(8,128)}) custom-call(bf16[16,192,256]{2,1,0:T(8,128)(2,1)S(1)} %all_to_all.10.own, bf16[16,192,256]{2,1,0:T(8,128)(2,1)S(1)} %collective-permute-done.29.other, bf16[256,128]{1,0:T(8,128)(2,1)S(1)} %get-tuple-element.51.o_keep, ...), custom_call_target="tpu_custom_call" | custom-call | tf_op jit(solution)/shard_map/emit/pallas_call | solution.py:412
  (73 shorter events, 19.6 us)
Async XLA Ops:
  9.5 2.8 %collective-permute-start = (bf16[256,512]{1,0:T(8,128)(2,1)}, bf16[256,512]{1,0:T(8,128)(2,1)S(1)}, u32[]{:S(2)}, u32[]{:S(2)}) collective-permute-start(bf16[256,512]{1,0:T(8,128)(2,1)} %get-tuple-element.28), channel_id=1, source_target_pairs={{0,4},{4,0},{1,5},{5,1},{2,6},{6,2},{3,7},{7,3},{8,12},{12,8},{9,1... | collective-permute-start | bytes 786440 | tf_op jit(solution)/shard_map/ppermute | solution.py:467
  13.3 51.3 %copy-start.3 = (bf16[256,256]{1,0:T(8,128)(2,1)S(1)}, bf16[256,256]{1,0:T(8,128)(2,1)}, u32[]{:S(2)}) copy-start(bf16[256,256]{1,0:T(8,128)(2,1)} %get-tuple-element.39.own) | copy-start | bytes 393220
  13.4 13.7 %collective-permute-start.3 = (bf16[512,256]{1,0:T(8,128)(2,1)S(1)}, bf16[512,256]{1,0:T(8,128)(2,1)S(1)}, u32[]{:S(2)}, u32[]{:S(2)}) collective-permute-start(bf16[512,256]{1,0:T(8,128)(2,1)S(1)} %get-tuple-element.29.q0), channel_id=1, source_target_pairs={{0,24},{8,0},{16,8},{24,16},{1,25},{9,1},{17,9},{25,17},{2,26},{10... | collective-permute-start | bytes 786440 | tf_op jit(solution)/shard_map/ppermute | solution.py:471
  16.3 18.2 %collective-permute-start.2 = (bf16[512,256]{1,0:T(8,128)(2,1)S(1)}, bf16[512,256]{1,0:T(8,128)(2,1)S(1)}, u32[]{:S(2)}, u32[]{:S(2)}) collective-permute-start(bf16[512,256]{1,0:T(8,128)(2,1)S(1)} %get-tuple-element.29.q0), channel_id=1, source_target_pairs={{0,16},{8,24},{16,0},{24,8},{1,17},{9,25},{17,1},{25,9},{2,18},{10... | collective-permute-start | bytes 786440 | tf_op jit(solution)/shard_map/ppermute | solution.py:471
  16.6 17.9 %collective-permute-start.1 = (bf16[512,256]{1,0:T(8,128)(2,1)S(1)}, bf16[512,256]{1,0:T(8,128)(2,1)S(1)}, u32[]{:S(2)}, u32[]{:S(2)}) collective-permute-start(bf16[512,256]{1,0:T(8,128)(2,1)S(1)} %get-tuple-element.29.q0), channel_id=1, source_target_pairs={{0,8},{8,16},{16,24},{24,0},{1,9},{9,17},{17,25},{25,1},{2,10},{10... | collective-permute-start | bytes 786440 | tf_op jit(solution)/shard_map/ppermute | solution.py:471
  17.3 17.2 %collective-permute-start.6 = (bf16[512,256]{1,0:T(8,128)(2,1)S(1)}, bf16[512,256]{1,0:T(8,128)(2,1)S(1)}, u32[]{:S(2)}, u32[]{:S(2)}) collective-permute-start(bf16[512,256]{1,0:T(8,128)(2,1)S(1)} %get-tuple-element.30.k0), channel_id=1, source_target_pairs={{0,96},{32,0},{64,32},{96,64},{1,97},{33,1},{65,33},{97,65},{2,98}... | collective-permute-start | bytes 786440 | tf_op jit(solution)/shard_map/ppermute | solution.py:471
  19.8 14.7 %collective-permute-start.5 = (bf16[512,256]{1,0:T(8,128)(2,1)S(1)}, bf16[512,256]{1,0:T(8,128)(2,1)S(1)}, u32[]{:S(2)}, u32[]{:S(2)}) collective-permute-start(bf16[512,256]{1,0:T(8,128)(2,1)S(1)} %get-tuple-element.30.k0), channel_id=1, source_target_pairs={{0,64},{32,96},{64,0},{96,32},{1,65},{33,97},{65,1},{97,33},{2,66}... | collective-permute-start | bytes 786440 | tf_op jit(solution)/shard_map/ppermute | solution.py:471
  27.0 7.7 %collective-permute-start.4 = (bf16[512,256]{1,0:T(8,128)(2,1)S(1)}, bf16[512,256]{1,0:T(8,128)(2,1)S(1)}, u32[]{:S(2)}, u32[]{:S(2)}) collective-permute-start(bf16[512,256]{1,0:T(8,128)(2,1)S(1)} %get-tuple-element.30.k0), channel_id=1, source_target_pairs={{0,32},{32,64},{64,96},{96,0},{1,33},{33,65},{65,97},{97,1},{2,34}... | collective-permute-start | bytes 786440 | tf_op jit(solution)/shard_map/ppermute | solution.py:471
  41.3 4.7 %collective-permute-start.9 = (f32[48,128]{1,0:T(8,128)S(1)}, f32[48,128]{1,0:T(8,128)S(1)}, u32[]{:S(2)}, u32[]{:S(2)}) collective-permute-start(f32[48,128]{1,0:T(8,128)S(1)} %row_stats.1.s0), channel_id=1, source_target_pairs={{0,24},{8,0},{16,8},{24,16},{1,25},{9,1},{17,9},{25,17},{2,26},{10... | collective-permute-start | bytes 73736 | tf_op jit(solution)/shard_map/ppermute | solution.py:471
  45.1 4.3 %collective-permute-start.8 = (f32[48,128]{1,0:T(8,128)S(1)}, f32[48,128]{1,0:T(8,128)S(1)}, u32[]{:S(2)}, u32[]{:S(2)}) collective-permute-start(f32[48,128]{1,0:T(8,128)S(1)} %row_stats.1.s0), channel_id=1, source_target_pairs={{0,16},{8,24},{16,0},{24,8},{1,17},{9,25},{17,1},{25,9},{2,18},{10... | collective-permute-start | bytes 73736 | tf_op jit(solution)/shard_map/ppermute | solution.py:471
  45.2 4.2 %collective-permute-start.7 = (f32[48,128]{1,0:T(8,128)S(1)}, f32[48,128]{1,0:T(8,128)S(1)}, u32[]{:S(2)}, u32[]{:S(2)}) collective-permute-start(f32[48,128]{1,0:T(8,128)S(1)} %row_stats.1.s0), channel_id=1, source_target_pairs={{0,8},{8,16},{16,24},{24,0},{1,9},{9,17},{17,25},{25,1},{2,10},{10... | collective-permute-start | bytes 73736 | tf_op jit(solution)/shard_map/ppermute | solution.py:471
  64.2 8.4 %collective-permute-start.10 = (f32[512,128]{1,0:T(8,128)S(1)}, f32[512,128]{1,0:T(8,128)S(1)}, u32[]{:S(2)}, u32[]{:S(2)}) collective-permute-start(f32[512,128]{1,0:T(8,128)S(1)} %get-tuple-element.32), channel_id=1, source_target_pairs={{0,24},{8,0},{16,8},{24,16},{1,25},{9,1},{17,9},{25,17},{2,26},{10... | collective-permute-start | bytes 786440 | tf_op jit(solution)/shard_map/ppermute | solution.py:476
  64.6 7.2 %collective-permute-start.16 = (bf16[256,256]{1,0:T(8,128)(2,1)S(1)}, bf16[256,256]{1,0:T(8,128)(2,1)S(1)}, u32[]{:S(2)}, u32[]{:S(2)}) collective-permute-start(bf16[256,256]{1,0:T(8,128)(2,1)S(1)} %copy-done.3), channel_id=1, source_target_pairs={{0,4},{4,0},{1,5},{5,1},{2,6},{6,2},{3,7},{7,3},{8,12},{12,8},{9,1... | collective-permute-start | bytes 393224 | tf_op jit(solution)/shard_map/ppermute | solution.py:467
  68.5 9.7 %collective-permute-start.11 = (f32[512,128]{1,0:T(8,128)}, f32[512,128]{1,0:T(8,128)S(1)}, u32[]{:S(2)}, u32[]{:S(2)}) collective-permute-start(f32[512,128]{1,0:T(8,128)} %get-tuple-element.33), channel_id=1, source_target_pairs={{0,16},{8,24},{16,0},{24,8},{1,17},{9,25},{17,1},{25,9},{2,18},{10... | collective-permute-start | bytes 786440 | tf_op jit(solution)/shard_map/ppermute | solution.py:476
  69.4 14.6 %collective-permute-start.12 = (f32[512,128]{1,0:T(8,128)}, f32[512,128]{1,0:T(8,128)S(1)}, u32[]{:S(2)}, u32[]{:S(2)}) collective-permute-start(f32[512,128]{1,0:T(8,128)} %get-tuple-element.34), channel_id=1, source_target_pairs={{0,8},{8,16},{16,24},{24,0},{1,9},{9,17},{17,25},{25,1},{2,10},{10... | collective-permute-start | bytes 786440 | tf_op jit(solution)/shard_map/ppermute | solution.py:476
  70.5 13.5 %collective-permute-start.13 = (f32[512,128]{1,0:T(8,128)}, f32[512,128]{1,0:T(8,128)S(1)}, u32[]{:S(2)}, u32[]{:S(2)}) collective-permute-start(f32[512,128]{1,0:T(8,128)} %get-tuple-element.36), channel_id=1, source_target_pairs={{0,96},{32,0},{64,32},{96,64},{1,97},{33,1},{65,33},{97,65},{2,98}... | collective-permute-start | bytes 786440 | tf_op jit(solution)/shard_map/ppermute | solution.py:476
  71.8 12.2 %collective-permute-start.14 = (f32[512,128]{1,0:T(8,128)}, f32[512,128]{1,0:T(8,128)S(1)}, u32[]{:S(2)}, u32[]{:S(2)}) collective-permute-start(f32[512,128]{1,0:T(8,128)} %get-tuple-element.37), channel_id=1, source_target_pairs={{0,64},{32,96},{64,0},{96,32},{1,65},{33,97},{65,1},{97,33},{2,66}... | collective-permute-start | bytes 786440 | tf_op jit(solution)/shard_map/ppermute | solution.py:476
  72.6 14.8 %collective-permute-start.15 = (f32[512,128]{1,0:T(8,128)}, f32[512,128]{1,0:T(8,128)S(1)}, u32[]{:S(2)}, u32[]{:S(2)}) collective-permute-start(f32[512,128]{1,0:T(8,128)} %get-tuple-element.38), channel_id=1, source_target_pairs={{0,32},{32,64},{64,96},{96,0},{1,33},{33,65},{65,97},{97,1},{2,34}... | collective-permute-start | bytes 786440 | tf_op jit(solution)/shard_map/ppermute | solution.py:476
  88.0 3.9 %collective-permute-start.17 = (f32[256,256]{1,0:T(8,128)S(1)}, f32[256,256]{1,0:T(8,128)S(1)}, u32[]{:S(2)}, u32[]{:S(2)}) collective-permute-start(f32[256,256]{1,0:T(8,128)S(1)} %get-tuple-element.41), channel_id=1, source_target_pairs={{0,4},{4,0},{1,5},{5,1},{2,6},{6,2},{3,7},{7,3},{8,12},{12,8},{9,1... | collective-permute-start | bytes 786440 | tf_op jit(solution)/shard_map/ppermute | solution.py:467
  88.6 7.2 %collective-permute-start.21 = (bf16[512,128]{1,0:T(8,128)(2,1)S(1)}, bf16[512,128]{1,0:T(8,128)(2,1)S(1)}, u32[]{:S(2)}, u32[]{:S(2)}) collective-permute-start(bf16[512,128]{1,0:T(8,128)(2,1)S(1)} %copy-done.8), channel_id=1, source_target_pairs={{0,24},{8,0},{16,8},{24,16},{1,25},{9,1},{17,9},{25,17},{2,26},{10... | collective-permute-start | bytes 393224 | tf_op jit(solution)/shard_map/ppermute | solution.py:476
  90.1 6.3 %collective-permute-start.22 = (bf16[512,128]{1,0:T(8,128)(2,1)S(1)}, bf16[512,128]{1,0:T(8,128)(2,1)S(1)}, u32[]{:S(2)}, u32[]{:S(2)}) collective-permute-start(bf16[512,128]{1,0:T(8,128)(2,1)S(1)} %copy-done.6), channel_id=1, source_target_pairs={{0,16},{8,24},{16,0},{24,8},{1,17},{9,25},{17,1},{25,9},{2,18},{10... | collective-permute-start | bytes 393224 | tf_op jit(solution)/shard_map/ppermute | solution.py:476
  91.1 8.8 %collective-permute-start.23 = (bf16[512,128]{1,0:T(8,128)(2,1)S(1)}, bf16[512,128]{1,0:T(8,128)(2,1)S(1)}, u32[]{:S(2)}, u32[]{:S(2)}) collective-permute-start(bf16[512,128]{1,0:T(8,128)(2,1)S(1)} %get-tuple-element.45), channel_id=1, source_target_pairs={{0,8},{8,16},{16,24},{24,0},{1,9},{9,17},{17,25},{25,1},{2,10},{10... | collective-permute-start | bytes 393224 | tf_op jit(solution)/shard_map/ppermute | solution.py:476
  91.9 9.4 %collective-permute-start.20 = (bf16[256,256]{1,0:T(8,128)(2,1)S(1)}, bf16[256,256]{1,0:T(8,128)(2,1)S(1)}, u32[]{:S(2)}, u32[]{:S(2)}) collective-permute-start(bf16[256,256]{1,0:T(8,128)(2,1)S(1)} %get-tuple-element.49), channel_id=1, source_target_pairs={{0,3},{1,0},{2,1},{3,2},{4,7},{5,4},{6,5},{7,6},{8,11},{9,8},{10,9... | collective-permute-start | bytes 393224 | tf_op jit(solution)/shard_map/ppermute | solution.py:471
  95.7 5.6 %collective-permute-start.19 = (bf16[256,256]{1,0:T(8,128)(2,1)S(1)}, bf16[256,256]{1,0:T(8,128)(2,1)S(1)}, u32[]{:S(2)}, u32[]{:S(2)}) collective-permute-start(bf16[256,256]{1,0:T(8,128)(2,1)S(1)} %get-tuple-element.49), channel_id=1, source_target_pairs={{0,2},{1,3},{2,0},{3,1},{4,6},{5,7},{6,4},{7,5},{8,10},{9,11},{10,... | collective-permute-start | bytes 393224 | tf_op jit(solution)/shard_map/ppermute | solution.py:471
  95.8 8.8 %collective-permute-start.18 = (bf16[256,256]{1,0:T(8,128)(2,1)S(1)}, bf16[256,256]{1,0:T(8,128)(2,1)S(1)}, u32[]{:S(2)}, u32[]{:S(2)}) collective-permute-start(bf16[256,256]{1,0:T(8,128)(2,1)S(1)} %get-tuple-element.49), channel_id=1, source_target_pairs={{0,1},{1,2},{2,3},{3,0},{4,5},{5,6},{6,7},{7,4},{8,9},{9,10},{10,1... | collective-permute-start | bytes 393224 | tf_op jit(solution)/shard_map/ppermute | solution.py:471
  104.9 3.0 %collective-permute-start.24 = (f32[640,256]{1,0:T(8,128)S(1)}, f32[640,256]{1,0:T(8,128)S(1)}, u32[]{:S(2)}, u32[]{:S(2)}) collective-permute-start(f32[640,256]{1,0:T(8,128)S(1)} %get-tuple-element.47), channel_id=1, source_target_pairs={{0,4},{4,0},{1,5},{5,1},{2,6},{6,2},{3,7},{7,3},{8,12},{12,8},{9,1... | collective-permute-start | bytes 1966088 | tf_op jit(solution)/shard_map/ppermute | solution.py:467
  108.7 13.2 %all-to-all-start = ((bf16[16,48,256]{2,1,0:T(8,128)(2,1)}), bf16[16,48,256]{2,1,0:T(8,128)(2,1)S(1)}, u32[]{:S(2)}, u32[]{:S(2)}) async-start(bf16[16,48,256]{2,1,0:T(8,128)(2,1)} %pack.1), calls=%async_computation | async-start | bytes 786432 | tf_op jit(solution)/shard_map/all_to_all | solution.py:501
  112.7 1.6 %collective-permute-start.25 = (bf16[256,128]{1,0:T(8,128)(2,1)S(1)}, bf16[256,128]{1,0:T(8,128)(2,1)S(1)}, u32[]{:S(2)}, u32[]{:S(2)}) collective-permute-start(bf16[256,128]{1,0:T(8,128)(2,1)S(1)} %get-tuple-element.52), channel_id=1, source_target_pairs={{0,4},{4,0},{1,5},{5,1},{2,6},{6,2},{3,7},{7,3},{8,12},{12,8},{9,1... | collective-permute-start | bytes 196616 | tf_op jit(solution)/shard_map/ppermute | solution.py:467
  121.9 2.7 %collective-permute-start.28 = (bf16[48,256]{1,0:T(8,128)(2,1)S(1)}, bf16[48,256]{1,0:T(8,128)(2,1)S(1)}, u32[]{:S(2)}, u32[]{:S(2)}) collective-permute-start(bf16[48,256]{1,0:T(8,128)(2,1)S(1)} %add_up.1.p0), channel_id=1, source_target_pairs={{0,3},{1,0},{2,1},{3,2},{4,7},{5,4},{6,5},{7,6},{8,11},{9,8},{10,9... | collective-permute-start | bytes 73736 | tf_op jit(solution)/shard_map/ppermute | solution.py:471
  123.0 4.3 %collective-permute-start.27 = (bf16[48,256]{1,0:T(8,128)(2,1)S(1)}, bf16[48,256]{1,0:T(8,128)(2,1)S(1)}, u32[]{:S(2)}, u32[]{:S(2)}) collective-permute-start(bf16[48,256]{1,0:T(8,128)(2,1)S(1)} %add_up.1.p0), channel_id=1, source_target_pairs={{0,2},{1,3},{2,0},{3,1},{4,6},{5,7},{6,4},{7,5},{8,10},{9,11},{10,... | collective-permute-start | bytes 73736 | tf_op jit(solution)/shard_map/ppermute | solution.py:471
  123.0 4.3 %collective-permute-start.26 = (bf16[48,256]{1,0:T(8,128)(2,1)S(1)}, bf16[48,256]{1,0:T(8,128)(2,1)S(1)}, u32[]{:S(2)}, u32[]{:S(2)}) collective-permute-start(bf16[48,256]{1,0:T(8,128)(2,1)S(1)} %add_up.1.p0), channel_id=1, source_target_pairs={{0,1},{1,2},{2,3},{3,0},{4,5},{5,6},{6,7},{7,4},{8,9},{9,10},{10,1... | collective-permute-start | bytes 73736 | tf_op jit(solution)/shard_map/ppermute | solution.py:471
  149.5 7.9 %collective-permute-start.29 = (bf16[16,192,256]{2,1,0:T(8,128)(2,1)S(1)}, bf16[16,192,256]{2,1,0:T(8,128)(2,1)S(1)}, u32[]{:S(2)}, u32[]{:S(2)}) collective-permute-start(bf16[16,192,256]{2,1,0:T(8,128)(2,1)S(1)} %all_to_all.10.own), channel_id=1, source_target_pairs={{0,4},{4,0},{1,5},{5,1},{2,6},{6,2},{3,7},{7,3},{8,12},{12,8},{9,1... | collective-permute-start | bytes 4718600 | tf_op jit(solution)/shard_map/ppermute | solution.py:467
  (11 other events, 231.4 us)

commit v6 on v4

--- a/solution.py
+++ b/solution.py
@@ -21,12 +21,13 @@
 f32 = jnp.float32
 bf16 = jnp.bfloat16
 WIRE = f32
+WIRE2 = bf16
 KT = 1280
 VMEM = pl.BlockSpec(memory_space=pltpu.VMEM)
 SMEM = pl.BlockSpec(memory_space=pltpu.SMEM)
 ANY = pl.BlockSpec(memory_space=pl.ANY)
 WIDE = pltpu.CompilerParams(vmem_limit_bytes=60 * 1024 * 1024)
-PARAMS = pltpu.CompilerParams(vmem_limit_bytes=48 * 1024 * 1024)
+PARAMS = pltpu.CompilerParams(vmem_limit_bytes=20 * 1024 * 1024)
 
 
 def dot(a, b, ca=1, cb=0):
@@ -110,6 +111,7 @@
         in_specs=[VMEM] * 2,
         out_specs=[VMEM] * 2,
         out_shape=[jax.ShapeDtypeStruct((512, 256), bf16)] * 2,
+        compiler_params=PARAMS,
         name="assemble",
     )(keep, other)
 
@@ -127,9 +129,9 @@
 
     def one(q, _):
         f = out[17, q]
+        words = [packed[f, keys[k]] for k in range(16)]
         n = 0
-        for k in range(16):
-            word = packed[f, keys[k]]
+        for k, word in enumerate(words):
             for r in range(4):
                 out[q, n + r] = k * 4 + ((word >> (2 * r)) & 3)
             n = n + (word >> 8)
@@ -148,6 +150,7 @@
         in_specs=[SMEM] * 2,
         out_specs=SMEM,
         out_shape=jax.ShapeDtypeStruct((24, 128), jnp.int32),
+        compiler_params=PARAMS,
         name="lists",
     )(slot, packed)
 
@@ -226,15 +229,9 @@
     )(lists, *qgs, *kvs)
 
 
-def grads_kernel(lists, s0, s1, s2, s3, q0, q1, q2, q3, k0, k1, k2, k3,
-                 o0, o1, o2, o3, a0, a1, a2, a3, b0, b1, b2, b3, qgall, kvall, both, acc, dva, norm):
-    fill_all((q0, q1, q2, q3), qgall)
-    fill_all((k0, k1, k2, k3), kvall)
-    both[...] = jnp.zeros_like(both)
-    dva[...] = jnp.zeros_like(dva)
+def merge_stats(stats, norm):
     for t in range(4):
         rows = [slice(4 * ((t - d) % 4), 4 * ((t - d) % 4) + 4) for d in range(4)]
-        stats = [ref[...] for ref in (s0, s1, s2, s3)]
         peaks = [stats[d][0:16][rows[d]] for d in range(4)]
         peak = jnp.maximum(jnp.maximum(peaks[0], peaks[1]), jnp.maximum(peaks[2], peaks[3]))
         total = jnp.zeros_like(peak)
@@ -245,50 +242,69 @@
             delta += fix * stats[d][32:48][rows[d]]
         norm[4 * t:4 * t + 4, :] = peak + jnp.log2(total)
         norm[16 + 4 * t:20 + 4 * t, :] = delta / total
+
+
+def slot_grads(lists, t, qgall, kvall, both, acc, dva, norm):
     row = lax.broadcasted_iota(jnp.int32, (CHUNK, HEAD), 0)
-
-    def frames(t, _):
-        counts, chunks, most = start_frames(lists, t, qgall, both)
-        lse = [norm[pl.ds(t * CHAINS + j, 1), :] for j in range(CHAINS)]
-        delta = [norm[pl.ds(16 + t * CHAINS + j, 1), :] for j in range(CHAINS)]
-        acc[...] = jnp.zeros_like(acc)
-
-        def chunk(ch, _):
-            at = [jnp.minimum(ch, chunks[j] - 1) * CB for j in range(CHAINS)]
-            kvs = [load_chunk(lists, t * CHAINS + j, at[j], kvall) for j in range(CHAINS)]
-            rs = [dot(kvs[j], both[j], 1, 1) for j in range(CHAINS)]
-            lows, pairs = [], []
+    counts, chunks, most = start_frames(lists, t, qgall, both)
+    lse = [norm[pl.ds(t * CHAINS + j, 1), :] for j in range(CHAINS)]
+    delta = [norm[pl.ds(16 + t * CHAINS + j, 1), :] for j in range(CHAINS)]
+    acc[...] = jnp.zeros_like(acc)
+
+    def chunk(ch, _):
+        at = [jnp.minimum(ch, chunks[j] - 1) * CB for j in range(CHAINS)]
+        kvs = [load_chunk(lists, t * CHAINS + j, at[j], kvall) for j in range(CHAINS)]
+        rs = [dot(kvs[j], both[j], 1, 1) for j in range(CHAINS)]
+        lows, pairs = [], []
+        for j in range(CHAINS):
+            s = jnp.where(row < (counts[j] - ch * CB) * BLK, rs[j][:, :FT] * SCALE2, NEG)
+            p = jnp.exp2(s - lse[j])
+            low = p.astype(bf16)
+            ds = (p * (rs[j][:, FT:] - delta[j]) * SCALE).astype(bf16)
+            lows.append(low)
+            pairs.append(jnp.concatenate([low, ds], axis=1))
+        for j in range(CHAINS):
+            product = dot(kvs[j], pairs[j], 0, 0)
+            acc[j, 0] += product[HEAD:, :FT]
+            acc[j, 1] += product[:HEAD, FT:]
+        dvs = [dot(lows[j], both[j, FT:, HEAD:]) for j in range(CHAINS)]
+        for i in range(CB):
             for j in range(CHAINS):
-                s = jnp.where(row < (counts[j] - ch * CB) * BLK, rs[j][:, :FT] * SCALE2, NEG)
-                p = jnp.exp2(s - lse[j])
-                low = p.astype(bf16)
-                ds = (p * (rs[j][:, FT:] - delta[j]) * SCALE).astype(bf16)
-                lows.append(low)
-                pairs.append(jnp.concatenate([low, ds], axis=1))
-            for j in range(CHAINS):
-                product = dot(kvs[j], pairs[j], 0, 0)
-                acc[j, 0] += product[HEAD:, :FT]
-                acc[j, 1] += product[:HEAD, FT:]
-            dvs = [dot(lows[j], both[j, FT:, HEAD:]) for j in range(CHAINS)]
-            for i in range(CB):
-                for j in range(CHAINS):
-                    to = pl.multiple_of(lists[t * CHAINS + j, at[j] + i] * BLK, BLK)
-                    dva[j, pl.ds(to, BLK), :] += dvs[j][i * BLK:(i + 1) * BLK, :]
-            return 0
-
-        lax.fori_loop(0, most, chunk, 0)
-        for j in range(CHAINS):
-            f = t * CHAINS + j
-            at = pl.multiple_of(lax.rem(f, 4) * FT, FT)
-            for d, (o, a) in enumerate(zip((o0, o1, o2, o3), (a0, a1, a2, a3))):
-                @pl.when(f // 4 == d)
-                def _():
-                    o[pl.ds(at, FT), :] = acc[j, 0].T.astype(o.dtype)
-                    a[pl.ds(at, FT), :] = acc[j, 1].T.astype(a.dtype)
-
+                to = pl.multiple_of(lists[t * CHAINS + j, at[j] + i] * BLK, BLK)
+                dva[j, pl.ds(to, BLK), :] += dvs[j][i * BLK:(i + 1) * BLK, :]
         return 0
 
-    lax.fori_loop(0, 16 // CHAINS, frames, 0)
+    lax.fori_loop(0, most, chunk, 0)
+
+
+def put_slot(acc, a):
+    for j in range(CHAINS):
+        dq = acc[j, 1].T
+        high = dq.astype(bf16)
+        rows = slice(j * FT, (j + 1) * FT)
+        a[rows, :HEAD] = acc[j, 0].T.astype(a.dtype)
+        if a.dtype == bf16:
+            a[rows, HEAD:2 * HEAD] = high
+            a[rows, 2 * HEAD:] = (dq - high.astype(f32)).astype(bf16)
+        else:
+            a[rows, HEAD:] = dq
+
+
+def grads_kernel(lists, s0, s1, s2, s3, q0, q1, q2, q3, k0, k1, k2, k3,
+                 a0, a1, a2, a3, b0, b1, b2, b3, qgall, kvall, both, acc, dva, norm):
+    fill_all((q0, q1, q2, q3), qgall)
+    fill_all((k0, k1, k2, k3), kvall)
+    both[...] = jnp.zeros_like(both)
+    dva[...] = jnp.zeros_like(dva)
+    merge_stats([ref[...] for ref in (s0, s1, s2, s3)], norm)
+
+    def slot(t, _):
+        slot_grads(lists, t, qgall, kvall, both, acc, dva, norm)
+        for d, a in enumerate((a0, a1, a2, a3)):
+            pl.when(t == d)(lambda a=a: put_slot(acc, a))
+        return 0
+
+    lax.fori_loop(0, 4, slot, 0)
     for d, b in enumerate((b0, b1, b2, b3)):
         total = dva[0, d * 512:(d + 1) * 512, :]
         for j in range(1, CHAINS):
@@ -297,14 +313,14 @@
 
 
 def attention_grads(lists, stats, qgs, kvs):
-    wire = [f32, bf16, bf16, bf16] + [WIRE] * 8
+    outs = [(2 * HEAD, f32)] + [(3 * HEAD, bf16)] * 3 + [(HEAD, t) for t in (f32, WIRE, WIRE2, WIRE)]
+    keys = pltpu.VMEM((2048, 2 * HEAD), bf16)
     return pl.pallas_call(
         grads_kernel,
         in_specs=[SMEM] + [VMEM] * 12,
-        out_specs=[VMEM] * 12,
-        out_shape=[jax.ShapeDtypeStruct((512, HEAD), t) for t in wire],
-        scratch_shapes=[pltpu.VMEM((2048, 2 * HEAD), bf16), pltpu.VMEM((2048, 2 * HEAD), bf16),
-                        pltpu.VMEM((CHAINS, 2 * FT, 2 * HEAD), bf16),
+        out_specs=[VMEM] * 8,
+        out_shape=[jax.ShapeDtypeStruct((512, lanes), t) for lanes, t in outs],
+        scratch_shapes=[keys, keys, pltpu.VMEM((CHAINS, 2 * FT, 2 * HEAD), bf16),
                         pltpu.VMEM((CHAINS, 2, HEAD, FT), f32), pltpu.VMEM((CHAINS, 2048, HEAD), f32),
                         pltpu.VMEM((32, 128), f32)],
         compiler_params=PARAMS,
@@ -312,10 +328,16 @@
     )(lists, *stats, *qgs, *kvs)
 
 
-def finish_kernel(a0, a1, a2, a3, b0, b1, b2, b3, own, other, uq, uv, after,
-                  rg_keep, rg_send, up):
-    dq = (a0[...] + a1[...].astype(f32) + a2[...].astype(f32) + a3[...].astype(f32)).astype(bf16)
-    dv = (b0[...] + b1[...].astype(f32) + b2[...].astype(f32) + b3[...].astype(f32)).astype(bf16)
+def finish_kernel(b0, b1, b2, b3, a0, a1, a2, a3, own, other, uq, uv, after,
+                  o_keep, o_send, rg_keep, rg_send, up):
+    out, dq, dv = a0[:, :HEAD], a0[:, HEAD:], b0[...]
+    for a, b in ((a1, b1), (a2, b2), (a3, b3)):
+        out += a[:, :HEAD].astype(f32)
+        dq += a[:, HEAD:2 * HEAD].astype(f32) + a[:, 2 * HEAD:].astype(f32)
+        dv += b[...].astype(f32)
+    out, dq, dv = out.astype(bf16), dq.astype(bf16), dv.astype(bf16)
+    o_keep[...] = out[:256]
+    o_send[...] = out[256:]
     for c in range(2):
         @pl.when(lax.axis_index("c") == c)
         def _():
@@ -329,18 +351,19 @@
     up[:, HEAD:] = dot(own[:, RANK:], dv[:256], 0, 0) + dot(other[:, RANK:], dv[256:], 0, 0)
 
 
-def finish(a, b, own, other, uq, uv, after):
+def finish(b, a, own, other, uq, uv, after):
     return pl.pallas_call(
         finish_kernel,
         in_specs=[VMEM] * 12 + [ANY],
-        out_specs=[VMEM] * 3,
-        out_shape=[jax.ShapeDtypeStruct((r, 256), f32) for r in (256, 256, 128)],
+        out_specs=[VMEM] * 5,
+        out_shape=[jax.ShapeDtypeStruct((256, HEAD), bf16)] * 2
+        + [jax.ShapeDtypeStruct((r, 256), f32) for r in (256, 256, 128)],
         compiler_params=PARAMS,
         name="finish",
-    )(*a, *b, own, other, uq, uv, after)
-
-
-def down_kernel(act_t, own, r1, r2, r3, after, mine, theirs):
+    )(*b, *a, own, other, uq, uv, after)
+
+
+def down_kernel(act_t, own, r1, r2, r3, mine, theirs):
     rg = (own[...] + r1[...].astype(f32) + r2[...].astype(f32) + r3[...].astype(f32)).astype(bf16)
     rows = mine.shape[0]
     for c in range(2):
@@ -350,16 +373,16 @@
             theirs[...] = dot(act_t[(1 - c) * rows:(2 - c) * rows, :], rg)
 
 
-def down_terms(act_t, own, others, after):
+def down_terms(act_t, own, others):
     rows = act_t.shape[0] // 2
     return pl.pallas_call(
         down_kernel,
-        in_specs=[VMEM] * 5 + [ANY],
+        in_specs=[VMEM] * 5,
         out_specs=[VMEM] * 2,
         out_shape=[jax.ShapeDtypeStruct((rows, 256), f32)] * 2,
         compiler_params=PARAMS,
         name="down_terms",
-    )(act_t, own, *others, after)
+    )(act_t, own, *others)
 
 
 def pack_kernel(mine, theirs, up, out):
@@ -472,14 +495,12 @@
     act_t = half(act, z, act.shape[1] // 4).T
     stats = spread(row_stats(lists, qgs, kvs), "y")
     parts = attention_grads(lists, stats, qgs, kvs)
-    a = collect(parts[4:8], "y")
-    b = collect(parts[8:], "x")
-    o0, o1, o2, o3 = collect(parts[:4], "y")
-    o = (o0 + o1.astype(f32) + o2.astype(f32) + o3.astype(f32)).astype(bf16)
-    o_keep, o_other = o[:256], swap(o[256:])
-    rg_keep, rg_send, up = finish(a, b, rank, swap(rank), uq, uv, act_t)
+    a = collect(parts[:4], "y")
+    b = collect(parts[4:], "x")
+    o_keep, o_send, rg_keep, rg_send, up = finish(b, a, rank, swap(rank), uq, uv, act_t)
+    o_other = swap(o_send)
     rg = rg_keep + swap(rg_send)
-    mine, theirs = down_terms(act_t, rg, spread(rg.astype(bf16), "z")[1:], o)
+    mine, theirs = down_terms(act_t, rg, spread(rg.astype(bf16), "z")[1:])
     terms = lax.all_to_all(pack(mine, swap(theirs), up), ("x", "y"), 0, 0, tiled=True)
     wide = lax.all_to_all(total_for_all(terms, o_other), ("z", "x", "y"), 0, 0, tiled=True)
     att, down_q, up_q, down_v, up_v = emit(wide, swap(wide), o_keep, o_other)

time: 163 us -> 156 us (0.957)
  starting transfers between devices: 41 us -> 37 us
  Pallas kernels: 41.5 us -> 39.4 us
  waiting for transfers between devices: 44 us -> 45.8 us
    ppermute x9 -> x6, starting transfers between devices: 8.63 us -> 6.15 us  [collect(): lax.ppermute(parts[d], axis, ring(4, -d))]
    pallas_call x1, Pallas kernels: 1.84 us -> 0.03 us  [assemble(): pl.pallas_call(assemble_kernel, in_specs=[VMEM] * 2, out_specs=[VMEM] * 2...]
    ppermute x9 -> x6, waiting for transfers between devices: 13.8 us -> 13.6 us  [collect(): lax.ppermute(parts[d], axis, ring(4, -d))]
  transfers between devices with their start and end apart: 28 -> 25, of which waited for: 15 -> 15; matrix products, arithmetic and copies ran while one was open for 3% -> 2% of each run, Pallas kernels for 4% -> 12%
where the time goes in v6:
time: 156 us
  waiting for transfers between devices  45.8 us (29%)
  Pallas kernels  39.4 us (25%)
  starting transfers between devices  37 us (24%)
  blocking collectives  26.2 us (17%)
  local copies, waits for them, and re-layouts  6.47 us (4%)
    all_to_all x1, blocking collectives, local(): lax.all_to_all(total_for_all(terms, o_other), ('z', 'x', 'y'), 0, 0, tile...  26.2 us
    ppermute x12, starting transfers between devices, spread(): one, three, two = [lax.ppermute(a, axis, ring(4, d)) for d in (1, 3, 2)]  17.1 us
    ppermute x12, waiting for transfers between devices, spread(): one, three, two = [lax.ppermute(a, axis, ring(4, d)) for d in (1, 3, 2)]  16.4 us
    ppermute x6, waiting for transfers between devices, collect(): lax.ppermute(parts[d], axis, ring(4, -d))  13.6 us
    pallas_call x1, Pallas kernels, attention_grads(): pl.pallas_call(grads_kernel, in_specs=[SMEM] + [VMEM] * 12, out_specs=[VM...  12.9 us
    ppermute x6, starting transfers between devices, swap(): return lax.ppermute(a, 'c', ring(2, 1))  9.72 us
    pallas_call x1, Pallas kernels, project(): pl.pallas_call(proj_kernel, grid=(width // KT,), in_specs=[pl.BlockSpec((...  8.86 us
    ppermute x6, waiting for transfers between devices, swap(): return lax.ppermute(a, 'c', ring(2, 1))  8.2 us
  transfers between devices with their start and end apart: 25, of which 15 were waited for; matrix products, arithmetic and copies ran while one was open for 2% of the time, Pallas kernels for 12%

profile of v6, /device:TPU:1, one launch (start us, length us, event | category | flops | bytes accessed | tf_op | source)
XLA Modules:
  0.0 155.8 jit_solution(2661249156049743080)
XLA Ops:
  0.7 8.9 %project.1 = (bf16[256,512]{1,0:T(8,128)(2,1)}, bf16[256,512]{1,0:T(8,128)(2,1)}, bf16[256,256]{1,0:T(8,128)(2,1)}) custom-call(bf16[256,5120]{1,0:T(8,128)(2,1)} %act.1, bf16[5120,256]{1,0:T(8,128)(2,1)} %wq.1, bf16[5120,256]{1,0:T(8,128)(2,1)} %wk.1, bf16[5120,256]{1,0:T(8,128)(2,1)} %wv.1, bf16[5120,128]{1,0:T(8,128)(2,1)} %down_q.1, ...), custom_call_target="tpu_custom_call" | custom-call | flops 2684354560 | bytes 13107200 | tf_op jit(solution)/shard_map/project/pallas_call | solution.py:85
  9.5 1.5 collective-permute-start
  11.0 1.4 collective-permute-done.other
  12.4 0.9 copy-done.2
  13.4 2.9 %collective-permute-start.3 = (bf16[512,256]{1,0:T(8,128)(2,1)S(1)}, bf16[512,256]{1,0:T(8,128)(2,1)S(1)}, u32[]{:S(2)}, u32[]{:S(2)}) collective-permute-start(bf16[512,256]{1,0:T(8,128)(2,1)S(1)} %get-tuple-element.27.q0), channel_id=1, source_target_pairs={{0,24},{8,0},{16,8},{24,16},{1,25},{9,1},{17,9},{25,17},{2,26},{10... | collective-permute-start | bytes 786440 | tf_op jit(solution)/shard_map/ppermute | solution.py:476
  17.3 2.5 %collective-permute-start.6 = (bf16[512,256]{1,0:T(8,128)(2,1)S(1)}, bf16[512,256]{1,0:T(8,128)(2,1)S(1)}, u32[]{:S(2)}, u32[]{:S(2)}) collective-permute-start(bf16[512,256]{1,0:T(8,128)(2,1)S(1)} %get-tuple-element.28.k0), channel_id=1, source_target_pairs={{0,96},{32,0},{64,32},{96,64},{1,97},{33,1},{65,33},{97,65},{2,98}... | collective-permute-start | bytes 786440 | tf_op jit(solution)/shard_map/ppermute | solution.py:476
  20.3 6.8 %collective-permute-done.3.q3 = bf16[512,256]{1,0:T(8,128)(2,1)S(1)} collective-permute-done((bf16[512,256]{1,0:T(8,128)(2,1)S(1)}, bf16[512,256]{1,0:T(8,128)(2,1)S(1)}, u32[]{:S(2)}, u32[]{:S(2)}) %collective-permute-start.3) | collective-permute-done | bytes 262176 | tf_op jit(solution)/shard_map/ppermute | solution.py:476
  27.0 1.2 collective-permute-start.4
  28.5 6.0 %lists.1 = s32[24,128]{1,0:T(8,128)S(1)} custom-call(s32[64]{0:T(128)S(1)} %copy-done.8, s32[64,64]{1,0:T(8,128)S(1)} %multiply_add_fusion.packed), custom_call_target="tpu_custom_call" | custom-call | tf_op jit(solution)/shard_map/lists/pallas_call | solution.py:148
  34.7 6.6 %row_stats.1.s0 = f32[48,128]{1,0:T(8,128)S(1)} custom-call(s32[24,128]{1,0:T(8,128)S(1)} %lists.1, bf16[512,256]{1,0:T(8,128)(2,1)S(1)} %get-tuple-element.27.q0, bf16[512,256]{1,0:T(8,128)(2,1)S(1)} %collective-permute-done.1.q1, bf16[512,256]{1,0:T(8,128)(2,1)S(1)} %collective-permute-done.2.q2, bf16[512,256]{1,0:T(8,128)(2,1)S(1)} %collective-permute-done.3.q3, ...), custom_call_target="tpu_custom_call" | custom-call | tf_op jit(solution)/shard_map/row_stats/pallas_call | solution.py:220
  41.3 3.8 %collective-permute-start.9 = (f32[48,128]{1,0:T(8,128)S(1)}, f32[48,128]{1,0:T(8,128)S(1)}, u32[]{:S(2)}, u32[]{:S(2)}) collective-permute-start(f32[48,128]{1,0:T(8,128)S(1)} %row_stats.1.s0), channel_id=1, source_target_pairs={{0,24},{8,0},{16,8},{24,16},{1,25},{9,1},{17,9},{25,17},{2,26},{10... | collective-permute-start | bytes 73736 | tf_op jit(solution)/shard_map/ppermute | solution.py:476
  45.8 2.7 %collective-permute-start.16 = (bf16[256,256]{1,0:T(8,128)(2,1)S(1)}, bf16[256,256]{1,0:T(8,128)(2,1)S(1)}, u32[]{:S(2)}, u32[]{:S(2)}) collective-permute-start(bf16[256,256]{1,0:T(8,128)(2,1)S(1)} %copy-done.3), channel_id=1, source_target_pairs={{0,4},{4,0},{1,5},{5,1},{2,6},{6,2},{3,7},{7,3},{8,12},{12,8},{9,1... | collective-permute-start | bytes 393224 | tf_op jit(solution)/shard_map/ppermute | solution.py:472
  49.4 12.9 %attention_grads.1 = (f32[512,256]{1,0:T(8,128)S(1)}, bf16[512,384]{1,0:T(8,128)(2,1)}, bf16[512,384]{1,0:T(8,128)(2,1)}, bf16[512,384]{1,0:T(8,128)(2,1)}, f32[...) custom-call(s32[24,128]{1,0:T(8,128)S(1)} %lists.1, ...), custom_call_target="tpu_custom_call" | custom-call | tf_op jit(solution)/shard_map/attention_grads/pallas_call | solution.py:318
  62.3 2.0 %collective-permute-start.11 = (bf16[512,128]{1,0:T(8,128)(2,1)S(1)}, bf16[512,128]{1,0:T(8,128)(2,1)S(1)}, u32[]{:S(2)}, u32[]{:S(2)}) collective-permute-start(bf16[512,128]{1,0:T(8,128)(2,1)S(1)} %get-tuple-element.31), channel_id=1, source_target_pairs={{0,64},{32,96},{64,0},{96,32},{1,65},{33,97},{65,1},{97,33},{2,66}... | collective-permute-start | bytes 393224 | tf_op jit(solution)/shard_map/ppermute | solution.py:481
  65.0 2.0 %collective-permute-start.14 = (bf16[512,384]{1,0:T(8,128)(2,1)}, bf16[512,384]{1,0:T(8,128)(2,1)S(1)}, u32[]{:S(2)}, u32[]{:S(2)}) collective-permute-start(bf16[512,384]{1,0:T(8,128)(2,1)} %get-tuple-element.35), channel_id=1, source_target_pairs={{0,16},{8,24},{16,0},{24,8},{1,17},{9,25},{17,1},{25,9},{2,18},{10... | collective-permute-start | bytes 1179656 | tf_op jit(solution)/shard_map/ppermute | solution.py:481
  67.0 1.1 collective-permute-start.10
  69.1 2.0 %constant_dynamic-slice_fusion = bf16[256,1280]{1,0:T(8,128)(2,1)} fusion(bf16[256,5120]{1,0:T(8,128)(2,1)} %act.1, s32[]{:T(128)S(6)} %select_n.3), kind=kLoop, calls=%fused_computation.2 | loop fusion | bytes 1310724 | tf_op jit(solution)/shard_map/dynamic_slice | solution.py:485
  71.1 1.3 copy.19
  72.4 1.1 collective-permute-done.10.b1
  73.5 2.2 %collective-permute-done.12.b3 = f32[512,128]{1,0:T(8,128)S(1)} collective-permute-done((f32[512,128]{1,0:T(8,128)}, f32[512,128]{1,0:T(8,128)S(1)}, u32[]{:S(2)}, u32[]{:S(2)}) %collective-permute-start.12) | collective-permute-done | bytes 262176 | tf_op jit(solution)/shard_map/ppermute | solution.py:481
  75.7 10.3 %collective-permute-done.15.a3 = bf16[512,384]{1,0:T(8,128)(2,1)S(1)} collective-permute-done((bf16[512,384]{1,0:T(8,128)(2,1)}, bf16[512,384]{1,0:T(8,128)(2,1)S(1)}, u32[]{:S(2)}, u32[]{:S(2)}) %collective-permute-start.15) | collective-permute-done | bytes 393248 | tf_op jit(solution)/shard_map/ppermute | solution.py:481
  89.0 1.2 collective-permute-done.17
  90.2 3.8 %collective-permute-start.20 = (bf16[256,256]{1,0:T(8,128)(2,1)S(1)}, bf16[256,256]{1,0:T(8,128)(2,1)S(1)}, u32[]{:S(2)}, u32[]{:S(2)}) collective-permute-start(bf16[256,256]{1,0:T(8,128)(2,1)S(1)} %get-tuple-element.45), channel_id=1, source_target_pairs={{0,3},{1,0},{2,1},{3,2},{4,7},{5,4},{6,5},{7,6},{8,11},{9,8},{10,9... | collective-permute-start | bytes 393224 | tf_op jit(solution)/shard_map/ppermute | solution.py:476
  94.7 5.0 %collective-permute-done.20.r3 = bf16[256,256]{1,0:T(8,128)(2,1)S(1)} collective-permute-done((bf16[256,256]{1,0:T(8,128)(2,1)S(1)}, bf16[256,256]{1,0:T(8,128)(2,1)S(1)}, u32[]{:S(2)}, u32[]{:S(2)}) %collective-permute-start.20) | collective-permute-done | bytes 131104 | tf_op jit(solution)/shard_map/ppermute | solution.py:476
  100.0 3.2 %collective-permute-done.18.r1 = bf16[256,256]{1,0:T(8,128)(2,1)S(1)} collective-permute-done((bf16[256,256]{1,0:T(8,128)(2,1)S(1)}, bf16[256,256]{1,0:T(8,128)(2,1)S(1)}, u32[]{:S(2)}, u32[]{:S(2)}) %collective-permute-start.18) | collective-permute-done | bytes 131104 | tf_op jit(solution)/shard_map/ppermute | solution.py:476
  104.5 1.7 %collective-permute-done.21.theirs = f32[640,256]{1,0:T(8,128)S(1)} collective-permute-done((f32[640,256]{1,0:T(8,128)S(1)}, f32[640,256]{1,0:T(8,128)S(1)}, u32[]{:S(2)}, u32[]{:S(2)}) %collective-permute-start.21) | collective-permute-done | bytes 655392 | tf_op jit(solution)/shard_map/ppermute | solution.py:472
  107.0 4.0 %all-to-all-start = ((bf16[16,48,256]{2,1,0:T(8,128)(2,1)}), bf16[16,48,256]{2,1,0:T(8,128)(2,1)S(1)}, u32[]{:S(2)}, u32[]{:S(2)}) async-start(bf16[16,48,256]{2,1,0:T(8,128)(2,1)} %pack.1), calls=%async_computation | async-start | bytes 786432 | tf_op jit(solution)/shard_map/all_to_all | solution.py:504
  112.7 7.6 %all-to-all-done.parts = bf16[16,48,256]{2,1,0:T(8,128)(2,1)S(1)} async-done(((bf16[16,48,256]{2,1,0:T(8,128)(2,1)}), bf16[16,48,256]{2,1,0:T(8,128)(2,1)S(1)}, u32[]{:S(2)}, u32[]{:S(2)}) %all-to-all-start) | async-done | bytes 393248 | tf_op jit(solution)/shard_map/all_to_all | solution.py:504
  120.4 26.2 %all_to_all.10.own = bf16[64,48,256]{2,1,0:T(8,128)(2,1)S(1)} all-to-all(bf16[64,48,256]{2,1,0:T(8,128)(2,1)S(1)} %total_for_all.1), channel_id=1, replica_groups=mesh['x'=4,'y'=4,'c'=2,'z'=4] {'z','x','y'}, dimensions={0} | all-to-all | bytes 3145728 | tf_op jit(solution)/shard_map/all_to_all | solution.py:505
  146.6 3.4 %collective-permute-start.23 = (bf16[64,48,256]{2,1,0:T(8,128)(2,1)S(1)}, bf16[64,48,256]{2,1,0:T(8,128)(2,1)S(1)}, u32[]{:S(2)}, u32[]{:S(2)}) collective-permute-start(bf16[64,48,256]{2,1,0:T(8,128)(2,1)S(1)} %all_to_all.10.own), channel_id=1, source_target_pairs={{0,4},{4,0},{1,5},{5,1},{2,6},{6,2},{3,7},{7,3},{8,12},{12,8},{9,1... | collective-permute-start | bytes 4718600 | tf_op jit(solution)/shard_map/ppermute | solution.py:472
  150.0 3.0 %collective-permute-done.23.other = bf16[64,48,256]{2,1,0:T(8,128)(2,1)S(1)} collective-permute-done((bf16[64,48,256]{2,1,0:T(8,128)(2,1)S(1)}, bf16[64,48,256]{2,1,0:T(8,128)(2,1)S(1)}, u32[]{:S(2)}, u32[]{:S(2)}) %collective-permute-start.23) | collective-permute-done | bytes 1572896 | tf_op jit(solution)/shard_map/ppermute | solution.py:472
  153.0 2.8 %emit.1 = (bf16[256,256]{1,0:T(8,128)(2,1)}, f32[5120,128]{1,0:T(8,128)}, f32[128,256]{1,0:T(8,128)}, f32[5120,128]{1,0:T(8,128)}, f32[128,256]{1,0:T(8,128)}) custom-call(bf16[64,48,256]{2,1,0:T(8,128)(2,1)S(1)} %all_to_all.10.own, bf16[64,48,256]{2,1,0:T(8,128)(2,1)S(1)} %collective-permute-done.23.other, bf16[256,128]{1,0:T(8,128)(2,1)S(1)} %copy-done.7, ...), custom_call_target="tpu_custom_call" | custom-call | tf_op jit(solution)/shard_map/emit/pallas_call | solution.py:433
  (62 shorter events, 13.1 us)
Async XLA Ops:
  0.6 27.6 %copy-start.13 = (s32[4]{0:T(128)S(1)}, s32[4]{0:T(128)}, u32[]{:S(2)}) copy-start(s32[4]{0:T(128)} %constant.14.clone) | copy-start | bytes 52
  0.7 27.8 %copy-start.12 = (s32[64,64]{1,0:T(8,128)S(1)}, s32[64,64]{1,0:T(8,128)}, u32[]{:S(2)}) copy-start(s32[64,64]{1,0:T(8,128)} %param.22) | copy-start | bytes 49156
  0.7 27.8 %copy-start.8 = (s32[64]{0:T(128)S(1)}, s32[64]{0:T(128)}, u32[]{:S(2)}) copy-start(s32[64]{0:T(128)} %slot.1) | copy-start | bytes 772
  9.5 2.8 %collective-permute-start = (bf16[256,512]{1,0:T(8,128)(2,1)}, bf16[256,512]{1,0:T(8,128)(2,1)S(1)}, u32[]{:S(2)}, u32[]{:S(2)}) collective-permute-start(bf16[256,512]{1,0:T(8,128)(2,1)} %get-tuple-element.26), channel_id=1, source_target_pairs={{0,4},{4,0},{1,5},{5,1},{2,6},{6,2},{3,7},{7,3},{8,12},{12,8},{9,1... | collective-permute-start | bytes 786440 | tf_op jit(solution)/shard_map/ppermute | solution.py:472
  13.3 32.5 %copy-start.3 = (bf16[256,256]{1,0:T(8,128)(2,1)S(1)}, bf16[256,256]{1,0:T(8,128)(2,1)}, u32[]{:S(2)}) copy-start(bf16[256,256]{1,0:T(8,128)(2,1)} %get-tuple-element.37.own) | copy-start | bytes 393220
  13.4 13.7 %collective-permute-start.3 = (bf16[512,256]{1,0:T(8,128)(2,1)S(1)}, bf16[512,256]{1,0:T(8,128)(2,1)S(1)}, u32[]{:S(2)}, u32[]{:S(2)}) collective-permute-start(bf16[512,256]{1,0:T(8,128)(2,1)S(1)} %get-tuple-element.27.q0), channel_id=1, source_target_pairs={{0,24},{8,0},{16,8},{24,16},{1,25},{9,1},{17,9},{25,17},{2,26},{10... | collective-permute-start | bytes 786440 | tf_op jit(solution)/shard_map/ppermute | solution.py:476
  16.3 18.2 %collective-permute-start.2 = (bf16[512,256]{1,0:T(8,128)(2,1)S(1)}, bf16[512,256]{1,0:T(8,128)(2,1)S(1)}, u32[]{:S(2)}, u32[]{:S(2)}) collective-permute-start(bf16[512,256]{1,0:T(8,128)(2,1)S(1)} %get-tuple-element.27.q0), channel_id=1, source_target_pairs={{0,16},{8,24},{16,0},{24,8},{1,17},{9,25},{17,1},{25,9},{2,18},{10... | collective-permute-start | bytes 786440 | tf_op jit(solution)/shard_map/ppermute | solution.py:476
  16.6 17.9 %collective-permute-start.1 = (bf16[512,256]{1,0:T(8,128)(2,1)S(1)}, bf16[512,256]{1,0:T(8,128)(2,1)S(1)}, u32[]{:S(2)}, u32[]{:S(2)}) collective-permute-start(bf16[512,256]{1,0:T(8,128)(2,1)S(1)} %get-tuple-element.27.q0), channel_id=1, source_target_pairs={{0,8},{8,16},{16,24},{24,0},{1,9},{9,17},{17,25},{25,1},{2,10},{10... | collective-permute-start | bytes 786440 | tf_op jit(solution)/shard_map/ppermute | solution.py:476
  17.3 17.2 %collective-permute-start.6 = (bf16[512,256]{1,0:T(8,128)(2,1)S(1)}, bf16[512,256]{1,0:T(8,128)(2,1)S(1)}, u32[]{:S(2)}, u32[]{:S(2)}) collective-permute-start(bf16[512,256]{1,0:T(8,128)(2,1)S(1)} %get-tuple-element.28.k0), channel_id=1, source_target_pairs={{0,96},{32,0},{64,32},{96,64},{1,97},{33,1},{65,33},{97,65},{2,98}... | collective-permute-start | bytes 786440 | tf_op jit(solution)/shard_map/ppermute | solution.py:476
  19.8 14.7 %collective-permute-start.5 = (bf16[512,256]{1,0:T(8,128)(2,1)S(1)}, bf16[512,256]{1,0:T(8,128)(2,1)S(1)}, u32[]{:S(2)}, u32[]{:S(2)}) collective-permute-start(bf16[512,256]{1,0:T(8,128)(2,1)S(1)} %get-tuple-element.28.k0), channel_id=1, source_target_pairs={{0,64},{32,96},{64,0},{96,32},{1,65},{33,97},{65,1},{97,33},{2,66}... | collective-permute-start | bytes 786440 | tf_op jit(solution)/shard_map/ppermute | solution.py:476
  27.0 7.7 %collective-permute-start.4 = (bf16[512,256]{1,0:T(8,128)(2,1)S(1)}, bf16[512,256]{1,0:T(8,128)(2,1)S(1)}, u32[]{:S(2)}, u32[]{:S(2)}) collective-permute-start(bf16[512,256]{1,0:T(8,128)(2,1)S(1)} %get-tuple-element.28.k0), channel_id=1, source_target_pairs={{0,32},{32,64},{64,96},{96,0},{1,33},{33,65},{65,97},{97,1},{2,34}... | collective-permute-start | bytes 786440 | tf_op jit(solution)/shard_map/ppermute | solution.py:476
  41.3 44.7 %copy-start = (bf16[128,256]{1,0:T(8,128)(2,1)S(1)}, bf16[128,256]{1,0:T(8,128)(2,1)}, u32[]{:S(2)}) copy-start(bf16[128,256]{1,0:T(8,128)(2,1)} %uq.1) | copy-start | bytes 196612
  41.3 44.7 %copy-start.1 = (bf16[128,256]{1,0:T(8,128)(2,1)S(1)}, bf16[128,256]{1,0:T(8,128)(2,1)}, u32[]{:S(2)}) copy-start(bf16[128,256]{1,0:T(8,128)(2,1)} %uv.1) | copy-start | bytes 196612
  41.3 7.1 %collective-permute-start.9 = (f32[48,128]{1,0:T(8,128)S(1)}, f32[48,128]{1,0:T(8,128)S(1)}, u32[]{:S(2)}, u32[]{:S(2)}) collective-permute-start(f32[48,128]{1,0:T(8,128)S(1)} %row_stats.1.s0), channel_id=1, source_target_pairs={{0,24},{8,0},{16,8},{24,16},{1,25},{9,1},{17,9},{25,17},{2,26},{10... | collective-permute-start | bytes 73736 | tf_op jit(solution)/shard_map/ppermute | solution.py:476
  45.1 4.3 %collective-permute-start.8 = (f32[48,128]{1,0:T(8,128)S(1)}, f32[48,128]{1,0:T(8,128)S(1)}, u32[]{:S(2)}, u32[]{:S(2)}) collective-permute-start(f32[48,128]{1,0:T(8,128)S(1)} %row_stats.1.s0), channel_id=1, source_target_pairs={{0,16},{8,24},{16,0},{24,8},{1,17},{9,25},{17,1},{25,9},{2,18},{10... | collective-permute-start | bytes 73736 | tf_op jit(solution)/shard_map/ppermute | solution.py:476
  45.2 4.2 %collective-permute-start.7 = (f32[48,128]{1,0:T(8,128)S(1)}, f32[48,128]{1,0:T(8,128)S(1)}, u32[]{:S(2)}, u32[]{:S(2)}) collective-permute-start(f32[48,128]{1,0:T(8,128)S(1)} %row_stats.1.s0), channel_id=1, source_target_pairs={{0,8},{8,16},{16,24},{24,0},{1,9},{9,17},{17,25},{25,1},{2,10},{10... | collective-permute-start | bytes 73736 | tf_op jit(solution)/shard_map/ppermute | solution.py:476
  45.8 21.2 %collective-permute-start.16 = (bf16[256,256]{1,0:T(8,128)(2,1)S(1)}, bf16[256,256]{1,0:T(8,128)(2,1)S(1)}, u32[]{:S(2)}, u32[]{:S(2)}) collective-permute-start(bf16[256,256]{1,0:T(8,128)(2,1)S(1)} %copy-done.3), channel_id=1, source_target_pairs={{0,4},{4,0},{1,5},{5,1},{2,6},{6,2},{3,7},{7,3},{8,12},{12,8},{9,1... | collective-permute-start | bytes 393224 | tf_op jit(solution)/shard_map/ppermute | solution.py:472
  62.3 5.8 %collective-permute-start.11 = (bf16[512,128]{1,0:T(8,128)(2,1)S(1)}, bf16[512,128]{1,0:T(8,128)(2,1)S(1)}, u32[]{:S(2)}, u32[]{:S(2)}) collective-permute-start(bf16[512,128]{1,0:T(8,128)(2,1)S(1)} %get-tuple-element.31), channel_id=1, source_target_pairs={{0,64},{32,96},{64,0},{96,32},{1,65},{33,97},{65,1},{97,33},{2,66}... | collective-permute-start | bytes 393224 | tf_op jit(solution)/shard_map/ppermute | solution.py:481
  64.3 11.4 %collective-permute-start.13 = (bf16[512,384]{1,0:T(8,128)(2,1)}, bf16[512,384]{1,0:T(8,128)(2,1)S(1)}, u32[]{:S(2)}, u32[]{:S(2)}) collective-permute-start(bf16[512,384]{1,0:T(8,128)(2,1)} %get-tuple-element.34), channel_id=1, source_target_pairs={{0,24},{8,0},{16,8},{24,16},{1,25},{9,1},{17,9},{25,17},{2,26},{10... | collective-permute-start | bytes 1179656 | tf_op jit(solution)/shard_map/ppermute | solution.py:481
  65.0 10.7 %collective-permute-start.14 = (bf16[512,384]{1,0:T(8,128)(2,1)}, bf16[512,384]{1,0:T(8,128)(2,1)S(1)}, u32[]{:S(2)}, u32[]{:S(2)}) collective-permute-start(bf16[512,384]{1,0:T(8,128)(2,1)} %get-tuple-element.35), channel_id=1, source_target_pairs={{0,16},{8,24},{16,0},{24,8},{1,17},{9,25},{17,1},{25,9},{2,18},{10... | collective-permute-start | bytes 1179656 | tf_op jit(solution)/shard_map/ppermute | solution.py:481
  67.0 19.0 %collective-permute-start.15 = (bf16[512,384]{1,0:T(8,128)(2,1)}, bf16[512,384]{1,0:T(8,128)(2,1)S(1)}, u32[]{:S(2)}, u32[]{:S(2)}) collective-permute-start(bf16[512,384]{1,0:T(8,128)(2,1)} %get-tuple-element.36), channel_id=1, source_target_pairs={{0,8},{8,16},{16,24},{24,0},{1,9},{9,17},{17,25},{25,1},{2,10},{10... | collective-permute-start | bytes 1179656 | tf_op jit(solution)/shard_map/ppermute | solution.py:481
  67.0 6.5 %collective-permute-start.10 = (f32[512,128]{1,0:T(8,128)}, f32[512,128]{1,0:T(8,128)S(1)}, u32[]{:S(2)}, u32[]{:S(2)}) collective-permute-start(f32[512,128]{1,0:T(8,128)} %get-tuple-element.30), channel_id=1, source_target_pairs={{0,96},{32,0},{64,32},{96,64},{1,97},{33,1},{65,33},{97,65},{2,98}... | collective-permute-start | bytes 786440 | tf_op jit(solution)/shard_map/ppermute | solution.py:481
  68.8 6.9 %collective-permute-start.12 = (f32[512,128]{1,0:T(8,128)}, f32[512,128]{1,0:T(8,128)S(1)}, u32[]{:S(2)}, u32[]{:S(2)}) collective-permute-start(f32[512,128]{1,0:T(8,128)} %get-tuple-element.32), channel_id=1, source_target_pairs={{0,32},{32,64},{64,96},{96,0},{1,33},{33,65},{65,97},{97,1},{2,34}... | collective-permute-start | bytes 786440 | tf_op jit(solution)/shard_map/ppermute | solution.py:481
  88.4 1.7 %collective-permute-start.17 = (f32[256,256]{1,0:T(8,128)S(1)}, f32[256,256]{1,0:T(8,128)S(1)}, u32[]{:S(2)}, u32[]{:S(2)}) collective-permute-start(f32[256,256]{1,0:T(8,128)S(1)} %get-tuple-element.39), channel_id=1, source_target_pairs={{0,4},{4,0},{1,5},{5,1},{2,6},{6,2},{3,7},{7,3},{8,12},{12,8},{9,1... | collective-permute-start | bytes 786440 | tf_op jit(solution)/shard_map/ppermute | solution.py:472
  90.2 9.5 %collective-permute-start.20 = (bf16[256,256]{1,0:T(8,128)(2,1)S(1)}, bf16[256,256]{1,0:T(8,128)(2,1)S(1)}, u32[]{:S(2)}, u32[]{:S(2)}) collective-permute-start(bf16[256,256]{1,0:T(8,128)(2,1)S(1)} %get-tuple-element.45), channel_id=1, source_target_pairs={{0,3},{1,0},{2,1},{3,2},{4,7},{5,4},{6,5},{7,6},{8,11},{9,8},{10,9... | collective-permute-start | bytes 393224 | tf_op jit(solution)/shard_map/ppermute | solution.py:476
  94.0 6.0 %collective-permute-start.19 = (bf16[256,256]{1,0:T(8,128)(2,1)S(1)}, bf16[256,256]{1,0:T(8,128)(2,1)S(1)}, u32[]{:S(2)}, u32[]{:S(2)}) collective-permute-start(bf16[256,256]{1,0:T(8,128)(2,1)S(1)} %get-tuple-element.45), channel_id=1, source_target_pairs={{0,2},{1,3},{2,0},{3,1},{4,6},{5,7},{6,4},{7,5},{8,10},{9,11},{10,... | collective-permute-start | bytes 393224 | tf_op jit(solution)/shard_map/ppermute | solution.py:476
  94.0 9.1 %collective-permute-start.18 = (bf16[256,256]{1,0:T(8,128)(2,1)S(1)}, bf16[256,256]{1,0:T(8,128)(2,1)S(1)}, u32[]{:S(2)}, u32[]{:S(2)}) collective-permute-start(bf16[256,256]{1,0:T(8,128)(2,1)S(1)} %get-tuple-element.45), channel_id=1, source_target_pairs={{0,1},{1,2},{2,3},{3,0},{4,5},{5,6},{6,7},{7,4},{8,9},{9,10},{10,1... | collective-permute-start | bytes 393224 | tf_op jit(solution)/shard_map/ppermute | solution.py:476
  103.6 2.6 %collective-permute-start.21 = (f32[640,256]{1,0:T(8,128)S(1)}, f32[640,256]{1,0:T(8,128)S(1)}, u32[]{:S(2)}, u32[]{:S(2)}) collective-permute-start(f32[640,256]{1,0:T(8,128)S(1)} %get-tuple-element.41), channel_id=1, source_target_pairs={{0,4},{4,0},{1,5},{5,1},{2,6},{6,2},{3,7},{7,3},{8,12},{12,8},{9,1... | collective-permute-start | bytes 1966088 | tf_op jit(solution)/shard_map/ppermute | solution.py:472
  107.0 13.2 %all-to-all-start = ((bf16[16,48,256]{2,1,0:T(8,128)(2,1)}), bf16[16,48,256]{2,1,0:T(8,128)(2,1)S(1)}, u32[]{:S(2)}, u32[]{:S(2)}) async-start(bf16[16,48,256]{2,1,0:T(8,128)(2,1)} %pack.1), calls=%async_computation | async-start | bytes 786432 | tf_op jit(solution)/shard_map/all_to_all | solution.py:504
  111.0 42.0 %copy-start.7 = (bf16[256,128]{1,0:T(8,128)(2,1)S(1)}, bf16[256,128]{1,0:T(8,128)(2,1)}, u32[]{:S(2)}) copy-start(bf16[256,128]{1,0:T(8,128)(2,1)} %copy-done.6) | copy-start | bytes 196612
  111.0 1.6 %collective-permute-start.22 = (bf16[256,128]{1,0:T(8,128)(2,1)S(1)}, bf16[256,128]{1,0:T(8,128)(2,1)S(1)}, u32[]{:S(2)}, u32[]{:S(2)}) collective-permute-start(bf16[256,128]{1,0:T(8,128)(2,1)S(1)} %copy-done.10), channel_id=1, source_target_pairs={{0,4},{4,0},{1,5},{5,1},{2,6},{6,2},{3,7},{7,3},{8,12},{12,8},{9,1... | collective-permute-start | bytes 196616 | tf_op jit(solution)/shard_map/ppermute | solution.py:472
  146.6 6.4 %collective-permute-start.23 = (bf16[64,48,256]{2,1,0:T(8,128)(2,1)S(1)}, bf16[64,48,256]{2,1,0:T(8,128)(2,1)S(1)}, u32[]{:S(2)}, u32[]{:S(2)}) collective-permute-start(bf16[64,48,256]{2,1,0:T(8,128)(2,1)S(1)} %all_to_all.10.own), channel_id=1, source_target_pairs={{0,4},{4,0},{1,5},{5,1},{2,6},{6,2},{3,7},{7,3},{8,12},{12,8},{9,1... | collective-permute-start | bytes 4718600 | tf_op jit(solution)/shard_map/ppermute | solution.py:472
  (7 other events, 49.5 us)

commit v7 on v6

--- a/solution.py
+++ b/solution.py
@@ -15,6 +15,7 @@
 CHUNK = 512
 CB = CHUNK // BLK
 CHAINS = 4
+STAT_CHAINS = 8
 SCALE = HEAD ** -0.5
 SCALE2 = SCALE * math.log2(math.e)
 NEG = -1e30
@@ -167,9 +168,10 @@
 
 
 def start_frames(lists, t, qgall, both):
+    chains = both.shape[0]
     counts = []
-    for j in range(CHAINS):
-        f = t * CHAINS + j
+    for j in range(chains):
+        f = t * chains + j
         at = pl.multiple_of(f * FT, FT)
         both[j, :FT, :HEAD] = qgall[pl.ds(at, FT), :HEAD]
         both[j, FT:, HEAD:] = qgall[pl.ds(at, FT), HEAD:]
@@ -191,11 +193,11 @@
         counts, chunks, most = start_frames(lists, t, qgall, both)
 
         def chunk(ch, carry):
-            kvs = [load_chunk(lists, t * CHAINS + j, jnp.minimum(ch, chunks[j] - 1) * CB, kvall)
-                   for j in range(CHAINS)]
-            rs = [dot(kvs[j], both[j], 1, 1) for j in range(CHAINS)]
+            kvs = [load_chunk(lists, t * STAT_CHAINS + j, jnp.minimum(ch, chunks[j] - 1) * CB, kvall)
+                   for j in range(STAT_CHAINS)]
+            rs = [dot(kvs[j], both[j], 1, 1) for j in range(STAT_CHAINS)]
             after = []
-            for j in range(CHAINS):
+            for j in range(STAT_CHAINS):
                 peak, total, delta = carry[j]
                 s = jnp.where(row < (counts[j] - ch * CB) * BLK, rs[j][:, :FT] * SCALE2, NEG)
                 new = jnp.maximum(peak, jnp.max(s, axis=0, keepdims=True))
@@ -207,13 +209,13 @@
             return tuple(after)
 
         zero = jnp.zeros((1, FT), f32)
-        carry = lax.fori_loop(0, most, chunk, ((zero + NEG, zero, zero),) * CHAINS)
-        for j in range(CHAINS):
+        carry = lax.fori_loop(0, most, chunk, ((zero + NEG, zero, zero),) * STAT_CHAINS)
+        for j in range(STAT_CHAINS):
             for i in range(3):
-                out[pl.ds(16 * i + t * CHAINS + j, 1), :] = carry[j][i]
+                out[pl.ds(16 * i + t * STAT_CHAINS + j, 1), :] = carry[j][i]
         return 0
 
-    lax.fori_loop(0, 16 // CHAINS, frames, 0)
+    lax.fori_loop(0, 16 // STAT_CHAINS, frames, 0)
 
 
 def row_stats(lists, qgs, kvs):
@@ -223,7 +225,7 @@
         out_specs=VMEM,
         out_shape=jax.ShapeDtypeStruct((48, 128), f32),
         scratch_shapes=[pltpu.VMEM((2048, 2 * HEAD), bf16), pltpu.VMEM((2048, 2 * HEAD), bf16),
-                        pltpu.VMEM((CHAINS, 2 * FT, 2 * HEAD), bf16)],
+                        pltpu.VMEM((STAT_CHAINS, 2 * FT, 2 * HEAD), bf16)],
         compiler_params=PARAMS,
         name="row_stats",
     )(lists, *qgs, *kvs)
@@ -363,6 +365,50 @@
     )(*b, *a, own, other, uq, uv, after)
 
 
+def columns_kernel(act, out, rows, sem):
+    width = rows.shape[1]
+    at = pl.multiple_of(lax.axis_index("z") * width, 128)
+    copy = pltpu.make_async_copy(act.at[:, pl.ds(at, width)], rows, sem)
+    copy.start()
+    copy.wait()
+    for i in range(width // 256):
+        out[i * 256:(i + 1) * 256, :] = rows[:, i * 256:(i + 1) * 256].T
+
+
+def columns(act, after):
+    rows, width = act.shape[0], act.shape[1] // 4
+
+    def kernel(act, after, out, part, sem):
+        columns_kernel(act, out, part, sem)
+
+    return pl.pallas_call(
+        kernel,
+        in_specs=[ANY, ANY],
+        out_specs=VMEM,
+        out_shape=jax.ShapeDtypeStruct((width, rows), bf16),
+        scratch_shapes=[pltpu.VMEM((rows, width), bf16), pltpu.SemaphoreType.DMA(())],
+        compiler_params=PARAMS,
+        name="columns",
+    )(act, after)
+
+
+def cores_kernel(keep, other, total, low):
+    rg = keep[...] + other[...]
+    total[...] = rg
+    low[...] = rg.astype(bf16)
+
+
+def add_cores(keep, other):
+    return pl.pallas_call(
+        cores_kernel,
+        in_specs=[VMEM] * 2,
+        out_specs=[VMEM] * 2,
+        out_shape=[jax.ShapeDtypeStruct((256, 256), t) for t in (f32, bf16)],
+        compiler_params=PARAMS,
+        name="add_cores",
+    )(keep, other)
+
+
 def down_kernel(act_t, own, r1, r2, r3, mine, theirs):
     rg = (own[...] + r1[...].astype(f32) + r2[...].astype(f32) + r3[...].astype(f32)).astype(bf16)
     rows = mine.shape[0]
@@ -477,30 +523,30 @@
     return [a, one, two, three]
 
 
+def relay(a, axis):
+    one, three = [lax.ppermute(a, axis, ring(4, d)) for d in (1, 3)]
+    return [a, one, lax.ppermute(one, axis, ring(4, 1)), three]
+
+
 def collect(parts, axis):
     return [parts[0]] + [lax.ppermute(parts[d], axis, ring(4, -d)) for d in (1, 2, 3)]
 
 
-def half(a, index, size):
-    return lax.dynamic_slice_in_dim(a, index * size, size, axis=1)
-
-
 def local(act, wq, wk, wv, dq, uq, dv, uv, grad_out, levels, order, slot):
-    z = lax.axis_index("z")
     keep, send, rank = project(act, wq, wk, wv, dq, dv, uq, uv, grad_out)
     kv, qg = assemble(keep, swap(send))
-    kvs = spread(kv, "x")
-    qgs = spread(qg, "y")
+    kvs = relay(kv, "x")
+    qgs = relay(qg, "y")
     lists = visible_lists(slot, levels, order)
-    act_t = half(act, z, act.shape[1] // 4).T
     stats = spread(row_stats(lists, qgs, kvs), "y")
     parts = attention_grads(lists, stats, qgs, kvs)
+    act_t = columns(act, parts[0])
     a = collect(parts[:4], "y")
     b = collect(parts[4:], "x")
     o_keep, o_send, rg_keep, rg_send, up = finish(b, a, rank, swap(rank), uq, uv, act_t)
     o_other = swap(o_send)
-    rg = rg_keep + swap(rg_send)
-    mine, theirs = down_terms(act_t, rg, spread(rg.astype(bf16), "z")[1:])
+    rg, low = add_cores(rg_keep, swap(rg_send))
+    mine, theirs = down_terms(act_t, rg, spread(low, "z")[1:])
     terms = lax.all_to_all(pack(mine, swap(theirs), up), ("x", "y"), 0, 0, tiled=True)
     wide = lax.all_to_all(total_for_all(terms, o_other), ("z", "x", "y"), 0, 0, tiled=True)
     att, down_q, up_q, down_v, up_v = emit(wide, swap(wide), o_keep, o_other)

time: 156 us -> 149 us (0.955)
  local copies, waits for them, and re-layouts: 6.47 us -> 0.98 us
  starting transfers between devices: 37 us -> 34.2 us
  waiting for transfers between devices: 45.8 us -> 47.7 us
    ppermute x12 -> x6, starting transfers between devices: 17.1 us -> 8.06 us  [spread(): one, three, two = [lax.ppermute(a, axis, ring(4, d)) for d in (1, 3, 2)]]
    ppermute x12 -> x6, waiting for transfers between devices: 16.4 us -> 8.64 us  [spread(): one, three, two = [lax.ppermute(a, axis, ring(4, d)) for d in (1, 3, 2)]]
    ppermute x0 -> x6, starting transfers between devices: none -> 6.02 us  [the longest x4 5.65 us: relay(): one, three = [lax.ppermute(a, axis, ring(4, d)) for d in (1, 3)]]
    ppermute x0 -> x6, waiting for transfers between devices: none -> 5.11 us  [the longest x4 4.21 us: relay(): one, three = [lax.ppermute(a, axis, ring(4, d)) for d in (1, 3)]]
    ppermute x6, waiting for transfers between devices: 13.6 us -> 17.9 us  [collect(): lax.ppermute(parts[d], axis, ring(4, -d))]
    unnamed x29 -> x18, local copies, waits for them, and re-layouts: 4.51 us -> 0.98 us
    dynamic_slice x1 -> x0, local copies, waits for them, and re-layouts: 1.96 us -> none  [half(): return lax.dynamic_slice_in_dim(a, index * size, size, axis=1)]
  transfers between devices with their start and end apart: 25 -> 25, of which waited for: 15 -> 18; matrix products, arithmetic and copies ran while one was open for 2% -> 0% of each run, Pallas kernels for 12% -> 12%
where the time goes in v7:
time: 149 us
  waiting for transfers between devices  47.7 us (32%)
  Pallas kernels  38.1 us (26%)
  starting transfers between devices  34.2 us (23%)
  blocking collectives  26.9 us (18%)
    all_to_all x1, blocking collectives, local(): lax.all_to_all(total_for_all(terms, o_other), ('z', 'x', 'y'), 0, 0, tile...  26.9 us
    ppermute x6, waiting for transfers between devices, collect(): lax.ppermute(parts[d], axis, ring(4, -d))  17.9 us
    pallas_call x1, Pallas kernels, attention_grads(): pl.pallas_call(grads_kernel, in_specs=[SMEM] + [VMEM] * 12, out_specs=[VM...  12 us
    ppermute x6, starting transfers between devices, swap(): return lax.ppermute(a, 'c', ring(2, 1))  9.62 us
    pallas_call x1, Pallas kernels, project(): pl.pallas_call(proj_kernel, grid=(width // KT,), in_specs=[pl.BlockSpec((...  8.86 us
    ppermute x6, waiting for transfers between devices, spread(): one, three, two = [lax.ppermute(a, axis, ring(4, d)) for d in (1, 3, 2)]  8.64 us
    ppermute x6, waiting for transfers between devices, swap(): return lax.ppermute(a, 'c', ring(2, 1))  8.2 us
    ppermute x6, starting transfers between devices, spread(): one, three, two = [lax.ppermute(a, axis, ring(4, d)) for d in (1, 3, 2)]  8.06 us
  transfers between devices with their start and end apart: 25, of which 18 were waited for; matrix products, arithmetic and copies ran while one was open for 0% of the time, Pallas kernels for 12%

profile of v7, /device:TPU:1, one launch (start us, length us, event | category | flops | bytes accessed | tf_op | source)
XLA Modules:
  0.0 148.9 jit_solution(17451570738839497155)
XLA Ops:
  0.7 8.9 %project.1 = (bf16[256,512]{1,0:T(8,128)(2,1)}, bf16[256,512]{1,0:T(8,128)(2,1)}, bf16[256,256]{1,0:T(8,128)(2,1)}) custom-call(bf16[256,5120]{1,0:T(8,128)(2,1)} %act.3, bf16[5120,256]{1,0:T(8,128)(2,1)} %wq.1, bf16[5120,256]{1,0:T(8,128)(2,1)} %wk.1, bf16[5120,256]{1,0:T(8,128)(2,1)} %wv.1, bf16[5120,128]{1,0:T(8,128)(2,1)} %down_q.1, ...), custom_call_target="tpu_custom_call" | custom-call | flops 2684354560 | bytes 13107200 | tf_op jit(solution)/shard_map/project/pallas_call | solution.py:86
  9.5 1.5 %collective-permute-start = (bf16[256,512]{1,0:T(8,128)(2,1)}, bf16[256,512]{1,0:T(8,128)(2,1)S(1)}, u32[]{:S(2)}, u32[]{:S(2)}) collective-permute-start(bf16[256,512]{1,0:T(8,128)(2,1)} %get-tuple-element.28), channel_id=1, source_target_pairs={{0,4},{4,0},{1,5},{5,1},{2,6},{6,2},{3,7},{7,3},{8,12},{12,8},{9,1... | collective-permute-start | bytes 786440 | tf_op jit(solution)/shard_map/ppermute | solution.py:518
  11.0 1.4 collective-permute-done.other
  12.4 0.9 copy-done.3
  13.4 1.5 collective-permute-start.1
  14.9 1.2 collective-permute-start.4
  16.1 1.5 %collective-permute-start.3 = (bf16[512,256]{1,0:T(8,128)(2,1)S(1)}, bf16[512,256]{1,0:T(8,128)(2,1)S(1)}, u32[]{:S(2)}, u32[]{:S(2)}) collective-permute-start(bf16[512,256]{1,0:T(8,128)(2,1)S(1)} %get-tuple-element.29.q0), channel_id=1, source_target_pairs={{0,24},{8,0},{16,8},{24,16},{1,25},{9,1},{17,9},{25,17},{2,26},{10... | collective-permute-start | bytes 786440 | tf_op jit(solution)/shard_map/ppermute | solution.py:527
  17.6 1.5 collective-permute-start.6
  19.1 3.5 %collective-permute-done.1.q1 = bf16[512,256]{1,0:T(8,128)(2,1)S(1)} collective-permute-done((bf16[512,256]{1,0:T(8,128)(2,1)S(1)}, bf16[512,256]{1,0:T(8,128)(2,1)S(1)}, u32[]{:S(2)}, u32[]{:S(2)}) %collective-permute-start.1) | collective-permute-done | bytes 262176 | tf_op jit(solution)/shard_map/ppermute | solution.py:527
  23.8 6.0 %lists.1 = s32[24,128]{1,0:T(8,128)S(1)} custom-call(s32[64]{0:T(128)S(1)} %copy-done.5, s32[64,64]{1,0:T(8,128)S(1)} %multiply_add_fusion.packed), custom_call_target="tpu_custom_call" | custom-call | tf_op jit(solution)/shard_map/lists/pallas_call | solution.py:149
  30.7 5.9 %row_stats.1.s0 = f32[48,128]{1,0:T(8,128)S(1)} custom-call(s32[24,128]{1,0:T(8,128)S(1)} %lists.1, bf16[512,256]{1,0:T(8,128)(2,1)S(1)} %get-tuple-element.29.q0, bf16[512,256]{1,0:T(8,128)(2,1)S(1)} %collective-permute-done.1.q1, bf16[512,256]{1,0:T(8,128)(2,1)S(1)} %collective-permute-done.2.q2, bf16[512,256]{1,0:T(8,128)(2,1)S(1)} %collective-permute-done.3.q3, ...), custom_call_target="tpu_custom_call" | custom-call | tf_op jit(solution)/shard_map/row_stats/pallas_call | solution.py:222
  36.7 2.2 %collective-permute-start.9 = (f32[48,128]{1,0:T(8,128)S(1)}, f32[48,128]{1,0:T(8,128)S(1)}, u32[]{:S(2)}, u32[]{:S(2)}) collective-permute-start(f32[48,128]{1,0:T(8,128)S(1)} %row_stats.1.s0), channel_id=1, source_target_pairs={{0,24},{8,0},{16,8},{24,16},{1,25},{9,1},{17,9},{25,17},{2,26},{10... | collective-permute-start | bytes 73736 | tf_op jit(solution)/shard_map/ppermute | solution.py:522
  40.2 3.3 %collective-permute-start.16 = (bf16[256,256]{1,0:T(8,128)(2,1)S(1)}, bf16[256,256]{1,0:T(8,128)(2,1)S(1)}, u32[]{:S(2)}, u32[]{:S(2)}) collective-permute-start(bf16[256,256]{1,0:T(8,128)(2,1)S(1)} %copy-done.4), channel_id=1, source_target_pairs={{0,4},{4,0},{1,5},{5,1},{2,6},{6,2},{3,7},{7,3},{8,12},{12,8},{9,1... | collective-permute-start | bytes 393224 | tf_op jit(solution)/shard_map/ppermute | solution.py:518
  43.7 12.0 %attention_grads.1 = (f32[512,256]{1,0:T(8,128)S(1)}, bf16[512,384]{1,0:T(8,128)(2,1)S(1)}, bf16[512,384]{1,0:T(8,128)(2,1)S(1)}, bf16[512,384]{1,0:T(8,128)(2,1...) custom-call(s32[24,128]{1,0:T(8,128)S(1)} %lists.1, ...), custom_call_target="tpu_custom_call" | custom-call | tf_op jit(solution)/shard_map/attention_grads/pallas_call | solution.py:320
  55.7 2.8 %collective-permute-start.11 = (bf16[512,128]{1,0:T(8,128)(2,1)S(1)}, bf16[512,128]{1,0:T(8,128)(2,1)S(1)}, u32[]{:S(2)}, u32[]{:S(2)}) collective-permute-start(bf16[512,128]{1,0:T(8,128)(2,1)S(1)} %get-tuple-element.34), channel_id=1, source_target_pairs={{0,64},{32,96},{64,0},{96,32},{1,65},{33,97},{65,1},{97,33},{2,66}... | collective-permute-start | bytes 393224 | tf_op jit(solution)/shard_map/ppermute | solution.py:532
  58.4 1.4 collective-permute-start.13
  59.9 1.3 collective-permute-start.14
  61.2 1.5 collective-permute-start.12
  63.0 4.2 %collective-permute-done.10.b1 = f32[512,128]{1,0:T(8,128)S(1)} collective-permute-done((f32[512,128]{1,0:T(8,128)S(1)}, f32[512,128]{1,0:T(8,128)S(1)}, u32[]{:S(2)}, u32[]{:S(2)}) %collective-permute-start.10) | collective-permute-done | bytes 262176 | tf_op jit(solution)/shard_map/ppermute | solution.py:532
  67.2 1.7 %collective-permute-done.12.b3 = f32[512,128]{1,0:T(8,128)S(1)} collective-permute-done((f32[512,128]{1,0:T(8,128)S(1)}, f32[512,128]{1,0:T(8,128)S(1)}, u32[]{:S(2)}, u32[]{:S(2)}) %collective-permute-start.12) | collective-permute-done | bytes 262176 | tf_op jit(solution)/shard_map/ppermute | solution.py:532
  69.7 11.1 %collective-permute-done.15.a3 = bf16[512,384]{1,0:T(8,128)(2,1)S(1)} collective-permute-done((bf16[512,384]{1,0:T(8,128)(2,1)S(1)}, bf16[512,384]{1,0:T(8,128)(2,1)S(1)}, u32[]{:S(2)}, u32[]{:S(2)}) %collective-permute-start.15) | collective-permute-done | bytes 393248 | tf_op jit(solution)/shard_map/ppermute | solution.py:532
  82.2 1.2 collective-permute-done.17.other
  83.4 3.8 %collective-permute-start.20 = (bf16[256,256]{1,0:T(8,128)(2,1)S(1)}, bf16[256,256]{1,0:T(8,128)(2,1)S(1)}, u32[]{:S(2)}, u32[]{:S(2)}) collective-permute-start(bf16[256,256]{1,0:T(8,128)(2,1)S(1)} %get-tuple-element.43), channel_id=1, source_target_pairs={{0,3},{1,0},{2,1},{3,2},{4,7},{5,4},{6,5},{7,6},{8,11},{9,8},{10,9... | collective-permute-start | bytes 393224 | tf_op jit(solution)/shard_map/ppermute | solution.py:522
  88.0 4.9 %collective-permute-done.20.r3 = bf16[256,256]{1,0:T(8,128)(2,1)S(1)} collective-permute-done((bf16[256,256]{1,0:T(8,128)(2,1)S(1)}, bf16[256,256]{1,0:T(8,128)(2,1)S(1)}, u32[]{:S(2)}, u32[]{:S(2)}) %collective-permute-start.20) | collective-permute-done | bytes 131104 | tf_op jit(solution)/shard_map/ppermute | solution.py:522
  93.2 3.2 %collective-permute-done.18.r1 = bf16[256,256]{1,0:T(8,128)(2,1)S(1)} collective-permute-done((bf16[256,256]{1,0:T(8,128)(2,1)S(1)}, bf16[256,256]{1,0:T(8,128)(2,1)S(1)}, u32[]{:S(2)}, u32[]{:S(2)}) %collective-permute-start.18) | collective-permute-done | bytes 131104 | tf_op jit(solution)/shard_map/ppermute | solution.py:522
  97.7 1.7 %collective-permute-done.21.theirs = f32[640,256]{1,0:T(8,128)S(1)} collective-permute-done((f32[640,256]{1,0:T(8,128)S(1)}, f32[640,256]{1,0:T(8,128)S(1)}, u32[]{:S(2)}, u32[]{:S(2)}) %collective-permute-start.21) | collective-permute-done | bytes 655392 | tf_op jit(solution)/shard_map/ppermute | solution.py:518
  100.2 3.6 %all-to-all-start = ((bf16[16,48,256]{2,1,0:T(8,128)(2,1)}), bf16[16,48,256]{2,1,0:T(8,128)(2,1)S(1)}, u32[]{:S(2)}, u32[]{:S(2)}) async-start(bf16[16,48,256]{2,1,0:T(8,128)(2,1)} %pack.1), calls=%async_computation | async-start | bytes 786432 | tf_op jit(solution)/shard_map/all_to_all | solution.py:550
  105.1 7.9 %all-to-all-done.parts = bf16[16,48,256]{2,1,0:T(8,128)(2,1)S(1)} async-done(((bf16[16,48,256]{2,1,0:T(8,128)(2,1)}), bf16[16,48,256]{2,1,0:T(8,128)(2,1)S(1)}, u32[]{:S(2)}, u32[]{:S(2)}) %all-to-all-start) | async-done | bytes 393248 | tf_op jit(solution)/shard_map/all_to_all | solution.py:550
  113.2 26.9 %all_to_all.10.own = bf16[64,48,256]{2,1,0:T(8,128)(2,1)S(1)} all-to-all(bf16[64,48,256]{2,1,0:T(8,128)(2,1)S(1)} %total_for_all.1), channel_id=1, replica_groups=mesh['x'=4,'y'=4,'c'=2,'z'=4] {'z','x','y'}, dimensions={0} | all-to-all | bytes 3145728 | tf_op jit(solution)/shard_map/all_to_all | solution.py:551
  140.1 2.9 %collective-permute-start.23 = (bf16[64,48,256]{2,1,0:T(8,128)(2,1)S(1)}, bf16[64,48,256]{2,1,0:T(8,128)(2,1)S(1)}, u32[]{:S(2)}, u32[]{:S(2)}) collective-permute-start(bf16[64,48,256]{2,1,0:T(8,128)(2,1)S(1)} %all_to_all.10.own), channel_id=1, source_target_pairs={{0,4},{4,0},{1,5},{5,1},{2,6},{6,2},{3,7},{7,3},{8,12},{12,8},{9,1... | collective-permute-start | bytes 4718600 | tf_op jit(solution)/shard_map/ppermute | solution.py:518
  143.0 3.0 %collective-permute-done.23.other = bf16[64,48,256]{2,1,0:T(8,128)(2,1)S(1)} collective-permute-done((bf16[64,48,256]{2,1,0:T(8,128)(2,1)S(1)}, bf16[64,48,256]{2,1,0:T(8,128)(2,1)S(1)}, u32[]{:S(2)}, u32[]{:S(2)}) %collective-permute-start.23) | collective-permute-done | bytes 1572896 | tf_op jit(solution)/shard_map/ppermute | solution.py:518
  146.1 2.8 %emit.1 = (bf16[256,256]{1,0:T(8,128)(2,1)}, f32[5120,128]{1,0:T(8,128)}, f32[128,256]{1,0:T(8,128)}, f32[5120,128]{1,0:T(8,128)}, f32[128,256]{1,0:T(8,128)}) custom-call(bf16[64,48,256]{2,1,0:T(8,128)(2,1)S(1)} %all_to_all.10.own, bf16[64,48,256]{2,1,0:T(8,128)(2,1)S(1)} %collective-permute-done.23.other, bf16[256,128]{1,0:T(8,128)(2,1)S(1)} %get-tuple-element.48.o_keep, ...), custom_call_target="tpu_custom_call" | custom-call | tf_op jit(solution)/shard_map/emit/pallas_call | solution.py:479
  (51 shorter events, 10.9 us)
Async XLA Ops:
  0.6 23.0 %copy-start.8 = (s32[4]{0:T(128)S(1)}, s32[4]{0:T(128)}, u32[]{:S(2)}) copy-start(s32[4]{0:T(128)} %constant.6.clone) | copy-start | bytes 52
  0.7 23.1 %copy-start.7 = (s32[64,64]{1,0:T(8,128)S(1)}, s32[64,64]{1,0:T(8,128)}, u32[]{:S(2)}) copy-start(s32[64,64]{1,0:T(8,128)} %param.22) | copy-start | bytes 49156
  0.7 23.2 %copy-start.5 = (s32[64]{0:T(128)S(1)}, s32[64]{0:T(128)}, u32[]{:S(2)}) copy-start(s32[64]{0:T(128)} %slot.1) | copy-start | bytes 772
  9.5 53.1 %copy-start = (bf16[256,5120]{1,0:T(8,128)(2,1)S(1)}, bf16[256,5120]{1,0:T(8,128)(2,1)}, u32[]{:S(2)}) copy-start(bf16[256,5120]{1,0:T(8,128)(2,1)} %act.3) | copy-start | bytes 7864324
  9.5 2.9 %collective-permute-start = (bf16[256,512]{1,0:T(8,128)(2,1)}, bf16[256,512]{1,0:T(8,128)(2,1)S(1)}, u32[]{:S(2)}, u32[]{:S(2)}) collective-permute-start(bf16[256,512]{1,0:T(8,128)(2,1)} %get-tuple-element.28), channel_id=1, source_target_pairs={{0,4},{4,0},{1,5},{5,1},{2,6},{6,2},{3,7},{7,3},{8,12},{12,8},{9,1... | collective-permute-start | bytes 786440 | tf_op jit(solution)/shard_map/ppermute | solution.py:518
  13.4 26.9 %copy-start.4 = (bf16[256,256]{1,0:T(8,128)(2,1)S(1)}, bf16[256,256]{1,0:T(8,128)(2,1)}, u32[]{:S(2)}) copy-start(bf16[256,256]{1,0:T(8,128)(2,1)} %get-tuple-element.39.own) | copy-start | bytes 393220
  13.4 9.1 %collective-permute-start.1 = (bf16[512,256]{1,0:T(8,128)(2,1)S(1)}, bf16[512,256]{1,0:T(8,128)(2,1)S(1)}, u32[]{:S(2)}, u32[]{:S(2)}) collective-permute-start(bf16[512,256]{1,0:T(8,128)(2,1)S(1)} %get-tuple-element.29.q0), channel_id=1, source_target_pairs={{0,8},{8,16},{16,24},{24,0},{1,9},{9,17},{17,25},{25,1},{2,10},{10... | collective-permute-start | bytes 786440 | tf_op jit(solution)/shard_map/ppermute | solution.py:527
  14.9 8.4 %collective-permute-start.4 = (bf16[512,256]{1,0:T(8,128)(2,1)S(1)}, bf16[512,256]{1,0:T(8,128)(2,1)S(1)}, u32[]{:S(2)}, u32[]{:S(2)}) collective-permute-start(bf16[512,256]{1,0:T(8,128)(2,1)S(1)} %get-tuple-element.30.k0), channel_id=1, source_target_pairs={{0,32},{32,64},{64,96},{96,0},{1,33},{33,65},{65,97},{97,1},{2,34}... | collective-permute-start | bytes 786440 | tf_op jit(solution)/shard_map/ppermute | solution.py:527
  16.1 13.8 %collective-permute-start.3 = (bf16[512,256]{1,0:T(8,128)(2,1)S(1)}, bf16[512,256]{1,0:T(8,128)(2,1)S(1)}, u32[]{:S(2)}, u32[]{:S(2)}) collective-permute-start(bf16[512,256]{1,0:T(8,128)(2,1)S(1)} %get-tuple-element.29.q0), channel_id=1, source_target_pairs={{0,24},{8,0},{16,8},{24,16},{1,25},{9,1},{17,9},{25,17},{2,26},{10... | collective-permute-start | bytes 786440 | tf_op jit(solution)/shard_map/ppermute | solution.py:527
  17.6 12.3 %collective-permute-start.6 = (bf16[512,256]{1,0:T(8,128)(2,1)S(1)}, bf16[512,256]{1,0:T(8,128)(2,1)S(1)}, u32[]{:S(2)}, u32[]{:S(2)}) collective-permute-start(bf16[512,256]{1,0:T(8,128)(2,1)S(1)} %get-tuple-element.30.k0), channel_id=1, source_target_pairs={{0,96},{32,0},{64,32},{96,64},{1,97},{33,1},{65,33},{97,65},{2,98}... | collective-permute-start | bytes 786440 | tf_op jit(solution)/shard_map/ppermute | solution.py:527
  22.5 8.0 %collective-permute-start.2 = (bf16[512,256]{1,0:T(8,128)(2,1)S(1)}, bf16[512,256]{1,0:T(8,128)(2,1)S(1)}, u32[]{:S(2)}, u32[]{:S(2)}) collective-permute-start(bf16[512,256]{1,0:T(8,128)(2,1)S(1)} %collective-permute-done.1.q1), channel_id=1, source_target_pairs={{0,8},{8,16},{16,24},{24,0},{1,9},{9,17},{17,25},{25,1},{2,10},{10... | collective-permute-start | bytes 786440 | tf_op jit(solution)/shard_map/ppermute | solution.py:528
  23.3 7.5 %collective-permute-start.5 = (bf16[512,256]{1,0:T(8,128)(2,1)S(1)}, bf16[512,256]{1,0:T(8,128)(2,1)S(1)}, u32[]{:S(2)}, u32[]{:S(2)}) collective-permute-start(bf16[512,256]{1,0:T(8,128)(2,1)S(1)} %collective-permute-done.4.k1), channel_id=1, source_target_pairs={{0,32},{32,64},{64,96},{96,0},{1,33},{33,65},{65,97},{97,1},{2,34}... | collective-permute-start | bytes 786440 | tf_op jit(solution)/shard_map/ppermute | solution.py:528
  36.7 6.8 %collective-permute-start.9 = (f32[48,128]{1,0:T(8,128)S(1)}, f32[48,128]{1,0:T(8,128)S(1)}, u32[]{:S(2)}, u32[]{:S(2)}) collective-permute-start(f32[48,128]{1,0:T(8,128)S(1)} %row_stats.1.s0), channel_id=1, source_target_pairs={{0,24},{8,0},{16,8},{24,16},{1,25},{9,1},{17,9},{25,17},{2,26},{10... | collective-permute-start | bytes 73736 | tf_op jit(solution)/shard_map/ppermute | solution.py:522
  38.9 4.6 %collective-permute-start.8 = (f32[48,128]{1,0:T(8,128)S(1)}, f32[48,128]{1,0:T(8,128)S(1)}, u32[]{:S(2)}, u32[]{:S(2)}) collective-permute-start(f32[48,128]{1,0:T(8,128)S(1)} %row_stats.1.s0), channel_id=1, source_target_pairs={{0,16},{8,24},{16,0},{24,8},{1,17},{9,25},{17,1},{25,9},{2,18},{10... | collective-permute-start | bytes 73736 | tf_op jit(solution)/shard_map/ppermute | solution.py:522
  39.8 3.9 %collective-permute-start.7 = (f32[48,128]{1,0:T(8,128)S(1)}, f32[48,128]{1,0:T(8,128)S(1)}, u32[]{:S(2)}, u32[]{:S(2)}) collective-permute-start(f32[48,128]{1,0:T(8,128)S(1)} %row_stats.1.s0), channel_id=1, source_target_pairs={{0,8},{8,16},{16,24},{24,0},{1,9},{9,17},{17,25},{25,1},{2,10},{10... | collective-permute-start | bytes 73736 | tf_op jit(solution)/shard_map/ppermute | solution.py:522
  40.2 40.6 %copy-start.1 = (bf16[128,256]{1,0:T(8,128)(2,1)S(1)}, bf16[128,256]{1,0:T(8,128)(2,1)}, u32[]{:S(2)}) copy-start(bf16[128,256]{1,0:T(8,128)(2,1)} %uq.1) | copy-start | bytes 196612
  40.2 40.6 %copy-start.2 = (bf16[128,256]{1,0:T(8,128)(2,1)S(1)}, bf16[128,256]{1,0:T(8,128)(2,1)}, u32[]{:S(2)}) copy-start(bf16[128,256]{1,0:T(8,128)(2,1)} %uv.1) | copy-start | bytes 196612
  40.2 21.0 %collective-permute-start.16 = (bf16[256,256]{1,0:T(8,128)(2,1)S(1)}, bf16[256,256]{1,0:T(8,128)(2,1)S(1)}, u32[]{:S(2)}, u32[]{:S(2)}) collective-permute-start(bf16[256,256]{1,0:T(8,128)(2,1)S(1)} %copy-done.4), channel_id=1, source_target_pairs={{0,4},{4,0},{1,5},{5,1},{2,6},{6,2},{3,7},{7,3},{8,12},{12,8},{9,1... | collective-permute-start | bytes 393224 | tf_op jit(solution)/shard_map/ppermute | solution.py:518
  55.7 5.6 %collective-permute-start.11 = (bf16[512,128]{1,0:T(8,128)(2,1)S(1)}, bf16[512,128]{1,0:T(8,128)(2,1)S(1)}, u32[]{:S(2)}, u32[]{:S(2)}) collective-permute-start(bf16[512,128]{1,0:T(8,128)(2,1)S(1)} %get-tuple-element.34), channel_id=1, source_target_pairs={{0,64},{32,96},{64,0},{96,32},{1,65},{33,97},{65,1},{97,33},{2,66}... | collective-permute-start | bytes 393224 | tf_op jit(solution)/shard_map/ppermute | solution.py:532
  58.4 10.5 %collective-permute-start.13 = (bf16[512,384]{1,0:T(8,128)(2,1)S(1)}, bf16[512,384]{1,0:T(8,128)(2,1)S(1)}, u32[]{:S(2)}, u32[]{:S(2)}) collective-permute-start(bf16[512,384]{1,0:T(8,128)(2,1)S(1)} %get-tuple-element.36), channel_id=1, source_target_pairs={{0,24},{8,0},{16,8},{24,16},{1,25},{9,1},{17,9},{25,17},{2,26},{10... | collective-permute-start | bytes 1179656 | tf_op jit(solution)/shard_map/ppermute | solution.py:532
  59.9 9.9 %collective-permute-start.14 = (bf16[512,384]{1,0:T(8,128)(2,1)S(1)}, bf16[512,384]{1,0:T(8,128)(2,1)S(1)}, u32[]{:S(2)}, u32[]{:S(2)}) collective-permute-start(bf16[512,384]{1,0:T(8,128)(2,1)S(1)} %get-tuple-element.37), channel_id=1, source_target_pairs={{0,16},{8,24},{16,0},{24,8},{1,17},{9,25},{17,1},{25,9},{2,18},{10... | collective-permute-start | bytes 1179656 | tf_op jit(solution)/shard_map/ppermute | solution.py:532
  61.2 19.6 %collective-permute-start.15 = (bf16[512,384]{1,0:T(8,128)(2,1)S(1)}, bf16[512,384]{1,0:T(8,128)(2,1)S(1)}, u32[]{:S(2)}, u32[]{:S(2)}) collective-permute-start(bf16[512,384]{1,0:T(8,128)(2,1)S(1)} %get-tuple-element.38), channel_id=1, source_target_pairs={{0,8},{8,16},{16,24},{24,0},{1,9},{9,17},{17,25},{25,1},{2,10},{10... | collective-permute-start | bytes 1179656 | tf_op jit(solution)/shard_map/ppermute | solution.py:532
  61.2 6.0 %collective-permute-start.10 = (f32[512,128]{1,0:T(8,128)S(1)}, f32[512,128]{1,0:T(8,128)S(1)}, u32[]{:S(2)}, u32[]{:S(2)}) collective-permute-start(f32[512,128]{1,0:T(8,128)S(1)} %get-tuple-element.33), channel_id=1, source_target_pairs={{0,96},{32,0},{64,32},{96,64},{1,97},{33,1},{65,33},{97,65},{2,98}... | collective-permute-start | bytes 786440 | tf_op jit(solution)/shard_map/ppermute | solution.py:532
  61.2 7.7 %collective-permute-start.12 = (f32[512,128]{1,0:T(8,128)S(1)}, f32[512,128]{1,0:T(8,128)S(1)}, u32[]{:S(2)}, u32[]{:S(2)}) collective-permute-start(f32[512,128]{1,0:T(8,128)S(1)} %get-tuple-element.35), channel_id=1, source_target_pairs={{0,32},{32,64},{64,96},{96,0},{1,33},{33,65},{65,97},{97,1},{2,34}... | collective-permute-start | bytes 786440 | tf_op jit(solution)/shard_map/ppermute | solution.py:532
  81.7 1.7 %collective-permute-start.17 = (f32[256,256]{1,0:T(8,128)S(1)}, f32[256,256]{1,0:T(8,128)S(1)}, u32[]{:S(2)}, u32[]{:S(2)}) collective-permute-start(f32[256,256]{1,0:T(8,128)S(1)} %get-tuple-element.41), channel_id=1, source_target_pairs={{0,4},{4,0},{1,5},{5,1},{2,6},{6,2},{3,7},{7,3},{8,12},{12,8},{9,1... | collective-permute-start | bytes 786440 | tf_op jit(solution)/shard_map/ppermute | solution.py:518
  83.4 9.5 %collective-permute-start.20 = (bf16[256,256]{1,0:T(8,128)(2,1)S(1)}, bf16[256,256]{1,0:T(8,128)(2,1)S(1)}, u32[]{:S(2)}, u32[]{:S(2)}) collective-permute-start(bf16[256,256]{1,0:T(8,128)(2,1)S(1)} %get-tuple-element.43), channel_id=1, source_target_pairs={{0,3},{1,0},{2,1},{3,2},{4,7},{5,4},{6,5},{7,6},{8,11},{9,8},{10,9... | collective-permute-start | bytes 393224 | tf_op jit(solution)/shard_map/ppermute | solution.py:522
  87.3 6.0 %collective-permute-start.19 = (bf16[256,256]{1,0:T(8,128)(2,1)S(1)}, bf16[256,256]{1,0:T(8,128)(2,1)S(1)}, u32[]{:S(2)}, u32[]{:S(2)}) collective-permute-start(bf16[256,256]{1,0:T(8,128)(2,1)S(1)} %get-tuple-element.43), channel_id=1, source_target_pairs={{0,2},{1,3},{2,0},{3,1},{4,6},{5,7},{6,4},{7,5},{8,10},{9,11},{10,... | collective-permute-start | bytes 393224 | tf_op jit(solution)/shard_map/ppermute | solution.py:522
  87.3 9.1 %collective-permute-start.18 = (bf16[256,256]{1,0:T(8,128)(2,1)S(1)}, bf16[256,256]{1,0:T(8,128)(2,1)S(1)}, u32[]{:S(2)}, u32[]{:S(2)}) collective-permute-start(bf16[256,256]{1,0:T(8,128)(2,1)S(1)} %get-tuple-element.43), channel_id=1, source_target_pairs={{0,1},{1,2},{2,3},{3,0},{4,5},{5,6},{6,7},{7,4},{8,9},{9,10},{10,1... | collective-permute-start | bytes 393224 | tf_op jit(solution)/shard_map/ppermute | solution.py:522
  96.8 2.6 %collective-permute-start.21 = (f32[640,256]{1,0:T(8,128)S(1)}, f32[640,256]{1,0:T(8,128)S(1)}, u32[]{:S(2)}, u32[]{:S(2)}) collective-permute-start(f32[640,256]{1,0:T(8,128)S(1)} %get-tuple-element.45), channel_id=1, source_target_pairs={{0,4},{4,0},{1,5},{5,1},{2,6},{6,2},{3,7},{7,3},{8,12},{12,8},{9,1... | collective-permute-start | bytes 1966088 | tf_op jit(solution)/shard_map/ppermute | solution.py:518
  100.2 12.9 %all-to-all-start = ((bf16[16,48,256]{2,1,0:T(8,128)(2,1)}), bf16[16,48,256]{2,1,0:T(8,128)(2,1)S(1)}, u32[]{:S(2)}, u32[]{:S(2)}) async-start(bf16[16,48,256]{2,1,0:T(8,128)(2,1)} %pack.1), calls=%async_computation | async-start | bytes 786432 | tf_op jit(solution)/shard_map/all_to_all | solution.py:550
  103.8 1.4 collective-permute-start.22
  140.1 6.0 %collective-permute-start.23 = (bf16[64,48,256]{2,1,0:T(8,128)(2,1)S(1)}, bf16[64,48,256]{2,1,0:T(8,128)(2,1)S(1)}, u32[]{:S(2)}, u32[]{:S(2)}) collective-permute-start(bf16[64,48,256]{2,1,0:T(8,128)(2,1)S(1)} %all_to_all.10.own), channel_id=1, source_target_pairs={{0,4},{4,0},{1,5},{5,1},{2,6},{6,2},{3,7},{7,3},{8,12},{12,8},{9,1... | collective-permute-start | bytes 4718600 | tf_op jit(solution)/shard_map/ppermute | solution.py:518
  (2 other events, 23.9 us)

commit v8 on v7

--- a/solution.py
+++ b/solution.py
@@ -15,7 +15,7 @@
 CHUNK = 512
 CB = CHUNK // BLK
 CHAINS = 4
-STAT_CHAINS = 8
+STAT_CHAINS = 4
 SCALE = HEAD ** -0.5
 SCALE2 = SCALE * math.log2(math.e)
 NEG = -1e30
@@ -546,7 +546,7 @@
     o_keep, o_send, rg_keep, rg_send, up = finish(b, a, rank, swap(rank), uq, uv, act_t)
     o_other = swap(o_send)
     rg, low = add_cores(rg_keep, swap(rg_send))
-    mine, theirs = down_terms(act_t, rg, spread(low, "z")[1:])
+    mine, theirs = down_terms(act_t, rg, relay(low, "z")[1:])
     terms = lax.all_to_all(pack(mine, swap(theirs), up), ("x", "y"), 0, 0, tiled=True)
     wide = lax.all_to_all(total_for_all(terms, o_other), ("z", "x", "y"), 0, 0, tiled=True)
     att, down_q, up_q, down_v, up_v = emit(wide, swap(wide), o_keep, o_other)

time: 149 us -> 149 us (level)
    ppermute x6 -> x3, waiting for transfers between devices: 8.64 us -> 0.19 us  [spread(): one, three, two = [lax.ppermute(a, axis, ring(4, d)) for d in (1, 3, 2)]]
    ppermute x2 -> x3, waiting for transfers between devices: 0.9 us -> 6.23 us  [relay(): return [a, one, lax.ppermute(one, axis, ring(4, 1)), three]]
    ppermute x6 -> x3, starting transfers between devices: 8.06 us -> 3.55 us  [spread(): one, three, two = [lax.ppermute(a, axis, ring(4, d)) for d in (1, 3, 2)]]
    ppermute x4 -> x6, starting transfers between devices: 5.65 us -> 9.55 us  [relay(): one, three = [lax.ppermute(a, axis, ring(4, d)) for d in (1, 3)]]
    ppermute x4 -> x6, waiting for transfers between devices: 4.21 us -> 7.7 us  [relay(): one, three = [lax.ppermute(a, axis, ring(4, d)) for d in (1, 3)]]
    ppermute x6, starting transfers between devices: 9.62 us -> 11.4 us  [swap(): return lax.ppermute(a, 'c', ring(2, 1))]
  transfers between devices with their start and end apart: 25 -> 25, of which waited for: 18 -> 16; matrix products, arithmetic and copies ran while one was open for 0% -> 0% of each run, Pallas kernels for 12% -> 12%
where the time goes in v8:
time: 149 us
  waiting for transfers between devices  47.8 us (32%)
  Pallas kernels  38.7 us (26%)
  starting transfers between devices  34.4 us (23%)
  blocking collectives  25.9 us (17%)
    all_to_all x1, blocking collectives, local(): lax.all_to_all(total_for_all(terms, o_other), ('z', 'x', 'y'), 0, 0, tile...  25.9 us
    ppermute x6, waiting for transfers between devices, collect(): lax.ppermute(parts[d], axis, ring(4, -d))  17.9 us
    pallas_call x1, Pallas kernels, attention_grads(): pl.pallas_call(grads_kernel, in_specs=[SMEM] + [VMEM] * 12, out_specs=[VM...  12 us
    ppermute x6, starting transfers between devices, swap(): return lax.ppermute(a, 'c', ring(2, 1))  11.4 us
    ppermute x6, starting transfers between devices, relay(): one, three = [lax.ppermute(a, axis, ring(4, d)) for d in (1, 3)]  9.55 us
    pallas_call x1, Pallas kernels, project(): pl.pallas_call(proj_kernel, grid=(width // KT,), in_specs=[pl.BlockSpec((...  8.86 us
    ppermute x6, waiting for transfers between devices, swap(): return lax.ppermute(a, 'c', ring(2, 1))  8.2 us
    ppermute x6, waiting for transfers between devices, relay(): one, three = [lax.ppermute(a, axis, ring(4, d)) for d in (1, 3)]  7.7 us
  transfers between devices with their start and end apart: 25, of which 16 were waited for; matrix products, arithmetic and copies ran while one was open for 0% of the time, Pallas kernels for 12%

profile of v8, /device:TPU:1, one launch (start us, length us, event | category | flops | bytes accessed | tf_op | source)
XLA Modules:
  0.0 148.8 jit_solution(11756183358694179626)
XLA Ops:
  0.7 8.9 %project.1 = (bf16[256,512]{1,0:T(8,128)(2,1)}, bf16[256,512]{1,0:T(8,128)(2,1)}, bf16[256,256]{1,0:T(8,128)(2,1)}) custom-call(bf16[256,5120]{1,0:T(8,128)(2,1)} %act.3, bf16[5120,256]{1,0:T(8,128)(2,1)} %wq.1, bf16[5120,256]{1,0:T(8,128)(2,1)} %wk.1, bf16[5120,256]{1,0:T(8,128)(2,1)} %wv.1, bf16[5120,128]{1,0:T(8,128)(2,1)} %down_q.1, ...), custom_call_target="tpu_custom_call" | custom-call | flops 2684354560 | bytes 13107200 | tf_op jit(solution)/shard_map/project/pallas_call | solution.py:86
  9.5 1.5 %collective-permute-start = (bf16[256,512]{1,0:T(8,128)(2,1)}, bf16[256,512]{1,0:T(8,128)(2,1)S(1)}, u32[]{:S(2)}, u32[]{:S(2)}) collective-permute-start(bf16[256,512]{1,0:T(8,128)(2,1)} %get-tuple-element.28), channel_id=1, source_target_pairs={{0,4},{4,0},{1,5},{5,1},{2,6},{6,2},{3,7},{7,3},{8,12},{12,8},{9,1... | collective-permute-start | bytes 786440 | tf_op jit(solution)/shard_map/ppermute | solution.py:518
  11.0 1.4 collective-permute-done.other
  13.4 1.5 collective-permute-start.1
  14.9 1.2 collective-permute-start.4
  16.1 1.5 %collective-permute-start.3 = (bf16[512,256]{1,0:T(8,128)(2,1)S(1)}, bf16[512,256]{1,0:T(8,128)(2,1)S(1)}, u32[]{:S(2)}, u32[]{:S(2)}) collective-permute-start(bf16[512,256]{1,0:T(8,128)(2,1)S(1)} %get-tuple-element.29.q0), channel_id=1, source_target_pairs={{0,24},{8,0},{16,8},{24,16},{1,25},{9,1},{17,9},{25,17},{2,26},{10... | collective-permute-start | bytes 786440 | tf_op jit(solution)/shard_map/ppermute | solution.py:527
  17.6 1.5 collective-permute-start.6
  19.1 3.5 %collective-permute-done.1.q1 = bf16[512,256]{1,0:T(8,128)(2,1)S(1)} collective-permute-done((bf16[512,256]{1,0:T(8,128)(2,1)S(1)}, bf16[512,256]{1,0:T(8,128)(2,1)S(1)}, u32[]{:S(2)}, u32[]{:S(2)}) %collective-permute-start.1) | collective-permute-done | bytes 262176 | tf_op jit(solution)/shard_map/ppermute | solution.py:527
  23.8 6.0 %lists.1 = s32[24,128]{1,0:T(8,128)S(1)} custom-call(s32[64]{0:T(128)S(1)} %copy-done.5, s32[64,64]{1,0:T(8,128)S(1)} %multiply_add_fusion.packed), custom_call_target="tpu_custom_call" | custom-call | tf_op jit(solution)/shard_map/lists/pallas_call | solution.py:149
  30.7 6.6 %row_stats.1.s0 = f32[48,128]{1,0:T(8,128)S(1)} custom-call(s32[24,128]{1,0:T(8,128)S(1)} %lists.1, bf16[512,256]{1,0:T(8,128)(2,1)S(1)} %get-tuple-element.29.q0, bf16[512,256]{1,0:T(8,128)(2,1)S(1)} %collective-permute-done.1.q1, bf16[512,256]{1,0:T(8,128)(2,1)S(1)} %collective-permute-done.2.q2, bf16[512,256]{1,0:T(8,128)(2,1)S(1)} %collective-permute-done.3.q3, ...), custom_call_target="tpu_custom_call" | custom-call | tf_op jit(solution)/shard_map/row_stats/pallas_call | solution.py:222
  37.3 2.2 %collective-permute-start.9 = (f32[48,128]{1,0:T(8,128)S(1)}, f32[48,128]{1,0:T(8,128)S(1)}, u32[]{:S(2)}, u32[]{:S(2)}) collective-permute-start(f32[48,128]{1,0:T(8,128)S(1)} %row_stats.1.s0), channel_id=1, source_target_pairs={{0,24},{8,0},{16,8},{24,16},{1,25},{9,1},{17,9},{25,17},{2,26},{10... | collective-permute-start | bytes 73736 | tf_op jit(solution)/shard_map/ppermute | solution.py:522
  40.9 3.3 %collective-permute-start.16 = (bf16[256,256]{1,0:T(8,128)(2,1)S(1)}, bf16[256,256]{1,0:T(8,128)(2,1)S(1)}, u32[]{:S(2)}, u32[]{:S(2)}) collective-permute-start(bf16[256,256]{1,0:T(8,128)(2,1)S(1)} %copy-done.4), channel_id=1, source_target_pairs={{0,4},{4,0},{1,5},{5,1},{2,6},{6,2},{3,7},{7,3},{8,12},{12,8},{9,1... | collective-permute-start | bytes 393224 | tf_op jit(solution)/shard_map/ppermute | solution.py:518
  44.4 12.0 %attention_grads.1 = (f32[512,256]{1,0:T(8,128)S(1)}, bf16[512,384]{1,0:T(8,128)(2,1)S(1)}, bf16[512,384]{1,0:T(8,128)(2,1)S(1)}, bf16[512,384]{1,0:T(8,128)(2,1...) custom-call(s32[24,128]{1,0:T(8,128)S(1)} %lists.1, ...), custom_call_target="tpu_custom_call" | custom-call | tf_op jit(solution)/shard_map/attention_grads/pallas_call | solution.py:320
  56.4 1.8 %collective-permute-start.11 = (bf16[512,128]{1,0:T(8,128)(2,1)S(1)}, bf16[512,128]{1,0:T(8,128)(2,1)S(1)}, u32[]{:S(2)}, u32[]{:S(2)}) collective-permute-start(bf16[512,128]{1,0:T(8,128)(2,1)S(1)} %get-tuple-element.34), channel_id=1, source_target_pairs={{0,64},{32,96},{64,0},{96,32},{1,65},{33,97},{65,1},{97,33},{2,66}... | collective-permute-start | bytes 393224 | tf_op jit(solution)/shard_map/ppermute | solution.py:532
  58.2 1.2 collective-permute-start.13
  59.4 1.3 collective-permute-start.14
  62.5 5.1 %collective-permute-done.10.b1 = f32[512,128]{1,0:T(8,128)S(1)} collective-permute-done((f32[512,128]{1,0:T(8,128)S(1)}, f32[512,128]{1,0:T(8,128)S(1)}, u32[]{:S(2)}, u32[]{:S(2)}) %collective-permute-start.10) | collective-permute-done | bytes 262176 | tf_op jit(solution)/shard_map/ppermute | solution.py:532
  67.7 2.0 %collective-permute-done.12.b3 = f32[512,128]{1,0:T(8,128)S(1)} collective-permute-done((f32[512,128]{1,0:T(8,128)S(1)}, f32[512,128]{1,0:T(8,128)S(1)}, u32[]{:S(2)}, u32[]{:S(2)}) %collective-permute-start.12) | collective-permute-done | bytes 262176 | tf_op jit(solution)/shard_map/ppermute | solution.py:532
  69.6 10.8 %collective-permute-done.15.a3 = bf16[512,384]{1,0:T(8,128)(2,1)S(1)} collective-permute-done((bf16[512,384]{1,0:T(8,128)(2,1)S(1)}, bf16[512,384]{1,0:T(8,128)(2,1)S(1)}, u32[]{:S(2)}, u32[]{:S(2)}) %collective-permute-start.15) | collective-permute-done | bytes 393248 | tf_op jit(solution)/shard_map/ppermute | solution.py:532
  81.8 1.2 collective-permute-done.17.other
  83.0 1.7 %collective-permute-start.18 = (bf16[256,256]{1,0:T(8,128)(2,1)S(1)}, bf16[256,256]{1,0:T(8,128)(2,1)S(1)}, u32[]{:S(2)}, u32[]{:S(2)}) collective-permute-start(bf16[256,256]{1,0:T(8,128)(2,1)S(1)} %get-tuple-element.43), channel_id=1, source_target_pairs={{0,1},{1,2},{2,3},{3,0},{4,5},{5,6},{6,7},{7,4},{8,9},{9,10},{10,1... | collective-permute-start | bytes 393224 | tf_op jit(solution)/shard_map/ppermute | solution.py:527
  84.7 2.2 %collective-permute-start.20 = (bf16[256,256]{1,0:T(8,128)(2,1)S(1)}, bf16[256,256]{1,0:T(8,128)(2,1)S(1)}, u32[]{:S(2)}, u32[]{:S(2)}) collective-permute-start(bf16[256,256]{1,0:T(8,128)(2,1)S(1)} %get-tuple-element.43), channel_id=1, source_target_pairs={{0,3},{1,0},{2,1},{3,2},{4,7},{5,4},{6,5},{7,6},{8,11},{9,8},{10,9... | collective-permute-start | bytes 393224 | tf_op jit(solution)/shard_map/ppermute | solution.py:527
  86.9 3.5 %collective-permute-done.18.r1 = bf16[256,256]{1,0:T(8,128)(2,1)S(1)} collective-permute-done((bf16[256,256]{1,0:T(8,128)(2,1)S(1)}, bf16[256,256]{1,0:T(8,128)(2,1)S(1)}, u32[]{:S(2)}, u32[]{:S(2)}) %collective-permute-start.18) | collective-permute-done | bytes 131104 | tf_op jit(solution)/shard_map/ppermute | solution.py:527
  90.4 5.3 %collective-permute-done.19.r2 = bf16[256,256]{1,0:T(8,128)(2,1)S(1)} collective-permute-done((bf16[256,256]{1,0:T(8,128)(2,1)S(1)}, bf16[256,256]{1,0:T(8,128)(2,1)S(1)}, u32[]{:S(2)}, u32[]{:S(2)}) %collective-permute-start.19) | collective-permute-done | bytes 131104 | tf_op jit(solution)/shard_map/ppermute | solution.py:528
  96.1 1.9 %collective-permute-start.21 = (f32[640,256]{1,0:T(8,128)S(1)}, f32[640,256]{1,0:T(8,128)S(1)}, u32[]{:S(2)}, u32[]{:S(2)}) collective-permute-start(f32[640,256]{1,0:T(8,128)S(1)} %get-tuple-element.45), channel_id=1, source_target_pairs={{0,4},{4,0},{1,5},{5,1},{2,6},{6,2},{3,7},{7,3},{8,12},{12,8},{9,1... | collective-permute-start | bytes 1966088 | tf_op jit(solution)/shard_map/ppermute | solution.py:518
  98.0 1.7 %collective-permute-done.21.theirs = f32[640,256]{1,0:T(8,128)S(1)} collective-permute-done((f32[640,256]{1,0:T(8,128)S(1)}, f32[640,256]{1,0:T(8,128)S(1)}, u32[]{:S(2)}, u32[]{:S(2)}) %collective-permute-start.21) | collective-permute-done | bytes 655392 | tf_op jit(solution)/shard_map/ppermute | solution.py:518
  100.5 3.7 %all-to-all-start = ((bf16[16,48,256]{2,1,0:T(8,128)(2,1)}), bf16[16,48,256]{2,1,0:T(8,128)(2,1)S(1)}, u32[]{:S(2)}, u32[]{:S(2)}) async-start(bf16[16,48,256]{2,1,0:T(8,128)(2,1)} %pack.1), calls=%async_computation | async-start | bytes 786432 | tf_op jit(solution)/shard_map/all_to_all | solution.py:550
  105.9 7.6 %all-to-all-done.parts = bf16[16,48,256]{2,1,0:T(8,128)(2,1)S(1)} async-done(((bf16[16,48,256]{2,1,0:T(8,128)(2,1)}), bf16[16,48,256]{2,1,0:T(8,128)(2,1)S(1)}, u32[]{:S(2)}, u32[]{:S(2)}) %all-to-all-start) | async-done | bytes 393248 | tf_op jit(solution)/shard_map/all_to_all | solution.py:550
  113.6 25.9 %all_to_all.10.own = bf16[64,48,256]{2,1,0:T(8,128)(2,1)S(1)} all-to-all(bf16[64,48,256]{2,1,0:T(8,128)(2,1)S(1)} %total_for_all.1), channel_id=1, replica_groups=mesh['x'=4,'y'=4,'c'=2,'z'=4] {'z','x','y'}, dimensions={0} | all-to-all | bytes 3145728 | tf_op jit(solution)/shard_map/all_to_all | solution.py:551
  139.5 3.4 %collective-permute-start.23 = (bf16[64,48,256]{2,1,0:T(8,128)(2,1)S(1)}, bf16[64,48,256]{2,1,0:T(8,128)(2,1)S(1)}, u32[]{:S(2)}, u32[]{:S(2)}) collective-permute-start(bf16[64,48,256]{2,1,0:T(8,128)(2,1)S(1)} %all_to_all.10.own), channel_id=1, source_target_pairs={{0,4},{4,0},{1,5},{5,1},{2,6},{6,2},{3,7},{7,3},{8,12},{12,8},{9,1... | collective-permute-start | bytes 4718600 | tf_op jit(solution)/shard_map/ppermute | solution.py:518
  142.9 3.0 %collective-permute-done.23.other = bf16[64,48,256]{2,1,0:T(8,128)(2,1)S(1)} collective-permute-done((bf16[64,48,256]{2,1,0:T(8,128)(2,1)S(1)}, bf16[64,48,256]{2,1,0:T(8,128)(2,1)S(1)}, u32[]{:S(2)}, u32[]{:S(2)}) %collective-permute-start.23) | collective-permute-done | bytes 1572896 | tf_op jit(solution)/shard_map/ppermute | solution.py:518
  145.9 2.8 %emit.1 = (bf16[256,256]{1,0:T(8,128)(2,1)}, f32[5120,128]{1,0:T(8,128)}, f32[128,256]{1,0:T(8,128)}, f32[5120,128]{1,0:T(8,128)}, f32[128,256]{1,0:T(8,128)}) custom-call(bf16[64,48,256]{2,1,0:T(8,128)(2,1)S(1)} %all_to_all.10.own, bf16[64,48,256]{2,1,0:T(8,128)(2,1)S(1)} %collective-permute-done.23.other, bf16[256,128]{1,0:T(8,128)(2,1)S(1)} %get-tuple-element.48.o_keep, ...), custom_call_target="tpu_custom_call" | custom-call | tf_op jit(solution)/shard_map/emit/pallas_call | solution.py:479
  (51 shorter events, 10.9 us)
Async XLA Ops:
  0.6 23.0 %copy-start.8 = (s32[4]{0:T(128)S(1)}, s32[4]{0:T(128)}, u32[]{:S(2)}) copy-start(s32[4]{0:T(128)} %constant.6.clone) | copy-start | bytes 52
  0.7 23.1 %copy-start.7 = (s32[64,64]{1,0:T(8,128)S(1)}, s32[64,64]{1,0:T(8,128)}, u32[]{:S(2)}) copy-start(s32[64,64]{1,0:T(8,128)} %param.22) | copy-start | bytes 49156
  0.7 23.2 %copy-start.5 = (s32[64]{0:T(128)S(1)}, s32[64]{0:T(128)}, u32[]{:S(2)}) copy-start(s32[64]{0:T(128)} %slot.1) | copy-start | bytes 772
  9.5 52.7 %copy-start = (bf16[256,5120]{1,0:T(8,128)(2,1)S(1)}, bf16[256,5120]{1,0:T(8,128)(2,1)}, u32[]{:S(2)}) copy-start(bf16[256,5120]{1,0:T(8,128)(2,1)} %act.3) | copy-start | bytes 7864324
  9.5 2.9 %collective-permute-start = (bf16[256,512]{1,0:T(8,128)(2,1)}, bf16[256,512]{1,0:T(8,128)(2,1)S(1)}, u32[]{:S(2)}, u32[]{:S(2)}) collective-permute-start(bf16[256,512]{1,0:T(8,128)(2,1)} %get-tuple-element.28), channel_id=1, source_target_pairs={{0,4},{4,0},{1,5},{5,1},{2,6},{6,2},{3,7},{7,3},{8,12},{12,8},{9,1... | collective-permute-start | bytes 786440 | tf_op jit(solution)/shard_map/ppermute | solution.py:518
  13.4 27.5 %copy-start.4 = (bf16[256,256]{1,0:T(8,128)(2,1)S(1)}, bf16[256,256]{1,0:T(8,128)(2,1)}, u32[]{:S(2)}) copy-start(bf16[256,256]{1,0:T(8,128)(2,1)} %get-tuple-element.39.own) | copy-start | bytes 393220
  13.4 9.1 %collective-permute-start.1 = (bf16[512,256]{1,0:T(8,128)(2,1)S(1)}, bf16[512,256]{1,0:T(8,128)(2,1)S(1)}, u32[]{:S(2)}, u32[]{:S(2)}) collective-permute-start(bf16[512,256]{1,0:T(8,128)(2,1)S(1)} %get-tuple-element.29.q0), channel_id=1, source_target_pairs={{0,8},{8,16},{16,24},{24,0},{1,9},{9,17},{17,25},{25,1},{2,10},{10... | collective-permute-start | bytes 786440 | tf_op jit(solution)/shard_map/ppermute | solution.py:527
  14.9 8.4 %collective-permute-start.4 = (bf16[512,256]{1,0:T(8,128)(2,1)S(1)}, bf16[512,256]{1,0:T(8,128)(2,1)S(1)}, u32[]{:S(2)}, u32[]{:S(2)}) collective-permute-start(bf16[512,256]{1,0:T(8,128)(2,1)S(1)} %get-tuple-element.30.k0), channel_id=1, source_target_pairs={{0,32},{32,64},{64,96},{96,0},{1,33},{33,65},{65,97},{97,1},{2,34}... | collective-permute-start | bytes 786440 | tf_op jit(solution)/shard_map/ppermute | solution.py:527
  16.1 13.8 %collective-permute-start.3 = (bf16[512,256]{1,0:T(8,128)(2,1)S(1)}, bf16[512,256]{1,0:T(8,128)(2,1)S(1)}, u32[]{:S(2)}, u32[]{:S(2)}) collective-permute-start(bf16[512,256]{1,0:T(8,128)(2,1)S(1)} %get-tuple-element.29.q0), channel_id=1, source_target_pairs={{0,24},{8,0},{16,8},{24,16},{1,25},{9,1},{17,9},{25,17},{2,26},{10... | collective-permute-start | bytes 786440 | tf_op jit(solution)/shard_map/ppermute | solution.py:527
  17.6 12.3 %collective-permute-start.6 = (bf16[512,256]{1,0:T(8,128)(2,1)S(1)}, bf16[512,256]{1,0:T(8,128)(2,1)S(1)}, u32[]{:S(2)}, u32[]{:S(2)}) collective-permute-start(bf16[512,256]{1,0:T(8,128)(2,1)S(1)} %get-tuple-element.30.k0), channel_id=1, source_target_pairs={{0,96},{32,0},{64,32},{96,64},{1,97},{33,1},{65,33},{97,65},{2,98}... | collective-permute-start | bytes 786440 | tf_op jit(solution)/shard_map/ppermute | solution.py:527
  22.5 8.0 %collective-permute-start.2 = (bf16[512,256]{1,0:T(8,128)(2,1)S(1)}, bf16[512,256]{1,0:T(8,128)(2,1)S(1)}, u32[]{:S(2)}, u32[]{:S(2)}) collective-permute-start(bf16[512,256]{1,0:T(8,128)(2,1)S(1)} %collective-permute-done.1.q1), channel_id=1, source_target_pairs={{0,8},{8,16},{16,24},{24,0},{1,9},{9,17},{17,25},{25,1},{2,10},{10... | collective-permute-start | bytes 786440 | tf_op jit(solution)/shard_map/ppermute | solution.py:528
  23.3 7.5 %collective-permute-start.5 = (bf16[512,256]{1,0:T(8,128)(2,1)S(1)}, bf16[512,256]{1,0:T(8,128)(2,1)S(1)}, u32[]{:S(2)}, u32[]{:S(2)}) collective-permute-start(bf16[512,256]{1,0:T(8,128)(2,1)S(1)} %collective-permute-done.4.k1), channel_id=1, source_target_pairs={{0,32},{32,64},{64,96},{96,0},{1,33},{33,65},{65,97},{97,1},{2,34}... | collective-permute-start | bytes 786440 | tf_op jit(solution)/shard_map/ppermute | solution.py:528
  37.3 6.9 %collective-permute-start.9 = (f32[48,128]{1,0:T(8,128)S(1)}, f32[48,128]{1,0:T(8,128)S(1)}, u32[]{:S(2)}, u32[]{:S(2)}) collective-permute-start(f32[48,128]{1,0:T(8,128)S(1)} %row_stats.1.s0), channel_id=1, source_target_pairs={{0,24},{8,0},{16,8},{24,16},{1,25},{9,1},{17,9},{25,17},{2,26},{10... | collective-permute-start | bytes 73736 | tf_op jit(solution)/shard_map/ppermute | solution.py:522
  39.6 4.6 %collective-permute-start.8 = (f32[48,128]{1,0:T(8,128)S(1)}, f32[48,128]{1,0:T(8,128)S(1)}, u32[]{:S(2)}, u32[]{:S(2)}) collective-permute-start(f32[48,128]{1,0:T(8,128)S(1)} %row_stats.1.s0), channel_id=1, source_target_pairs={{0,16},{8,24},{16,0},{24,8},{1,17},{9,25},{17,1},{25,9},{2,18},{10... | collective-permute-start | bytes 73736 | tf_op jit(solution)/shard_map/ppermute | solution.py:522
  40.5 3.9 %collective-permute-start.7 = (f32[48,128]{1,0:T(8,128)S(1)}, f32[48,128]{1,0:T(8,128)S(1)}, u32[]{:S(2)}, u32[]{:S(2)}) collective-permute-start(f32[48,128]{1,0:T(8,128)S(1)} %row_stats.1.s0), channel_id=1, source_target_pairs={{0,8},{8,16},{16,24},{24,0},{1,9},{9,17},{17,25},{25,1},{2,10},{10... | collective-permute-start | bytes 73736 | tf_op jit(solution)/shard_map/ppermute | solution.py:522
  40.9 39.5 %copy-start.1 = (bf16[128,256]{1,0:T(8,128)(2,1)S(1)}, bf16[128,256]{1,0:T(8,128)(2,1)}, u32[]{:S(2)}) copy-start(bf16[128,256]{1,0:T(8,128)(2,1)} %uq.1) | copy-start | bytes 196612
  40.9 39.5 %copy-start.2 = (bf16[128,256]{1,0:T(8,128)(2,1)S(1)}, bf16[128,256]{1,0:T(8,128)(2,1)}, u32[]{:S(2)}) copy-start(bf16[128,256]{1,0:T(8,128)(2,1)} %uv.1) | copy-start | bytes 196612
  40.9 19.8 %collective-permute-start.16 = (bf16[256,256]{1,0:T(8,128)(2,1)S(1)}, bf16[256,256]{1,0:T(8,128)(2,1)S(1)}, u32[]{:S(2)}, u32[]{:S(2)}) collective-permute-start(bf16[256,256]{1,0:T(8,128)(2,1)S(1)} %copy-done.4), channel_id=1, source_target_pairs={{0,4},{4,0},{1,5},{5,1},{2,6},{6,2},{3,7},{7,3},{8,12},{12,8},{9,1... | collective-permute-start | bytes 393224 | tf_op jit(solution)/shard_map/ppermute | solution.py:518
  56.4 5.5 %collective-permute-start.11 = (bf16[512,128]{1,0:T(8,128)(2,1)S(1)}, bf16[512,128]{1,0:T(8,128)(2,1)S(1)}, u32[]{:S(2)}, u32[]{:S(2)}) collective-permute-start(bf16[512,128]{1,0:T(8,128)(2,1)S(1)} %get-tuple-element.34), channel_id=1, source_target_pairs={{0,64},{32,96},{64,0},{96,32},{1,65},{33,97},{65,1},{97,33},{2,66}... | collective-permute-start | bytes 393224 | tf_op jit(solution)/shard_map/ppermute | solution.py:532
  58.2 11.5 %collective-permute-start.13 = (bf16[512,384]{1,0:T(8,128)(2,1)S(1)}, bf16[512,384]{1,0:T(8,128)(2,1)S(1)}, u32[]{:S(2)}, u32[]{:S(2)}) collective-permute-start(bf16[512,384]{1,0:T(8,128)(2,1)S(1)} %get-tuple-element.36), channel_id=1, source_target_pairs={{0,24},{8,0},{16,8},{24,16},{1,25},{9,1},{17,9},{25,17},{2,26},{10... | collective-permute-start | bytes 1179656 | tf_op jit(solution)/shard_map/ppermute | solution.py:532
  59.4 10.2 %collective-permute-start.14 = (bf16[512,384]{1,0:T(8,128)(2,1)S(1)}, bf16[512,384]{1,0:T(8,128)(2,1)S(1)}, u32[]{:S(2)}, u32[]{:S(2)}) collective-permute-start(bf16[512,384]{1,0:T(8,128)(2,1)S(1)} %get-tuple-element.37), channel_id=1, source_target_pairs={{0,16},{8,24},{16,0},{24,8},{1,17},{9,25},{17,1},{25,9},{2,18},{10... | collective-permute-start | bytes 1179656 | tf_op jit(solution)/shard_map/ppermute | solution.py:532
  60.7 19.6 %collective-permute-start.15 = (bf16[512,384]{1,0:T(8,128)(2,1)S(1)}, bf16[512,384]{1,0:T(8,128)(2,1)S(1)}, u32[]{:S(2)}, u32[]{:S(2)}) collective-permute-start(bf16[512,384]{1,0:T(8,128)(2,1)S(1)} %get-tuple-element.38), channel_id=1, source_target_pairs={{0,8},{8,16},{16,24},{24,0},{1,9},{9,17},{17,25},{25,1},{2,10},{10... | collective-permute-start | bytes 1179656 | tf_op jit(solution)/shard_map/ppermute | solution.py:532
  60.7 6.9 %collective-permute-start.10 = (f32[512,128]{1,0:T(8,128)S(1)}, f32[512,128]{1,0:T(8,128)S(1)}, u32[]{:S(2)}, u32[]{:S(2)}) collective-permute-start(f32[512,128]{1,0:T(8,128)S(1)} %get-tuple-element.33), channel_id=1, source_target_pairs={{0,96},{32,0},{64,32},{96,64},{1,97},{33,1},{65,33},{97,65},{2,98}... | collective-permute-start | bytes 786440 | tf_op jit(solution)/shard_map/ppermute | solution.py:532
  61.9 7.7 %collective-permute-start.12 = (f32[512,128]{1,0:T(8,128)S(1)}, f32[512,128]{1,0:T(8,128)S(1)}, u32[]{:S(2)}, u32[]{:S(2)}) collective-permute-start(f32[512,128]{1,0:T(8,128)S(1)} %get-tuple-element.35), channel_id=1, source_target_pairs={{0,32},{32,64},{64,96},{96,0},{1,33},{33,65},{65,97},{97,1},{2,34}... | collective-permute-start | bytes 786440 | tf_op jit(solution)/shard_map/ppermute | solution.py:532
  81.2 1.7 %collective-permute-start.17 = (f32[256,256]{1,0:T(8,128)S(1)}, f32[256,256]{1,0:T(8,128)S(1)}, u32[]{:S(2)}, u32[]{:S(2)}) collective-permute-start(f32[256,256]{1,0:T(8,128)S(1)} %get-tuple-element.41), channel_id=1, source_target_pairs={{0,4},{4,0},{1,5},{5,1},{2,6},{6,2},{3,7},{7,3},{8,12},{12,8},{9,1... | collective-permute-start | bytes 786440 | tf_op jit(solution)/shard_map/ppermute | solution.py:518
  83.0 7.4 %collective-permute-start.18 = (bf16[256,256]{1,0:T(8,128)(2,1)S(1)}, bf16[256,256]{1,0:T(8,128)(2,1)S(1)}, u32[]{:S(2)}, u32[]{:S(2)}) collective-permute-start(bf16[256,256]{1,0:T(8,128)(2,1)S(1)} %get-tuple-element.43), channel_id=1, source_target_pairs={{0,1},{1,2},{2,3},{3,0},{4,5},{5,6},{6,7},{7,4},{8,9},{9,10},{10,1... | collective-permute-start | bytes 393224 | tf_op jit(solution)/shard_map/ppermute | solution.py:527
  84.7 5.7 %collective-permute-start.20 = (bf16[256,256]{1,0:T(8,128)(2,1)S(1)}, bf16[256,256]{1,0:T(8,128)(2,1)S(1)}, u32[]{:S(2)}, u32[]{:S(2)}) collective-permute-start(bf16[256,256]{1,0:T(8,128)(2,1)S(1)} %get-tuple-element.43), channel_id=1, source_target_pairs={{0,3},{1,0},{2,1},{3,2},{4,7},{5,4},{6,5},{7,6},{8,11},{9,8},{10,9... | collective-permute-start | bytes 393224 | tf_op jit(solution)/shard_map/ppermute | solution.py:527
  90.4 5.3 %collective-permute-start.19 = (bf16[256,256]{1,0:T(8,128)(2,1)S(1)}, bf16[256,256]{1,0:T(8,128)(2,1)S(1)}, u32[]{:S(2)}, u32[]{:S(2)}) collective-permute-start(bf16[256,256]{1,0:T(8,128)(2,1)S(1)} %collective-permute-done.18.r1), channel_id=1, source_target_pairs={{0,1},{1,2},{2,3},{3,0},{4,5},{5,6},{6,7},{7,4},{8,9},{9,10},{10,1... | collective-permute-start | bytes 393224 | tf_op jit(solution)/shard_map/ppermute | solution.py:528
  96.1 3.6 %collective-permute-start.21 = (f32[640,256]{1,0:T(8,128)S(1)}, f32[640,256]{1,0:T(8,128)S(1)}, u32[]{:S(2)}, u32[]{:S(2)}) collective-permute-start(f32[640,256]{1,0:T(8,128)S(1)} %get-tuple-element.45), channel_id=1, source_target_pairs={{0,4},{4,0},{1,5},{5,1},{2,6},{6,2},{3,7},{7,3},{8,12},{12,8},{9,1... | collective-permute-start | bytes 1966088 | tf_op jit(solution)/shard_map/ppermute | solution.py:518
  100.5 13.0 %all-to-all-start = ((bf16[16,48,256]{2,1,0:T(8,128)(2,1)}), bf16[16,48,256]{2,1,0:T(8,128)(2,1)S(1)}, u32[]{:S(2)}, u32[]{:S(2)}) async-start(bf16[16,48,256]{2,1,0:T(8,128)(2,1)} %pack.1), calls=%async_computation | async-start | bytes 786432 | tf_op jit(solution)/shard_map/all_to_all | solution.py:550
  104.3 1.6 %collective-permute-start.22 = (bf16[256,128]{1,0:T(8,128)(2,1)S(1)}, bf16[256,128]{1,0:T(8,128)(2,1)S(1)}, u32[]{:S(2)}, u32[]{:S(2)}) collective-permute-start(bf16[256,128]{1,0:T(8,128)(2,1)S(1)} %get-tuple-element.47), channel_id=1, source_target_pairs={{0,4},{4,0},{1,5},{5,1},{2,6},{6,2},{3,7},{7,3},{8,12},{12,8},{9,1... | collective-permute-start | bytes 196616 | tf_op jit(solution)/shard_map/ppermute | solution.py:518
  139.5 6.4 %collective-permute-start.23 = (bf16[64,48,256]{2,1,0:T(8,128)(2,1)S(1)}, bf16[64,48,256]{2,1,0:T(8,128)(2,1)S(1)}, u32[]{:S(2)}, u32[]{:S(2)}) collective-permute-start(bf16[64,48,256]{2,1,0:T(8,128)(2,1)S(1)} %all_to_all.10.own), channel_id=1, source_target_pairs={{0,4},{4,0},{1,5},{5,1},{2,6},{6,2},{3,7},{7,3},{8,12},{12,8},{9,1... | collective-permute-start | bytes 4718600 | tf_op jit(solution)/shard_map/ppermute | solution.py:518
  (2 other events, 23.9 us)

commit v9 on v8

--- a/solution.py
+++ b/solution.py
@@ -23,7 +23,7 @@
 bf16 = jnp.bfloat16
 WIRE = f32
 WIRE2 = bf16
-KT = 1280
+KT = 2560
 VMEM = pl.BlockSpec(memory_space=pltpu.VMEM)
 SMEM = pl.BlockSpec(memory_space=pltpu.SMEM)
 ANY = pl.BlockSpec(memory_space=pl.ANY)
@@ -448,46 +448,71 @@
     )(mine, theirs, up)
 
 
-def emit_kernel(own, other, o_keep, o_other, att, down_q, up_q, down_v, up_v):
-    zz = pl.program_id(0)
-    halves = [own, other]
-    for c in range(2):
-        @pl.when(lax.axis_index("c") == c)
-        def _():
-            for cc in range(2):
-                src = halves[(c + cc) % 2]
-                for i in range(16):
-                    part = src[zz * 16 + i].astype(f32)
-                    at = cc * 640 + i * 40
-                    down_q[at:at + 40, :] = part[:40, :RANK]
-                    down_v[at:at + 40, :] = part[:40, RANK:]
-
-            @pl.when(zz == 0)
+def half_kernel(src, down_q, down_v, up):
+    for i in range(16):
+        part = src[pl.program_id(0) * 16 + i].astype(f32)
+        down_q[i * 40:(i + 1) * 40, :] = part[:40, :RANK]
+        down_v[i * 40:(i + 1) * 40, :] = part[:40, RANK:]
+
+    @pl.when(pl.program_id(0) == 0)
+    def _():
+        for i in range(16):
+            up[i * 8:(i + 1) * 8, :] = src[lax.axis_index("z") * 16 + i].astype(f32)[40:, :]
+
+
+def own_kernel(src, down_q, down_v, up):
+    half_kernel(src, down_q, down_v, up)
+
+
+def other_kernel(src, own_up, o_keep, o_other, q_in, v_in, att, down_q, up_q, down_v, up_v, other_up):
+    half_kernel(src, down_q, down_v, other_up)
+
+    @pl.when(pl.program_id(0) == 0)
+    def _():
+        ups, outs = [own_up, other_up], [o_keep, o_other]
+        for c in range(2):
+            @pl.when(lax.axis_index("c") == c)
             def _():
-                outs = [o_keep, o_other]
                 for cc in range(2):
-                    src = halves[(c + cc) % 2]
-                    att[:, cc * HEAD:(cc + 1) * HEAD] = outs[(c + cc) % 2][...]
-                    for i in range(16):
-                        part = src[lax.axis_index("z") * 16 + i].astype(f32)
-                        up_q[i * 8:(i + 1) * 8, cc * HEAD:(cc + 1) * HEAD] = part[40:, :HEAD]
-                        up_v[i * 8:(i + 1) * 8, cc * HEAD:(cc + 1) * HEAD] = part[40:, HEAD:]
-
-
-def emit(own, other, o_keep, o_other):
-    whole = lambda a: pl.BlockSpec(a, lambda k: (0,) * len(a))
-    return pl.pallas_call(
-        emit_kernel,
+                    lanes = slice(cc * HEAD, (cc + 1) * HEAD)
+                    att[:, lanes] = outs[(c + cc) % 2][...]
+                    up_q[:, lanes] = ups[(c + cc) % 2][:, :RANK]
+                    up_v[:, lanes] = ups[(c + cc) % 2][:, RANK:]
+
+
+def whole_block(shape):
+    return pl.BlockSpec(shape, lambda k: (0,) * len(shape))
+
+
+def emit_own(own):
+    mine = pl.BlockSpec((640, RANK), lambda k: (k * 2 + lax.axis_index("c"), 0))
+    down = jax.ShapeDtypeStruct((5120, RANK), f32)
+    return pl.pallas_call(
+        own_kernel,
         grid=(4,),
-        in_specs=[whole(a.shape) for a in (own, other, o_keep, o_other)],
-        out_specs=[whole((256, 256)), pl.BlockSpec((1280, RANK), lambda k: (k, 0)), whole((RANK, 256)),
-                   pl.BlockSpec((1280, RANK), lambda k: (k, 0)), whole((RANK, 256))],
-        out_shape=[jax.ShapeDtypeStruct((256, 256), bf16), jax.ShapeDtypeStruct((5120, RANK), f32),
-                   jax.ShapeDtypeStruct((RANK, 256), f32), jax.ShapeDtypeStruct((5120, RANK), f32),
-                   jax.ShapeDtypeStruct((RANK, 256), f32)],
-        compiler_params=PARAMS,
-        name="emit",
-    )(own, other, o_keep, o_other)
+        in_specs=[whole_block(own.shape)],
+        out_specs=[mine, mine, whole_block((RANK, 256))],
+        out_shape=[down, down, jax.ShapeDtypeStruct((RANK, 256), f32)],
+        compiler_params=PARAMS,
+        name="emit_own",
+    )(own)
+
+
+def emit_other(other, own_up, o_keep, o_other, down_q, down_v):
+    theirs = pl.BlockSpec((640, RANK), lambda k: (k * 2 + 1 - lax.axis_index("c"), 0))
+    down = jax.ShapeDtypeStruct((5120, RANK), f32)
+    up = jax.ShapeDtypeStruct((RANK, 256), f32)
+    return pl.pallas_call(
+        other_kernel,
+        grid=(4,),
+        in_specs=[whole_block(a.shape) for a in (other, own_up, o_keep, o_other)] + [ANY, ANY],
+        out_specs=[whole_block((256, 256)), theirs, whole_block((RANK, 256)), theirs, whole_block((RANK, 256))],
+        out_shape=[jax.ShapeDtypeStruct((256, 256), bf16), down, up, down, up],
+        input_output_aliases={4: 1, 5: 3},
+        scratch_shapes=[pltpu.VMEM((RANK, 256), f32)],
+        compiler_params=PARAMS,
+        name="emit_other",
+    )(other, own_up, o_keep, o_other, down_q, down_v)
 
 
 def total_kernel(parts, after, out):
@@ -546,10 +571,11 @@
     o_keep, o_send, rg_keep, rg_send, up = finish(b, a, rank, swap(rank), uq, uv, act_t)
     o_other = swap(o_send)
     rg, low = add_cores(rg_keep, swap(rg_send))
-    mine, theirs = down_terms(act_t, rg, relay(low, "z")[1:])
+    mine, theirs = down_terms(act_t, rg, spread(low, "z")[1:])
     terms = lax.all_to_all(pack(mine, swap(theirs), up), ("x", "y"), 0, 0, tiled=True)
     wide = lax.all_to_all(total_for_all(terms, o_other), ("z", "x", "y"), 0, 0, tiled=True)
-    att, down_q, up_q, down_v, up_v = emit(wide, swap(wide), o_keep, o_other)
+    down_q, down_v, own_up = emit_own(wide)
+    att, down_q, up_q, down_v, up_v = emit_other(swap(wide), own_up, o_keep, o_other, down_q, down_v)
     return att, down_q, up_q, down_v, up_v
 
 

time: 149 us -> 148 us (level)
  waiting for transfers between devices: 47.8 us -> 45.4 us
    ppermute x3 -> x6, waiting for transfers between devices: 0.19 us -> 8.63 us  [spread(): one, three, two = [lax.ppermute(a, axis, ring(4, d)) for d in (1, 3, 2)]]
    ppermute x3 -> x2, waiting for transfers between devices: 6.23 us -> 0.89 us  [relay(): return [a, one, lax.ppermute(one, axis, ring(4, 1)), three]]
    ppermute x3 -> x6, starting transfers between devices: 3.55 us -> 8.08 us  [spread(): one, three, two = [lax.ppermute(a, axis, ring(4, d)) for d in (1, 3, 2)]]
    ppermute x6 -> x4, starting transfers between devices: 9.55 us -> 5.65 us  [relay(): one, three = [lax.ppermute(a, axis, ring(4, d)) for d in (1, 3)]]
    ppermute x6 -> x4, waiting for transfers between devices: 7.7 us -> 4.21 us  [relay(): one, three = [lax.ppermute(a, axis, ring(4, d)) for d in (1, 3)]]
    ppermute x6, waiting for transfers between devices: 8.2 us -> 6.2 us  [swap(): return lax.ppermute(a, 'c', ring(2, 1))]
    pallas_call x1 -> x2, Pallas kernels: 2.83 us -> 4.17 us  [the longest x1 2.18 us: emit_other(): pl.pallas_call(other_kernel, grid=(4,), in_specs=[whole_block(a.shape) fo...]
  transfers between devices with their start and end apart: 25 -> 25, of which waited for: 16 -> 17; matrix products, arithmetic and copies ran while one was open for 0% -> 0% of each run, Pallas kernels for 12% -> 14%
where the time goes in v9:
time: 148 us
  waiting for transfers between devices  45.4 us (31%)
  Pallas kernels  40 us (27%)
  starting transfers between devices  34.1 us (23%)
  blocking collectives  26.2 us (18%)
    all_to_all x1, blocking collectives, local(): lax.all_to_all(total_for_all(terms, o_other), ('z', 'x', 'y'), 0, 0, tile...  26.2 us
    ppermute x6, waiting for transfers between devices, collect(): lax.ppermute(parts[d], axis, ring(4, -d))  17.8 us
    pallas_call x1, Pallas kernels, attention_grads(): pl.pallas_call(grads_kernel, in_specs=[SMEM] + [VMEM] * 12, out_specs=[VM...  12 us
    ppermute x6, starting transfers between devices, swap(): return lax.ppermute(a, 'c', ring(2, 1))  10.3 us
    pallas_call x1, Pallas kernels, project(): pl.pallas_call(proj_kernel, grid=(width // KT,), in_specs=[pl.BlockSpec((...  8.8 us
    ppermute x6, waiting for transfers between devices, spread(): one, three, two = [lax.ppermute(a, axis, ring(4, d)) for d in (1, 3, 2)]  8.63 us
    ppermute x6, starting transfers between devices, spread(): one, three, two = [lax.ppermute(a, axis, ring(4, d)) for d in (1, 3, 2)]  8.08 us
    all_to_all x1, waiting for transfers between devices, local(): lax.all_to_all(pack(mine, swap(theirs), up), ('x', 'y'), 0, 0, tiled=True)  7.6 us
  transfers between devices with their start and end apart: 25, of which 17 were waited for; matrix products, arithmetic and copies ran while one was open for 0% of the time, Pallas kernels for 14%

profile of v9, /device:TPU:1, one launch (start us, length us, event | category | flops | bytes accessed | tf_op | source)
XLA Modules:
  0.0 147.6 jit_solution(3650752599604079109)
XLA Ops:
  0.7 8.8 %project.1 = (bf16[256,512]{1,0:T(8,128)(2,1)}, bf16[256,512]{1,0:T(8,128)(2,1)}, bf16[256,256]{1,0:T(8,128)(2,1)}) custom-call(bf16[256,5120]{1,0:T(8,128)(2,1)} %act.3, bf16[5120,256]{1,0:T(8,128)(2,1)} %wq.1, bf16[5120,256]{1,0:T(8,128)(2,1)} %wk.1, bf16[5120,256]{1,0:T(8,128)(2,1)} %wv.1, bf16[5120,128]{1,0:T(8,128)(2,1)} %down_q.1, ...), custom_call_target="tpu_custom_call" | custom-call | flops 2684354560 | bytes 13107200 | tf_op jit(solution)/shard_map/project/pallas_call | solution.py:86
  9.5 1.5 %collective-permute-start = (bf16[256,512]{1,0:T(8,128)(2,1)}, bf16[256,512]{1,0:T(8,128)(2,1)S(1)}, u32[]{:S(2)}, u32[]{:S(2)}) collective-permute-start(bf16[256,512]{1,0:T(8,128)(2,1)} %get-tuple-element.31), channel_id=1, source_target_pairs={{0,4},{4,0},{1,5},{5,1},{2,6},{6,2},{3,7},{7,3},{8,12},{12,8},{9,1... | collective-permute-start | bytes 786440 | tf_op jit(solution)/shard_map/ppermute | solution.py:543
  11.0 1.4 collective-permute-done.other
  13.3 1.5 collective-permute-start.1
  14.8 1.2 collective-permute-start.4
  16.0 1.5 %collective-permute-start.3 = (bf16[512,256]{1,0:T(8,128)(2,1)S(1)}, bf16[512,256]{1,0:T(8,128)(2,1)S(1)}, u32[]{:S(2)}, u32[]{:S(2)}) collective-permute-start(bf16[512,256]{1,0:T(8,128)(2,1)S(1)} %get-tuple-element.32.q0), channel_id=1, source_target_pairs={{0,24},{8,0},{16,8},{24,16},{1,25},{9,1},{17,9},{25,17},{2,26},{10... | collective-permute-start | bytes 786440 | tf_op jit(solution)/shard_map/ppermute | solution.py:552
  17.5 1.5 collective-permute-start.6
  19.0 3.5 %collective-permute-done.1.q1 = bf16[512,256]{1,0:T(8,128)(2,1)S(1)} collective-permute-done((bf16[512,256]{1,0:T(8,128)(2,1)S(1)}, bf16[512,256]{1,0:T(8,128)(2,1)S(1)}, u32[]{:S(2)}, u32[]{:S(2)}) %collective-permute-start.1) | collective-permute-done | bytes 262176 | tf_op jit(solution)/shard_map/ppermute | solution.py:552
  23.8 6.0 %lists.1 = s32[24,128]{1,0:T(8,128)S(1)} custom-call(s32[64]{0:T(128)S(1)} %copy-done.5, s32[64,64]{1,0:T(8,128)S(1)} %multiply_add_fusion.packed), custom_call_target="tpu_custom_call" | custom-call | tf_op jit(solution)/shard_map/lists/pallas_call | solution.py:149
  30.7 6.6 %row_stats.1.s0 = f32[48,128]{1,0:T(8,128)S(1)} custom-call(s32[24,128]{1,0:T(8,128)S(1)} %lists.1, bf16[512,256]{1,0:T(8,128)(2,1)S(1)} %get-tuple-element.32.q0, bf16[512,256]{1,0:T(8,128)(2,1)S(1)} %collective-permute-done.1.q1, bf16[512,256]{1,0:T(8,128)(2,1)S(1)} %collective-permute-done.2.q2, bf16[512,256]{1,0:T(8,128)(2,1)S(1)} %collective-permute-done.3.q3, ...), custom_call_target="tpu_custom_call" | custom-call | tf_op jit(solution)/shard_map/row_stats/pallas_call | solution.py:222
  37.3 2.2 %collective-permute-start.9 = (f32[48,128]{1,0:T(8,128)S(1)}, f32[48,128]{1,0:T(8,128)S(1)}, u32[]{:S(2)}, u32[]{:S(2)}) collective-permute-start(f32[48,128]{1,0:T(8,128)S(1)} %row_stats.1.s0), channel_id=1, source_target_pairs={{0,24},{8,0},{16,8},{24,16},{1,25},{9,1},{17,9},{25,17},{2,26},{10... | collective-permute-start | bytes 73736 | tf_op jit(solution)/shard_map/ppermute | solution.py:547
  40.8 3.3 %collective-permute-start.16 = (bf16[256,256]{1,0:T(8,128)(2,1)S(1)}, bf16[256,256]{1,0:T(8,128)(2,1)S(1)}, u32[]{:S(2)}, u32[]{:S(2)}) collective-permute-start(bf16[256,256]{1,0:T(8,128)(2,1)S(1)} %copy-done.4), channel_id=1, source_target_pairs={{0,4},{4,0},{1,5},{5,1},{2,6},{6,2},{3,7},{7,3},{8,12},{12,8},{9,1... | collective-permute-start | bytes 393224 | tf_op jit(solution)/shard_map/ppermute | solution.py:543
  44.3 12.0 %attention_grads.1 = (f32[512,256]{1,0:T(8,128)S(1)}, bf16[512,384]{1,0:T(8,128)(2,1)S(1)}, bf16[512,384]{1,0:T(8,128)(2,1)S(1)}, bf16[512,384]{1,0:T(8,128)(2,1...) custom-call(s32[24,128]{1,0:T(8,128)S(1)} %lists.1, ...), custom_call_target="tpu_custom_call" | custom-call | tf_op jit(solution)/shard_map/attention_grads/pallas_call | solution.py:320
  56.3 1.8 %collective-permute-start.11 = (bf16[512,128]{1,0:T(8,128)(2,1)S(1)}, bf16[512,128]{1,0:T(8,128)(2,1)S(1)}, u32[]{:S(2)}, u32[]{:S(2)}) collective-permute-start(bf16[512,128]{1,0:T(8,128)(2,1)S(1)} %get-tuple-element.37), channel_id=1, source_target_pairs={{0,64},{32,96},{64,0},{96,32},{1,65},{33,97},{65,1},{97,33},{2,66}... | collective-permute-start | bytes 393224 | tf_op jit(solution)/shard_map/ppermute | solution.py:557
  58.1 1.2 collective-permute-start.13
  59.3 1.3 collective-permute-start.14
  60.7 1.1 collective-permute-start.10
  62.5 5.1 %collective-permute-done.10.b1 = f32[512,128]{1,0:T(8,128)S(1)} collective-permute-done((f32[512,128]{1,0:T(8,128)S(1)}, f32[512,128]{1,0:T(8,128)S(1)}, u32[]{:S(2)}, u32[]{:S(2)}) %collective-permute-start.10) | collective-permute-done | bytes 262176 | tf_op jit(solution)/shard_map/ppermute | solution.py:557
  67.6 2.0 %collective-permute-done.12.b3 = f32[512,128]{1,0:T(8,128)S(1)} collective-permute-done((f32[512,128]{1,0:T(8,128)S(1)}, f32[512,128]{1,0:T(8,128)S(1)}, u32[]{:S(2)}, u32[]{:S(2)}) %collective-permute-start.12) | collective-permute-done | bytes 262176 | tf_op jit(solution)/shard_map/ppermute | solution.py:557
  69.6 10.7 %collective-permute-done.15.a3 = bf16[512,384]{1,0:T(8,128)(2,1)S(1)} collective-permute-done((bf16[512,384]{1,0:T(8,128)(2,1)S(1)}, bf16[512,384]{1,0:T(8,128)(2,1)S(1)}, u32[]{:S(2)}, u32[]{:S(2)}) %collective-permute-start.15) | collective-permute-done | bytes 393248 | tf_op jit(solution)/shard_map/ppermute | solution.py:557
  81.7 1.2 collective-permute-done.17.other
  82.9 3.8 %collective-permute-start.20 = (bf16[256,256]{1,0:T(8,128)(2,1)S(1)}, bf16[256,256]{1,0:T(8,128)(2,1)S(1)}, u32[]{:S(2)}, u32[]{:S(2)}) collective-permute-start(bf16[256,256]{1,0:T(8,128)(2,1)S(1)} %get-tuple-element.46), channel_id=1, source_target_pairs={{0,3},{1,0},{2,1},{3,2},{4,7},{5,4},{6,5},{7,6},{8,11},{9,8},{10,9... | collective-permute-start | bytes 393224 | tf_op jit(solution)/shard_map/ppermute | solution.py:547
  87.5 4.9 %collective-permute-done.20.r3 = bf16[256,256]{1,0:T(8,128)(2,1)S(1)} collective-permute-done((bf16[256,256]{1,0:T(8,128)(2,1)S(1)}, bf16[256,256]{1,0:T(8,128)(2,1)S(1)}, u32[]{:S(2)}, u32[]{:S(2)}) %collective-permute-start.20) | collective-permute-done | bytes 131104 | tf_op jit(solution)/shard_map/ppermute | solution.py:547
  92.7 3.2 %collective-permute-done.18.r1 = bf16[256,256]{1,0:T(8,128)(2,1)S(1)} collective-permute-done((bf16[256,256]{1,0:T(8,128)(2,1)S(1)}, bf16[256,256]{1,0:T(8,128)(2,1)S(1)}, u32[]{:S(2)}, u32[]{:S(2)}) %collective-permute-start.18) | collective-permute-done | bytes 131104 | tf_op jit(solution)/shard_map/ppermute | solution.py:547
  97.2 1.7 %collective-permute-done.21.theirs = f32[640,256]{1,0:T(8,128)S(1)} collective-permute-done((f32[640,256]{1,0:T(8,128)S(1)}, f32[640,256]{1,0:T(8,128)S(1)}, u32[]{:S(2)}, u32[]{:S(2)}) %collective-permute-start.21) | collective-permute-done | bytes 655392 | tf_op jit(solution)/shard_map/ppermute | solution.py:543
  99.7 3.7 %all-to-all-start = ((bf16[16,48,256]{2,1,0:T(8,128)(2,1)}), bf16[16,48,256]{2,1,0:T(8,128)(2,1)S(1)}, u32[]{:S(2)}, u32[]{:S(2)}) async-start(bf16[16,48,256]{2,1,0:T(8,128)(2,1)} %pack.1), calls=%async_computation | async-start | bytes 786432 | tf_op jit(solution)/shard_map/all_to_all | solution.py:575
  105.1 7.6 %all-to-all-done.parts = bf16[16,48,256]{2,1,0:T(8,128)(2,1)S(1)} async-done(((bf16[16,48,256]{2,1,0:T(8,128)(2,1)}), bf16[16,48,256]{2,1,0:T(8,128)(2,1)S(1)}, u32[]{:S(2)}, u32[]{:S(2)}) %all-to-all-start) | async-done | bytes 393248 | tf_op jit(solution)/shard_map/all_to_all | solution.py:575
  112.8 26.2 %all_to_all.10.src = bf16[64,48,256]{2,1,0:T(8,128)(2,1)S(1)} all-to-all(bf16[64,48,256]{2,1,0:T(8,128)(2,1)S(1)} %total_for_all.1), channel_id=1, replica_groups=mesh['x'=4,'y'=4,'c'=2,'z'=4] {'z','x','y'}, dimensions={0} | all-to-all | bytes 3145728 | tf_op jit(solution)/shard_map/all_to_all | solution.py:576
  139.0 3.4 %collective-permute-start.23 = (bf16[64,48,256]{2,1,0:T(8,128)(2,1)S(1)}, bf16[64,48,256]{2,1,0:T(8,128)(2,1)S(1)}, u32[]{:S(2)}, u32[]{:S(2)}) collective-permute-start(bf16[64,48,256]{2,1,0:T(8,128)(2,1)S(1)} %all_to_all.10.src), channel_id=1, source_target_pairs={{0,4},{4,0},{1,5},{5,1},{2,6},{6,2},{3,7},{7,3},{8,12},{12,8},{9,1... | collective-permute-start | bytes 4718600 | tf_op jit(solution)/shard_map/ppermute | solution.py:543
  142.4 2.0 %emit_own.1 = (f32[5120,128]{1,0:T(8,128)}, f32[5120,128]{1,0:T(8,128)}, f32[128,256]{1,0:T(8,128)S(1)}) custom-call(bf16[64,48,256]{2,1,0:T(8,128)(2,1)S(1)} %all_to_all.10.src), custom_call_target="tpu_custom_call" | custom-call | tf_op jit(solution)/shard_map/emit_own/pallas_call | solution.py:490
  144.4 1.0 collective-permute-done.23.src
  145.4 2.2 %emit_other.1 = (bf16[256,256]{1,0:T(8,128)(2,1)}, f32[5120,128]{1,0:T(8,128)}, f32[128,256]{1,0:T(8,128)}, f32[5120,128]{1,0:T(8,128)}, f32[128,256]{1,0:T(8,128)}) custom-call(bf16[64,48,256]{2,1,0:T(8,128)(2,1)S(1)} %collective-permute-done.23.src, f32[128,256]{1,0:T(8,128)S(1)} %get-tuple-element.51.own_up, ...), custom_call_target="tpu_custom_call", output_to_operand_aliasing={{1}: (4, {}), {3}: (5, {})} | custom-call | tf_op jit(solution)/shard_map/emit_other/pallas_call | solution.py:505
  (52 shorter events, 11.7 us)
Async XLA Ops:
  0.6 22.9 %copy-start.8 = (s32[4]{0:T(128)S(1)}, s32[4]{0:T(128)}, u32[]{:S(2)}) copy-start(s32[4]{0:T(128)} %constant.6.clone) | copy-start | bytes 52
  0.7 23.1 %copy-start.7 = (s32[64,64]{1,0:T(8,128)S(1)}, s32[64,64]{1,0:T(8,128)}, u32[]{:S(2)}) copy-start(s32[64,64]{1,0:T(8,128)} %param.22) | copy-start | bytes 49156
  0.7 23.1 %copy-start.5 = (s32[64]{0:T(128)S(1)}, s32[64]{0:T(128)}, u32[]{:S(2)}) copy-start(s32[64]{0:T(128)} %slot.1) | copy-start | bytes 772
  9.5 52.7 %copy-start = (bf16[256,5120]{1,0:T(8,128)(2,1)S(1)}, bf16[256,5120]{1,0:T(8,128)(2,1)}, u32[]{:S(2)}) copy-start(bf16[256,5120]{1,0:T(8,128)(2,1)} %act.3) | copy-start | bytes 7864324
  9.5 2.9 %collective-permute-start = (bf16[256,512]{1,0:T(8,128)(2,1)}, bf16[256,512]{1,0:T(8,128)(2,1)S(1)}, u32[]{:S(2)}, u32[]{:S(2)}) collective-permute-start(bf16[256,512]{1,0:T(8,128)(2,1)} %get-tuple-element.31), channel_id=1, source_target_pairs={{0,4},{4,0},{1,5},{5,1},{2,6},{6,2},{3,7},{7,3},{8,12},{12,8},{9,1... | collective-permute-start | bytes 786440 | tf_op jit(solution)/shard_map/ppermute | solution.py:543
  13.3 27.5 %copy-start.4 = (bf16[256,256]{1,0:T(8,128)(2,1)S(1)}, bf16[256,256]{1,0:T(8,128)(2,1)}, u32[]{:S(2)}) copy-start(bf16[256,256]{1,0:T(8,128)(2,1)} %get-tuple-element.42.own) | copy-start | bytes 393220
  13.3 9.1 %collective-permute-start.1 = (bf16[512,256]{1,0:T(8,128)(2,1)S(1)}, bf16[512,256]{1,0:T(8,128)(2,1)S(1)}, u32[]{:S(2)}, u32[]{:S(2)}) collective-permute-start(bf16[512,256]{1,0:T(8,128)(2,1)S(1)} %get-tuple-element.32.q0), channel_id=1, source_target_pairs={{0,8},{8,16},{16,24},{24,0},{1,9},{9,17},{17,25},{25,1},{2,10},{10... | collective-permute-start | bytes 786440 | tf_op jit(solution)/shard_map/ppermute | solution.py:552
  14.8 8.4 %collective-permute-start.4 = (bf16[512,256]{1,0:T(8,128)(2,1)S(1)}, bf16[512,256]{1,0:T(8,128)(2,1)S(1)}, u32[]{:S(2)}, u32[]{:S(2)}) collective-permute-start(bf16[512,256]{1,0:T(8,128)(2,1)S(1)} %get-tuple-element.33.k0), channel_id=1, source_target_pairs={{0,32},{32,64},{64,96},{96,0},{1,33},{33,65},{65,97},{97,1},{2,34}... | collective-permute-start | bytes 786440 | tf_op jit(solution)/shard_map/ppermute | solution.py:552
  16.0 13.8 %collective-permute-start.3 = (bf16[512,256]{1,0:T(8,128)(2,1)S(1)}, bf16[512,256]{1,0:T(8,128)(2,1)S(1)}, u32[]{:S(2)}, u32[]{:S(2)}) collective-permute-start(bf16[512,256]{1,0:T(8,128)(2,1)S(1)} %get-tuple-element.32.q0), channel_id=1, source_target_pairs={{0,24},{8,0},{16,8},{24,16},{1,25},{9,1},{17,9},{25,17},{2,26},{10... | collective-permute-start | bytes 786440 | tf_op jit(solution)/shard_map/ppermute | solution.py:552
  17.5 12.3 %collective-permute-start.6 = (bf16[512,256]{1,0:T(8,128)(2,1)S(1)}, bf16[512,256]{1,0:T(8,128)(2,1)S(1)}, u32[]{:S(2)}, u32[]{:S(2)}) collective-permute-start(bf16[512,256]{1,0:T(8,128)(2,1)S(1)} %get-tuple-element.33.k0), channel_id=1, source_target_pairs={{0,96},{32,0},{64,32},{96,64},{1,97},{33,1},{65,33},{97,65},{2,98}... | collective-permute-start | bytes 786440 | tf_op jit(solution)/shard_map/ppermute | solution.py:552
  22.5 8.0 %collective-permute-start.2 = (bf16[512,256]{1,0:T(8,128)(2,1)S(1)}, bf16[512,256]{1,0:T(8,128)(2,1)S(1)}, u32[]{:S(2)}, u32[]{:S(2)}) collective-permute-start(bf16[512,256]{1,0:T(8,128)(2,1)S(1)} %collective-permute-done.1.q1), channel_id=1, source_target_pairs={{0,8},{8,16},{16,24},{24,0},{1,9},{9,17},{17,25},{25,1},{2,10},{10... | collective-permute-start | bytes 786440 | tf_op jit(solution)/shard_map/ppermute | solution.py:553
  23.2 7.5 %collective-permute-start.5 = (bf16[512,256]{1,0:T(8,128)(2,1)S(1)}, bf16[512,256]{1,0:T(8,128)(2,1)S(1)}, u32[]{:S(2)}, u32[]{:S(2)}) collective-permute-start(bf16[512,256]{1,0:T(8,128)(2,1)S(1)} %collective-permute-done.4.k1), channel_id=1, source_target_pairs={{0,32},{32,64},{64,96},{96,0},{1,33},{33,65},{65,97},{97,1},{2,34}... | collective-permute-start | bytes 786440 | tf_op jit(solution)/shard_map/ppermute | solution.py:553
  37.3 6.8 %collective-permute-start.9 = (f32[48,128]{1,0:T(8,128)S(1)}, f32[48,128]{1,0:T(8,128)S(1)}, u32[]{:S(2)}, u32[]{:S(2)}) collective-permute-start(f32[48,128]{1,0:T(8,128)S(1)} %row_stats.1.s0), channel_id=1, source_target_pairs={{0,24},{8,0},{16,8},{24,16},{1,25},{9,1},{17,9},{25,17},{2,26},{10... | collective-permute-start | bytes 73736 | tf_op jit(solution)/shard_map/ppermute | solution.py:547
  39.5 4.6 %collective-permute-start.8 = (f32[48,128]{1,0:T(8,128)S(1)}, f32[48,128]{1,0:T(8,128)S(1)}, u32[]{:S(2)}, u32[]{:S(2)}) collective-permute-start(f32[48,128]{1,0:T(8,128)S(1)} %row_stats.1.s0), channel_id=1, source_target_pairs={{0,16},{8,24},{16,0},{24,8},{1,17},{9,25},{17,1},{25,9},{2,18},{10... | collective-permute-start | bytes 73736 | tf_op jit(solution)/shard_map/ppermute | solution.py:547
  40.4 3.9 %collective-permute-start.7 = (f32[48,128]{1,0:T(8,128)S(1)}, f32[48,128]{1,0:T(8,128)S(1)}, u32[]{:S(2)}, u32[]{:S(2)}) collective-permute-start(f32[48,128]{1,0:T(8,128)S(1)} %row_stats.1.s0), channel_id=1, source_target_pairs={{0,8},{8,16},{16,24},{24,0},{1,9},{9,17},{17,25},{25,1},{2,10},{10... | collective-permute-start | bytes 73736 | tf_op jit(solution)/shard_map/ppermute | solution.py:547
  40.8 39.5 %copy-start.1 = (bf16[128,256]{1,0:T(8,128)(2,1)S(1)}, bf16[128,256]{1,0:T(8,128)(2,1)}, u32[]{:S(2)}) copy-start(bf16[128,256]{1,0:T(8,128)(2,1)} %uq.1) | copy-start | bytes 196612
  40.8 39.5 %copy-start.2 = (bf16[128,256]{1,0:T(8,128)(2,1)S(1)}, bf16[128,256]{1,0:T(8,128)(2,1)}, u32[]{:S(2)}) copy-start(bf16[128,256]{1,0:T(8,128)(2,1)} %uv.1) | copy-start | bytes 196612
  40.8 19.8 %collective-permute-start.16 = (bf16[256,256]{1,0:T(8,128)(2,1)S(1)}, bf16[256,256]{1,0:T(8,128)(2,1)S(1)}, u32[]{:S(2)}, u32[]{:S(2)}) collective-permute-start(bf16[256,256]{1,0:T(8,128)(2,1)S(1)} %copy-done.4), channel_id=1, source_target_pairs={{0,4},{4,0},{1,5},{5,1},{2,6},{6,2},{3,7},{7,3},{8,12},{12,8},{9,1... | collective-permute-start | bytes 393224 | tf_op jit(solution)/shard_map/ppermute | solution.py:543
  56.3 5.5 %collective-permute-start.11 = (bf16[512,128]{1,0:T(8,128)(2,1)S(1)}, bf16[512,128]{1,0:T(8,128)(2,1)S(1)}, u32[]{:S(2)}, u32[]{:S(2)}) collective-permute-start(bf16[512,128]{1,0:T(8,128)(2,1)S(1)} %get-tuple-element.37), channel_id=1, source_target_pairs={{0,64},{32,96},{64,0},{96,32},{1,65},{33,97},{65,1},{97,33},{2,66}... | collective-permute-start | bytes 393224 | tf_op jit(solution)/shard_map/ppermute | solution.py:557
  58.1 11.5 %collective-permute-start.13 = (bf16[512,384]{1,0:T(8,128)(2,1)S(1)}, bf16[512,384]{1,0:T(8,128)(2,1)S(1)}, u32[]{:S(2)}, u32[]{:S(2)}) collective-permute-start(bf16[512,384]{1,0:T(8,128)(2,1)S(1)} %get-tuple-element.39), channel_id=1, source_target_pairs={{0,24},{8,0},{16,8},{24,16},{1,25},{9,1},{17,9},{25,17},{2,26},{10... | collective-permute-start | bytes 1179656 | tf_op jit(solution)/shard_map/ppermute | solution.py:557
  59.3 10.2 %collective-permute-start.14 = (bf16[512,384]{1,0:T(8,128)(2,1)S(1)}, bf16[512,384]{1,0:T(8,128)(2,1)S(1)}, u32[]{:S(2)}, u32[]{:S(2)}) collective-permute-start(bf16[512,384]{1,0:T(8,128)(2,1)S(1)} %get-tuple-element.40), channel_id=1, source_target_pairs={{0,16},{8,24},{16,0},{24,8},{1,17},{9,25},{17,1},{25,9},{2,18},{10... | collective-permute-start | bytes 1179656 | tf_op jit(solution)/shard_map/ppermute | solution.py:557
  60.7 19.6 %collective-permute-start.15 = (bf16[512,384]{1,0:T(8,128)(2,1)S(1)}, bf16[512,384]{1,0:T(8,128)(2,1)S(1)}, u32[]{:S(2)}, u32[]{:S(2)}) collective-permute-start(bf16[512,384]{1,0:T(8,128)(2,1)S(1)} %get-tuple-element.41), channel_id=1, source_target_pairs={{0,8},{8,16},{16,24},{24,0},{1,9},{9,17},{17,25},{25,1},{2,10},{10... | collective-permute-start | bytes 1179656 | tf_op jit(solution)/shard_map/ppermute | solution.py:557
  60.7 6.9 %collective-permute-start.10 = (f32[512,128]{1,0:T(8,128)S(1)}, f32[512,128]{1,0:T(8,128)S(1)}, u32[]{:S(2)}, u32[]{:S(2)}) collective-permute-start(f32[512,128]{1,0:T(8,128)S(1)} %get-tuple-element.36), channel_id=1, source_target_pairs={{0,96},{32,0},{64,32},{96,64},{1,97},{33,1},{65,33},{97,65},{2,98}... | collective-permute-start | bytes 786440 | tf_op jit(solution)/shard_map/ppermute | solution.py:557
  61.8 7.7 %collective-permute-start.12 = (f32[512,128]{1,0:T(8,128)S(1)}, f32[512,128]{1,0:T(8,128)S(1)}, u32[]{:S(2)}, u32[]{:S(2)}) collective-permute-start(f32[512,128]{1,0:T(8,128)S(1)} %get-tuple-element.38), channel_id=1, source_target_pairs={{0,32},{32,64},{64,96},{96,0},{1,33},{33,65},{65,97},{97,1},{2,34}... | collective-permute-start | bytes 786440 | tf_op jit(solution)/shard_map/ppermute | solution.py:557
  81.2 1.7 %collective-permute-start.17 = (f32[256,256]{1,0:T(8,128)S(1)}, f32[256,256]{1,0:T(8,128)S(1)}, u32[]{:S(2)}, u32[]{:S(2)}) collective-permute-start(f32[256,256]{1,0:T(8,128)S(1)} %get-tuple-element.44), channel_id=1, source_target_pairs={{0,4},{4,0},{1,5},{5,1},{2,6},{6,2},{3,7},{7,3},{8,12},{12,8},{9,1... | collective-permute-start | bytes 786440 | tf_op jit(solution)/shard_map/ppermute | solution.py:543
  82.9 9.5 %collective-permute-start.20 = (bf16[256,256]{1,0:T(8,128)(2,1)S(1)}, bf16[256,256]{1,0:T(8,128)(2,1)S(1)}, u32[]{:S(2)}, u32[]{:S(2)}) collective-permute-start(bf16[256,256]{1,0:T(8,128)(2,1)S(1)} %get-tuple-element.46), channel_id=1, source_target_pairs={{0,3},{1,0},{2,1},{3,2},{4,7},{5,4},{6,5},{7,6},{8,11},{9,8},{10,9... | collective-permute-start | bytes 393224 | tf_op jit(solution)/shard_map/ppermute | solution.py:547
  86.7 6.0 %collective-permute-start.19 = (bf16[256,256]{1,0:T(8,128)(2,1)S(1)}, bf16[256,256]{1,0:T(8,128)(2,1)S(1)}, u32[]{:S(2)}, u32[]{:S(2)}) collective-permute-start(bf16[256,256]{1,0:T(8,128)(2,1)S(1)} %get-tuple-element.46), channel_id=1, source_target_pairs={{0,2},{1,3},{2,0},{3,1},{4,6},{5,7},{6,4},{7,5},{8,10},{9,11},{10,... | collective-permute-start | bytes 393224 | tf_op jit(solution)/shard_map/ppermute | solution.py:547
  86.8 9.1 %collective-permute-start.18 = (bf16[256,256]{1,0:T(8,128)(2,1)S(1)}, bf16[256,256]{1,0:T(8,128)(2,1)S(1)}, u32[]{:S(2)}, u32[]{:S(2)}) collective-permute-start(bf16[256,256]{1,0:T(8,128)(2,1)S(1)} %get-tuple-element.46), channel_id=1, source_target_pairs={{0,1},{1,2},{2,3},{3,0},{4,5},{5,6},{6,7},{7,4},{8,9},{9,10},{10,1... | collective-permute-start | bytes 393224 | tf_op jit(solution)/shard_map/ppermute | solution.py:547
  96.3 2.6 %collective-permute-start.21 = (f32[640,256]{1,0:T(8,128)S(1)}, f32[640,256]{1,0:T(8,128)S(1)}, u32[]{:S(2)}, u32[]{:S(2)}) collective-permute-start(f32[640,256]{1,0:T(8,128)S(1)} %get-tuple-element.48), channel_id=1, source_target_pairs={{0,4},{4,0},{1,5},{5,1},{2,6},{6,2},{3,7},{7,3},{8,12},{12,8},{9,1... | collective-permute-start | bytes 1966088 | tf_op jit(solution)/shard_map/ppermute | solution.py:543
  99.7 13.0 %all-to-all-start = ((bf16[16,48,256]{2,1,0:T(8,128)(2,1)}), bf16[16,48,256]{2,1,0:T(8,128)(2,1)S(1)}, u32[]{:S(2)}, u32[]{:S(2)}) async-start(bf16[16,48,256]{2,1,0:T(8,128)(2,1)} %pack.1), calls=%async_computation | async-start | bytes 786432 | tf_op jit(solution)/shard_map/all_to_all | solution.py:575
  103.4 1.6 %collective-permute-start.22 = (bf16[256,128]{1,0:T(8,128)(2,1)S(1)}, bf16[256,128]{1,0:T(8,128)(2,1)S(1)}, u32[]{:S(2)}, u32[]{:S(2)}) collective-permute-start(bf16[256,128]{1,0:T(8,128)(2,1)S(1)} %get-tuple-element.50), channel_id=1, source_target_pairs={{0,4},{4,0},{1,5},{5,1},{2,6},{6,2},{3,7},{7,3},{8,12},{12,8},{9,1... | collective-permute-start | bytes 196616 | tf_op jit(solution)/shard_map/ppermute | solution.py:543
  139.0 6.4 %collective-permute-start.23 = (bf16[64,48,256]{2,1,0:T(8,128)(2,1)S(1)}, bf16[64,48,256]{2,1,0:T(8,128)(2,1)S(1)}, u32[]{:S(2)}, u32[]{:S(2)}) collective-permute-start(bf16[64,48,256]{2,1,0:T(8,128)(2,1)S(1)} %all_to_all.10.src), channel_id=1, source_target_pairs={{0,4},{4,0},{1,5},{5,1},{2,6},{6,2},{3,7},{7,3},{8,12},{12,8},{9,1... | collective-permute-start | bytes 4718600 | tf_op jit(solution)/shard_map/ppermute | solution.py:543
  (2 other events, 23.9 us)
